TPU v7x, 32 devices: a whole 2x2x4 slice. The times are simulated.
32 devices in a mesh: dp: 4 (over y, x), mp: 8 (over z, core).
Axes of the slice: x: 2, y: 2, z: 4, core: 2. Of those that a mesh axis runs over, the one named last changes fastest.
Arguments:
- image: bfloat16 [4, 32, 128, 1024], P('dp', 'mp'), may hold values from -24 to 24
- embedding: bfloat16 [4, 1024], P('dp'), may hold values from -6 to 6
- extents: int32 [4, 2], P('dp'), may hold values from 8 to 64, as said below
- gain_first: float32 [1024], replicated, may hold values from 0.1 to 1.9
- conv_first: bfloat16 [9, 1024, 1024], P(None, 'mp'), may hold values from -0.0625 to 0.0625
- gain_second: float32 [1024], replicated, may hold values from 0.1 to 1.9
- conv_second: bfloat16 [9, 1024, 1024], P(None, 'mp'), may hold values from -0.0625 to 0.0625
- shift_weight: bfloat16 [1024, 1024], P(None, 'mp'), may hold values from -0.1875 to 0.1875
- down_weight: bfloat16 [4, 1024, 2048], P(None, 'mp'), may hold values from -0.09375 to 0.09375
- ada_weight: bfloat16 [1024, 8192], P(None, 'mp'), may hold values from -0.09375 to 0.09375
- qkv_weight: bfloat16 [3, 2048, 2048], P(None, None, 'mp'), may hold values from -0.125 to 0.125
- out_weight: bfloat16 [2048, 2048], P('mp'), may hold values from -1 to 1
- up_weight: bfloat16 [2048, 8192], P(None, 'mp'), may hold values from -0.125 to 0.125
- proj_weight: bfloat16 [8192, 2048], P('mp'), may hold values from -0.0625 to 0.0625
- cotangent: bfloat16 [4, 16, 64, 2048], P('dp', 'mp'), may hold values from -6 to 6
Outputs:
- output: bfloat16 [4, 16, 64, 2048], P('dp', 'mp')
- image_grad: bfloat16 [4, 32, 128, 1024], P('dp', 'mp')
- embedding_grad: float32 [4, 1024], P('dp')
- gain_first_grad: float32 [1024], P(('dp', 'mp'))
- conv_first_grad: float32 [9, 1024, 1024], P(None, 'dp', 'mp')
- gain_second_grad: float32 [1024], P(('dp', 'mp'))
- conv_second_grad: float32 [9, 1024, 1024], P(None, 'dp', 'mp')
- shift_weight_grad: float32 [1024, 1024], P('dp', 'mp')
- down_weight_grad: float32 [4, 1024, 2048], P(None, 'dp', 'mp')
- ada_weight_grad: float32 [1024, 8192], P('dp', 'mp')
- qkv_weight_grad: float32 [3, 2048, 2048], P(None, 'dp', 'mp')
- out_weight_grad: float32 [2048, 2048], P('mp', 'dp')
- up_weight_grad: float32 [2048, 8192], P('dp', 'mp')
- proj_weight_grad: float32 [8192, 2048], P('mp', 'dp')
Inputs may be any that keep to these rules, and one draw needn't show every extreme that they name: extents[b, 0] is the height and extents[b, 1] the width, in tokens, of the valid top-left part of image b; heights are 8 or more and widths 64 // 4 or more; in every draw one image is valid everywhere.
All inputs are finite; a program needn't handle non-finite values.
Results may differ from a plain program's by a relative error of at most 0.028.
Values may be sent and summed in bfloat16 or wider, within the bound.
A program may use at most 448 MiB of HBM per device.

v0:
```python
from functools import partial
import math

import jax
import jax.numpy as jnp
from jax import lax
from jax.sharding import PartitionSpec as P

HEAD_DIM = 128
GROUPS = 32


GROUP_EPSILON = 1e-05
LAYER_EPSILON = 1e-06
MASKED_SCORE = -1000000000.0
PRECISE = lax.Precision.HIGHEST


def padded_2(block, sides, width):
    for axis, dim in sides:
        count = lax.axis_size(axis)
        forward = [(i, i + 1) for i in range(count - 1)]
        backward = [(target, source) for source, target in forward]
        low = lax.ppermute(
            lax.slice_in_dim(block, block.shape[dim] - width, None, axis=dim), axis, forward
        )
        high = lax.ppermute(lax.slice_in_dim(block, 0, width, axis=dim), axis, backward)
        block = jnp.concatenate([low, block, high], axis=dim)
    return block


def strip_padded(strip):
    rimmed = padded_2(strip, (("mp", 0),), 1)
    return jnp.pad(rimmed, ((0, 0), (1, 1), (0, 0)))


def unfolded(padded, row_count, col_count, flipped):
    pieces = []
    for tap_index in range(9):
        row_off, col_off = divmod(tap_index, 3)
        if flipped:
            row_off, col_off = (2 - row_off, 2 - col_off)
        pieces.append(padded[row_off : row_off + row_count, col_off : col_off + col_count])
    stacked = jnp.stack(pieces, axis=2)
    return stacked.reshape(row_count * col_count, 9, padded.shape[-1])


def group_totals(first_term, second_term):
    return lax.psum((first_term, second_term), "mp")


def group_sums(values):
    return jnp.sum(values.reshape(values.shape[0], GROUPS, -1), axis=(0, 2))


def spread_groups(per_group, channel_count):
    return jnp.repeat(per_group, channel_count // GROUPS)


def group_forward(values, pixel_total):
    channel_count = values.shape[1]
    counted = pixel_total * (channel_count // GROUPS)
    first_sum, second_sum = group_totals(group_sums(values), group_sums(values * values))
    average = first_sum / counted
    inverse = lax.rsqrt(second_sum / counted - average * average + GROUP_EPSILON)
    normed = (values - spread_groups(average, channel_count)) * spread_groups(
        inverse, channel_count
    )
    return (normed, inverse)


def group_backward(incoming, pre_act, normed, inverse, gain_vec, pixel_total):
    sigmoid_part = jax.nn.sigmoid(pre_act)
    through = incoming * sigmoid_part * (1.0 + pre_act * (1.0 - sigmoid_part))
    gain_part = jnp.sum(through * normed, axis=0)
    scaled = through * gain_vec
    channel_count = normed.shape[1]
    counted = pixel_total * (channel_count // GROUPS)
    first_sum, second_sum = group_totals(group_sums(scaled), group_sums(scaled * normed))
    first_mean = spread_groups(first_sum / counted, channel_count)
    second_mean = spread_groups(second_sum / counted, channel_count)
    outgoing = spread_groups(inverse, channel_count) * (scaled - first_mean - normed * second_mean)
    return (outgoing, gain_part)


def layer_forward(stream):
    centre = stream - jnp.mean(stream, axis=1, keepdims=True)
    inverse = lax.rsqrt(jnp.mean(centre * centre, axis=1, keepdims=True) + LAYER_EPSILON)
    return (centre * inverse, inverse)


def layer_backward(incoming, normed, inverse, scale_vec):
    through = incoming * (1.0 + scale_vec)
    outgoing = inverse * (
        through
        - jnp.mean(through, axis=1, keepdims=True)
        - normed * jnp.mean(through * normed, axis=1, keepdims=True)
    )
    return (outgoing, jnp.sum(incoming * normed, axis=0), jnp.sum(incoming, axis=0))


def gather_tokens(local_rows, row_fn):
    return row_fn(lax.all_gather(local_rows, "mp", axis=0, tiled=True), jnp.int32(0))


def scatter_tokens(term_fn, row_count):
    return lax.psum_scatter(
        term_fn(jnp.int32(0), row_count * lax.axis_size("mp")).astype(jnp.bfloat16),
        "mp",
        scatter_dimension=0,
        tiled=True,
    ).astype(jnp.float32)


def fold_tokens(local_rows, fold_fn, initial):
    return fold_fn(initial, lax.all_gather(local_rows, "mp", axis=0, tiled=True), jnp.int32(0))


def gain_order(vector, devices_dp, devices_mp):
    return vector.reshape(devices_dp, devices_mp, -1).transpose(1, 0, 2).reshape(-1)


def attend_forward(queries, key_rows, value_rows, key_valid, block_rows):
    score_scale = 1.0 / math.sqrt(queries.shape[-1])

    def one_block(query_block):
        raw_scores = jnp.einsum(
            "qhd,khd->hqk", query_block, key_rows, preferred_element_type=jnp.float32
        )
        logits = jnp.where(key_valid[None, None, :], raw_scores * score_scale, MASKED_SCORE)
        peak_score = jnp.max(logits, axis=-1, keepdims=True)
        exponent = jnp.exp(logits - peak_score)
        totals = jnp.sum(exponent, axis=-1, keepdims=True)
        mix_weights = (exponent / totals).astype(jnp.bfloat16)
        mixed_heads = jnp.einsum(
            "hqk,khd->qhd", mix_weights, value_rows, preferred_element_type=jnp.float32
        )
        return (mixed_heads, (peak_score + jnp.log(totals))[..., 0])

    blocks = queries.reshape(-1, block_rows, queries.shape[1], queries.shape[2])
    mixed_heads, log_totals = lax.map(one_block, blocks)
    return (mixed_heads.reshape(queries.shape), log_totals)


def attend_backward(queries, key_rows, value_rows, key_valid, log_totals, grad_mixed, block_rows):
    score_scale = 1.0 / math.sqrt(queries.shape[-1])
    block_shape = (-1, block_rows, queries.shape[1], queries.shape[2])

    def one_block(running, inputs):
        grad_keys, grad_values = running
        query_block, grad_block, log_block = inputs
        raw_scores = jnp.einsum(
            "qhd,khd->hqk", query_block, key_rows, preferred_element_type=jnp.float32
        )
        logits = jnp.where(key_valid[None, None, :], raw_scores * score_scale, MASKED_SCORE)
        mix_weights = jnp.exp(logits - log_block[..., None])
        grad_weights = jnp.einsum(
            "qhd,khd->hqk", grad_block, value_rows, preferred_element_type=jnp.float32
        )
        inner_sum = jnp.sum(mix_weights * grad_weights, axis=-1, keepdims=True)
        grad_scores = (mix_weights * (grad_weights - inner_sum) * score_scale).astype(jnp.bfloat16)
        grad_query = jnp.einsum(
            "hqk,khd->qhd", grad_scores, key_rows, preferred_element_type=jnp.float32
        )
        grad_keys = grad_keys + jnp.einsum(
            "hqk,qhd->khd", grad_scores, query_block, preferred_element_type=jnp.float32
        )
        grad_values = grad_values + jnp.einsum(
            "hqk,qhd->khd",
            mix_weights.astype(jnp.bfloat16),
            grad_block,
            preferred_element_type=jnp.float32,
        )
        return ((grad_keys, grad_values), grad_query)

    zero_rows = jnp.zeros(key_rows.shape, jnp.float32)
    (grad_keys, grad_values), grad_query = lax.scan(
        one_block,
        (zero_rows, zero_rows),
        (queries.reshape(block_shape), grad_mixed.reshape(block_shape), log_totals),
    )
    return (grad_query.reshape(queries.shape), grad_keys, grad_values)


def local(
    image,
    embedding,
    extents,
    gain_first,
    conv_first,
    gain_second,
    conv_second,
    shift_weight,
    down_weight,
    ada_weight,
    qkv_weight,
    out_weight,
    up_weight,
    proj_weight,
    cotangent,
):
    strip_rows, canvas_cols, channel_count = (image.shape[1], image.shape[2], image.shape[3])
    width_all = out_weight.shape[1]
    devices_mp = lax.axis_size("mp")
    devices_dp = lax.axis_size("dp")
    pixel_count = strip_rows * canvas_cols
    pixel_total = pixel_count * devices_mp
    token_rows = strip_rows // 2
    token_cols = canvas_cols // 2
    local_tokens = token_rows * token_cols
    token_total = local_tokens * devices_mp
    block_rows = min(512, token_total)
    local_width = out_weight.shape[0]
    head_count = local_width // HEAD_DIM
    hidden_local = up_weight.shape[1]
    kernel_first, kernel_second, kernel_down = (
        lax.all_gather(conv_first, "mp", axis=1, tiled=True),
        lax.all_gather(conv_second, "mp", axis=1, tiled=True),
        lax.all_gather(down_weight, "mp", axis=1, tiled=True),
    )
    shift_full, modulation = (
        lax.all_gather(
            jnp.dot(embedding, shift_weight, preferred_element_type=jnp.float32),
            "mp",
            axis=1,
            tiled=True,
        ),
        lax.all_gather(
            jnp.dot(embedding, ada_weight, preferred_element_type=jnp.float32),
            "mp",
            axis=1,
            tiled=True,
        ),
    )
    shift_vector = shift_full[0]
    scale_attend = modulation[0, :width_all]
    shift_attend = modulation[0, width_all : 2 * width_all]
    scale_mlp = modulation[0, 2 * width_all : 3 * width_all]
    shift_mlp = modulation[0, 3 * width_all :]
    base_pixels = image[0].astype(jnp.float32).reshape(pixel_count, channel_count)
    normed_first, inverse_first = group_forward(base_pixels, pixel_total)
    pre_first = normed_first * gain_first
    hidden_first = jax.nn.silu(pre_first).astype(jnp.bfloat16)
    patch_first = unfolded(
        strip_padded(hidden_first.reshape(strip_rows, canvas_cols, channel_count)),
        strip_rows,
        canvas_cols,
        False,
    )
    conv_output = (
        jnp.einsum("ptc,tcd->pd", patch_first, kernel_first, preferred_element_type=jnp.float32)
        + shift_vector
    )
    normed_second, inverse_second = group_forward(conv_output, pixel_total)
    pre_second = normed_second * gain_second
    hidden_second = jax.nn.silu(pre_second).astype(jnp.bfloat16)
    patch_second = unfolded(
        strip_padded(hidden_second.reshape(strip_rows, canvas_cols, channel_count)),
        strip_rows,
        canvas_cols,
        False,
    )
    residual = base_pixels + jnp.einsum(
        "ptc,tcd->pd", patch_second, kernel_second, preferred_element_type=jnp.float32
    )
    residual_low = residual.astype(jnp.bfloat16).reshape(
        token_rows, 2, token_cols, 2, channel_count
    )
    down_patch = residual_low.transpose(0, 2, 1, 3, 4).reshape(local_tokens, 4 * channel_count)
    down_matrix = kernel_down.reshape(4 * channel_count, width_all)
    stream = jnp.dot(down_patch, down_matrix, preferred_element_type=jnp.float32)
    normed_attend, inverse_attend = layer_forward(stream)
    input_attend = (normed_attend * (1.0 + scale_attend) + shift_attend).astype(jnp.bfloat16)

    def project_rows(piece, start):
        produced = jnp.einsum(
            "le,jef->ljf", piece, qkv_weight, preferred_element_type=jnp.float32
        ).astype(jnp.bfloat16)
        return jnp.concatenate([piece, produced.reshape(piece.shape[0], 3 * local_width)], axis=1)

    gathered_attend = gather_tokens(input_attend, project_rows)
    all_attend = gathered_attend[:, :width_all]
    qkv_rows = gathered_attend[:, width_all:].reshape(token_total, 3, head_count, HEAD_DIM)
    queries = qkv_rows[:, 0]
    key_rows = qkv_rows[:, 1]
    value_rows = qkv_rows[:, 2]
    token_index = jnp.arange(token_total, dtype=jnp.int32)
    key_valid = (token_index // token_cols < extents[0, 0]) & (
        token_index % token_cols < extents[0, 1]
    )
    mixed_heads, log_totals = attend_forward(queries, key_rows, value_rows, key_valid, block_rows)
    mixed_low = mixed_heads.reshape(token_total, local_width).astype(jnp.bfloat16)

    def out_rows(start, row_count):
        return jnp.dot(mixed_low, out_weight, preferred_element_type=jnp.float32)

    stream_mid = stream + scatter_tokens(out_rows, local_tokens)
    normed_mlp, inverse_mlp = layer_forward(stream_mid)
    input_mlp = (normed_mlp * (1.0 + scale_mlp) + shift_mlp).astype(jnp.bfloat16)

    def expand_rows(piece, start):
        upper_piece = jnp.dot(piece, up_weight, preferred_element_type=jnp.float32)
        return jnp.concatenate(
            [piece, jax.nn.gelu(upper_piece, approximate=True).astype(jnp.bfloat16)], axis=1
        )

    gathered_mlp = gather_tokens(input_mlp, expand_rows)
    all_mlp = gathered_mlp[:, :width_all]
    activated = gathered_mlp[:, width_all:]

    def proj_rows(start, row_count):
        return jnp.dot(activated, proj_weight, preferred_element_type=jnp.float32)

    final_stream = stream_mid + scatter_tokens(proj_rows, local_tokens)
    output = final_stream.astype(jnp.bfloat16).reshape(1, token_rows, token_cols, width_all)
    grad_final = cotangent[0].reshape(local_tokens, width_all).astype(jnp.float32)
    grad_final_low = grad_final.astype(jnp.bfloat16)

    def fold_mlp(running, piece, start):
        grad_proj = jnp.einsum("lf,le->fe", activated, piece, preferred_element_type=jnp.float32)
        grad_act = jnp.einsum("le,fe->lf", piece, proj_weight, preferred_element_type=jnp.float32)
        return (grad_proj, grad_act)

    grad_proj, grad_act = fold_tokens(
        grad_final_low,
        fold_mlp,
        (
            jnp.zeros((hidden_local, width_all), jnp.float32),
            jnp.zeros((token_total, hidden_local), jnp.float32),
        ),
    )
    upper_proj = jnp.dot(all_mlp, up_weight, preferred_element_type=jnp.float32)
    gelu_pull = jax.vjp(partial(jax.nn.gelu, approximate=True), upper_proj)[1]
    grad_upper = gelu_pull(grad_act)[0].astype(jnp.bfloat16)
    grad_up = jnp.einsum("le,lf->ef", all_mlp, grad_upper, preferred_element_type=jnp.float32)

    def back_mlp_rows(start, row_count):
        return jnp.einsum("lf,ef->le", grad_upper, up_weight, preferred_element_type=jnp.float32)

    grad_normed_mlp = scatter_tokens(back_mlp_rows, local_tokens)
    grad_mid_norm, grad_scale_mlp, grad_shift_mlp = layer_backward(
        grad_normed_mlp, normed_mlp, inverse_mlp, scale_mlp
    )
    grad_mid = grad_final + grad_mid_norm
    grad_mid_low = grad_mid.astype(jnp.bfloat16)

    def fold_attend(running, piece, start):
        grad_out = jnp.einsum("lh,le->he", mixed_low, piece, preferred_element_type=jnp.float32)
        grad_mixed = jnp.einsum("le,he->lh", piece, out_weight, preferred_element_type=jnp.float32)
        return (grad_out, grad_mixed)

    grad_out, grad_mixed = fold_tokens(
        grad_mid_low,
        fold_attend,
        (
            jnp.zeros((local_width, width_all), jnp.float32),
            jnp.zeros((token_total, local_width), jnp.float32),
        ),
    )
    grad_mixed_low = grad_mixed.astype(jnp.bfloat16).reshape(token_total, head_count, HEAD_DIM)
    grad_query, grad_keys, grad_values = attend_backward(
        queries, key_rows, value_rows, key_valid, log_totals, grad_mixed_low, block_rows
    )
    grad_qkv = (
        jnp.stack([grad_query, grad_keys, grad_values], axis=1)
        .astype(jnp.bfloat16)
        .reshape(token_total, 3, local_width)
    )
    grad_qkv_weight = jnp.einsum(
        "le,ljf->jef", all_attend, grad_qkv, preferred_element_type=jnp.float32
    )

    def back_attend_rows(start, row_count):
        return jnp.einsum("ljf,jef->le", grad_qkv, qkv_weight, preferred_element_type=jnp.float32)

    grad_normed_attend = scatter_tokens(back_attend_rows, local_tokens)
    grad_stream_norm, grad_scale_attend, grad_shift_attend = layer_backward(
        grad_normed_attend, normed_attend, inverse_attend, scale_attend
    )
    grad_stream = grad_mid + grad_stream_norm
    grad_stream_low = grad_stream.astype(jnp.bfloat16)
    grad_down = jnp.einsum(
        "lk,le->ke", down_patch, grad_stream_low, preferred_element_type=jnp.float32
    ).reshape(4, channel_count, width_all)
    grad_tap_patch = jnp.einsum(
        "le,ke->lk", grad_stream_low, down_matrix, preferred_element_type=jnp.float32
    )
    grad_residual = (
        grad_tap_patch.reshape(token_rows, token_cols, 2, 2, channel_count)
        .transpose(0, 2, 1, 3, 4)
        .reshape(pixel_count, channel_count)
    )
    grad_residual_low = grad_residual.astype(jnp.bfloat16)
    back_second = unfolded(
        strip_padded(grad_residual_low.reshape(strip_rows, canvas_cols, channel_count)),
        strip_rows,
        canvas_cols,
        True,
    )
    grad_hidden_second = jnp.einsum(
        "ptd,tcd->pc", back_second, kernel_second, preferred_element_type=jnp.float32
    )
    grad_conv_output, grad_gain_second = group_backward(
        grad_hidden_second, pre_second, normed_second, inverse_second, gain_second, pixel_total
    )
    grad_shift = jnp.sum(grad_conv_output, axis=0)
    grad_conv_low = grad_conv_output.astype(jnp.bfloat16)
    back_first = unfolded(
        strip_padded(grad_conv_low.reshape(strip_rows, canvas_cols, channel_count)),
        strip_rows,
        canvas_cols,
        True,
    )
    grad_hidden_first = jnp.einsum(
        "ptd,tcd->pc", back_first, kernel_first, preferred_element_type=jnp.float32
    )
    grad_base, grad_gain_first = group_backward(
        grad_hidden_first, pre_first, normed_first, inverse_first, gain_first, pixel_total
    )
    image_grad = (
        (grad_residual + grad_base)
        .astype(jnp.bfloat16)
        .reshape(1, strip_rows, canvas_cols, channel_count)
    )
    grad_modulation = jnp.concatenate(
        [grad_scale_attend, grad_shift_attend, grad_scale_mlp, grad_shift_mlp]
    )
    shift_columns, ada_columns, gain_first_cols, gain_second_cols = (
        lax.psum_scatter(
            grad_shift[None].astype(jnp.bfloat16), "mp", scatter_dimension=1, tiled=True
        ).astype(jnp.float32),
        lax.psum_scatter(
            grad_modulation[None].astype(jnp.bfloat16), "mp", scatter_dimension=1, tiled=True
        ).astype(jnp.float32),
        lax.psum_scatter(
            gain_order(grad_gain_first, devices_dp, devices_mp).astype(jnp.bfloat16),
            "mp",
            scatter_dimension=0,
            tiled=True,
        ).astype(jnp.float32),
        lax.psum_scatter(
            gain_order(grad_gain_second, devices_dp, devices_mp).astype(jnp.bfloat16),
            "mp",
            scatter_dimension=0,
            tiled=True,
        ).astype(jnp.float32),
    )
    embed_float = embedding.astype(jnp.float32)
    grad_shift_weight = jnp.dot(embed_float.T, shift_columns, precision=PRECISE)
    grad_ada_weight = jnp.dot(embed_float.T, ada_columns, precision=PRECISE)
    embed_term = jnp.dot(
        shift_columns, shift_weight.astype(jnp.float32).T, precision=PRECISE
    ) + jnp.dot(ada_columns, ada_weight.astype(jnp.float32).T, precision=PRECISE)
    embedding_grad = lax.psum(embed_term, "mp")
    grad_conv_first = jnp.einsum(
        "ptc,pd->tcd", patch_first, grad_conv_low, preferred_element_type=jnp.float32
    )
    grad_conv_second = jnp.einsum(
        "ptc,pd->tcd", patch_second, grad_residual_low, preferred_element_type=jnp.float32
    )
    first_cols, second_cols, down_cols = (
        lax.psum_scatter(
            grad_conv_first.astype(jnp.bfloat16), "mp", scatter_dimension=2, tiled=True
        ).astype(jnp.float32),
        lax.psum_scatter(
            grad_conv_second.astype(jnp.bfloat16), "mp", scatter_dimension=2, tiled=True
        ).astype(jnp.float32),
        lax.psum_scatter(
            grad_down.astype(jnp.bfloat16), "mp", scatter_dimension=2, tiled=True
        ).astype(jnp.float32),
    )
    summed = (
        lax.psum_scatter(
            first_cols.astype(jnp.bfloat16), "dp", scatter_dimension=1, tiled=True
        ).astype(jnp.float32),
        lax.psum_scatter(
            second_cols.astype(jnp.bfloat16), "dp", scatter_dimension=1, tiled=True
        ).astype(jnp.float32),
        lax.psum_scatter(
            down_cols.astype(jnp.bfloat16), "dp", scatter_dimension=1, tiled=True
        ).astype(jnp.float32),
        lax.psum_scatter(
            gain_first_cols.astype(jnp.bfloat16), "dp", scatter_dimension=0, tiled=True
        ).astype(jnp.float32),
        lax.psum_scatter(
            gain_second_cols.astype(jnp.bfloat16), "dp", scatter_dimension=0, tiled=True
        ).astype(jnp.float32),
        lax.psum_scatter(
            grad_shift_weight.astype(jnp.bfloat16), "dp", scatter_dimension=0, tiled=True
        ).astype(jnp.float32),
        lax.psum_scatter(
            grad_ada_weight.astype(jnp.bfloat16), "dp", scatter_dimension=0, tiled=True
        ).astype(jnp.float32),
        lax.psum_scatter(
            grad_qkv_weight.astype(jnp.bfloat16), "dp", scatter_dimension=1, tiled=True
        ).astype(jnp.float32),
        lax.psum_scatter(
            grad_out.astype(jnp.bfloat16), "dp", scatter_dimension=1, tiled=True
        ).astype(jnp.float32),
        lax.psum_scatter(
            grad_up.astype(jnp.bfloat16), "dp", scatter_dimension=0, tiled=True
        ).astype(jnp.float32),
        lax.psum_scatter(
            grad_proj.astype(jnp.bfloat16), "dp", scatter_dimension=1, tiled=True
        ).astype(jnp.float32),
    )
    return (
        output,
        image_grad,
        embedding_grad,
        summed[3],
        summed[0],
        summed[4],
        summed[1],
        summed[5],
        summed[2],
        summed[6],
        summed[7],
        summed[8],
        summed[9],
        summed[10],
    )


def solution(mesh):
    placed = (
        P("dp", "mp", None, None),
        P("dp", None),
        P("dp", None),
        P(),
        P(None, "mp", None),
        P(),
        P(None, "mp", None),
        P(None, "mp"),
        P(None, "mp", None),
        P(None, "mp"),
        P(None, None, "mp"),
        P("mp", None),
        P(None, "mp"),
        P("mp", None),
        P("dp", "mp", None, None),
    )
    return jax.shard_map(
        local,
        mesh=mesh,
        in_specs=placed,
        out_specs=(
            P("dp", "mp", None, None),
            P("dp", "mp", None, None),
            P("dp", None),
            P(("dp", "mp")),
            P(None, "dp", "mp"),
            P(("dp", "mp")),
            P(None, "dp", "mp"),
            P("dp", "mp"),
            P(None, "dp", "mp"),
            P("dp", "mp"),
            P(None, "dp", "mp"),
            P("mp", "dp"),
            P("dp", "mp"),
            P("mp", "dp"),
        ),
        check_vma=False,
    )
```

profile of v0, /device:TPU:9, one launch (start us, length us, event | category | flops | bytes accessed | tf_op | source)
XLA Modules:
  0.0 2125.8 jit_solution(9223546664565131111)
XLA Ops:
  11.4 10.2 all-reduce.11
  31.6 19.8 all-gather.2
  53.4 19.5 all-gather.1
  85.7 94.0 %all-gather.11.cloned.1.call-done = bf16[9,1024,1024]{2,1,0:T(8,128)(2,1)} async-done(((bf16[9,128,1024]{2,1,0:T(8,128)(2,1)}), bf16[9,1024,1024]{2,1,0:T(8,128)(2,1)}) %all-gather.11.cloned.1.call-update) | async-done | bytes 18874384 | tf_op jit(solution)/shard_map/all_gather | solution.py:217
  179.7 17.4 fusion.136
  197.5 15.4 all-reduce.10
  223.3 9.7 collective-permute-done.2
  248.0 102.9 %all-gather.13.cloned.1.call-done = bf16[9,1024,1024]{2,1,0:T(8,128)(2,1)} async-done(((bf16[9,128,1024]{2,1,0:T(8,128)(2,1)}), bf16[9,1024,1024]{2,1,0:T(8,128)(2,1)}) %all-gather.13.cloned.1.call-update) | async-done | bytes 18874384 | tf_op jit(solution)/shard_map/all_gather | solution.py:218
  350.9 17.4 fusion.99
  376.1 125.8 %all-gather.15.cloned.1.call-done = bf16[4,1024,2048]{2,1,0:T(8,128)(2,1)} async-done(((bf16[4,128,2048]{2,1,0:T(8,128)(2,1)}), bf16[4,1024,2048]{2,1,0:T(8,128)(2,1)}) %all-gather.15.cloned.1.call-update) | async-done | bytes 16777232 | tf_op jit(solution)/shard_map/all_gather | solution.py:219
  513.3 46.1 %all-gather.17.cloned.1.call-done = bf16[1024,2048]{1,0:T(8,128)(2,1)} async-done(((bf16[128,2048]{1,0:T(8,128)(2,1)}), bf16[1024,2048]{1,0:T(8,128)(2,1)}) %all-gather.17.cloned.1.call-update) | async-done | bytes 4194320 | tf_op jit(solution)/shard_map/all_gather | solution.py:103
  575.1 13.0 while.28
  595.6 47.9 %reduce-scatter.27.cloned.1.call-done = bf16[128,2048]{1,0:T(8,128)(2,1)} async-done(((bf16[1024,2048]{1,0:T(8,128)(2,1)}), bf16[128,2048]{1,0:T(8,128)(2,1)}) %reduce-scatter.27.cloned.1.call-update) | async-done | bytes 524304 | tf_op jit(solution)/shard_map/reduce_scatter | solution.py:107
  647.3 43.3 %all-gather.21.cloned.1.call-done = bf16[1024,2048]{1,0:T(8,128)(2,1)} async-done(((bf16[128,2048]{1,0:T(8,128)(2,1)}), bf16[1024,2048]{1,0:T(8,128)(2,1)}) %all-gather.21.cloned.1.call-update) | async-done | bytes 4194320 | tf_op jit(solution)/shard_map/all_gather | solution.py:116
  690.7 10.0 fusion.188
  700.7 38.1 %all-gather.19.cloned.1.call-done = bf16[1024,2048]{1,0:T(8,128)(2,1)} async-done(((bf16[128,2048]{1,0:T(8,128)(2,1)}), bf16[1024,2048]{1,0:T(8,128)(2,1)}) %all-gather.19.cloned.1.call-update) | async-done | bytes 4194320 | tf_op jit(solution)/shard_map/all_gather | solution.py:103
  738.7 13.4 fusion.84
  760.2 10.3 convolution_convert_fusion.7
  770.5 37.6 %reduce-scatter.31.cloned.1.call-done = bf16[128,2048]{1,0:T(8,128)(2,1)} async-done(((bf16[1024,2048]{1,0:T(8,128)(2,1)}), bf16[128,2048]{1,0:T(8,128)(2,1)}) %reduce-scatter.31.cloned.1.call-update) | async-done | bytes 524304 | tf_op jit(solution)/shard_map/reduce_scatter | solution.py:107
  810.0 48.6 %reduce-scatter.29.cloned.1.call-done = bf16[128,2048]{1,0:T(8,128)(2,1)} async-done(((bf16[1024,2048]{1,0:T(8,128)(2,1)}), bf16[128,2048]{1,0:T(8,128)(2,1)}) %reduce-scatter.29.cloned.1.call-update) | async-done | bytes 524304 | tf_op jit(solution)/shard_map/reduce_scatter | solution.py:107
  862.4 45.8 %all-gather.23.cloned.1.call-done = bf16[1024,2048]{1,0:T(8,128)(2,1)} async-done(((bf16[128,2048]{1,0:T(8,128)(2,1)}), bf16[1024,2048]{1,0:T(8,128)(2,1)}) %all-gather.23.cloned.1.call-update) | async-done | bytes 4194320 | tf_op jit(solution)/shard_map/all_gather | solution.py:116
  915.6 54.8 %while.29 = (s32[]{:T(128)}, f32[1024,2,128]{0,2,1:T(8,128)}, f32[1024,2,128]{0,2,1:T(8,128)}, bf16[2,512,2,128]{3,1,2,0:T(8,128)(2,1)}, bf16[2,512,2,128]{3,1,2...) while((s32[]{:T(128)}, f32[1024,2,128]{0,2,1:T(8,128)}, ...), condition=%wide.region_27.28_spmd.clone, body=%wide.region_25.27_spmd.clone.sunk | while | flops 1357925376 | bytes 81279256 | solution.py:177
  989.8 48.3 %reduce-scatter.33.cloned.1.call-done = bf16[128,2048]{1,0:T(8,128)(2,1)} async-done(((bf16[1024,2048]{1,0:T(8,128)(2,1)}), bf16[128,2048]{1,0:T(8,128)(2,1)}) %reduce-scatter.33.cloned.1.call-update) | async-done | bytes 524304 | tf_op jit(solution)/shard_map/reduce_scatter | solution.py:107
  1041.2 12.5 fusion.187
  1090.2 18.3 multiply_reduce_fusion.5
  1108.9 10.0 all-reduce.9
  1134.8 17.3 convolution_convert_fusion.1
  1152.1 43.5 %copy.153 = bf16[9,1024,1024]{1,0,2:T(8,128)(2,1)} copy(bf16[9,1024,1024]{2,1,0:T(8,128)(2,1)} %convolution_convert_fusion.1) | data formatting | bytes 37748736
  1195.6 25.0 %copy.162 = bf16[128,8,9,1024]{3,1,2,0:T(8,128)(2,1)} copy(bf16[128,8,9,1024]{3,2,1,0:T(8,128)(2,1)} %bitcast.398) | data formatting | bytes 37748736
  1221.2 9.5 convolution_convert_fusion.5
  1230.7 10.4 convolution_convert_fusion.4
  1254.6 17.2 convolution_convert_fusion.2
  1271.9 43.6 %copy.151 = bf16[9,1024,1024]{1,0,2:T(8,128)(2,1)} copy(bf16[9,1024,1024]{2,1,0:T(8,128)(2,1)} %convolution_convert_fusion.2) | data formatting | bytes 37748736
  1315.5 24.8 %copy.161 = bf16[128,8,9,1024]{3,1,2,0:T(8,128)(2,1)} copy(bf16[128,8,9,1024]{3,2,1,0:T(8,128)(2,1)} %bitcast.399) | data formatting | bytes 37748736
  1345.7 16.8 reduce-scatter.41.cloned.1.call-done
  1362.5 188.6 %reduce-scatter.61.cloned.1.call-done = bf16[128,9216]{1,0:T(8,128)(2,1)} async-done(((bf16[1024,9216]{1,0:T(8,128)(2,1)}), bf16[128,9216]{1,0:T(8,128)(2,1)}) %reduce-scatter.61.cloned.1.call-update) | async-done | bytes 2359312
  1565.7 41.1 %reduce-scatter.51.cloned.1.call-done = bf16[512,1024]{1,0:T(8,128)(2,1)} async-done(((bf16[2048,1024]{1,0:T(8,128)(2,1)}), bf16[512,1024]{1,0:T(8,128)(2,1)}) %reduce-scatter.51.cloned.1.call-update) | async-done | bytes 1048592 | tf_op jit(solution)/shard_map/reduce_scatter | solution.py:500
  1609.7 52.7 %reduce-scatter.53.cloned.1.call-done = bf16[1024,512]{1,0:T(8,128)(2,1)} async-done(((bf16[1024,2048]{1,0:T(8,128)(2,1)}), bf16[1024,512]{1,0:T(8,128)(2,1)}) %reduce-scatter.53.cloned.1.call-update) | async-done | bytes 1048592 | tf_op jit(solution)/shard_map/reduce_scatter | solution.py:503
  1665.2 28.4 %reduce-scatter.49.cloned.1.call-done = bf16[256,512]{1,0:T(8,128)(2,1)} async-done(((bf16[256,2048]{1,0:T(8,128)(2,1)}), bf16[256,512]{1,0:T(8,128)(2,1)}) %reduce-scatter.49.cloned.1.call-update) | async-done | bytes 262160 | tf_op jit(solution)/shard_map/reduce_scatter | solution.py:497
  1695.5 45.2 %reduce-scatter.47.cloned.1.call-done = bf16[3,512,256]{1,2,0:T(8,128)(2,1)} async-done(((bf16[3,2048,256]{1,2,0:T(8,128)(2,1)}), bf16[3,512,256]{1,2,0:T(8,128)(2,1)}) %reduce-scatter.47.cloned.1.call-update) | async-done | bytes 786448 | tf_op jit(solution)/shard_map/reduce_scatter | solution.py:494
  1752.1 8.7 collective-permute-done.7
  1767.2 164.9 %reduce-scatter.59.cloned.1.call-done = bf16[128,9216]{1,0:T(8,128)(2,1)} async-done(((bf16[1024,9216]{1,0:T(8,128)(2,1)}), bf16[128,9216]{1,0:T(8,128)(2,1)}) %reduce-scatter.59.cloned.1.call-update) | async-done | bytes 2359312
  1952.9 18.6 fusion.135
  1971.6 11.6 all-reduce.12
  1983.7 14.3 all-reduce.8
  2015.5 20.0 reduce-scatter.43.cloned.1.call-done
  2037.6 38.5 %reduce-scatter.37.cloned.1.call-done = bf16[9,256,128]{2,1,0:T(8,128)(2,1)} async-done(((bf16[9,1024,128]{2,1,0:T(8,128)(2,1)}), bf16[9,256,128]{2,1,0:T(8,128)(2,1)}) %reduce-scatter.37.cloned.1.call-update) | async-done | bytes 589840 | tf_op jit(solution)/shard_map/reduce_scatter | solution.py:476
  2078.3 38.6 %reduce-scatter.35.cloned.1.call-done = bf16[9,256,128]{2,1,0:T(8,128)(2,1)} async-done(((bf16[9,1024,128]{2,1,0:T(8,128)(2,1)}), bf16[9,256,128]{2,1,0:T(8,128)(2,1)}) %reduce-scatter.35.cloned.1.call-update) | async-done | bytes 589840 | tf_op jit(solution)/shard_map/reduce_scatter | solution.py:473
  (437 shorter events, 367.5 us)
Async XLA Ops:
  7.2 552.2 %copy-start = (bf16[3,2048,256]{2,1,0:T(8,128)(2,1)S(1)}, bf16[3,2048,256]{2,1,0:T(8,128)(2,1)}, u32[]{:S(2)}) copy-start(bf16[3,2048,256]{2,1,0:T(8,128)(2,1)} %param.29) | copy-start | bytes 9437188
  7.2 172.5 %all-gather.11.cloned.1.call-start = ((), (), s32[]{:S(2)}) async-start(), calls=%async_computation.18 | async-start | bytes 21233664 | tf_op jit(solution)/shard_map/all_gather | solution.py:217
  8.0 343.0 %all-gather.13.cloned.1.call-start = ((), (), s32[]{:S(2)}) async-start(), calls=%async_computation.19 | async-start | bytes 21233664 | tf_op jit(solution)/shard_map/all_gather | solution.py:218
  8.7 493.1 %all-gather.15.cloned.1.call-start = ((), (), s32[]{:S(2)}) async-start(), calls=%async_computation.20 | async-start | bytes 18874368 | tf_op jit(solution)/shard_map/all_gather | solution.py:219
  9.4 549.9 %all-gather.17.cloned.1.call-start = ((), (), s32[]{:S(2)}) async-start(), calls=%async_computation.21 | async-start | bytes 4718592 | tf_op jit(solution)/shard_map/all_gather | solution.py:103
  21.8 58.0 %copy-start.40 = (f32[1024]{0:T(1024)}, f32[1024]{0:T(1024)S(1)}, u32[]{:S(2)}) copy-start(f32[1024]{0:T(1024)S(1)} %sub.145) | copy-start | bytes 12292
  21.9 57.8 %copy-start.42 = (f32[1024]{0:T(1024)}, f32[1024]{0:T(1024)S(1)}, u32[]{:S(2)}) copy-start(f32[1024]{0:T(1024)S(1)} %mul.327) | copy-start | bytes 12292
  21.9 51.1 %copy-start.7 = (bf16[1,4,128,1024]{3,2,1,0:T(8,128)(2,1)S(1)}, bf16[1,4,128,1024]{3,2,1,0:T(8,128)(2,1)}, u32[]{:S(2)}) copy-start(bf16[1,4,128,1024]{3,2,1,0:T(8,128)(2,1)} %param.19) | copy-start | bytes 3145732
  24.0 49.6 %collective-permute-start = (bf16[1,128,1024]{2,1,0:T(8,128)(2,1)S(1)}, bf16[1,128,1024]{2,1,0:T(8,128)(2,1)S(1)}, u32[]{:S(2)}, u32[]{:S(2)}) collective-permute-start(bf16[1,128,1024]{2,1,0:T(8,128)(2,1)S(1)} %get-tuple-element.445), channel_id=1, source_target_pairs={{0,1},{1,2},{2,3},{3,4},{4,5},{5,6},{6,7},{8,9},{9,10},{10,11},{11... | collective-permute-start | bytes 786440 | tf_op jit(solution)/shard_map/ppermute | solution.py:24
  28.1 45.5 %collective-permute-start.1 = (bf16[1,128,1024]{2,1,0:T(8,128)(2,1)S(1)}, bf16[1,128,1024]{2,1,0:T(8,128)(2,1)S(1)}, u32[]{:S(2)}, u32[]{:S(2)}) collective-permute-start(bf16[1,128,1024]{2,1,0:T(8,128)(2,1)S(1)} %get-tuple-element.446), channel_id=1, source_target_pairs={{1,0},{2,1},{3,2},{4,3},{5,4},{6,5},{7,6},{9,8},{10,9},{11,10},{12... | collective-permute-start | bytes 786440 | tf_op jit(solution)/shard_map/ppermute | solution.py:27
  51.4 190.6 %copy-start.50 = (f32[8,1,128]{2,1,0:T(1,128)}, f32[8,1,128]{2,1,0:T(1,128)S(1)}, u32[]{:S(2)}) copy-start(f32[8,1,128]{2,1,0:T(1,128)S(1)} %all-gather.2) | copy-start | bytes 12292
  215.5 17.5 collective-permute-start.2
  219.9 16.1 collective-permute-start.3
  223.3 287.4 %copy-start.37 = (f32[1,2048]{1,0:T(1,128)}, f32[1,2048]{1,0:T(1,128)S(1)}, u32[]{:S(2)}) copy-start(f32[1,2048]{1,0:T(1,128)S(1)} %get-tuple-element.450) | copy-start | bytes 24580
  510.4 54.6 %copy-start.56 = (f32[128]{0:T(128)}, f32[128]{0:T(128)S(1)}, u32[]{:S(2)}) copy-start(f32[128]{0:T(128)S(1)} %broadcast_multiply_fusion.5) | copy-start | bytes 1540
  510.7 54.4 %copy-start.58 = (f32[128]{0:T(128)}, f32[128]{0:T(128)S(1)}, u32[]{:S(2)}) copy-start(f32[128]{0:T(128)S(1)} %add_rsqrt_fusion.1) | copy-start | bytes 1540
  512.4 131.1 %reduce-scatter.27.cloned.1.call-start = ((), (), s32[]{:S(2)}) async-start(), calls=%async_computation.22 | async-start | bytes 4718592 | tf_op jit(solution)/shard_map/reduce_scatter | solution.py:107
  595.0 95.7 %all-gather.21.cloned.1.call-start = ((), (), s32[]{:S(2)}) async-start(), calls=%async_computation.25 | async-start | bytes 4718592 | tf_op jit(solution)/shard_map/all_gather | solution.py:116
  595.6 143.2 %all-gather.19.cloned.1.call-start = ((), (), s32[]{:S(2)}) async-start(), calls=%async_computation.23 | async-start | bytes 4718592 | tf_op jit(solution)/shard_map/all_gather | solution.py:103
  647.1 161.1 %reduce-scatter.31.cloned.1.call-start = ((), (), s32[]{:S(2)}) async-start(), calls=%async_computation.26 | async-start | bytes 4718592 | tf_op jit(solution)/shard_map/reduce_scatter | solution.py:107
  759.7 99.0 %reduce-scatter.29.cloned.1.call-start = ((), (), s32[]{:S(2)}) async-start(), calls=%async_computation.24 | async-start | bytes 4718592 | tf_op jit(solution)/shard_map/reduce_scatter | solution.py:107
  770.5 137.7 %all-gather.23.cloned.1.call-start = ((), (), s32[]{:S(2)}) async-start(), calls=%async_computation.27 | async-start | bytes 4718592 | tf_op jit(solution)/shard_map/all_gather | solution.py:116
  862.3 175.8 %reduce-scatter.33.cloned.1.call-start = ((), (), s32[]{:S(2)}) async-start(), calls=%async_computation.28 | async-start | bytes 4718592 | tf_op jit(solution)/shard_map/reduce_scatter | solution.py:107
  989.6 48.5 %copy-start.57 = (f32[128]{0:T(128)S(1)}, f32[128]{0:T(128)}, u32[]{:S(2)}) copy-start(f32[128]{0:T(128)} %copy-done.56) | copy-start | bytes 1540
  989.6 48.5 %copy-start.59 = (f32[128]{0:T(128)S(1)}, f32[128]{0:T(128)}, u32[]{:S(2)}) copy-start(f32[128]{0:T(128)} %copy-done.58) | copy-start | bytes 1540
  989.6 50.1 %copy-start.25 = (f32[128,2048]{1,0:T(8,128)S(1)}, f32[128,2048]{1,0:T(8,128)}, u32[]{:S(2)}) copy-start(f32[128,2048]{1,0:T(8,128)} %get-tuple-element.397) | copy-start | bytes 3145732
  989.6 351.4 %reduce-scatter.55.cloned.1.call-start = ((), (), s32[]{:S(2)}) async-start(), calls=%async_computation.39 | async-start | bytes 294912 | tf_op jit(solution)/shard_map/reshape.14
  1061.5 15.4 collective-permute-start.4
  1064.1 12.8 collective-permute-start.5
  1123.3 219.6 %reduce-scatter.57.cloned.1.call-start = ((), (), s32[]{:S(2)}) async-start(), calls=%async_computation.40 | async-start | bytes 2359296 | tf_op jit(solution)/shard_map/reshape.16
  1125.2 237.2 %reduce-scatter.41.cloned.1.call-start = ((), (), s32[]{:S(2)}) async-start(), calls=%async_computation.32 | async-start | bytes 18874368 | tf_op jit(solution)/shard_map/reduce_scatter | solution.py:468
  1133.6 417.5 %reduce-scatter.61.cloned.1.call-start = ((), (), s32[]{:S(2)}) async-start(), calls=%async_computation.42 | async-start | bytes 21233664
  1220.7 386.2 %reduce-scatter.51.cloned.1.call-start = ((), (), s32[]{:S(2)}) async-start(), calls=%async_computation.37 | async-start | bytes 5242880 | tf_op jit(solution)/shard_map/reduce_scatter | solution.py:500
  1230.7 431.7 %reduce-scatter.53.cloned.1.call-start = ((), (), s32[]{:S(2)}) async-start(), calls=%async_computation.38 | async-start | bytes 5242880 | tf_op jit(solution)/shard_map/reduce_scatter | solution.py:503
  1241.2 452.4 %reduce-scatter.49.cloned.1.call-start = ((), (), s32[]{:S(2)}) async-start(), calls=%async_computation.36 | async-start | bytes 1310720 | tf_op jit(solution)/shard_map/reduce_scatter | solution.py:497
  1246.7 494.0 %reduce-scatter.47.cloned.1.call-start = ((), (), s32[]{:S(2)}) async-start(), calls=%async_computation.35 | async-start | bytes 3932160 | tf_op jit(solution)/shard_map/reduce_scatter | solution.py:494
  1254.6 677.5 %reduce-scatter.59.cloned.1.call-start = ((), (), s32[]{:S(2)}) async-start(), calls=%async_computation.41 | async-start | bytes 21233664
  1340.3 671.6 %reduce-scatter.39.cloned.1.call-start = ((), (), s32[]{:S(2)}) async-start(), calls=%async_computation.31 | async-start | bytes 327680 | tf_op jit(solution)/shard_map/reduce_scatter | solution.py:488
  1342.8 670.6 %reduce-scatter.45.cloned.1.call-start = ((), (), s32[]{:S(2)}) async-start(), calls=%async_computation.34 | async-start | bytes 2621440 | tf_op jit(solution)/shard_map/reduce_scatter | solution.py:491
  1345.7 689.9 %reduce-scatter.43.cloned.1.call-start = ((), (), s32[]{:S(2)}) async-start(), calls=%async_computation.33 | async-start | bytes 2621440 | tf_op jit(solution)/shard_map/reduce_scatter | solution.py:479
  1362.5 713.6 %reduce-scatter.37.cloned.1.call-start = ((), (), s32[]{:S(2)}) async-start(), calls=%async_computation.30 | async-start | bytes 2949120 | tf_op jit(solution)/shard_map/reduce_scatter | solution.py:476
  1563.2 553.7 %reduce-scatter.35.cloned.1.call-start = ((), (), s32[]{:S(2)}) async-start(), calls=%async_computation.29 | async-start | bytes 2949120 | tf_op jit(solution)/shard_map/reduce_scatter | solution.py:473
  1609.6 139.4 %copy-start.32 = (bf16[1024,1]{1,0:T(8,128)(2,1)S(1)}, bf16[1024,1]{1,0:T(8,128)(2,1)}, u32[]{:S(2)}) copy-start(bf16[1024,1]{1,0:T(8,128)(2,1)} %reduce-scatter.57.cloned.1.call-done) | copy-start | bytes 6148
  1609.7 142.2 %copy-start.34 = (bf16[1024,128]{1,0:T(8,128)(2,1)S(1)}, bf16[1024,128]{1,0:T(8,128)(2,1)}, u32[]{:S(2)}) copy-start(bf16[1024,128]{1,0:T(8,128)(2,1)} %param.26) | copy-start | bytes 786436
  1609.7 142.2 %copy-start.39 = (bf16[128,1]{1,0:T(8,128)(2,1)S(1)}, bf16[128,1]{1,0:T(8,128)(2,1)}, u32[]{:S(2)}) copy-start(bf16[128,1]{1,0:T(8,128)(2,1)} %reduce-scatter.55.cloned.1.call-done) | copy-start | bytes 772
  1743.2 8.8 collective-permute-start.6
  1746.9 13.8 collective-permute-start.7
  2007.5 111.5 %copy-start.1 = (bf16[3,2048,256]{2,1,0:T(8,128)(2,1)S(1)}, bf16[3,2048,256]{2,1,0:T(8,128)(2,1)}, u32[]{:S(2)}) copy-start(bf16[3,2048,256]{2,1,0:T(8,128)(2,1)} %param.29) | copy-start | bytes 9437188
  (57 other events, 467.4 us)
Sparse Core Ops, SparseCore 0:
  9.6 169.9 all-gather.10
  181.3 169.5 all-gather.12
  352.5 149.2 all-gather.14
  512.6 46.7 all-gather.16
  595.1 48.3 reduce-scatter.26
  645.0 45.6 all-gather.20
  692.8 45.8 all-gather.18
  759.8 48.2 reduce-scatter.30
  810.5 48.1 reduce-scatter.28
  862.5 45.6 all-gather.22
  989.7 48.3 reduce-scatter.32
  1123.4 27.6 reduce-scatter.54
  1154.1 35.1 reduce-scatter.56
  1191.6 170.7 reduce-scatter.40
  1364.8 186.3 reduce-scatter.60
  1554.3 52.5 reduce-scatter.50
  1609.7 52.6 reduce-scatter.52
  1666.0 27.6 reduce-scatter.48
  1696.6 43.9 reduce-scatter.46
  1742.8 189.2 reduce-scatter.58
  1934.9 23.4 reduce-scatter.38
  1961.6 35.6 reduce-scatter.44
  2000.3 35.1 reduce-scatter.42
  2038.7 37.3 reduce-scatter.36
  2079.5 37.3 reduce-scatter.34
where the time goes:
time: 2140 us; the launch traced here: 2130 us
  waiting for transfers between devices  1340 us (63%)
  matrix products  284 us (13%)
  local copies, waits for them, and re-layouts  279 us (13%)
  blocking collectives  109 us (5%)
  other arithmetic  72.1 us (3%)
  starting transfers between devices  28.6 us (1%)
    unnamed x27, waiting for transfers between devices  356 us
    unnamed x166, local copies, waits for them, and re-layouts  217 us
    reduce_scatter x4, waiting for transfers between devices, scatter_tokens(): lax.psum_scatter(term_fn(jnp.int32(0), row_count * lax.axis_size('mp')).a...  182 us
    all_gather x1, waiting for transfers between devices, local(): lax.all_gather(down_weight, 'mp', axis=1, tiled=True)  126 us
    all_gather x1, waiting for transfers between devices, local(): lax.all_gather(conv_second, 'mp', axis=1, tiled=True)  103 us
    all_gather x1, waiting for transfers between devices, local(): lax.all_gather(conv_first, 'mp', axis=1, tiled=True)  94 us
    all_gather x2, waiting for transfers between devices, fold_tokens(): lax.all_gather(local_rows, 'mp', axis=0, tiled=True)  89.1 us
    all_gather x2, waiting for transfers between devices, gather_tokens(): lax.all_gather(local_rows, 'mp', axis=0, tiled=True)  84.2 us
  transfers between devices with their start and end apart: 33, of which 24 were waited for; matrix products, arithmetic and copies ran while one was open for 20% of the time, Pallas kernels for 0%

commit v1 on v0

v1 whole, which is shorter than its diff:
```python
from functools import partial
import math

import jax
import jax.numpy as jnp
from jax import lax
from jax.experimental import pallas as pl
from jax.experimental.pallas import tpu as pltpu
from jax.sharding import PartitionSpec as P

HEAD_DIM = 128
GROUPS = 32


GROUP_EPSILON = 1e-05
LAYER_EPSILON = 1e-06
MASKED_SCORE = -1000000000.0
PRECISE = lax.Precision.HIGHEST


def group_spread(per_channel, size):
    grouped = jnp.sum(per_channel.reshape(-1, size), axis=1)
    return jnp.repeat(grouped, size)


def group_forward(values, size):
    counted = values.shape[0] * size
    average = group_spread(jnp.sum(values, axis=0), size) / counted
    centre = values - average
    inverse = lax.rsqrt(
        group_spread(jnp.sum(centre * centre, axis=0), size) / counted + GROUP_EPSILON
    )
    return (centre * inverse, inverse)


def group_backward(incoming, normed, inverse, gain_vec, size):
    pre_act = normed * gain_vec
    sigmoid_part = jax.nn.sigmoid(pre_act)
    through = incoming * sigmoid_part * (1.0 + pre_act * (1.0 - sigmoid_part))
    counted = normed.shape[0] * size
    gain_part = jnp.sum(through * normed, axis=0)
    plain_part = jnp.sum(through, axis=0)
    first_mean = group_spread(plain_part * gain_vec, size) / counted
    second_mean = group_spread(gain_part * gain_vec, size) / counted
    outgoing = inverse * (through * gain_vec - first_mean - normed * second_mean)
    return (outgoing, gain_part)


def windows(planes, flipped):
    row_count, col_count, depth = planes.shape
    padded = jnp.pad(planes, ((1, 1), (1, 1), (0, 0)))
    pieces = []
    for tap_index in range(9):
        row_off, col_off = divmod(tap_index, 3)
        if flipped:
            row_off, col_off = (2 - row_off, 2 - col_off)
        pieces.append(padded[row_off : row_off + row_count, col_off : col_off + col_count])
    return jnp.stack(pieces, axis=2).reshape(row_count * col_count, 9, depth)


def gather_rows(rows):
    return lax.all_gather(rows, "mp", axis=0, tiled=True)


def scatter_rows(rows):
    return lax.psum_scatter(
        rows.astype(jnp.bfloat16), "mp", scatter_dimension=0, tiled=True
    ).astype(jnp.float32)


def conv_scatter(hidden, kernel, n):
    patch = windows(hidden, False)
    depth = kernel.shape[2] // n
    total = jnp.einsum("ptc,tcd->pd", patch, kernel, preferred_element_type=jnp.float32)
    parts = total.astype(jnp.bfloat16).reshape(-1, n, depth).transpose(1, 0, 2)
    return lax.psum_scatter(parts, "mp", scatter_dimension=0, tiled=False).astype(jnp.float32)


def conv_backward(grad_low, hidden, kernel, n):
    row_count, col_count, depth = hidden.shape
    gathered = lax.all_gather(grad_low, "mp", axis=1, tiled=True)
    padded = jnp.pad(gathered, ((col_count, col_count), (0, 0)))
    taps = kernel.reshape(3, 3 * depth, kernel.shape[2])
    acc = sum(
        jnp.einsum(
            "pd,td->pt",
            padded[(2 - i) * col_count : (2 - i) * col_count + row_count * col_count],
            taps[i],
            preferred_element_type=jnp.float32,
        )
        for i in range(3)
    )
    grad_kernel = jnp.einsum(
        "ptc,pd->tcd", windows(hidden, False), gathered, preferred_element_type=jnp.float32
    )
    return (join_columns(acc, col_count), grad_kernel)


def dp_rows(grad, dim):
    return lax.psum_scatter(
        grad.astype(jnp.bfloat16), "dp", scatter_dimension=dim, tiled=True
    ).astype(jnp.float32)


def by_images(grad, m):
    taps, own, outs = grad.shape
    return grad.astype(jnp.bfloat16).reshape(taps * own, m, outs // m).transpose(1, 0, 2)


def turn_kernel(parts, taps, m, n):
    own = parts.shape[1] // taps
    outs = parts.shape[2] * m
    mine = lax.psum_scatter(parts, "dp", scatter_dimension=0, tiled=False)
    ratio = n // m
    pieces = mine.reshape(taps, own, ratio, outs // n)
    me = lax.axis_index("mp") % ratio
    result = jnp.zeros((taps, ratio, own, outs // n), jnp.bfloat16)
    for shift in range(ratio):
        route = []
        for i in range(m):
            for j in range(n):
                target = (j // ratio) * n + ratio * i + (j % ratio + shift) % ratio
                route.append((i * n + j, target))
        half = lax.dynamic_index_in_dim(pieces, (me + shift) % ratio, axis=2, keepdims=False)
        moved = lax.ppermute(half, ("dp", "mp"), route)
        place = (me - shift + ratio) % ratio
        result = lax.dynamic_update_slice(result, moved[:, None], (0, place, 0, 0))
    return result.reshape(taps, ratio * own, outs // n).astype(jnp.float32)


def layer_forward(stream):
    centre = stream - jnp.mean(stream, axis=1, keepdims=True)
    inverse = lax.rsqrt(jnp.mean(centre * centre, axis=1, keepdims=True) + LAYER_EPSILON)
    return (centre * inverse, inverse)


def layer_backward(incoming, normed, inverse, scale_vec):
    through = incoming * (1.0 + scale_vec)
    outgoing = inverse * (
        through
        - jnp.mean(through, axis=1, keepdims=True)
        - normed * jnp.mean(through * normed, axis=1, keepdims=True)
    )
    return (outgoing, jnp.sum(incoming * normed, axis=0), jnp.sum(incoming, axis=0))


def attend_forward(queries, key_rows, value_rows, key_valid, block_rows):
    score_scale = 1.0 / math.sqrt(queries.shape[-1])

    def one_block(query_block):
        raw_scores = jnp.einsum(
            "qhd,khd->hqk", query_block, key_rows, preferred_element_type=jnp.float32
        )
        logits = jnp.where(key_valid[None, None, :], raw_scores * score_scale, MASKED_SCORE)
        peak_score = jnp.max(logits, axis=-1, keepdims=True)
        exponent = jnp.exp(logits - peak_score)
        totals = jnp.sum(exponent, axis=-1, keepdims=True)
        mix_weights = (exponent / totals).astype(jnp.bfloat16)
        mixed_heads = jnp.einsum(
            "hqk,khd->qhd", mix_weights, value_rows, preferred_element_type=jnp.float32
        )
        return (mixed_heads, (peak_score + jnp.log(totals))[..., 0])

    blocks = queries.reshape(-1, block_rows, queries.shape[1], queries.shape[2])
    mixed_heads, log_totals = lax.map(one_block, blocks)
    return (mixed_heads.reshape(queries.shape), log_totals)


def attend_backward(queries, key_rows, value_rows, key_valid, log_totals, grad_mixed, block_rows):
    score_scale = 1.0 / math.sqrt(queries.shape[-1])
    block_shape = (-1, block_rows, queries.shape[1], queries.shape[2])

    def one_block(running, inputs):
        grad_keys, grad_values = running
        query_block, grad_block, log_block = inputs
        raw_scores = jnp.einsum(
            "qhd,khd->hqk", query_block, key_rows, preferred_element_type=jnp.float32
        )
        logits = jnp.where(key_valid[None, None, :], raw_scores * score_scale, MASKED_SCORE)
        mix_weights = jnp.exp(logits - log_block[..., None])
        grad_weights = jnp.einsum(
            "qhd,khd->hqk", grad_block, value_rows, preferred_element_type=jnp.float32
        )
        inner_sum = jnp.sum(mix_weights * grad_weights, axis=-1, keepdims=True)
        grad_scores = (mix_weights * (grad_weights - inner_sum) * score_scale).astype(jnp.bfloat16)
        grad_query = jnp.einsum(
            "hqk,khd->qhd", grad_scores, key_rows, preferred_element_type=jnp.float32
        )
        grad_keys = grad_keys + jnp.einsum(
            "hqk,qhd->khd", grad_scores, query_block, preferred_element_type=jnp.float32
        )
        grad_values = grad_values + jnp.einsum(
            "hqk,qhd->khd",
            mix_weights.astype(jnp.bfloat16),
            grad_block,
            preferred_element_type=jnp.float32,
        )
        return ((grad_keys, grad_values), grad_query)

    zero_rows = jnp.zeros(key_rows.shape, jnp.float32)
    (grad_keys, grad_values), grad_query = lax.scan(
        one_block,
        (zero_rows, zero_rows),
        (queries.reshape(block_shape), grad_mixed.reshape(block_shape), log_totals),
    )
    return (grad_query.reshape(queries.shape), grad_keys, grad_values)


MESH = pl.DeviceIdType.MESH
CONV_PARTS = 4
TOKEN_PARTS = 4
VMEM_BYTES = 60 * 1024 * 1024


class Line:
    def __init__(self, chips):
        self.chips = chips
        self.dp = lax.axis_index("dp")
        self.mp = lax.axis_index("mp")
        self.z = self.mp // 2
        self.c = self.mp % 2
        self.has_up = self.z < chips - 1
        self.has_down = self.z > 0
        self.up = (self.dp, self.mp + 2)
        self.down = (self.dp, self.mp - 2)
        self.sibling = (self.dp, 2 * self.z + 1 - self.c)

    def barrier(self):
        bar = pltpu.get_barrier_semaphore()
        pl.semaphore_signal(bar, inc=1, device_id=self.sibling, device_id_type=MESH)

        @pl.when(self.has_up)
        def _():
            pl.semaphore_signal(bar, inc=1, device_id=self.up, device_id_type=MESH)

        @pl.when(self.has_down)
        def _():
            pl.semaphore_signal(bar, inc=1, device_id=self.down, device_id_type=MESH)

        middle = jnp.logical_and(self.has_up, self.has_down)

        @pl.when(middle)
        def _():
            pl.semaphore_wait(bar, 3)

        @pl.when(jnp.logical_not(middle))
        def _():
            pl.semaphore_wait(bar, 2)


def remote(src, dst, send, recv, target):
    return pltpu.make_async_remote_copy(
        src_ref=src,
        dst_ref=dst,
        send_sem=send,
        recv_sem=recv,
        device_id=target,
        device_id_type=MESH,
    )


def gather_sems(chips):
    return [pltpu.SemaphoreType.DMA((3, 2, chips)), pltpu.SemaphoreType.DMA((3, 2, chips))]


def line_gather(line, x_ref, slot, send, recv, on_own, on_pair):
    chips = line.chips
    z, c = line.z, line.c
    line.barrier()

    def hop(stream, step, src, block, target):
        return remote(src, slot(block), send.at[stream, 0, step], recv.at[stream, 0, step], target)

    def across(way, step, src, block):
        return remote(src, slot(block), send.at[2, way, step], recv.at[2, way, step], line.sibling)

    @pl.when(line.has_up)
    def _():
        hop(0, 1, x_ref, line.mp, line.up).start()

    @pl.when(line.has_down)
    def _():
        hop(1, 1, x_ref, line.mp, line.down).start()

    across(0, 0, x_ref, line.mp).start()
    slot(line.mp)[...] = x_ref[...]
    on_own()
    across(0, 0, x_ref, line.mp).wait_recv()
    on_pair(z)
    for step in range(1, chips):
        below, above = z - step, z + step

        @pl.when(below >= 0)
        def _():
            block = 2 * below + c
            hop(0, step, slot(block), block, line.up).wait_recv()
            if step + 1 < chips:

                @pl.when(line.has_up)
                def _():
                    hop(0, step + 1, slot(block), block, line.up).start()

            across(0, step, slot(block), block).start()

        @pl.when(above < chips)
        def _():
            block = 2 * above + c
            hop(1, step, slot(block), block, line.down).wait_recv()
            if step + 1 < chips:

                @pl.when(line.has_down)
                def _():
                    hop(1, step + 1, slot(block), block, line.down).start()

            across(1, step, slot(block), block).start()

        @pl.when(below >= 0)
        def _():
            across(0, step, slot(2 * below + c), 2 * below + c).wait_recv()
            on_pair(below)

        @pl.when(above < chips)
        def _():
            across(1, step, slot(2 * above + c), 2 * above + c).wait_recv()
            on_pair(above)

    @pl.when(line.has_up)
    def _():
        hop(0, 1, x_ref, line.mp, line.up).wait_send()

    @pl.when(line.has_down)
    def _():
        hop(1, 1, x_ref, line.mp, line.down).wait_send()

    across(0, 0, x_ref, line.mp).wait_send()
    for step in range(1, chips):
        below, above = z - step, z + step

        @pl.when(below >= 0)
        def _():
            block = 2 * below + c
            if step + 1 < chips:

                @pl.when(line.has_up)
                def _():
                    hop(0, step + 1, slot(block), block, line.up).wait_send()

            across(0, step, slot(block), block).wait_send()

        @pl.when(above < chips)
        def _():
            block = 2 * above + c
            if step + 1 < chips:

                @pl.when(line.has_down)
                def _():
                    hop(1, step + 1, slot(block), block, line.down).wait_send()

            across(1, step, slot(block), block).wait_send()


def scatter_scratch(chips, rows, cols, parts):
    block = (chips, rows, cols)
    return [
        pltpu.VMEM(block, jnp.float32),
        pltpu.VMEM(block, jnp.bfloat16),
        pltpu.VMEM(block, jnp.bfloat16),
        pltpu.VMEM((2,) + block, jnp.bfloat16),
        pltpu.SemaphoreType.DMA((2, 3, chips, parts)),
    ]


def line_scatter(line, scratch, parts, produce, finish, tile):
    chips = line.chips
    z = line.z
    kept, out_ref, in_ref, moving, sems = scratch
    count = kept.shape[1] // parts
    line.barrier()

    def span(part):
        return pl.ds(part * count, count)

    def across(chip, part):
        return remote(
            out_ref.at[chip, span(part)],
            in_ref.at[chip, span(part)],
            sems.at[0, 0, chip, part],
            sems.at[1, 0, chip, part],
            line.sibling,
        )

    def hop(way, chip, part):
        target = line.up if way == 0 else line.down
        ref = moving.at[way, chip, span(part)]
        return remote(
            ref, ref, sems.at[0, 1 + way, chip, part], sems.at[1, 1 + way, chip, part], target
        )

    items = []
    for step in range(chips - 1):
        for part in range(parts):
            items.append((0, chips - 1 - step + z, part, step >= z))
            items.append((1, step - (chips - 1 - z), part, step >= chips - 1 - z))
    for part in range(parts):
        items.append((2, z, part, None))

    def run(active, body):
        if active is None:
            body()
        else:
            pl.when(active)(body)

    def start(item):
        way, chip, part, active = item

        def body():
            produce(chip, part, count, kept.at[chip], out_ref.at[chip])
            across(chip, part).start()

        run(active, body)

    def tiles(part, body):
        @pl.loop(0, count // tile)
        def _(index):
            body(pl.ds(pl.multiple_of(part * count + index * tile, tile), tile))

    def close(item):
        way, chip, part, active = item

        def body():
            across(chip, part).wait_recv()
            if way < 2:
                later = line.has_down if way == 0 else line.has_up

                @pl.when(later)
                def _():
                    hop(way, chip, part).wait_recv()

                    def add(rows):
                        moving[way, chip, rows] = (
                            kept[chip, rows]
                            + in_ref[chip, rows].astype(jnp.float32)
                            + moving[way, chip, rows].astype(jnp.float32)
                        ).astype(jnp.bfloat16)

                    tiles(part, add)

                @pl.when(jnp.logical_not(later))
                def _():
                    def add(rows):
                        moving[way, chip, rows] = (
                            kept[chip, rows] + in_ref[chip, rows].astype(jnp.float32)
                        ).astype(jnp.bfloat16)

                    tiles(part, add)

                hop(way, chip, part).start()
            else:

                def total(rows):
                    return kept[chip, rows] + in_ref[chip, rows].astype(jnp.float32)

                def from_side(side, rows):
                    return moving[side, chip, rows].astype(jnp.float32)

                both = jnp.logical_and(line.has_down, line.has_up)

                @pl.when(both)
                def _():
                    hop(0, chip, part).wait_recv()
                    hop(1, chip, part).wait_recv()
                    tiles(
                        part,
                        lambda rows: finish(
                            part, rows, total(rows) + from_side(0, rows) + from_side(1, rows)
                        ),
                    )

                for side, present in ((0, line.has_down), (1, line.has_up)):

                    @pl.when(jnp.logical_and(present, jnp.logical_not(both)))
                    def _():
                        hop(side, chip, part).wait_recv()
                        tiles(
                            part,
                            lambda rows: finish(part, rows, total(rows) + from_side(side, rows)),
                        )

        run(active, body)

    lag = 2
    for index, item in enumerate(items):
        start(item)
        if index >= lag:
            close(items[index - lag])
    for item in items[-lag:]:
        close(item)
    for way, chip, part, active in items:

        def body():
            across(chip, part).wait_send()
            if way < 2:
                hop(way, chip, part).wait_send()

        run(active, body)


def whole(count):
    return [pl.BlockSpec(memory_space=pltpu.VMEM)] * count


def comm_params(number):
    return pltpu.CompilerParams(
        collective_id=number, has_side_effects=True, vmem_limit_bytes=VMEM_BYTES
    )


def pick(c, low, high):
    return jnp.where(c == 0, low, high), jnp.where(c == 0, high, low)


def conv_scatter_kernel(chips, breadth, x_ref, w_ref, o_ref, *scratch):
    line = Line(chips)
    pixels, own = o_ref.shape
    tile = 512

    def produce(chip, part, count, mine, other):
        columns = pl.ds(pl.multiple_of(chip * 2 * own, 2 * own), 2 * own)

        @pl.loop(0, count // tile)
        def _(index):
            base = pl.multiple_of(part * count + index * tile, tile)
            total = jnp.zeros((tile, 2 * own), jnp.float32)
            for i in range(3):
                total += jnp.dot(
                    x_ref[pl.ds(base + i * breadth, tile)],
                    w_ref[i, :, columns],
                    preferred_element_type=jnp.float32,
                )
            first, second = pick(line.c, total[:, :own], total[:, own:])
            mine[pl.ds(base, tile)] = first
            other[pl.ds(base, tile)] = second.astype(jnp.bfloat16)

    def finish(part, rows, total):
        o_ref[rows] = total

    line_scatter(line, scratch, CONV_PARTS, produce, finish, tile)


def side_by_side(hidden):
    rows, cols, depth = hidden.shape
    padded = jnp.pad(hidden, ((1, 1), (1, 1), (0, 0)))
    return jnp.concatenate([padded[:, j : j + cols] for j in range(3)], axis=2).reshape(
        (rows + 2) * cols, 3 * depth
    )


def conv_scatter_fused(spread, kernel, cols, n, number):
    own = kernel.shape[2] // n
    depth = kernel.shape[1]
    pixels = spread.shape[0] - 2 * cols
    chips = n // 2
    return pl.pallas_call(
        partial(conv_scatter_kernel, chips, cols),
        out_shape=jax.ShapeDtypeStruct((pixels, own), jnp.float32),
        in_specs=whole(2),
        out_specs=whole(1)[0],
        scratch_shapes=scatter_scratch(chips, pixels, own, CONV_PARTS),
        compiler_params=comm_params(number),
    )(spread, kernel.reshape(3, 3 * depth, kernel.shape[2]))


def conv_back_kernel(chips, breadth, g_ref, w_ref, xt_ref, acc_ref, wg_ref, held, sums, send, recv):
    line = Line(chips)
    pixels, own = g_ref.shape
    wide = w_ref.shape[1]
    tile = 512
    zero = jnp.zeros((breadth, own), jnp.bfloat16)
    for block in range(2 * chips):
        held[block, pl.ds(0, breadth)] = zero
        held[block, pl.ds(breadth + pixels, breadth)] = zero

    def slot(block):
        return held.at[block, pl.ds(breadth, pixels)]

    def pair(chip, rows):
        return jnp.concatenate([held[2 * chip, rows], held[2 * chip + 1, rows]], axis=1)

    def on_own():
        @pl.loop(0, pixels // tile)
        def _(index):
            acc_ref[pl.ds(pl.multiple_of(index * tile, tile), tile)] = jnp.zeros(
                (tile, wide), jnp.float32
            )

    def on_pair(chip):
        columns = pl.ds(pl.multiple_of(chip * 2 * own, 2 * own), 2 * own)

        @pl.loop(0, pixels // tile)
        def _(index):
            base = pl.multiple_of(index * tile, tile)
            total = acc_ref[pl.ds(base, tile)]
            for i in range(3):
                total += lax.dot_general(
                    pair(chip, pl.ds(base + (2 - i) * breadth, tile)),
                    w_ref[i, :, columns],
                    (((1,), (1,)), ((), ())),
                    preferred_element_type=jnp.float32,
                )
            acc_ref[pl.ds(base, tile)] = total

        for i in range(3):
            sums[...] = jnp.zeros_like(sums)

            @pl.loop(0, pixels // tile)
            def _(index):
                base = pl.multiple_of(index * tile, tile)
                sums[...] += jnp.dot(
                    xt_ref[:, pl.ds(base + i * breadth, tile)],
                    pair(chip, pl.ds(base + breadth, tile)),
                    preferred_element_type=jnp.float32,
                )

            wg_ref[chip, i] = sums[...].astype(jnp.bfloat16)

    line_gather(line, g_ref, slot, send, recv, on_own, on_pair)


def conv_back_fused(grad_low, spread_turned, kernel, cols, n, number):
    pixels, own = grad_low.shape
    depth = kernel.shape[1]
    chips = n // 2
    return pl.pallas_call(
        partial(conv_back_kernel, chips, cols),
        out_shape=(
            jax.ShapeDtypeStruct((pixels, 3 * depth), jnp.float32),
            jax.ShapeDtypeStruct((chips, 3, 3 * depth, 2 * own), jnp.bfloat16),
        ),
        in_specs=whole(3),
        out_specs=tuple(whole(2)),
        scratch_shapes=[
            pltpu.VMEM((n, pixels + 2 * cols, own), jnp.bfloat16),
            pltpu.VMEM((3 * depth, 2 * own), jnp.float32),
        ]
        + gather_sems(chips),
        compiler_params=comm_params(number),
    )(grad_low, kernel.reshape(3, 3 * depth, kernel.shape[2]), spread_turned)


def join_columns(acc, cols):
    pixels, wide = acc.shape
    depth = wide // 3
    planes = acc.reshape(-1, cols, wide)
    none = jnp.zeros_like(planes[:, :1, :depth])
    left = jnp.concatenate([planes[:, 1:, :depth], none], axis=1)
    right = jnp.concatenate([none, planes[:, :-1, 2 * depth :]], axis=1)
    return (left + planes[:, :, depth : 2 * depth] + right).reshape(pixels, depth)


def product(x, w, turned):
    return lax.dot_general(
        x, w, (((1,), (1 if turned else 0,)), ((), ())), preferred_element_type=jnp.float32
    )


def tokens_scatter_kernel(chips, turned, x_ref, w_ref, o_ref, *scratch):
    line = Line(chips)
    tokens, width = o_ref.shape
    cut = width // TOKEN_PARTS
    depth = x_ref.shape[1] // w_ref.shape[0]

    def produce(chip, part, count, mine, other):
        rows = pl.ds(pl.multiple_of(chip * 2 * tokens, 2 * tokens), 2 * tokens)
        columns = pl.ds(part * cut, cut)
        total = None
        for j in range(w_ref.shape[0]):
            w = w_ref[j, columns] if turned else w_ref[j, :, columns]
            term = product(x_ref[rows, pl.ds(j * depth, depth)], w, turned)
            total = term if total is None else total + term
        first, second = pick(line.c, total[:tokens], total[tokens:])
        mine[pl.ds(part * count, count)] = first
        other[pl.ds(part * count, count)] = second.astype(jnp.bfloat16)

    def finish(part, rows, total):
        o_ref[:, pl.ds(part * cut, cut)] = total

    line_scatter(line, scratch, TOKEN_PARTS, produce, finish, tokens)


def tokens_scatter(x, w, turned, n, number):
    tokens = x.shape[0] // n
    width = w.shape[1] if turned else w.shape[2]
    chips = n // 2
    return pl.pallas_call(
        partial(tokens_scatter_kernel, chips, turned),
        out_shape=jax.ShapeDtypeStruct((tokens, width), jnp.float32),
        in_specs=whole(2),
        out_specs=whole(1)[0],
        scratch_shapes=scatter_scratch(chips, TOKEN_PARTS * tokens, width // TOKEN_PARTS, TOKEN_PARTS),
        compiler_params=comm_params(number),
    )(x, w)


def tokens_gather_kernel(chips, turned, shape_out, outs, x_ref, w_ref, *refs):
    line = Line(chips)
    held = refs[0]
    results = refs[1 : 1 + outs]
    send, recv = refs[1 + outs :]
    tokens = x_ref.shape[0]
    across = w_ref.shape[1 if turned else 2]
    cut = min(across, 512)

    def slot(block):
        return held.at[pl.ds(pl.multiple_of(block * tokens, tokens), tokens)]

    def on_pair(chip):
        rows = pl.ds(pl.multiple_of(chip * 2 * tokens, 2 * tokens), 2 * tokens)
        for j in range(w_ref.shape[0]):
            for start in range(0, across, cut):
                w = w_ref[j, pl.ds(start, cut)] if turned else w_ref[j, :, pl.ds(start, cut)]
                values = shape_out(product(held[rows], w, turned))
                for ref, value in zip(results, values):
                    ref[rows, pl.ds(j * across + start, cut)] = value.astype(ref.dtype)

    line_gather(line, x_ref, slot, send, recv, lambda: None, on_pair)


def tokens_gather(x, w, turned, kinds, shape_out, n, number):
    tokens, width = x.shape
    across = w.shape[0] * w.shape[1 if turned else 2]
    chips = n // 2
    return pl.pallas_call(
        partial(tokens_gather_kernel, chips, turned, shape_out, len(kinds)),
        out_shape=(jax.ShapeDtypeStruct((tokens * n, width), x.dtype),)
        + tuple(jax.ShapeDtypeStruct((tokens * n, across), kind) for kind in kinds),
        in_specs=whole(2),
        out_specs=tuple(whole(1 + len(kinds))),
        scratch_shapes=gather_sems(chips),
        compiler_params=comm_params(number),
    )(x, w)


def local(
    image,
    embedding,
    extents,
    gain_first,
    conv_first,
    gain_second,
    conv_second,
    shift_weight,
    down_weight,
    ada_weight,
    qkv_weight,
    out_weight,
    up_weight,
    proj_weight,
    cotangent,
):
    strip_rows, canvas_cols, channel_count = (image.shape[1], image.shape[2], image.shape[3])
    width_all = out_weight.shape[1]
    n = lax.axis_size("mp")
    m = lax.axis_size("dp")
    me_mp = lax.axis_index("mp")
    me_dp = lax.axis_index("dp")
    rows_all = strip_rows * n
    pixel_total = rows_all * canvas_cols
    own = channel_count // n
    size = channel_count // GROUPS
    token_rows = strip_rows // 2
    token_cols = canvas_cols // 2
    local_tokens = token_rows * token_cols
    token_total = local_tokens * n
    block_rows = min(512, token_total)
    local_width = out_weight.shape[0]
    head_count = local_width // HEAD_DIM

    shift_vector = jnp.dot(embedding, shift_weight, preferred_element_type=jnp.float32)[0]
    modulation = lax.all_gather(
        jnp.dot(embedding, ada_weight, preferred_element_type=jnp.float32), "mp", axis=1, tiled=True
    )
    scale_attend = modulation[0, :width_all]
    shift_attend = modulation[0, width_all : 2 * width_all]
    scale_mlp = modulation[0, 2 * width_all : 3 * width_all]
    shift_mlp = modulation[0, 3 * width_all :]
    own_first = lax.dynamic_slice_in_dim(gain_first, me_mp * own, own)
    own_second = lax.dynamic_slice_in_dim(gain_second, me_mp * own, own)

    pixels_low = lax.all_to_all(image[0], "mp", 2, 0, tiled=True)
    pixels = pixels_low.astype(jnp.float32).reshape(pixel_total, own)
    normed_first, inverse_first = group_forward(pixels, size)
    hidden_first = (
        jax.nn.silu(normed_first * own_first)
        .astype(jnp.bfloat16)
        .reshape(rows_all, canvas_cols, own)
    )
    fused = own % 128 == 0 and n == 2 * m
    spread_first = side_by_side(hidden_first)
    if fused:
        conv_output = conv_scatter_fused(spread_first, conv_first, canvas_cols, n, 0)
    else:
        conv_output = conv_scatter(hidden_first, conv_first, n)
    conv_output = conv_output + shift_vector
    normed_second, inverse_second = group_forward(conv_output, size)
    hidden_second = (
        jax.nn.silu(normed_second * own_second)
        .astype(jnp.bfloat16)
        .reshape(rows_all, canvas_cols, own)
    )
    spread_second = side_by_side(hidden_second)
    if fused:
        conv_again = conv_scatter_fused(spread_second, conv_second, canvas_cols, n, 1)
    else:
        conv_again = conv_scatter(hidden_second, conv_second, n)
    residual = pixels + conv_again
    down_patch = (
        residual.astype(jnp.bfloat16)
        .reshape(rows_all // 2, 2, token_cols, 2, own)
        .transpose(0, 2, 1, 3, 4)
        .reshape(token_total, 4 * own)
    )
    down_matrix = down_weight.reshape(4 * own, width_all)
    stream = tokens_scatter(down_patch, down_matrix[None], False, n, 2)
    normed_attend, inverse_attend = layer_forward(stream)
    input_attend = (normed_attend * (1.0 + scale_attend) + shift_attend).astype(jnp.bfloat16)
    all_attend, qkv_rows = tokens_gather(
        input_attend, qkv_weight, False, (jnp.bfloat16,), lambda value: (value,), n, 3
    )
    qkv_rows = qkv_rows.reshape(token_total, 3, head_count, HEAD_DIM)
    queries = qkv_rows[:, 0]
    key_rows = qkv_rows[:, 1]
    value_rows = qkv_rows[:, 2]
    token_index = jnp.arange(token_total, dtype=jnp.int32)
    key_valid = (token_index // token_cols < extents[0, 0]) & (
        token_index % token_cols < extents[0, 1]
    )
    mixed_heads, log_totals = attend_forward(queries, key_rows, value_rows, key_valid, block_rows)
    mixed_low = mixed_heads.reshape(token_total, local_width).astype(jnp.bfloat16)
    stream_mid = stream + tokens_scatter(mixed_low, out_weight[None], False, n, 4)
    normed_mlp, inverse_mlp = layer_forward(stream_mid)
    input_mlp = (normed_mlp * (1.0 + scale_mlp) + shift_mlp).astype(jnp.bfloat16)
    all_mlp, upper_proj, activated = tokens_gather(
        input_mlp,
        up_weight[None],
        False,
        (jnp.float32, jnp.bfloat16),
        lambda value: (value, jax.nn.gelu(value, approximate=True)),
        n,
        5,
    )
    final_stream = stream_mid + scatter_rows(
        jnp.dot(activated, proj_weight, preferred_element_type=jnp.float32)
    )
    output = final_stream.astype(jnp.bfloat16).reshape(1, token_rows, token_cols, width_all)

    grad_final_low = cotangent[0].reshape(local_tokens, width_all)
    grad_final = grad_final_low.astype(jnp.float32)
    all_final = gather_rows(grad_final_low)
    grad_act = jnp.einsum("le,fe->lf", all_final, proj_weight, preferred_element_type=jnp.float32)
    gelu_pull = jax.vjp(partial(jax.nn.gelu, approximate=True), upper_proj)[1]
    grad_upper = gelu_pull(grad_act)[0].astype(jnp.bfloat16)
    grad_normed_mlp = tokens_scatter(grad_upper, up_weight[None], True, n, 6)
    grad_proj = jnp.einsum("lf,le->fe", activated, all_final, preferred_element_type=jnp.float32)
    grad_up = jnp.einsum("le,lf->ef", all_mlp, grad_upper, preferred_element_type=jnp.float32)
    grad_mid_norm, grad_scale_mlp, grad_shift_mlp = layer_backward(
        grad_normed_mlp, normed_mlp, inverse_mlp, scale_mlp
    )
    grad_mid = grad_final + grad_mid_norm
    all_mid, grad_mixed_low = tokens_gather(
        grad_mid.astype(jnp.bfloat16),
        out_weight[None],
        True,
        (jnp.bfloat16,),
        lambda value: (value,),
        n,
        7,
    )
    grad_mixed_low = grad_mixed_low.reshape(token_total, head_count, HEAD_DIM)
    grad_out = jnp.einsum("lh,le->he", mixed_low, all_mid, preferred_element_type=jnp.float32)
    grad_query, grad_keys, grad_values = attend_backward(
        queries, key_rows, value_rows, key_valid, log_totals, grad_mixed_low, block_rows
    )
    grad_qkv = (
        jnp.stack([grad_query, grad_keys, grad_values], axis=1)
        .astype(jnp.bfloat16)
        .reshape(token_total, 3, local_width)
    )
    grad_normed_attend = tokens_scatter(
        grad_qkv.reshape(token_total, 3 * local_width), qkv_weight, True, n, 8
    )
    grad_qkv_weight = jnp.einsum(
        "le,ljf->jef", all_attend, grad_qkv, preferred_element_type=jnp.float32
    )
    grad_stream_norm, grad_scale_attend, grad_shift_attend = layer_backward(
        grad_normed_attend, normed_attend, inverse_attend, scale_attend
    )
    grad_stream = grad_mid + grad_stream_norm
    all_stream, grad_tap_patch = tokens_gather(
        grad_stream.astype(jnp.bfloat16),
        down_matrix[None],
        True,
        (jnp.float32,),
        lambda value: (value,),
        n,
        9,
    )
    grad_down = jnp.einsum(
        "lk,le->ke", down_patch, all_stream, preferred_element_type=jnp.float32
    ).reshape(4, own, width_all)
    grad_residual = (
        grad_tap_patch.reshape(rows_all // 2, token_cols, 2, 2, own)
        .transpose(0, 2, 1, 3, 4)
        .reshape(pixel_total, own)
    )
    def back(grad_low, hidden, spread, kernel, number):
        if fused:
            acc, parts = conv_back_fused(grad_low, spread.T, kernel, canvas_cols, n, number)
            return join_columns(acc, canvas_cols), parts.reshape(m, 9 * own, -1)
        grad_hidden, grad_kernel = conv_backward(grad_low, hidden, kernel, n)
        return grad_hidden, by_images(grad_kernel, m)

    grad_hidden_second, parts_second = back(
        grad_residual.astype(jnp.bfloat16), hidden_second, spread_second, conv_second, 10
    )
    grad_conv_output, grad_gain_second = group_backward(
        grad_hidden_second, normed_second, inverse_second, own_second, size
    )
    grad_shift = jnp.sum(grad_conv_output, axis=0)
    grad_hidden_first, parts_first = back(
        grad_conv_output.astype(jnp.bfloat16), hidden_first, spread_first, conv_first, 11
    )
    grad_base, grad_gain_first = group_backward(
        grad_hidden_first, normed_first, inverse_first, own_first, size
    )
    image_turned = (grad_residual + grad_base).astype(jnp.bfloat16)
    image_grad = lax.all_to_all(
        image_turned.reshape(rows_all, canvas_cols, own), "mp", 0, 2, tiled=True
    )[None]

    grad_modulation = jnp.concatenate(
        [grad_scale_attend, grad_shift_attend, grad_scale_mlp, grad_shift_mlp]
    )
    ada_columns = lax.psum_scatter(
        grad_modulation[None].astype(jnp.bfloat16), "mp", scatter_dimension=1, tiled=True
    ).astype(jnp.float32)
    embed_float = embedding.astype(jnp.float32)
    embed_term = jnp.dot(
        grad_shift[None], shift_weight.astype(jnp.float32).T, precision=PRECISE
    ) + jnp.dot(ada_columns, ada_weight.astype(jnp.float32).T, precision=PRECISE)
    embedding_grad = lax.psum(embed_term, "mp")
    packed = jnp.concatenate([embed_float[0], grad_shift, ada_columns[0]])
    every = lax.all_gather(packed, "dp", axis=0)
    embed_count = embedding.shape[1]
    embed_rows = lax.dynamic_slice_in_dim(
        every[:, :embed_count], me_dp * (embed_count // m), embed_count // m, axis=1
    )
    grad_shift_weight = jnp.dot(
        embed_rows.T, every[:, embed_count : embed_count + own], precision=PRECISE
    )
    grad_ada_weight = jnp.dot(embed_rows.T, every[:, embed_count + own :], precision=PRECISE)
    gains = lax.all_gather(jnp.stack([grad_gain_first, grad_gain_second]), ("dp", "mp"), axis=0)
    gains = jnp.sum(gains.reshape(m, n, 2, own), axis=0).transpose(1, 0, 2).reshape(2, -1)
    piece = channel_count // (m * n)
    gains = lax.dynamic_slice_in_dim(gains, (me_dp * n + me_mp) * piece, piece, axis=1)
    return (
        output,
        image_grad,
        embedding_grad,
        gains[0],
        turn_kernel(parts_first, 9, m, n),
        gains[1],
        turn_kernel(parts_second, 9, m, n),
        grad_shift_weight,
        turn_kernel(by_images(grad_down, m), 4, m, n),
        grad_ada_weight,
        dp_rows(grad_qkv_weight, 1),
        dp_rows(grad_out, 1),
        dp_rows(grad_up, 0),
        dp_rows(grad_proj, 1),
    )


def solution(mesh):
    placed = (
        P("dp", "mp", None, None),
        P("dp", None),
        P("dp", None),
        P(),
        P(None, "mp", None),
        P(),
        P(None, "mp", None),
        P(None, "mp"),
        P(None, "mp", None),
        P(None, "mp"),
        P(None, None, "mp"),
        P("mp", None),
        P(None, "mp"),
        P("mp", None),
        P("dp", "mp", None, None),
    )
    return jax.shard_map(
        local,
        mesh=mesh,
        in_specs=placed,
        out_specs=(
            P("dp", "mp", None, None),
            P("dp", "mp", None, None),
            P("dp", None),
            P(("dp", "mp")),
            P(None, "dp", "mp"),
            P(("dp", "mp")),
            P(None, "dp", "mp"),
            P("dp", "mp"),
            P(None, "dp", "mp"),
            P("dp", "mp"),
            P(None, "dp", "mp"),
            P("mp", "dp"),
            P("dp", "mp"),
            P("mp", "dp"),
        ),
        check_vma=False,
    )
```

time: 2140 us -> 1310 us (0.61)
  waiting for transfers between devices: 1340 us -> 66.1 us
  Pallas kernels: 0 us -> 727 us
  local copies, waits for them, and re-layouts: 279 us -> 111 us
  matrix products: 284 us -> 119 us
  blocking collectives: 109 us -> 140 us
    pallas_call x0 -> x12, Pallas kernels: none -> 727 us  [the longest x4 211 us: tokens_scatter(): pl.pallas_call(partial(tokens_scatter_kernel, chips, turned), out_shape=j...]
    all_gather x7 -> x1, waiting for transfers between devices: 496 us -> 0.01 us  [gather_rows(): return lax.all_gather(rows, 'mp', axis=0, tiled=True)]
    reduce_scatter x14 -> x5, waiting for transfers between devices: 464 us -> 7.65 us  [the longest x4 7.63 us: dp_rows(): lax.psum_scatter(grad.astype(jnp.bfloat16), 'dp', scatter_dimension=dim,...]
    unnamed x27 -> x13, waiting for transfers between devices: 356 us -> 0.88 us
    unnamed x166 -> x74, local copies, waits for them, and re-layouts: 217 us -> 13 us
    dot_general x21 -> x9, matrix products: 212 us -> 45.1 us  [the longest x1 12.6 us: local(): jnp.einsum('le,fe->lf', all_final, proj_weight, preferred_element_type=jn...]
    all_gather x1 -> x2, blocking collectives: 19.8 us -> 59.7 us  [the longest x1 53.5 us: local(): lax.all_gather(jnp.stack([grad_gain_first, grad_gain_second]), ('dp', 'mp...]
    ppermute x8 -> x6, waiting for transfers between devices: 21.3 us -> 57.6 us  [turn_kernel(): moved = lax.ppermute(half, ('dp', 'mp'), route)]
  transfers between devices with their start and end apart: 33 -> 18, of which waited for: 24 -> 5; matrix products, arithmetic and copies ran while one was open for 20% -> 17% of each run, Pallas kernels for 0% -> 49%
where the time goes in v1:
time: 1310 us; the launch traced here: 1300 us
  Pallas kernels  727 us (55%)
  blocking collectives  140 us (11%)
  matrix products  119 us (9%)
  local copies, waits for them, and re-layouts  111 us (8%)
  other arithmetic  76.8 us (6%)
  waiting for transfers between devices  66.1 us (5%)
  starting transfers between devices  43.8 us (3%)
  between operations  15.5 us (1%)
    pallas_call x4, Pallas kernels, tokens_scatter(): pl.pallas_call(partial(tokens_scatter_kernel, chips, turned), out_shape=j...  211 us
    pallas_call x4, Pallas kernels, tokens_gather(): pl.pallas_call(partial(tokens_gather_kernel, chips, turned, shape_out, le...  180 us
    pallas_call x2, Pallas kernels, conv_back_fused(): pl.pallas_call(partial(conv_back_kernel, chips, cols), out_shape=(jax.Sha...  180 us
    pallas_call x2, Pallas kernels, conv_scatter_fused(): pl.pallas_call(partial(conv_scatter_kernel, chips, cols), out_shape=jax.S...  156 us
    ppermute x6, waiting for transfers between devices, turn_kernel(): moved = lax.ppermute(half, ('dp', 'mp'), route)  57.6 us
    all_gather x1, blocking collectives, local(): lax.all_gather(jnp.stack([grad_gain_first, grad_gain_second]), ('dp', 'mp...  53.5 us
    all_gather x1, blocking collectives, local(): lax.all_gather(jnp.dot(embedding, ada_weight, preferred_element_type=jnp....  44.7 us
    psum x1, blocking collectives, local(): embedding_grad = lax.psum(embed_term, 'mp')  35.2 us
  transfers between devices with their start and end apart: 18, of which 5 were waited for; matrix products, arithmetic and copies ran while one was open for 17% of the time, Pallas kernels for 49%

profile of v1, /device:TPU:9, one launch (start us, length us, event | category | flops | bytes accessed | tf_op | source)
XLA Modules:
  0.0 1299.1 jit_solution(3515912696489757975)
XLA Ops:
  9.7 5.8 all-to-all-start
  18.2 44.7 %all-gather = f32[8192]{0:T(1024)S(1)} all-gather(f32[1024]{0:T(1024)S(1)} %bitcast.351), channel_id=2, replica_groups=mesh['dp'=4,'mp'=8] {'mp'}, dimensions={0}, use_global_device_ids=true | all-gather | bytes 36864 | tf_op jit(solution)/shard_map/all_gather | solution.py:779
  75.4 78.2 %shard_map.254 = f32[4096,128]{1,0:T(8,128)} custom-call(bf16[4352,384]{1,0:T(8,128)(2,1)} %bitcast.286, bf16[3,384,1024]{2,1,0:T(8,128)(2,1)} %bitcast.298), custom_call_target="tpu_custom_call" | custom-call | tf_op jit(solution)/shard_map/pallas_call | solution.py:563
  164.1 78.0 %shard_map.255 = f32[4096,128]{1,0:T(8,128)} custom-call(bf16[4352,384]{1,0:T(8,128)(2,1)} %bitcast.288, bf16[3,384,1024]{2,1,0:T(8,128)(2,1)} %bitcast.296), custom_call_target="tpu_custom_call" | custom-call | tf_op jit(solution)/shard_map/pallas_call | solution.py:563
  246.6 41.8 %shard_map.256 = f32[128,2048]{1,0:T(8,128)} custom-call(bf16[1024,512]{1,0:T(8,128)(2,1)} %reshape.468.x_ref, bf16[1,512,2048]{2,1,0:T(8,128)(2,1)} %bitcast.301), custom_call_target="tpu_custom_call" | custom-call | tf_op jit(solution)/shard_map/pallas_call | solution.py:694
  292.5 39.2 %shard_map.257 = (bf16[1024,2048]{1,0:T(8,128)(2,1)}, bf16[1024,768]{1,0:T(8,128)(2,1)}) custom-call(bf16[128,2048]{1,0:T(8,128)(2,1)} %add_convert_fusion.4.x_ref, bf16[3,2048,256]{2,1,0:T(8,128)(2,1)} %w_ref.3), custom_call_target="tpu_custom_call" | custom-call | tf_op jit(solution)/shard_map/pallas_call | solution.py:732
  331.7 4.3 reshape.469
  340.4 13.0 %while.28 = (s32[]{:T(128)}, bf16[2,512,2,128]{3,1,2,0:T(8,128)(2,1)}, f32[2,2,512]{2,1,0:T(2,128)S(1)}, bf16[2,512,2,128]{3,1,2,0:T(8,128)(2,1)}, bf16[1024,2,1...) while((s32[]{:T(128)}, ...), condition=%wide.region_14.15_spmd.clone, body=%wide.region_11.14_spmd.clone.sunk | while | flops 549468160 | bytes 20746444 | solution.py:165
  356.8 47.5 %shard_map.258 = f32[128,2048]{1,0:T(8,128)} custom-call(bf16[1024,256]{1,0:T(8,128)(2,1)} %bitcast.322, bf16[1,256,2048]{2,1,0:T(8,128)(2,1)} %bitcast.314), custom_call_target="tpu_custom_call" | custom-call | tf_op jit(solution)/shard_map/pallas_call | solution.py:694
  407.7 40.7 %shard_map.259 = (bf16[1024,2048]{1,0:T(8,128)(2,1)}, f32[1024,1024]{1,0:T(8,128)}, bf16[1024,1024]{1,0:T(8,128)(2,1)}) custom-call(bf16[128,2048]{1,0:T(8,128)(2,1)} %add_convert_fusion.3.x_ref, bf16[1,2048,1024]{2,1,0:T(8,128)(2,1)} %bitcast.290), custom_call_target="tpu_custom_call" | custom-call | tf_op jit(solution)/shard_map/pallas_call | solution.py:732
  448.5 9.3 convolution_convert_fusion.2
  460.3 12.6 fusion.84.x_ref
  472.9 73.6 %shard_map.260 = f32[128,2048]{1,0:T(8,128)} custom-call(bf16[1024,1024]{1,0:T(8,128)(2,1)} %fusion.84.x_ref, bf16[1,2048,1024]{2,1,0:T(8,128)(2,1)} %bitcast.291), custom_call_target="tpu_custom_call" | custom-call | tf_op jit(solution)/shard_map/pallas_call | solution.py:694
  548.6 3.8 fusion.126
  552.4 39.5 %shard_map.261 = (bf16[1024,2048]{1,0:T(8,128)(2,1)}, bf16[1024,256]{1,0:T(8,128)(2,1)}) custom-call(bf16[128,2048]{1,0:T(8,128)(2,1)} %get-tuple-element.406.x_ref, bf16[1,256,2048]{2,1,0:T(8,128)(2,1)} %bitcast.315), custom_call_target="tpu_custom_call" | custom-call | tf_op jit(solution)/shard_map/pallas_call | solution.py:732
  593.9 53.5 %while.29 = (s32[]{:T(128)}, f32[1024,2,128]{0,2,1:T(8,128)}, f32[1024,2,128]{0,2,1:T(8,128)}, bf16[2,512,2,128]{3,1,0,2:T(8,128)(2,1)}, bf16[2,512,2,128]{3,1,2...) while((s32[]{:T(128)}, f32[1024,2,128]{0,2,1:T(8,128)}, ...), condition=%wide.region_22.23_spmd.clone, body=%wide.region_20.22_spmd.clone.sunk | while | flops 1357925376 | bytes 72890592 | solution.py:201
  603.5 8.0 fusion.192
  611.6 8.2 fusion.190
  630.8 8.0 fusion.192
  638.9 8.5 fusion.190
  656.1 4.9 convert_element_type.186.x_ref
  661.0 48.1 %shard_map.262 = f32[128,2048]{1,0:T(8,128)} custom-call(bf16[1024,768]{1,0:T(8,128)(2,1)} %convert_element_type.186.x_ref, bf16[3,2048,256]{2,1,0:T(8,128)(2,1)} %w_ref.3), custom_call_target="tpu_custom_call" | custom-call | tf_op jit(solution)/shard_map/pallas_call | solution.py:694
  715.7 60.5 %shard_map.263 = (bf16[1024,2048]{1,0:T(8,128)(2,1)}, f32[1024,512]{1,0:T(8,128)}) custom-call(bf16[128,2048]{1,0:T(8,128)(2,1)} %add_convert_fusion.1.x_ref, bf16[1,512,2048]{2,1,0:T(8,128)(2,1)} %bitcast.302), custom_call_target="tpu_custom_call" | custom-call | tf_op jit(solution)/shard_map/pallas_call | solution.py:732
  776.2 5.8 fusion.92
  782.0 4.5 reshape.485
  790.8 4.4 convolution_convert_fusion.3
  795.3 5.8 copy.162
  808.5 84.2 %shard_map.264 = (f32[4096,384]{1,0:T(8,128)}, bf16[4,3,384,256]{3,2,1,0:T(8,128)(2,1)}) custom-call(bf16[4096,128]{1,0:T(8,128)(2,1)} %bitcast.312, bf16[3,384,1024]{2,1,0:T(8,128)(2,1)} %bitcast.297, bf16[384,4352]{1,0:T(8,128)(2,1)} %bitcast.295), custom_call_target="tpu_custom_call" | custom-call | tf_op jit(solution)/shard_map/pallas_call | solution.py:633
  892.7 5.8 copy.163
  907.7 3.9 fusion.110
  911.6 95.5 %shard_map.265 = (f32[4096,384]{1,0:T(8,128)}, bf16[4,3,384,256]{3,2,1,0:T(8,128)(2,1)}) custom-call(bf16[4096,128]{1,0:T(8,128)(2,1)} %get-tuple-element.417.g_ref, bf16[3,384,1024]{2,1,0:T(8,128)(2,1)} %bitcast.299, bf16[384,4352]{1,0:T(8,128)(2,1)} %bitcast.294), custom_call_target="tpu_custom_call" | custom-call | tf_op jit(solution)/shard_map/pallas_call | solution.py:633
  1007.2 9.4 convolution_convert_fusion
  1016.6 9.4 convolution_convert_fusion.1
  1030.5 3.9 copy.161
  1035.6 7.7 fusion.95
  1046.3 4.4 fusion.122
  1052.3 4.6 add_convert_fusion
  1056.9 21.1 %all-to-all-start.1 = ((bf16[32,128,128]{2,1,0:T(8,128)(2,1)}), bf16[32,128,128]{2,1,0:T(8,128)(2,1)}, u32[]{:S(2)}, u32[]{:S(2)}) async-start(bf16[32,128,128]{2,1,0:T(8,128)(2,1)} %add_convert_fusion), calls=%async_computation.2 | async-start | bytes 2097152 | tf_op jit(solution)/shard_map/all_to_all | solution.py:936
  1078.0 53.5 %all-gather.3 = f32[32,2,128]{2,1,0:T(2,128)S(1)} all-gather(f32[1,2,128]{2,1,0:T(2,128)S(1)} %maximum_bitcast_fusion), channel_id=3, replica_groups=mesh['dp'=4,'mp'=8] {'dp','mp'}, dimensions={0}, use_global_device_ids=true | all-gather | bytes 33792 | tf_op jit(solution)/shard_map/all_gather | solution.py:961
  1133.6 6.3 all-gather.4
  1143.8 4.9 collective-permute-start.4
  1153.9 35.2 %psum.7 = f32[1,1024]{1,0:T(1,128)} all-reduce(f32[1,1024]{1,0:T(1,128)S(1)} %bitcast.352), channel_id=1, replica_groups=mesh['dp'=4,'mp'=8] {'mp'}, use_global_device_ids=true, to_apply=%region_39.40 | all-reduce | flops 1024 | bytes 8192 | tf_op jit(solution)/shard_map/psum | solution.py:950
  1202.5 5.9 collective-permute-start.3
  1213.7 41.0 %collective-permute-done.2 = bf16[9,128,128]{2,1,0:T(8,128)(2,1)} collective-permute-done((bf16[9,128,128]{2,1,0:T(8,128)(2,1)S(1)}, bf16[9,128,128]{2,1,0:T(8,128)(2,1)}, u32[]{:S(2)}, u32[]{:S(2)}) %collective-permute-start.2) | collective-permute-done | bytes 294944 | tf_op jit(solution)/shard_map/ppermute | solution.py:125
  1255.8 5.2 collective-permute-done.3
  1262.0 5.3 collective-permute-done
  1267.5 6.1 collective-permute-done.1
  1281.6 7.6 reduce-scatter.20.cloned.1.call-done
  (301 shorter events, 176.7 us)
Async XLA Ops:
  7.2 10.7 copy-start
  7.2 10.7 copy-start.18
  9.7 53.1 %copy-start.34 = (s32[1,2]{1,0:T(1,128)S(1)}, s32[1,2]{1,0:T(1,128)}, u32[]{:S(2)}) copy-start(s32[1,2]{1,0:T(1,128)} %param.21) | copy-start | bytes 28
  9.7 53.7 %copy-start.13 = (bf16[1024,128]{1,0:T(8,128)(2,1)S(1)}, bf16[1024,128]{1,0:T(8,128)(2,1)}, u32[]{:S(2)}) copy-start(bf16[1024,128]{1,0:T(8,128)(2,1)} %param.26) | copy-start | bytes 786436
  9.7 53.9 %all-to-all-start = ((bf16[4,128,1024]{1,0,2:T(4,128)(2,1)}), bf16[4,128,1024]{1,0,2:T(4,128)(2,1)S(1)}, u32[]{:S(2)}, u32[]{:S(2)}) async-start(bf16[4,128,1024]{1,0,2:T(4,128)(2,1)} %bitcast.316), calls=%async_computation | async-start | bytes 2097152 | tf_op jit(solution)/shard_map/all_to_all | solution.py:789
  15.5 444.8 %all-gather.7.cloned.1.call-start = ((), (), s32[]{:S(2)}) async-start(), calls=%async_computation.12 | async-start | bytes 4718592 | tf_op jit(solution)/shard_map/all_gather | solution.py:62
  16.2 532.4 %reduce-scatter.18.cloned.1.call-start = ((), (), s32[]{:S(2)}) async-start(), calls=%async_computation.11 | async-start | bytes 4718592 | tf_op jit(solution)/shard_map/reduce_scatter | solution.py:66
  17.1 52.8 %copy-start.30 = (f32[128]{0:T(128)}, f32[128]{0:T(128)S(1)}, u32[]{:S(2)}) copy-start(f32[128]{0:T(128)S(1)} %dynamic_slice.46) | copy-start | bytes 1540
  17.8 140.8 %copy-start.32 = (f32[128]{0:T(128)}, f32[128]{0:T(128)S(1)}, u32[]{:S(2)}) copy-start(f32[128]{0:T(128)S(1)} %dynamic_slice.47) | copy-start | bytes 1540
  63.6 95.1 %copy-start.20 = (f32[128]{0:T(128)}, f32[128]{0:T(128)S(1)}, u32[]{:S(2)}) copy-start(f32[128]{0:T(128)S(1)} %convolution_bitcast_fusion) | copy-start | bytes 1540
  66.0 3.9 copy-start.22
  69.9 3.1 copy-start.26
  156.2 4.8 copy-start.24
  158.7 3.2 copy-start.28
  288.5 3.0 copy-start.4
  343.7 1.2 copy-start.15
  457.8 674.6 %reduce-scatter.28.cloned.1.call-start = ((), (), s32[]{:S(2)}) async-start(), calls=%async_computation.17 | async-start | bytes 2359296 | tf_op jit(solution)/shard_map/reshape.9
  598.5 2.3 copy-start.1
  598.5 2.3 copy-start.7
  624.4 3.6 copy-start.1
  624.4 3.6 copy-start.7
  712.8 428.6 %reduce-scatter.34.cloned.1.call-start = ((), (), s32[]{:S(2)}) async-start(), calls=%async_computation.20 | async-start | bytes 2621440
  715.7 60.5 %copy-start.12 = (bf16[512,1024]{1,0:T(8,128)(2,1)S(1)}, bf16[512,1024]{1,0:T(8,128)(2,1)}, u32[]{:S(2)}) copy-start(bf16[512,1024]{1,0:T(8,128)(2,1)} %copy.179) | copy-start | bytes 3145732
  789.8 402.5 %reduce-scatter.22.cloned.1.call-start = ((), (), s32[]{:S(2)}) async-start(), calls=%async_computation.14 | async-start | bytes 1310720 | tf_op jit(solution)/shard_map/reduce_scatter | solution.py:100
  795.3 400.9 %reduce-scatter.32.cloned.1.call-start = ((), (), s32[]{:S(2)}) async-start(), calls=%async_computation.19 | async-start | bytes 2949120
  892.7 315.7 %reduce-scatter.30.cloned.1.call-start = ((), (), s32[]{:S(2)}) async-start(), calls=%async_computation.18 | async-start | bytes 2949120
  901.2 2.5 copy-start.2
  901.3 2.5 copy-start.21
  901.3 2.5 copy-start.25
  901.3 2.5 copy-start.29
  901.3 2.5 copy-start.33
  1007.1 268.9 %reduce-scatter.26.cloned.1.call-start = ((), (), s32[]{:S(2)}) async-start(), calls=%async_computation.16 | async-start | bytes 5242880 | tf_op jit(solution)/shard_map/reduce_scatter | solution.py:100
  1016.5 262.3 %reduce-scatter.24.cloned.1.call-start = ((), (), s32[]{:S(2)}) async-start(), calls=%async_computation.15 | async-start | bytes 5242880 | tf_op jit(solution)/shard_map/reduce_scatter | solution.py:100
  1026.0 2.1 copy-start.8
  1026.0 263.2 %reduce-scatter.20.cloned.1.call-start = ((), (), s32[]{:S(2)}) async-start(), calls=%async_computation.13 | async-start | bytes 3932160 | tf_op jit(solution)/shard_map/reduce_scatter | solution.py:100
  1030.5 5.1 copy-start.17
  1043.3 3.0 copy-start.3
  1043.3 3.0 copy-start.23
  1043.3 3.0 copy-start.27
  1043.4 3.0 copy-start.31
  1056.8 75.3 %copy-start.14 = (bf16[1024,128]{1,0:T(8,128)(2,1)S(1)}, bf16[1024,128]{1,0:T(8,128)(2,1)}, u32[]{:S(2)}) copy-start(bf16[1024,128]{1,0:T(8,128)(2,1)} %param.26) | copy-start | bytes 786436
  1056.9 132.3 %all-to-all-start.1 = ((bf16[32,128,128]{2,1,0:T(8,128)(2,1)}), bf16[32,128,128]{2,1,0:T(8,128)(2,1)}, u32[]{:S(2)}, u32[]{:S(2)}) async-start(bf16[32,128,128]{2,1,0:T(8,128)(2,1)} %add_convert_fusion), calls=%async_computation.2 | async-start | bytes 2097152 | tf_op jit(solution)/shard_map/all_to_all | solution.py:936
  1143.8 50.4 %collective-permute-start.4 = (bf16[4,128,256]{2,1,0:T(8,128)(2,1)S(1)}, bf16[4,128,256]{2,1,0:T(8,128)(2,1)}, u32[]{:S(2)}, u32[]{:S(2)}) collective-permute-start(bf16[4,128,256]{2,1,0:T(8,128)(2,1)S(1)} %bitcast.335), channel_id=1, source_target_pairs={{0,0},{1,1},{2,8},{3,9},{4,16},{5,17},{6,24},{7,25},{8,2},{9,3},{1... | collective-permute-start | bytes 786440 | tf_op jit(solution)/shard_map/ppermute | solution.py:125
  1151.5 43.7 %collective-permute-start.5 = (bf16[4,128,256]{2,1,0:T(8,128)(2,1)}, bf16[4,128,256]{2,1,0:T(8,128)(2,1)}, u32[]{:S(2)}, u32[]{:S(2)}) collective-permute-start(bf16[4,128,256]{2,1,0:T(8,128)(2,1)} %bitcast.251), channel_id=1, source_target_pairs={{0,1},{1,0},{2,9},{3,8},{4,17},{5,16},{6,25},{7,24},{8,3},{9,2},{1... | collective-permute-start | bytes 786440 | tf_op jit(solution)/shard_map/ppermute | solution.py:125
  1199.5 55.2 %collective-permute-start.2 = (bf16[9,128,128]{2,1,0:T(8,128)(2,1)S(1)}, bf16[9,128,128]{2,1,0:T(8,128)(2,1)}, u32[]{:S(2)}, u32[]{:S(2)}) collective-permute-start(bf16[9,128,128]{2,1,0:T(8,128)(2,1)S(1)} %bitcast.331), channel_id=1, source_target_pairs={{0,0},{1,1},{2,8},{3,9},{4,16},{5,17},{6,24},{7,25},{8,2},{9,3},{1... | collective-permute-start | bytes 884744 | tf_op jit(solution)/shard_map/ppermute | solution.py:125
  1202.5 58.5 %collective-permute-start.3 = (bf16[9,128,128]{2,1,0:T(8,128)(2,1)S(1)}, bf16[9,128,128]{2,1,0:T(8,128)(2,1)}, u32[]{:S(2)}, u32[]{:S(2)}) collective-permute-start(bf16[9,128,128]{2,1,0:T(8,128)(2,1)S(1)} %bitcast.332), channel_id=1, source_target_pairs={{0,1},{1,0},{2,9},{3,8},{4,17},{5,16},{6,25},{7,24},{8,3},{9,2},{1... | collective-permute-start | bytes 884744 | tf_op jit(solution)/shard_map/ppermute | solution.py:125
  1211.7 55.6 %collective-permute-start = (bf16[9,128,128]{2,1,0:T(8,128)(2,1)S(1)}, bf16[9,128,128]{2,1,0:T(8,128)(2,1)S(1)}, u32[]{:S(2)}, u32[]{:S(2)}) collective-permute-start(bf16[9,128,128]{2,1,0:T(8,128)(2,1)S(1)} %bitcast.334), channel_id=1, source_target_pairs={{0,0},{1,1},{2,8},{3,9},{4,16},{5,17},{6,24},{7,25},{8,2},{9,3},{1... | collective-permute-start | bytes 884744 | tf_op jit(solution)/shard_map/ppermute | solution.py:125
  1213.6 60.0 %collective-permute-start.1 = (bf16[9,128,128]{2,1,0:T(8,128)(2,1)S(1)}, bf16[9,128,128]{2,1,0:T(8,128)(2,1)S(1)}, u32[]{:S(2)}, u32[]{:S(2)}) collective-permute-start(bf16[9,128,128]{2,1,0:T(8,128)(2,1)S(1)} %bitcast.333), channel_id=1, source_target_pairs={{0,1},{1,0},{2,9},{3,8},{4,17},{5,16},{6,25},{7,24},{8,3},{9,2},{1... | collective-permute-start | bytes 884744 | tf_op jit(solution)/shard_map/ppermute | solution.py:125
  (10 other events, 9.5 us)
Sparse Core Ops, SparseCore 0:
  17.9 57.1 all-gather.6
  457.9 65.6 reduce-scatter.17
  713.0 45.4 reduce-scatter.27
  789.9 39.3 reduce-scatter.33
  832.9 27.7 reduce-scatter.21
  892.8 52.5 reduce-scatter.31
  1007.2 52.4 reduce-scatter.29
  1062.7 52.6 reduce-scatter.25
  1118.6 74.4 reduce-scatter.23
  1195.9 93.2 reduce-scatter.19

commit v2 on v1

--- a/solution.py
+++ b/solution.py
@@ -96,23 +96,16 @@
     return (join_columns(acc, col_count), grad_kernel)
 
 
-def dp_rows(grad, dim):
-    return lax.psum_scatter(
-        grad.astype(jnp.bfloat16), "dp", scatter_dimension=dim, tiled=True
-    ).astype(jnp.float32)
-
-
 def by_images(grad, m):
     taps, own, outs = grad.shape
     return grad.astype(jnp.bfloat16).reshape(taps * own, m, outs // m).transpose(1, 0, 2)
 
 
-def turn_kernel(parts, taps, m, n):
-    own = parts.shape[1] // taps
-    outs = parts.shape[2] * m
-    mine = lax.psum_scatter(parts, "dp", scatter_dimension=0, tiled=False)
+def turn_kernel(mine, taps, m, n):
+    own = mine.shape[0] // taps
+    outs = mine.shape[1] * m
     ratio = n // m
-    pieces = mine.reshape(taps, own, ratio, outs // n)
+    pieces = mine.astype(jnp.bfloat16).reshape(taps, own, ratio, outs // n)
     me = lax.axis_index("mp") % ratio
     result = jnp.zeros((taps, ratio, own, outs // n), jnp.bfloat16)
     for shift in range(ratio):
@@ -126,6 +119,10 @@
         place = (me - shift + ratio) % ratio
         result = lax.dynamic_update_slice(result, moved[:, None], (0, place, 0, 0))
     return result.reshape(taps, ratio * own, outs // n).astype(jnp.float32)
+
+
+def added(received):
+    return jnp.sum(received.astype(jnp.float32), axis=0)
 
 
 def layer_forward(stream):
@@ -213,8 +210,9 @@
 
 
 class Line:
-    def __init__(self, chips):
+    def __init__(self, chips, images):
         self.chips = chips
+        self.images = images
         self.dp = lax.axis_index("dp")
         self.mp = lax.axis_index("mp")
         self.z = self.mp // 2
@@ -225,8 +223,35 @@
         self.down = (self.dp, self.mp - 2)
         self.sibling = (self.dp, 2 * self.z + 1 - self.c)
 
-    def barrier(self):
+    def count(self, axis):
+        return {"dp": self.images, "mp": 2 * self.chips, "all": 2 * self.chips * self.images}[axis]
+
+    def index(self, axis):
+        return {"dp": self.dp, "mp": self.mp, "all": self.dp * 2 * self.chips + self.mp}[axis]
+
+    def place(self, axis, index):
+        if axis == "dp":
+            return (index, self.mp)
+        if axis == "mp":
+            return (self.dp, index)
+        return (index // (2 * self.chips), index % (2 * self.chips))
+
+    def peer(self, axis, step):
+        return lax.rem(self.index(axis) + step, self.count(axis))
+
+    def barrier(self, axes, neighbours):
         bar = pltpu.get_barrier_semaphore()
+        if "all" in axes:
+            axes = ("all",)
+        steady = 0
+        for axis in axes:
+            for step in range(1, self.count(axis)):
+                target = self.place(axis, self.peer(axis, step))
+                pl.semaphore_signal(bar, inc=1, device_id=target, device_id_type=MESH)
+            steady += self.count(axis) - 1
+        if "all" in axes or "mp" in axes or not neighbours:
+            pl.semaphore_wait(bar, steady)
+            return
         pl.semaphore_signal(bar, inc=1, device_id=self.sibling, device_id_type=MESH)
 
         @pl.when(self.has_up)
@@ -241,11 +266,88 @@
 
         @pl.when(middle)
         def _():
-            pl.semaphore_wait(bar, 3)
+            pl.semaphore_wait(bar, steady + 3)
 
         @pl.when(jnp.logical_not(middle))
         def _():
-            pl.semaphore_wait(bar, 2)
+            pl.semaphore_wait(bar, steady + 2)
+
+
+class Rider:
+    def __init__(self, axis, array, cut=None):
+        self.axis = axis
+        self.array = array
+        self.cut = cut
+
+    def result(self, count):
+        shape = list(self.array.shape)
+        if self.cut is not None:
+            shape[self.cut] //= count
+        return jax.ShapeDtypeStruct((count,) + tuple(shape), self.array.dtype)
+
+    def piece(self, ref, index, count):
+        if self.cut is None:
+            return ref
+        size = self.array.shape[self.cut] // count
+        where = [slice(None)] * len(self.array.shape)
+        where[self.cut] = pl.ds(pl.multiple_of(index * size, size), size)
+        return ref.at[tuple(where)]
+
+    def copies(self, line, src, dst, send, recv):
+        count, me = line.count(self.axis), line.index(self.axis)
+        made = [pltpu.make_async_copy(self.piece(src, me, count), dst.at[me], send.at[0])]
+        for step in range(1, count):
+            peer = line.peer(self.axis, step)
+            made.append(
+                remote(
+                    self.piece(src, peer, count),
+                    dst.at[me],
+                    send.at[step],
+                    recv.at[step],
+                    line.place(self.axis, peer),
+                )
+            )
+        return made
+
+
+def comm_call(kernel, inputs, out_shapes, scratch, riders, n, m, number, neighbours=True):
+    chips = n // 2
+    sizes = {"dp": m, "mp": n, "all": m * n}
+    counts = [sizes[rider.axis] for rider in riders]
+    ride_shapes = tuple(rider.result(count) for rider, count in zip(riders, counts))
+    any_spec = pl.BlockSpec(memory_space=pl.ANY)
+    ni, nr, no = len(inputs), len(riders), len(out_shapes)
+
+    def body(*refs):
+        main_in, ride_in = refs[:ni], refs[ni : ni + nr]
+        rest = refs[ni + nr :]
+        main_out, ride_out = rest[:no], rest[no : no + nr]
+        rest = rest[no + nr :]
+        main_scratch, sems = rest[: len(scratch)], rest[len(scratch) :]
+        line = Line(chips, m)
+        line.barrier(sorted(set(rider.axis for rider in riders)), neighbours)
+        copies = []
+        for index, rider in enumerate(riders):
+            copies += rider.copies(
+                line, ride_in[index], ride_out[index], sems[2 * index], sems[2 * index + 1]
+            )
+        for copy in copies:
+            copy.start()
+        kernel(line, *main_in, *main_out, *main_scratch)
+        for copy in copies:
+            copy.wait()
+
+    ride_sems = []
+    for count in counts:
+        ride_sems += [pltpu.SemaphoreType.DMA((count,)), pltpu.SemaphoreType.DMA((count,))]
+    return pl.pallas_call(
+        body,
+        out_shape=tuple(out_shapes) + ride_shapes,
+        in_specs=whole(ni) + [any_spec] * nr,
+        out_specs=tuple(whole(no) + [any_spec] * nr),
+        scratch_shapes=list(scratch) + ride_sems,
+        compiler_params=comm_params(number),
+    )(*inputs, *[rider.array for rider in riders])
 
 
 def remote(src, dst, send, recv, target):
@@ -266,7 +368,6 @@
 def line_gather(line, x_ref, slot, send, recv, on_own, on_pair):
     chips = line.chips
     z, c = line.z, line.c
-    line.barrier()
 
     def hop(stream, step, src, block, target):
         return remote(src, slot(block), send.at[stream, 0, step], recv.at[stream, 0, step], target)
@@ -375,7 +476,6 @@
     z = line.z
     kept, out_ref, in_ref, moving, sems = scratch
     count = kept.shape[1] // parts
-    line.barrier()
 
     def span(part):
         return pl.ds(part * count, count)
@@ -519,8 +619,7 @@
     return jnp.where(c == 0, low, high), jnp.where(c == 0, high, low)
 
 
-def conv_scatter_kernel(chips, breadth, x_ref, w_ref, o_ref, *scratch):
-    line = Line(chips)
+def conv_scatter_kernel(breadth, line, x_ref, w_ref, o_ref, *scratch):
     pixels, own = o_ref.shape
     tile = 512
 
@@ -555,23 +654,24 @@
     )
 
 
-def conv_scatter_fused(spread, kernel, cols, n, number):
+def conv_scatter_fused(spread, kernel, cols, n, m, number, riders=()):
     own = kernel.shape[2] // n
     depth = kernel.shape[1]
     pixels = spread.shape[0] - 2 * cols
-    chips = n // 2
-    return pl.pallas_call(
-        partial(conv_scatter_kernel, chips, cols),
-        out_shape=jax.ShapeDtypeStruct((pixels, own), jnp.float32),
-        in_specs=whole(2),
-        out_specs=whole(1)[0],
-        scratch_shapes=scatter_scratch(chips, pixels, own, CONV_PARTS),
-        compiler_params=comm_params(number),
-    )(spread, kernel.reshape(3, 3 * depth, kernel.shape[2]))
-
-
-def conv_back_kernel(chips, breadth, g_ref, w_ref, xt_ref, acc_ref, wg_ref, held, sums, send, recv):
-    line = Line(chips)
+    return comm_call(
+        partial(conv_scatter_kernel, cols),
+        (spread, kernel.reshape(3, 3 * depth, kernel.shape[2])),
+        (jax.ShapeDtypeStruct((pixels, own), jnp.float32),),
+        scatter_scratch(n // 2, pixels, own, CONV_PARTS),
+        riders,
+        n,
+        m,
+        number,
+    )
+
+
+def conv_back_kernel(breadth, line, g_ref, w_ref, xt_ref, acc_ref, wg_ref, held, sums, send, recv):
+    chips = line.chips
     pixels, own = g_ref.shape
     wide = w_ref.shape[1]
     tile = 512
@@ -626,25 +726,27 @@
     line_gather(line, g_ref, slot, send, recv, on_own, on_pair)
 
 
-def conv_back_fused(grad_low, spread_turned, kernel, cols, n, number):
+def conv_back_fused(grad_low, spread_turned, kernel, cols, n, m, number, riders=()):
     pixels, own = grad_low.shape
     depth = kernel.shape[1]
     chips = n // 2
-    return pl.pallas_call(
-        partial(conv_back_kernel, chips, cols),
-        out_shape=(
+    return comm_call(
+        partial(conv_back_kernel, cols),
+        (grad_low, kernel.reshape(3, 3 * depth, kernel.shape[2]), spread_turned),
+        (
             jax.ShapeDtypeStruct((pixels, 3 * depth), jnp.float32),
             jax.ShapeDtypeStruct((chips, 3, 3 * depth, 2 * own), jnp.bfloat16),
         ),
-        in_specs=whole(3),
-        out_specs=tuple(whole(2)),
-        scratch_shapes=[
+        [
             pltpu.VMEM((n, pixels + 2 * cols, own), jnp.bfloat16),
             pltpu.VMEM((3 * depth, 2 * own), jnp.float32),
         ]
         + gather_sems(chips),
-        compiler_params=comm_params(number),
-    )(grad_low, kernel.reshape(3, 3 * depth, kernel.shape[2]), spread_turned)
+        riders,
+        n,
+        m,
+        number,
+    )
 
 
 def join_columns(acc, cols):
@@ -663,8 +765,7 @@
     )
 
 
-def tokens_scatter_kernel(chips, turned, x_ref, w_ref, o_ref, *scratch):
-    line = Line(chips)
+def tokens_scatter_kernel(turned, line, x_ref, w_ref, o_ref, *scratch):
     tokens, width = o_ref.shape
     cut = width // TOKEN_PARTS
     depth = x_ref.shape[1] // w_ref.shape[0]
@@ -687,22 +788,22 @@
     line_scatter(line, scratch, TOKEN_PARTS, produce, finish, tokens)
 
 
-def tokens_scatter(x, w, turned, n, number):
+def tokens_scatter(x, w, turned, n, m, number, riders=()):
     tokens = x.shape[0] // n
     width = w.shape[1] if turned else w.shape[2]
-    chips = n // 2
-    return pl.pallas_call(
-        partial(tokens_scatter_kernel, chips, turned),
-        out_shape=jax.ShapeDtypeStruct((tokens, width), jnp.float32),
-        in_specs=whole(2),
-        out_specs=whole(1)[0],
-        scratch_shapes=scatter_scratch(chips, TOKEN_PARTS * tokens, width // TOKEN_PARTS, TOKEN_PARTS),
-        compiler_params=comm_params(number),
-    )(x, w)
-
-
-def tokens_gather_kernel(chips, turned, shape_out, outs, x_ref, w_ref, *refs):
-    line = Line(chips)
+    return comm_call(
+        partial(tokens_scatter_kernel, turned),
+        (x, w),
+        (jax.ShapeDtypeStruct((tokens, width), jnp.float32),),
+        scatter_scratch(n // 2, TOKEN_PARTS * tokens, width // TOKEN_PARTS, TOKEN_PARTS),
+        riders,
+        n,
+        m,
+        number,
+    )
+
+
+def tokens_gather_kernel(turned, shape_out, outs, line, x_ref, w_ref, *refs):
     held = refs[0]
     results = refs[1 : 1 + outs]
     send, recv = refs[1 + outs :]
@@ -725,19 +826,29 @@
     line_gather(line, x_ref, slot, send, recv, lambda: None, on_pair)
 
 
-def tokens_gather(x, w, turned, kinds, shape_out, n, number):
+def tokens_gather(x, w, turned, kinds, shape_out, n, m, number, riders=()):
     tokens, width = x.shape
     across = w.shape[0] * w.shape[1 if turned else 2]
-    chips = n // 2
-    return pl.pallas_call(
-        partial(tokens_gather_kernel, chips, turned, shape_out, len(kinds)),
-        out_shape=(jax.ShapeDtypeStruct((tokens * n, width), x.dtype),)
+    return comm_call(
+        partial(tokens_gather_kernel, turned, shape_out, len(kinds)),
+        (x, w),
+        (jax.ShapeDtypeStruct((tokens * n, width), x.dtype),)
         + tuple(jax.ShapeDtypeStruct((tokens * n, across), kind) for kind in kinds),
-        in_specs=whole(2),
-        out_specs=tuple(whole(1 + len(kinds))),
-        scratch_shapes=gather_sems(chips),
-        compiler_params=comm_params(number),
-    )(x, w)
+        gather_sems(n // 2),
+        riders,
+        n,
+        m,
+        number,
+    )
+
+
+def exchange(riders, n, m, number):
+    return comm_call(lambda line: None, (), (), [], riders, n, m, number, neighbours=False)
+
+
+def tiled_up(vector):
+    count = -(-vector.shape[0] // 1024) * 1024
+    return jnp.pad(vector.astype(jnp.float32), (0, count - vector.shape[0])).reshape(-1, 128)
 
 
 def local(
@@ -775,18 +886,25 @@
     local_width = out_weight.shape[0]
     head_count = local_width // HEAD_DIM
 
+    fused = own % 128 == 0 and n == 2 * m
     shift_vector = jnp.dot(embedding, shift_weight, preferred_element_type=jnp.float32)[0]
-    modulation = lax.all_gather(
-        jnp.dot(embedding, ada_weight, preferred_element_type=jnp.float32), "mp", axis=1, tiled=True
-    )
-    scale_attend = modulation[0, :width_all]
-    shift_attend = modulation[0, width_all : 2 * width_all]
-    scale_mlp = modulation[0, 2 * width_all : 3 * width_all]
-    shift_mlp = modulation[0, 3 * width_all :]
+    columns = jnp.dot(embedding, ada_weight, preferred_element_type=jnp.float32)[0]
+    riders = (Rider("mp", tiled_up(columns)),)
+    if fused:
+        modulation, pixels_low = exchange(
+            riders + (Rider("mp", image[0].reshape(-1, channel_count), 1),), n, m, 12
+        )
+    else:
+        (modulation,) = exchange(riders, n, m, 12)
+        pixels_low = lax.all_to_all(image[0], "mp", 2, 0, tiled=True)
+    modulation = modulation.reshape(n, -1)[:, : columns.shape[0]].reshape(-1)
+    scale_attend = modulation[:width_all]
+    shift_attend = modulation[width_all : 2 * width_all]
+    scale_mlp = modulation[2 * width_all : 3 * width_all]
+    shift_mlp = modulation[3 * width_all :]
     own_first = lax.dynamic_slice_in_dim(gain_first, me_mp * own, own)
     own_second = lax.dynamic_slice_in_dim(gain_second, me_mp * own, own)
 
-    pixels_low = lax.all_to_all(image[0], "mp", 2, 0, tiled=True)
     pixels = pixels_low.astype(jnp.float32).reshape(pixel_total, own)
     normed_first, inverse_first = group_forward(pixels, size)
     hidden_first = (
@@ -794,10 +912,9 @@
         .astype(jnp.bfloat16)
         .reshape(rows_all, canvas_cols, own)
     )
-    fused = own % 128 == 0 and n == 2 * m
     spread_first = side_by_side(hidden_first)
     if fused:
-        conv_output = conv_scatter_fused(spread_first, conv_first, canvas_cols, n, 0)
+        (conv_output,) = conv_scatter_fused(spread_first, conv_first, canvas_cols, n, m, 0)
     else:
         conv_output = conv_scatter(hidden_first, conv_first, n)
     conv_output = conv_output + shift_vector
@@ -809,7 +926,7 @@
     )
     spread_second = side_by_side(hidden_second)
     if fused:
-        conv_again = conv_scatter_fused(spread_second, conv_second, canvas_cols, n, 1)
+        (conv_again,) = conv_scatter_fused(spread_second, conv_second, canvas_cols, n, m, 1)
     else:
         conv_again = conv_scatter(hidden_second, conv_second, n)
     residual = pixels + conv_again
@@ -820,11 +937,11 @@
         .reshape(token_total, 4 * own)
     )
     down_matrix = down_weight.reshape(4 * own, width_all)
-    stream = tokens_scatter(down_patch, down_matrix[None], False, n, 2)
+    (stream,) = tokens_scatter(down_patch, down_matrix[None], False, n, m, 2)
     normed_attend, inverse_attend = layer_forward(stream)
     input_attend = (normed_attend * (1.0 + scale_attend) + shift_attend).astype(jnp.bfloat16)
     all_attend, qkv_rows = tokens_gather(
-        input_attend, qkv_weight, False, (jnp.bfloat16,), lambda value: (value,), n, 3
+        input_attend, qkv_weight, False, (jnp.bfloat16,), lambda value: (value,), n, m, 3
     )
     qkv_rows = qkv_rows.reshape(token_total, 3, head_count, HEAD_DIM)
     queries = qkv_rows[:, 0]
@@ -836,7 +953,8 @@
     )
     mixed_heads, log_totals = attend_forward(queries, key_rows, value_rows, key_valid, block_rows)
     mixed_low = mixed_heads.reshape(token_total, local_width).astype(jnp.bfloat16)
-    stream_mid = stream + tokens_scatter(mixed_low, out_weight[None], False, n, 4)
+    (attended,) = tokens_scatter(mixed_low, out_weight[None], False, n, m, 4)
+    stream_mid = stream + attended
     normed_mlp, inverse_mlp = layer_forward(stream_mid)
     input_mlp = (normed_mlp * (1.0 + scale_mlp) + shift_mlp).astype(jnp.bfloat16)
     all_mlp, upper_proj, activated = tokens_gather(
@@ -846,6 +964,7 @@
         (jnp.float32, jnp.bfloat16),
         lambda value: (value, jax.nn.gelu(value, approximate=True)),
         n,
+        m,
         5,
     )
     final_stream = stream_mid + scatter_rows(
@@ -859,21 +978,31 @@
     grad_act = jnp.einsum("le,fe->lf", all_final, proj_weight, preferred_element_type=jnp.float32)
     gelu_pull = jax.vjp(partial(jax.nn.gelu, approximate=True), upper_proj)[1]
     grad_upper = gelu_pull(grad_act)[0].astype(jnp.bfloat16)
-    grad_normed_mlp = tokens_scatter(grad_upper, up_weight[None], True, n, 6)
     grad_proj = jnp.einsum("lf,le->fe", activated, all_final, preferred_element_type=jnp.float32)
+    grad_normed_mlp, sums_proj = tokens_scatter(
+        grad_upper,
+        up_weight[None],
+        True,
+        n,
+        m,
+        6,
+        (Rider("dp", grad_proj.astype(jnp.bfloat16), 1),),
+    )
     grad_up = jnp.einsum("le,lf->ef", all_mlp, grad_upper, preferred_element_type=jnp.float32)
     grad_mid_norm, grad_scale_mlp, grad_shift_mlp = layer_backward(
         grad_normed_mlp, normed_mlp, inverse_mlp, scale_mlp
     )
     grad_mid = grad_final + grad_mid_norm
-    all_mid, grad_mixed_low = tokens_gather(
+    all_mid, grad_mixed_low, sums_up = tokens_gather(
         grad_mid.astype(jnp.bfloat16),
         out_weight[None],
         True,
         (jnp.bfloat16,),
         lambda value: (value,),
         n,
+        m,
         7,
+        (Rider("dp", grad_up.astype(jnp.bfloat16), 0),),
     )
     grad_mixed_low = grad_mixed_low.reshape(token_total, head_count, HEAD_DIM)
     grad_out = jnp.einsum("lh,le->he", mixed_low, all_mid, preferred_element_type=jnp.float32)
@@ -885,98 +1014,140 @@
         .astype(jnp.bfloat16)
         .reshape(token_total, 3, local_width)
     )
-    grad_normed_attend = tokens_scatter(
-        grad_qkv.reshape(token_total, 3 * local_width), qkv_weight, True, n, 8
+    grad_qkv = grad_qkv.reshape(token_total, 3 * local_width)
+    grad_normed_attend, sums_out = tokens_scatter(
+        grad_qkv, qkv_weight, True, n, m, 8, (Rider("dp", grad_out.astype(jnp.bfloat16), 1),)
     )
     grad_qkv_weight = jnp.einsum(
-        "le,ljf->jef", all_attend, grad_qkv, preferred_element_type=jnp.float32
+        "le,lf->ef", all_attend, grad_qkv, preferred_element_type=jnp.float32
     )
     grad_stream_norm, grad_scale_attend, grad_shift_attend = layer_backward(
         grad_normed_attend, normed_attend, inverse_attend, scale_attend
     )
     grad_stream = grad_mid + grad_stream_norm
-    all_stream, grad_tap_patch = tokens_gather(
+    grad_modulation = jnp.concatenate(
+        [
+            tiled_up(piece)
+            for piece in jnp.concatenate(
+                [grad_scale_attend, grad_shift_attend, grad_scale_mlp, grad_shift_mlp]
+            ).reshape(n, -1)
+        ]
+    )
+    all_stream, grad_tap_patch, sums_qkv, ada_columns = tokens_gather(
         grad_stream.astype(jnp.bfloat16),
         down_matrix[None],
         True,
         (jnp.float32,),
         lambda value: (value,),
         n,
+        m,
         9,
+        (
+            Rider("dp", grad_qkv_weight.astype(jnp.bfloat16), 0),
+            Rider("mp", grad_modulation, 0),
+        ),
     )
     grad_down = jnp.einsum(
         "lk,le->ke", down_patch, all_stream, preferred_element_type=jnp.float32
-    ).reshape(4, own, width_all)
+    )
+    ada_columns = added(ada_columns).reshape(-1)[: columns.shape[0]]
     grad_residual = (
         grad_tap_patch.reshape(rows_all // 2, token_cols, 2, 2, own)
         .transpose(0, 2, 1, 3, 4)
         .reshape(pixel_total, own)
     )
-    def back(grad_low, hidden, spread, kernel, number):
+    def back(grad_low, hidden, spread, kernel, number, riders):
         if fused:
-            acc, parts = conv_back_fused(grad_low, spread.T, kernel, canvas_cols, n, number)
-            return join_columns(acc, canvas_cols), parts.reshape(m, 9 * own, -1)
+            acc, parts, *ridden = conv_back_fused(
+                grad_low, spread.T, kernel, canvas_cols, n, m, number, riders
+            )
+            return join_columns(acc, canvas_cols), parts.reshape(m, 9 * own, -1), ridden
         grad_hidden, grad_kernel = conv_backward(grad_low, hidden, kernel, n)
-        return grad_hidden, by_images(grad_kernel, m)
-
-    grad_hidden_second, parts_second = back(
-        grad_residual.astype(jnp.bfloat16), hidden_second, spread_second, conv_second, 10
+        return grad_hidden, by_images(grad_kernel, m), exchange(riders, n, m, number)
+
+    grad_hidden_second, parts_second, (sums_down, every_small) = back(
+        grad_residual.astype(jnp.bfloat16),
+        hidden_second,
+        spread_second,
+        conv_second,
+        10,
+        (
+            Rider("dp", grad_down.astype(jnp.bfloat16), 1),
+            Rider("dp", jnp.concatenate([tiled_up(embedding[0]), tiled_up(ada_columns)])),
+        ),
     )
     grad_conv_output, grad_gain_second = group_backward(
         grad_hidden_second, normed_second, inverse_second, own_second, size
     )
     grad_shift = jnp.sum(grad_conv_output, axis=0)
-    grad_hidden_first, parts_first = back(
-        grad_conv_output.astype(jnp.bfloat16), hidden_first, spread_first, conv_first, 11
+    grad_hidden_first, parts_first, (sums_second, every_shift) = back(
+        grad_conv_output.astype(jnp.bfloat16),
+        hidden_first,
+        spread_first,
+        conv_first,
+        11,
+        (Rider("dp", parts_second, 0), Rider("dp", tiled_up(grad_shift))),
     )
     grad_base, grad_gain_first = group_backward(
         grad_hidden_first, normed_first, inverse_first, own_first, size
     )
     image_turned = (grad_residual + grad_base).astype(jnp.bfloat16)
-    image_grad = lax.all_to_all(
-        image_turned.reshape(rows_all, canvas_cols, own), "mp", 0, 2, tiled=True
-    )[None]
-
-    grad_modulation = jnp.concatenate(
-        [grad_scale_attend, grad_shift_attend, grad_scale_mlp, grad_shift_mlp]
-    )
-    ada_columns = lax.psum_scatter(
-        grad_modulation[None].astype(jnp.bfloat16), "mp", scatter_dimension=1, tiled=True
-    ).astype(jnp.float32)
-    embed_float = embedding.astype(jnp.float32)
     embed_term = jnp.dot(
         grad_shift[None], shift_weight.astype(jnp.float32).T, precision=PRECISE
-    ) + jnp.dot(ada_columns, ada_weight.astype(jnp.float32).T, precision=PRECISE)
-    embedding_grad = lax.psum(embed_term, "mp")
-    packed = jnp.concatenate([embed_float[0], grad_shift, ada_columns[0]])
-    every = lax.all_gather(packed, "dp", axis=0)
+    ) + jnp.dot(ada_columns[None], ada_weight.astype(jnp.float32).T, precision=PRECISE)
+    small = jnp.concatenate(
+        [tiled_up(embed_term[0]), tiled_up(jnp.concatenate([grad_gain_first, grad_gain_second]))]
+    )
+    riders = (Rider("dp", parts_first, 0), Rider("all", small))
+    if fused:
+        sums_first, small, image_turned = exchange(
+            riders + (Rider("mp", image_turned, 0),), n, m, 13
+        )
+        image_grad = image_turned.transpose(1, 0, 2).reshape(image.shape)
+    else:
+        sums_first, small = exchange(riders, n, m, 13)
+        image_grad = lax.all_to_all(
+            image_turned.reshape(rows_all, canvas_cols, own), "mp", 0, 2, tiled=True
+        )[None]
+
+    small = small.reshape(m, n, -1)
     embed_count = embedding.shape[1]
-    embed_rows = lax.dynamic_slice_in_dim(
-        every[:, :embed_count], me_dp * (embed_count // m), embed_count // m, axis=1
-    )
-    grad_shift_weight = jnp.dot(
-        embed_rows.T, every[:, embed_count : embed_count + own], precision=PRECISE
-    )
-    grad_ada_weight = jnp.dot(embed_rows.T, every[:, embed_count + own :], precision=PRECISE)
-    gains = lax.all_gather(jnp.stack([grad_gain_first, grad_gain_second]), ("dp", "mp"), axis=0)
-    gains = jnp.sum(gains.reshape(m, n, 2, own), axis=0).transpose(1, 0, 2).reshape(2, -1)
+    embedding_grad = jnp.sum(
+        lax.dynamic_index_in_dim(small, me_dp, axis=0, keepdims=False)[:, :embed_count], axis=0
+    )[None]
+    gain_start = -(-embed_count // 1024) * 1024
+    gains = jnp.sum(small[:, :, gain_start : gain_start + 2 * own], axis=0)
+    gains = gains.reshape(n, 2, own).transpose(1, 0, 2).reshape(2, -1)
     piece = channel_count // (m * n)
     gains = lax.dynamic_slice_in_dim(gains, (me_dp * n + me_mp) * piece, piece, axis=1)
+    every_small = every_small.reshape(m, -1)
+    embed_rows = lax.dynamic_slice_in_dim(
+        every_small[:, :embed_count], me_dp * (embed_count // m), embed_count // m, axis=1
+    )
+    grad_shift_weight = jnp.dot(
+        embed_rows.T, every_shift.reshape(m, -1)[:, :own], precision=PRECISE
+    )
+    grad_ada_weight = jnp.dot(
+        embed_rows.T,
+        every_small[:, gain_start : gain_start + columns.shape[0]],
+        precision=PRECISE,
+    )
+    qkv_grad = added(sums_qkv).reshape(-1, 3, local_width).transpose(1, 0, 2)
     return (
         output,
         image_grad,
         embedding_grad,
         gains[0],
-        turn_kernel(parts_first, 9, m, n),
+        turn_kernel(added(sums_first)[0], 9, m, n),
         gains[1],
-        turn_kernel(parts_second, 9, m, n),
+        turn_kernel(added(sums_second)[0], 9, m, n),
         grad_shift_weight,
-        turn_kernel(by_images(grad_down, m), 4, m, n),
+        turn_kernel(added(sums_down), 4, m, n),
         grad_ada_weight,
-        dp_rows(grad_qkv_weight, 1),
-        dp_rows(grad_out, 1),
-        dp_rows(grad_up, 0),
-        dp_rows(grad_proj, 1),
+        qkv_grad,
+        added(sums_out),
+        added(sums_up),
+        added(sums_proj),
     )
 
 

time: 1310 us -> 1180 us (0.901)
  blocking collectives: 140 us -> 0 us
  Pallas kernels: 727 us -> 816 us
  waiting for transfers between devices: 66.1 us -> 12.2 us
  local copies, waits for them, and re-layouts: 111 us -> 84.8 us
  starting transfers between devices: 43.8 us -> 29.2 us
    all_gather x3 -> x0, blocking collectives: 104 us -> none  [the longest x1 53.5 us: local(): lax.all_gather(jnp.stack([grad_gain_first, grad_gain_second]), ('dp', 'mp...]
    pallas_call x12 -> x14, Pallas kernels: 727 us -> 816 us  [comm_call(): pl.pallas_call(body, out_shape=tuple(out_shapes) + ride_shapes, in_specs=...]
    ppermute x6, waiting for transfers between devices: 57.6 us -> 11.5 us  [turn_kernel(): moved = lax.ppermute(half, ('dp', 'mp'), route)]
    psum x1 -> x0, blocking collectives: 35.2 us -> none  [local(): embedding_grad = lax.psum(embed_term, 'mp')]
    all_to_all x2 -> x0, starting transfers between devices: 26.9 us -> none  [the longest x1 21.1 us: local(): lax.all_to_all(image_turned.reshape(rows_all, canvas_cols, own), 'mp', 0,...]
    reduce_sum x1 -> x10, other arithmetic: 0.02 us -> 19 us  [the longest x8 18.4 us: added(): return jnp.sum(received.astype(jnp.float32), axis=0)]
  transfers between devices with their start and end apart: 18 -> 8, of which waited for: 5 -> 1; matrix products, arithmetic and copies ran while one was open for 17% -> 14% of each run, Pallas kernels for 49% -> 51%
where the time goes in v2:
time: 1180 us; the launch traced here: 1170 us
  Pallas kernels  816 us (69%)
  matrix products  120 us (10%)
  other arithmetic  88 us (7%)
  local copies, waits for them, and re-layouts  84.8 us (7%)
  starting transfers between devices  29.2 us (2%)
  between operations  15.4 us (1%)
  waiting for transfers between devices  12.2 us (1%)
    pallas_call x14, Pallas kernels, comm_call(): pl.pallas_call(body, out_shape=tuple(out_shapes) + ride_shapes, in_specs=...  816 us
    ppermute x6, starting transfers between devices, turn_kernel(): moved = lax.ppermute(half, ('dp', 'mp'), route)  29.1 us
  transfers between devices with their start and end apart: 8, of which 1 were waited for; matrix products, arithmetic and copies ran while one was open for 14% of the time, Pallas kernels for 51%

profile of v2, /device:TPU:9, one launch (start us, length us, event | category | flops | bytes accessed | tf_op | source)
XLA Modules:
  0.0 1166.1 jit_solution(11018865017454351186)
XLA Ops:
  10.4 52.1 %shard_map.254 = (f32[8,8,128]{2,1,0:T(8,128)}, bf16[8,512,128]{2,1,0:T(8,128)(2,1)}) custom-call(f32[8,128]{1,0:T(8,128)} %bitcast.368, bf16[512,1024]{1,0:T(8,128)(2,1)} %bitcast.356), custom_call_target="tpu_custom_call" | custom-call | tf_op jit(solution)/shard_map/pallas_call | solution.py:343
  73.1 77.4 %shard_map.255 = f32[4096,128]{1,0:T(8,128)} custom-call(bf16[4352,384]{1,0:T(8,128)(2,1)} %bitcast.321, bf16[3,384,1024]{2,1,0:T(8,128)(2,1)} %bitcast.334), custom_call_target="tpu_custom_call" | custom-call | tf_op jit(solution)/shard_map/pallas_call | solution.py:343
  161.8 78.3 %shard_map.256 = f32[4096,128]{1,0:T(8,128)} custom-call(bf16[4352,384]{1,0:T(8,128)(2,1)} %bitcast.323, bf16[3,384,1024]{2,1,0:T(8,128)(2,1)} %bitcast.332), custom_call_target="tpu_custom_call" | custom-call | tf_op jit(solution)/shard_map/pallas_call | solution.py:343
  243.9 41.9 %shard_map.257 = f32[128,2048]{1,0:T(8,128)} custom-call(bf16[1024,512]{1,0:T(8,128)(2,1)} %reshape.553.refs_0_, bf16[1,512,2048]{2,1,0:T(8,128)(2,1)} %bitcast.336), custom_call_target="tpu_custom_call" | custom-call | tf_op jit(solution)/shard_map/pallas_call | solution.py:343
  289.8 39.9 %shard_map.258 = (bf16[1024,2048]{1,0:T(8,128)(2,1)}, bf16[1024,768]{1,0:T(8,128)(2,1)}) custom-call(bf16[128,2048]{1,0:T(8,128)(2,1)} %add_convert_fusion.3.refs_0_, bf16[3,2048,256]{2,1,0:T(8,128)(2,1)} %refs_1_.3), custom_call_target="tpu_custom_call" | custom-call | tf_op jit(solution)/shard_map/pallas_call | solution.py:343
  329.8 4.3 reshape.554
  339.2 12.5 %while.28 = (s32[]{:T(128)}, bf16[2,512,2,128]{3,1,2,0:T(8,128)(2,1)}, f32[2,2,512]{2,1,0:T(2,128)S(1)}, bf16[2,512,2,128]{3,1,2,0:T(8,128)(2,1)}, bf16[1024,2,1...) while((s32[]{:T(128)}, ...), condition=%wide.region_13.14_spmd.clone, body=%wide.region_10.13_spmd.clone.sunk | while | flops 549468160 | bytes 16553093 | solution.py:162
  355.0 47.1 %shard_map.259 = f32[128,2048]{1,0:T(8,128)} custom-call(bf16[1024,256]{1,0:T(8,128)(2,1)} %bitcast.350, bf16[1,256,2048]{2,1,0:T(8,128)(2,1)} %bitcast.343), custom_call_target="tpu_custom_call" | custom-call | tf_op jit(solution)/shard_map/pallas_call | solution.py:343
  405.5 40.6 %shard_map.260 = (bf16[1024,2048]{1,0:T(8,128)(2,1)}, f32[1024,1024]{1,0:T(8,128)}, bf16[1024,1024]{1,0:T(8,128)(2,1)}) custom-call(bf16[128,2048]{1,0:T(8,128)(2,1)} %add_convert_fusion.2.refs_0_, bf16[1,2048,1024]{2,1,0:T(8,128)(2,1)} %bitcast.328), custom_call_target="tpu_custom_call" | custom-call | tf_op jit(solution)/shard_map/pallas_call | solution.py:343
  446.2 9.3 convolution_convert_fusion.2
  455.5 5.8 copy.101
  461.3 5.8 copy.102
  467.1 9.9 convolution_convert_fusion.1.refs_2_
  477.0 8.0 fusion.84.refs_0_
  485.1 59.4 %shard_map.261 = (f32[128,2048]{1,0:T(8,128)}, bf16[4,1024,512]{2,1,0:T(8,128)(2,1)}) custom-call(bf16[1024,1024]{1,0:T(8,128)(2,1)} %fusion.84.refs_0_, bf16[1,2048,1024]{2,1,0:T(8,128)(2,1)} %bitcast.329, bf16[1024,2048]{1,0:T(8,128)(2,1)} %convolution_convert_fusion.1.refs_2_), custom_call_target="tpu_custom_call" | custom-call | tf_op jit(solution)/shard_map/pallas_call | solution.py:343
  546.5 4.5 convert_reduce_fusion
  551.0 6.2 convolution_convert_fusion.refs_2_
  557.3 3.8 fusion.115
  561.0 53.0 %shard_map.262 = (bf16[1024,2048]{1,0:T(8,128)(2,1)}, bf16[1024,256]{1,0:T(8,128)(2,1)}, bf16[4,512,1024]{2,1,0:T(8,128)(2,1)}) custom-call(bf16[128,2048]{1,0:T(8,128)(2,1)} %get-tuple-element.391.refs_0_, bf16[1,256,2048]{2,1,0:T(8,128)(2,1)} %bitcast.344, bf16[2048,1024]{1,0:T(8,128)(2,1)} %convolution_convert_fusion.refs_2_), custom_call_target="tpu_custom_call" | custom-call | tf_op jit(solution)/shard_map/pallas_call | solution.py:343
  614.1 4.4 convolution_convert_fusion.5.refs_2_
  620.5 57.3 %while.29 = (s32[]{:T(128)}, f32[1024,2,128]{0,2,1:T(8,128)}, f32[1024,2,128]{0,2,1:T(8,128)}, bf16[2,512,2,128]{3,1,0,2:T(8,128)(2,1)}, bf16[2,512,2,128]{3,1,2...) while((s32[]{:T(128)}, f32[1024,2,128]{0,2,1:T(8,128)}, ...), condition=%wide.region_21.22_spmd.clone, body=%wide.region_19.21_spmd.clone.sunk | while | flops 1357925376 | bytes 58212044 | solution.py:198
  621.8 4.3 subtract_exponential_fusion.3
  629.0 8.2 fusion.182
  637.1 8.0 fusion.184
  645.1 3.7 fusion.183
  650.1 4.3 subtract_exponential_fusion.3
  657.3 8.5 fusion.182
  665.8 8.0 fusion.184
  673.8 4.0 fusion.183
  686.5 4.9 convert_element_type.159.refs_0_
  691.4 44.0 %shard_map.263 = (f32[128,2048]{1,0:T(8,128)}, bf16[4,256,512]{2,1,0:T(8,128)(2,1)}) custom-call(bf16[1024,768]{1,0:T(8,128)(2,1)} %convert_element_type.159.refs_0_, bf16[3,2048,256]{2,1,0:T(8,128)(2,1)} %refs_1_.3, bf16[256,2048]{1,0:T(8,128)(2,1)} %convolution_convert_fusion.5.refs_2_), custom_call_target="tpu_custom_call" | custom-call | tf_op jit(solution)/shard_map/pallas_call | solution.py:343
  737.3 7.5 convolution_convert_fusion.3.refs_2_
  746.1 42.9 %shard_map.264 = (bf16[1024,2048]{1,0:T(8,128)(2,1)}, f32[1024,512]{1,0:T(8,128)}, bf16[4,512,768]{2,1,0:T(8,128)(2,1)}, f32[8,8,128]{2,1,0:T(8,128)}) custom-call(bf16[128,2048]{1,0:T(8,128)(2,1)} %add_convert_fusion.refs_0_, bf16[1,512,2048]{2,1,0:T(8,128)(2,1)} %bitcast.337, bf16[2048,768]{1,0:T(8,128)(2,1)} %convolution_convert_fusion.3.refs_2_, ...), custom_call_target="tpu_custom_call" | custom-call | tf_op jit(solution)/shard_map/pallas_call | solution.py:343
  789.0 5.9 convolution_convert_fusion.4.refs_3_
  794.9 3.5 reshape.556
  804.0 85.7 %shard_map.265 = (f32[4096,384]{1,0:T(8,128)}, bf16[4,3,384,256]{3,2,1,0:T(8,128)(2,1)}, bf16[4,512,512]{2,1,0:T(8,128)(2,1)}, f32[4,16,128]{2,1,0:T(8,128)}) custom-call(bf16[4096,128]{1,0:T(8,128)(2,1)} %convert_element_type.163.refs_0_, bf16[3,384,1024]{2,1,0:T(8,128)(2,1)} %bitcast.333, bf16[384,4352]{1,0:T(8,128)(2,1)} %bitcast.330, ...), custom_call_target="tpu_custom_call" | custom-call | tf_op jit(solution)/shard_map/pallas_call | solution.py:343
  899.0 3.9 fusion.100
  908.0 19.4 %collective-permute-start.4 = (bf16[4,128,256]{2,1,0:T(8,128)(2,1)}, bf16[4,128,256]{2,1,0:T(8,128)(2,1)}, u32[]{:S(2)}, u32[]{:S(2)}) collective-permute-start(bf16[4,128,256]{2,1,0:T(8,128)(2,1)} %bitcast.285), channel_id=1, source_target_pairs={{0,0},{1,1},{2,8},{3,9},{4,16},{5,17},{6,24},{7,25},{8,2},{9,3},{1... | collective-permute-start | bytes 786440 | tf_op jit(solution)/shard_map/ppermute | solution.py:118
  927.5 105.4 %shard_map.266 = (f32[4096,384]{1,0:T(8,128)}, bf16[4,3,384,256]{3,2,1,0:T(8,128)(2,1)}, bf16[4,1,1152,256]{3,2,1,0:T(8,128)(2,1)}, f32[4,8,128]{2,1,0:T(8,128)}) custom-call(bf16[4096,128]{1,0:T(8,128)(2,1)} %get-tuple-element.404.refs_0_, bf16[3,384,1024]{2,1,0:T(8,128)(2,1)} %bitcast.335, bf16[384,4352]{1,0:T(8,128)(2,1)} %bitcast.331, ...), custom_call_target="tpu_custom_call" | custom-call | tf_op jit(solution)/shard_map/pallas_call | solution.py:343
  1046.7 2.9 fusion.117
  1049.7 4.3 fusion.111
  1057.9 4.6 fusion.96.refs_2_
  1062.4 48.5 %shard_map.267 = (bf16[4,1,1152,256]{3,2,1,0:T(8,128)(2,1)}, f32[32,16,128]{2,1,0:T(8,128)}, bf16[8,512,128]{2,1,0:T(8,128)(2,1)}) custom-call(bf16[4,1152,256]{2,1,0:T(8,128)(2,1)} %bitcast.347, f32[16,128]{1,0:T(8,128)} %pad_maximum_fusion.4.refs_1_, bf16[4096,128]{1,0:T(8,128)(2,1)} %fusion.96.refs_2_), custom_call_target="tpu_custom_call" | custom-call | tf_op jit(solution)/shard_map/pallas_call | solution.py:343
  1115.5 4.7 collective-permute-start
  1121.9 3.8 convert_reduce_fusion.2
  1132.2 3.0 copy.110
  1135.2 3.1 copy.111
  1146.2 11.5 collective-permute-done.1
  (294 shorter events, 140.5 us)
Async XLA Ops:
  7.2 459.9 %all-gather.2.cloned.1.call-start = ((), (), s32[]{:S(2)}) async-start(), calls=%async_computation.2 | async-start | bytes 4718592 | tf_op jit(solution)/shard_map/all_gather | solution.py:62
  7.9 549.3 %reduce-scatter.2.cloned.1.call-start = ((), (), s32[]{:S(2)}) async-start(), calls=%async_computation.1 | async-start | bytes 4718592 | tf_op jit(solution)/shard_map/reduce_scatter | solution.py:66
  62.5 5.2 copy-start.4
  64.8 4.9 copy-start.31
  66.9 2.8 copy-start.35
  70.8 85.5 %copy-start.29 = (f32[128]{0:T(128)}, f32[128]{0:T(128)S(1)}, u32[]{:S(2)}) copy-start(f32[128]{0:T(128)S(1)} %convolution_bitcast_fusion) | copy-start | bytes 1540
  153.0 5.6 copy-start.33
  155.5 3.9 copy-start.37
  156.3 3.2 copy-start.41
  285.8 3.0 copy-start.27
  285.8 3.0 copy-start.2
  334.1 3.4 copy-start.43
  467.1 9.9 copy-start.44
  467.1 9.9 copy-start.45
  467.1 9.9 copy-start.47
  546.5 4.6 copy-start.16
  546.5 4.5 copy-start.46
  561.0 53.0 %copy-start.18 = (bf16[2,512,2,128]{3,2,1,0:T(2,128)(2,1)S(1)}, bf16[2,512,2,128]{3,2,1,0:T(2,128)(2,1)}, u32[]{:S(2)}) copy-start(bf16[2,512,2,128]{3,2,1,0:T(2,128)(2,1)} %copy-done.17) | copy-start | bytes 1572868
  621.8 4.3 copy-start.10
  621.8 4.5 copy-start.7
  650.1 4.3 copy-start.10
  650.1 4.5 copy-start.7
  737.2 7.6 copy-start.24
  737.3 7.6 copy-start.12
  737.3 7.5 copy-start.13
  746.1 42.9 %copy-start.15 = (bf16[1024,512]{1,0:T(8,128)(2,1)S(1)}, bf16[1024,512]{1,0:T(8,128)(2,1)}, u32[]{:S(2)}) copy-start(bf16[1024,512]{1,0:T(8,128)(2,1)} %reshape.553.refs_0_) | copy-start | bytes 3145732
  800.9 2.4 copy-start.26
  892.4 2.5 copy-start.1
  892.4 2.5 copy-start.30
  892.4 2.5 copy-start.34
  892.4 2.5 copy-start.38
  892.5 2.5 copy-start.42
  899.0 4.5 copy-start.22
  899.0 4.8 copy-start.28
  908.0 230.3 %collective-permute-start.4 = (bf16[4,128,256]{2,1,0:T(8,128)(2,1)}, bf16[4,128,256]{2,1,0:T(8,128)(2,1)}, u32[]{:S(2)}, u32[]{:S(2)}) collective-permute-start(bf16[4,128,256]{2,1,0:T(8,128)(2,1)} %bitcast.285), channel_id=1, source_target_pairs={{0,0},{1,1},{2,8},{3,9},{4,16},{5,17},{6,24},{7,25},{8,2},{9,3},{1... | collective-permute-start | bytes 786440 | tf_op jit(solution)/shard_map/ppermute | solution.py:118
  927.5 212.2 %collective-permute-start.5 = (bf16[4,128,256]{2,1,0:T(8,128)(2,1)S(1)}, bf16[4,128,256]{2,1,0:T(8,128)(2,1)}, u32[]{:S(2)}, u32[]{:S(2)}) collective-permute-start(bf16[4,128,256]{2,1,0:T(8,128)(2,1)S(1)} %bitcast.361), channel_id=1, source_target_pairs={{0,1},{1,0},{2,9},{3,8},{4,17},{5,16},{6,25},{7,24},{8,3},{9,2},{1... | collective-permute-start | bytes 786440 | tf_op jit(solution)/shard_map/ppermute | solution.py:118
  1041.4 100.4 %collective-permute-start.2 = (bf16[9,128,128]{2,1,0:T(8,128)(2,1)}, bf16[9,128,128]{2,1,0:T(8,128)(2,1)}, u32[]{:S(2)}, u32[]{:S(2)}) collective-permute-start(bf16[9,128,128]{2,1,0:T(8,128)(2,1)} %bitcast.281), channel_id=1, source_target_pairs={{0,0},{1,1},{2,8},{3,9},{4,16},{5,17},{6,24},{7,25},{8,2},{9,3},{1... | collective-permute-start | bytes 884744 | tf_op jit(solution)/shard_map/ppermute | solution.py:118
  1044.0 98.8 %collective-permute-start.3 = (bf16[9,128,128]{2,1,0:T(8,128)(2,1)}, bf16[9,128,128]{2,1,0:T(8,128)(2,1)}, u32[]{:S(2)}, u32[]{:S(2)}) collective-permute-start(bf16[9,128,128]{2,1,0:T(8,128)(2,1)} %bitcast.280), channel_id=1, source_target_pairs={{0,1},{1,0},{2,9},{3,8},{4,17},{5,16},{6,25},{7,24},{8,3},{9,2},{1... | collective-permute-start | bytes 884744 | tf_op jit(solution)/shard_map/ppermute | solution.py:118
  1046.7 2.9 copy-start.9
  1046.7 2.9 copy-start.32
  1046.7 2.9 copy-start.36
  1046.7 2.9 copy-start.40
  1053.9 4.0 copy-start.5
  1115.5 28.4 %collective-permute-start = (bf16[9,128,128]{2,1,0:T(8,128)(2,1)}, bf16[9,128,128]{2,1,0:T(8,128)(2,1)}, u32[]{:S(2)}, u32[]{:S(2)}) collective-permute-start(bf16[9,128,128]{2,1,0:T(8,128)(2,1)} %bitcast.283), channel_id=1, source_target_pairs={{0,0},{1,1},{2,8},{3,9},{4,16},{5,17},{6,24},{7,25},{8,2},{9,3},{1... | collective-permute-start | bytes 884744 | tf_op jit(solution)/shard_map/ppermute | solution.py:118
  1121.9 3.8 copy-start.14
  1127.9 2.3 copy-start.20
  1135.2 3.1 copy-start.23
  1138.3 19.3 %collective-permute-start.1 = (bf16[9,128,128]{2,1,0:T(8,128)(2,1)S(1)}, bf16[9,128,128]{2,1,0:T(8,128)(2,1)S(1)}, u32[]{:S(2)}, u32[]{:S(2)}) collective-permute-start(bf16[9,128,128]{2,1,0:T(8,128)(2,1)S(1)} %bitcast.360), channel_id=1, source_target_pairs={{0,1},{1,0},{2,9},{3,8},{4,17},{5,16},{6,25},{7,24},{8,3},{9,2},{1... | collective-permute-start | bytes 884744 | tf_op jit(solution)/shard_map/ppermute | solution.py:118
  (11 other events, 14.9 us)
Sparse Core Ops, SparseCore 0:
  9.6 62.5 all-gather.1
  455.6 52.7 reduce-scatter.1

commit v3 on v2

--- a/solution.py
+++ b/solution.py
@@ -141,68 +141,6 @@
     return (outgoing, jnp.sum(incoming * normed, axis=0), jnp.sum(incoming, axis=0))
 
 
-def attend_forward(queries, key_rows, value_rows, key_valid, block_rows):
-    score_scale = 1.0 / math.sqrt(queries.shape[-1])
-
-    def one_block(query_block):
-        raw_scores = jnp.einsum(
-            "qhd,khd->hqk", query_block, key_rows, preferred_element_type=jnp.float32
-        )
-        logits = jnp.where(key_valid[None, None, :], raw_scores * score_scale, MASKED_SCORE)
-        peak_score = jnp.max(logits, axis=-1, keepdims=True)
-        exponent = jnp.exp(logits - peak_score)
-        totals = jnp.sum(exponent, axis=-1, keepdims=True)
-        mix_weights = (exponent / totals).astype(jnp.bfloat16)
-        mixed_heads = jnp.einsum(
-            "hqk,khd->qhd", mix_weights, value_rows, preferred_element_type=jnp.float32
-        )
-        return (mixed_heads, (peak_score + jnp.log(totals))[..., 0])
-
-    blocks = queries.reshape(-1, block_rows, queries.shape[1], queries.shape[2])
-    mixed_heads, log_totals = lax.map(one_block, blocks)
-    return (mixed_heads.reshape(queries.shape), log_totals)
-
-
-def attend_backward(queries, key_rows, value_rows, key_valid, log_totals, grad_mixed, block_rows):
-    score_scale = 1.0 / math.sqrt(queries.shape[-1])
-    block_shape = (-1, block_rows, queries.shape[1], queries.shape[2])
-
-    def one_block(running, inputs):
-        grad_keys, grad_values = running
-        query_block, grad_block, log_block = inputs
-        raw_scores = jnp.einsum(
-            "qhd,khd->hqk", query_block, key_rows, preferred_element_type=jnp.float32
-        )
-        logits = jnp.where(key_valid[None, None, :], raw_scores * score_scale, MASKED_SCORE)
-        mix_weights = jnp.exp(logits - log_block[..., None])
-        grad_weights = jnp.einsum(
-            "qhd,khd->hqk", grad_block, value_rows, preferred_element_type=jnp.float32
-        )
-        inner_sum = jnp.sum(mix_weights * grad_weights, axis=-1, keepdims=True)
-        grad_scores = (mix_weights * (grad_weights - inner_sum) * score_scale).astype(jnp.bfloat16)
-        grad_query = jnp.einsum(
-            "hqk,khd->qhd", grad_scores, key_rows, preferred_element_type=jnp.float32
-        )
-        grad_keys = grad_keys + jnp.einsum(
-            "hqk,qhd->khd", grad_scores, query_block, preferred_element_type=jnp.float32
-        )
-        grad_values = grad_values + jnp.einsum(
-            "hqk,qhd->khd",
-            mix_weights.astype(jnp.bfloat16),
-            grad_block,
-            preferred_element_type=jnp.float32,
-        )
-        return ((grad_keys, grad_values), grad_query)
-
-    zero_rows = jnp.zeros(key_rows.shape, jnp.float32)
-    (grad_keys, grad_values), grad_query = lax.scan(
-        one_block,
-        (zero_rows, zero_rows),
-        (queries.reshape(block_shape), grad_mixed.reshape(block_shape), log_totals),
-    )
-    return (grad_query.reshape(queries.shape), grad_keys, grad_values)
-
-
 MESH = pl.DeviceIdType.MESH
 CONV_PARTS = 4
 TOKEN_PARTS = 4
@@ -670,7 +608,7 @@
     )
 
 
-def conv_back_kernel(breadth, line, g_ref, w_ref, xt_ref, acc_ref, wg_ref, held, sums, send, recv):
+def conv_back_kernel(breadth, line, g_ref, w_ref, x_ref, acc_ref, wg_ref, held, sums, send, recv):
     chips = line.chips
     pixels, own = g_ref.shape
     wide = w_ref.shape[1]
@@ -715,9 +653,10 @@
             @pl.loop(0, pixels // tile)
             def _(index):
                 base = pl.multiple_of(index * tile, tile)
-                sums[...] += jnp.dot(
-                    xt_ref[:, pl.ds(base + i * breadth, tile)],
+                sums[...] += lax.dot_general(
+                    x_ref[pl.ds(base + i * breadth, tile)],
                     pair(chip, pl.ds(base + breadth, tile)),
+                    (((0,), (0,)), ((), ())),
                     preferred_element_type=jnp.float32,
                 )
 
@@ -726,13 +665,13 @@
     line_gather(line, g_ref, slot, send, recv, on_own, on_pair)
 
 
-def conv_back_fused(grad_low, spread_turned, kernel, cols, n, m, number, riders=()):
+def conv_back_fused(grad_low, spread, kernel, cols, n, m, number, riders=()):
     pixels, own = grad_low.shape
     depth = kernel.shape[1]
     chips = n // 2
     return comm_call(
         partial(conv_back_kernel, cols),
-        (grad_low, kernel.reshape(3, 3 * depth, kernel.shape[2]), spread_turned),
+        (grad_low, kernel.reshape(3, 3 * depth, kernel.shape[2]), spread),
         (
             jax.ShapeDtypeStruct((pixels, 3 * depth), jnp.float32),
             jax.ShapeDtypeStruct((chips, 3, 3 * depth, 2 * own), jnp.bfloat16),
@@ -849,6 +788,123 @@
 def tiled_up(vector):
     count = -(-vector.shape[0] // 1024) * 1024
     return jnp.pad(vector.astype(jnp.float32), (0, count - vector.shape[0])).reshape(-1, 128)
+
+
+def attend_scatter_kernel(line, x_ref, valid_ref, w_ref, o_ref, mixed_ref, *scratch):
+    tokens, width = o_ref.shape
+    wide = mixed_ref.shape[1]
+    cut = width // TOKEN_PARTS
+    scale = 1.0 / math.sqrt(HEAD_DIM)
+
+    def attend(rows):
+        for head in range(wide // HEAD_DIM):
+            where = [pl.ds(j * wide + head * HEAD_DIM, HEAD_DIM) for j in range(3)]
+            scores = product(x_ref[rows, where[0]], x_ref[:, where[1]], True) * scale
+            scores = jnp.where(valid_ref[0:1] > 0.5, scores, MASKED_SCORE)
+            exponent = jnp.exp(scores - jnp.max(scores, axis=1, keepdims=True))
+            inverse = 1.0 / jnp.sum(exponent, axis=1, keepdims=True)
+            mixed_ref[rows, pl.ds(head * HEAD_DIM, HEAD_DIM)] = product(
+                (exponent * inverse).astype(jnp.bfloat16), x_ref[:, where[2]], False
+            ).astype(jnp.bfloat16)
+
+    def produce(chip, part, count, mine, other):
+        rows = pl.ds(pl.multiple_of(chip * 2 * tokens, 2 * tokens), 2 * tokens)
+        if part == 0:
+            attend(rows)
+        total = product(mixed_ref[rows], w_ref[:, pl.ds(part * cut, cut)], False)
+        first, second = pick(line.c, total[:tokens], total[tokens:])
+        mine[pl.ds(part * count, count)] = first
+        other[pl.ds(part * count, count)] = second.astype(jnp.bfloat16)
+
+    def finish(part, rows, total):
+        o_ref[:, pl.ds(part * cut, cut)] = total
+
+    line_scatter(line, scratch, TOKEN_PARTS, produce, finish, tokens)
+
+
+def attend_scatter(qkv_rows, valid, out_weight, n, m, number):
+    total = qkv_rows.shape[0]
+    tokens = total // n
+    width = out_weight.shape[1]
+    return comm_call(
+        attend_scatter_kernel,
+        (qkv_rows, jnp.broadcast_to(valid[None], (8, total)), out_weight),
+        (
+            jax.ShapeDtypeStruct((tokens, width), jnp.float32),
+            jax.ShapeDtypeStruct((total, out_weight.shape[0]), jnp.bfloat16),
+        ),
+        scatter_scratch(n // 2, TOKEN_PARTS * tokens, width // TOKEN_PARTS, TOKEN_PARTS),
+        (),
+        n,
+        m,
+        number,
+    )
+
+
+def attend_gather_kernel(
+    line, g_ref, w_ref, x_ref, kt_ref, valid_ref, held, grad_ref, keys_sum, values_sum, send, recv
+):
+    tokens = g_ref.shape[0]
+    wide = w_ref.shape[0]
+    heads = wide // HEAD_DIM
+    scale = 1.0 / math.sqrt(HEAD_DIM)
+
+    def slot(block):
+        return held.at[pl.ds(pl.multiple_of(block * tokens, tokens), tokens)]
+
+    def on_own():
+        keys_sum[...] = jnp.zeros_like(keys_sum)
+        values_sum[...] = jnp.zeros_like(values_sum)
+
+    def on_pair(chip):
+        rows = pl.ds(pl.multiple_of(chip * 2 * tokens, 2 * tokens), 2 * tokens)
+        for head in range(heads):
+            place = pl.ds(head * HEAD_DIM, HEAD_DIM)
+            where = [pl.ds(j * wide + head * HEAD_DIM, HEAD_DIM) for j in range(3)]
+            grad = product(held[rows], w_ref[place], True).astype(jnp.bfloat16)
+            query = x_ref[rows, where[0]]
+            scores = product(x_ref[:, where[1]], query, True) * scale
+            scores = jnp.where(valid_ref[:, 0:1] > 0.5, scores, MASKED_SCORE)
+            exponent = jnp.exp(scores - jnp.max(scores, axis=0, keepdims=True))
+            probs = exponent * (1.0 / jnp.sum(exponent, axis=0, keepdims=True))
+            values_sum[:, place] += product(probs.astype(jnp.bfloat16), grad, False)
+            grad_probs = product(x_ref[:, where[2]], grad, True)
+            inner = jnp.sum(probs * grad_probs, axis=0, keepdims=True)
+            grad_scores = (probs * (grad_probs - inner) * scale).astype(jnp.bfloat16)
+            keys_sum[:, place] += product(grad_scores, query, False)
+            grad_ref[rows, where[0]] = product(kt_ref[place], grad_scores, False).T.astype(
+                jnp.bfloat16
+            )
+
+    line_gather(line, g_ref, slot, send, recv, on_own, on_pair)
+    grad_ref[:, pl.ds(wide, wide)] = keys_sum[...].astype(jnp.bfloat16)
+    grad_ref[:, pl.ds(2 * wide, wide)] = values_sum[...].astype(jnp.bfloat16)
+
+
+def attend_gather(grad_mid, out_weight, qkv_rows, valid, n, m, number, riders):
+    tokens, width = grad_mid.shape
+    total = tokens * n
+    wide = out_weight.shape[0]
+    return comm_call(
+        attend_gather_kernel,
+        (
+            grad_mid,
+            out_weight,
+            qkv_rows,
+            qkv_rows[:, wide : 2 * wide].T,
+            jnp.broadcast_to(valid[:, None], (total, 128)),
+        ),
+        (
+            jax.ShapeDtypeStruct((total, width), jnp.bfloat16),
+            jax.ShapeDtypeStruct((total, 3 * wide), jnp.bfloat16),
+        ),
+        [pltpu.VMEM((total, wide), jnp.float32), pltpu.VMEM((total, wide), jnp.float32)]
+        + gather_sems(n // 2),
+        riders,
+        n,
+        m,
+        number,
+    )
 
 
 def local(
@@ -882,9 +938,7 @@
     token_cols = canvas_cols // 2
     local_tokens = token_rows * token_cols
     token_total = local_tokens * n
-    block_rows = min(512, token_total)
     local_width = out_weight.shape[0]
-    head_count = local_width // HEAD_DIM
 
     fused = own % 128 == 0 and n == 2 * m
     shift_vector = jnp.dot(embedding, shift_weight, preferred_element_type=jnp.float32)[0]
@@ -943,17 +997,12 @@
     all_attend, qkv_rows = tokens_gather(
         input_attend, qkv_weight, False, (jnp.bfloat16,), lambda value: (value,), n, m, 3
     )
-    qkv_rows = qkv_rows.reshape(token_total, 3, head_count, HEAD_DIM)
-    queries = qkv_rows[:, 0]
-    key_rows = qkv_rows[:, 1]
-    value_rows = qkv_rows[:, 2]
     token_index = jnp.arange(token_total, dtype=jnp.int32)
     key_valid = (token_index // token_cols < extents[0, 0]) & (
         token_index % token_cols < extents[0, 1]
     )
-    mixed_heads, log_totals = attend_forward(queries, key_rows, value_rows, key_valid, block_rows)
-    mixed_low = mixed_heads.reshape(token_total, local_width).astype(jnp.bfloat16)
-    (attended,) = tokens_scatter(mixed_low, out_weight[None], False, n, m, 4)
+    valid = key_valid.astype(jnp.float32)
+    attended, mixed_low = attend_scatter(qkv_rows, valid, out_weight, n, m, 4)
     stream_mid = stream + attended
     normed_mlp, inverse_mlp = layer_forward(stream_mid)
     input_mlp = (normed_mlp * (1.0 + scale_mlp) + shift_mlp).astype(jnp.bfloat16)
@@ -974,7 +1023,7 @@
 
     grad_final_low = cotangent[0].reshape(local_tokens, width_all)
     grad_final = grad_final_low.astype(jnp.float32)
-    all_final = gather_rows(grad_final_low)
+    all_final = gather_rows(lax.optimization_barrier((grad_final_low, qkv_rows))[0])
     grad_act = jnp.einsum("le,fe->lf", all_final, proj_weight, preferred_element_type=jnp.float32)
     gelu_pull = jax.vjp(partial(jax.nn.gelu, approximate=True), upper_proj)[1]
     grad_upper = gelu_pull(grad_act)[0].astype(jnp.bfloat16)
@@ -993,28 +1042,17 @@
         grad_normed_mlp, normed_mlp, inverse_mlp, scale_mlp
     )
     grad_mid = grad_final + grad_mid_norm
-    all_mid, grad_mixed_low, sums_up = tokens_gather(
+    all_mid, grad_qkv, sums_up = attend_gather(
         grad_mid.astype(jnp.bfloat16),
-        out_weight[None],
-        True,
-        (jnp.bfloat16,),
-        lambda value: (value,),
+        out_weight,
+        qkv_rows,
+        valid,
         n,
         m,
         7,
         (Rider("dp", grad_up.astype(jnp.bfloat16), 0),),
     )
-    grad_mixed_low = grad_mixed_low.reshape(token_total, head_count, HEAD_DIM)
     grad_out = jnp.einsum("lh,le->he", mixed_low, all_mid, preferred_element_type=jnp.float32)
-    grad_query, grad_keys, grad_values = attend_backward(
-        queries, key_rows, value_rows, key_valid, log_totals, grad_mixed_low, block_rows
-    )
-    grad_qkv = (
-        jnp.stack([grad_query, grad_keys, grad_values], axis=1)
-        .astype(jnp.bfloat16)
-        .reshape(token_total, 3, local_width)
-    )
-    grad_qkv = grad_qkv.reshape(token_total, 3 * local_width)
     grad_normed_attend, sums_out = tokens_scatter(
         grad_qkv, qkv_weight, True, n, m, 8, (Rider("dp", grad_out.astype(jnp.bfloat16), 1),)
     )
@@ -1059,7 +1097,7 @@
     def back(grad_low, hidden, spread, kernel, number, riders):
         if fused:
             acc, parts, *ridden = conv_back_fused(
-                grad_low, spread.T, kernel, canvas_cols, n, m, number, riders
+                grad_low, spread, kernel, canvas_cols, n, m, number, riders
             )
             return join_columns(acc, canvas_cols), parts.reshape(m, 9 * own, -1), ridden
         grad_hidden, grad_kernel = conv_backward(grad_low, hidden, kernel, n)

time: 1180 us -> 1130 us (0.958)
  matrix products: 120 us -> 55.7 us
  waiting for transfers between devices: 12.2 us -> 61.5 us
  local copies, waits for them, and re-layouts: 84.8 us -> 52.8 us
  Pallas kernels: 816 us -> 835 us
    dot_general x14 -> x0, matrix products: 62 us -> none  [the longest x2 16.7 us: one_block(): jnp.einsum('hqk,qhd->khd', grad_scores, query_block, preferred_element_ty...]
    ppermute x6, waiting for transfers between devices: 11.5 us -> 61.5 us  [turn_kernel(): moved = lax.ppermute(half, ('dp', 'mp'), route)]
    pallas_call x14, Pallas kernels: 816 us -> 835 us  [comm_call(): pl.pallas_call(body, out_shape=tuple(out_shapes) + ride_shapes, in_specs=...]
    reshape x3 -> x0, local copies, waits for them, and re-layouts: 15.9 us -> none  [the longest x2 11.6 us: side_by_side(): jnp.concatenate([padded[:, j:j + cols] for j in range(3)], axis=2)]
  transfers between devices with their start and end apart: 8 -> 8, of which waited for: 1 -> 1; matrix products, arithmetic and copies ran while one was open for 14% -> 7% of each run, Pallas kernels for 51% -> 17%
where the time goes in v3:
time: 1130 us; the launch traced here: 1120 us
  Pallas kernels  835 us (74%)
  other arithmetic  78.8 us (7%)
  waiting for transfers between devices  61.5 us (5%)
  matrix products  55.7 us (5%)
  local copies, waits for them, and re-layouts  52.8 us (5%)
  starting transfers between devices  17.5 us (2%)
  between operations  15.2 us (1%)
    pallas_call x14, Pallas kernels, comm_call(): pl.pallas_call(body, out_shape=tuple(out_shapes) + ride_shapes, in_specs=...  835 us
    ppermute x6, waiting for transfers between devices, turn_kernel(): moved = lax.ppermute(half, ('dp', 'mp'), route)  61.5 us
  transfers between devices with their start and end apart: 8, of which 1 were waited for; matrix products, arithmetic and copies ran while one was open for 7% of the time, Pallas kernels for 17%

profile of v3, /device:TPU:9, one launch (start us, length us, event | category | flops | bytes accessed | tf_op | source)
XLA Modules:
  0.0 1116.5 jit_solution(15055470044269413508)
XLA Ops:
  10.6 27.8 %shard_map.254 = (f32[8,8,128]{2,1,0:T(8,128)}, bf16[8,512,128]{2,1,0:T(8,128)(2,1)}) custom-call(f32[8,128]{1,0:T(8,128)} %bitcast.263, bf16[512,1024]{1,0:T(8,128)(2,1)} %bitcast.251), custom_call_target="tpu_custom_call" | custom-call | tf_op jit(solution)/shard_map/pallas_call | solution.py:281
  45.9 2.3 pad_maximum_fusion
  48.3 77.1 %shard_map.255 = f32[4096,128]{1,0:T(8,128)} custom-call(bf16[4352,384]{1,0:T(8,128)(2,1)} %bitcast.228, bf16[3,384,1024]{2,1,0:T(8,128)(2,1)} %bitcast.237), custom_call_target="tpu_custom_call" | custom-call | tf_op jit(solution)/shard_map/pallas_call | solution.py:281
  130.4 2.3 multiply_convert_fusion
  133.6 2.4 pad_maximum_fusion.1
  136.0 78.3 %shard_map.256 = f32[4096,128]{1,0:T(8,128)} custom-call(bf16[4352,384]{1,0:T(8,128)(2,1)} %bitcast.226, bf16[3,384,1024]{2,1,0:T(8,128)(2,1)} %bitcast.235), custom_call_target="tpu_custom_call" | custom-call | tf_op jit(solution)/shard_map/pallas_call | solution.py:281
  218.1 41.9 %shard_map.257 = f32[128,2048]{1,0:T(8,128)} custom-call(bf16[1024,512]{1,0:T(8,128)(2,1)} %reshape.567.refs_0_, bf16[1,512,2048]{2,1,0:T(8,128)(2,1)} %bitcast.239), custom_call_target="tpu_custom_call" | custom-call | tf_op jit(solution)/shard_map/pallas_call | solution.py:281
  264.0 40.2 %shard_map.258 = (bf16[1024,2048]{1,0:T(8,128)(2,1)}, bf16[1024,768]{1,0:T(8,128)(2,1)}) custom-call(bf16[128,2048]{1,0:T(8,128)(2,1)} %add_convert_fusion.3.refs_0_, bf16[3,2048,256]{2,1,0:T(8,128)(2,1)} %refs_1_.5), custom_call_target="tpu_custom_call" | custom-call | tf_op jit(solution)/shard_map/pallas_call | solution.py:281
  306.8 82.0 %shard_map.259 = (f32[128,2048]{1,0:T(8,128)}, bf16[1024,256]{1,0:T(8,128)(2,1)}) custom-call(bf16[1024,768]{1,0:T(8,128)(2,1)} %get-tuple-element.48.refs_0_.refs_2_, f32[8,1024]{1,0:T(8,128)} %broadcast_in_dim.42.refs_1_, bf16[256,2048]{1,0:T(8,128)(2,1)} %refs_1_.4), custom_call_target="tpu_custom_call" | custom-call | tf_op jit(solution)/shard_map/pallas_call | solution.py:281
  392.2 42.8 %shard_map.260 = (bf16[1024,2048]{1,0:T(8,128)(2,1)}, f32[1024,1024]{1,0:T(8,128)}, bf16[1024,1024]{1,0:T(8,128)(2,1)}) custom-call(bf16[128,2048]{1,0:T(8,128)(2,1)} %add_convert_fusion.2.refs_0_, bf16[1,2048,1024]{2,1,0:T(8,128)(2,1)} %bitcast.233), custom_call_target="tpu_custom_call" | custom-call | tf_op jit(solution)/shard_map/pallas_call | solution.py:281
  435.0 9.3 convolution_convert_fusion.2
  444.3 2.6 copy.49
  448.8 9.5 convolution_convert_fusion.1.refs_2_
  458.3 8.0 fusion.6.refs_0_
  466.4 65.8 %shard_map.261 = (f32[128,2048]{1,0:T(8,128)}, bf16[4,1024,512]{2,1,0:T(8,128)(2,1)}) custom-call(bf16[1024,1024]{1,0:T(8,128)(2,1)} %fusion.6.refs_0_, bf16[1,2048,1024]{2,1,0:T(8,128)(2,1)} %bitcast.234, bf16[1024,2048]{1,0:T(8,128)(2,1)} %convolution_convert_fusion.1.refs_2_), custom_call_target="tpu_custom_call" | custom-call | tf_op jit(solution)/shard_map/pallas_call | solution.py:281
  534.2 4.5 convert_reduce_fusion
  538.7 6.3 convolution_convert_fusion.refs_5_
  545.0 3.8 fusion.48
  549.8 54.1 %shard_map.262 = (bf16[1024,2048]{1,0:T(8,128)(2,1)}, bf16[1024,768]{1,0:T(8,128)(2,1)}, bf16[4,512,1024]{2,1,0:T(8,128)(2,1)}) custom-call(bf16[128,2048]{1,0:T(8,128)(2,1)} %get-tuple-element.134.refs_0_, bf16[256,2048]{1,0:T(8,128)(2,1)} %refs_1_.4, bf16[1024,768]{1,0:T(8,128)(2,1)} %get-tuple-element.48.refs_0_.refs_2_, ...), custom_call_target="tpu_custom_call" | custom-call | tf_op jit(solution)/shard_map/pallas_call | solution.py:281
  603.8 4.4 convolution_convert_fusion.5.refs_2_
  608.3 43.4 %shard_map.263 = (f32[128,2048]{1,0:T(8,128)}, bf16[4,256,512]{2,1,0:T(8,128)(2,1)}) custom-call(bf16[1024,768]{1,0:T(8,128)(2,1)} %get-tuple-element.55.refs_0_, bf16[3,2048,256]{2,1,0:T(8,128)(2,1)} %refs_1_.5, bf16[256,2048]{1,0:T(8,128)(2,1)} %convolution_convert_fusion.5.refs_2_), custom_call_target="tpu_custom_call" | custom-call | tf_op jit(solution)/shard_map/pallas_call | solution.py:281
  653.5 7.5 convolution_convert_fusion.3.refs_2_
  662.4 43.2 %shard_map.264 = (bf16[1024,2048]{1,0:T(8,128)(2,1)}, f32[1024,512]{1,0:T(8,128)}, bf16[4,512,768]{2,1,0:T(8,128)(2,1)}, f32[8,8,128]{2,1,0:T(8,128)}) custom-call(bf16[128,2048]{1,0:T(8,128)(2,1)} %add_convert_fusion.refs_0_, bf16[1,512,2048]{2,1,0:T(8,128)(2,1)} %bitcast.240, bf16[2048,768]{1,0:T(8,128)(2,1)} %convolution_convert_fusion.3.refs_2_, ...), custom_call_target="tpu_custom_call" | custom-call | tf_op jit(solution)/shard_map/pallas_call | solution.py:281
  705.6 3.5 reshape.569
  709.1 2.7 copy.50
  713.9 3.7 convolution_convert_fusion.4.refs_3_
  718.2 87.7 %shard_map.265 = (f32[4096,384]{1,0:T(8,128)}, bf16[4,3,384,256]{3,2,1,0:T(8,128)(2,1)}, bf16[4,512,512]{2,1,0:T(8,128)(2,1)}, f32[4,16,128]{2,1,0:T(8,128)}) custom-call(bf16[4096,128]{1,0:T(8,128)(2,1)} %convert_element_type.153.refs_0_, bf16[3,384,1024]{2,1,0:T(8,128)(2,1)} %bitcast.236, bf16[4352,384]{1,0:T(8,128)(2,1)} %bitcast.227, ...), custom_call_target="tpu_custom_call" | custom-call | tf_op jit(solution)/shard_map/pallas_call | solution.py:281
  805.9 2.7 fusion.51
  808.7 2.4 fusion.11
  811.1 2.4 fusion.45
  815.0 3.9 fusion.22
  819.8 100.4 %shard_map.266 = (f32[4096,384]{1,0:T(8,128)}, bf16[4,3,384,256]{3,2,1,0:T(8,128)(2,1)}, bf16[4,1,1152,256]{3,2,1,0:T(8,128)(2,1)}, f32[4,8,128]{2,1,0:T(8,128)}) custom-call(bf16[4096,128]{1,0:T(8,128)(2,1)} %get-tuple-element.145.refs_0_, bf16[3,384,1024]{2,1,0:T(8,128)(2,1)} %bitcast.238, bf16[4352,384]{1,0:T(8,128)(2,1)} %bitcast.229, ...), custom_call_target="tpu_custom_call" | custom-call | tf_op jit(solution)/shard_map/pallas_call | solution.py:281
  920.3 2.9 fusion.50
  923.2 4.3 fusion.44
  931.3 4.6 fusion.18.refs_2_
  935.8 50.3 %shard_map.267 = (bf16[4,1,1152,256]{3,2,1,0:T(8,128)(2,1)}, f32[32,16,128]{2,1,0:T(8,128)}, bf16[8,512,128]{2,1,0:T(8,128)(2,1)}) custom-call(bf16[4,1152,256]{2,1,0:T(8,128)(2,1)} %bitcast.248, f32[16,128]{1,0:T(8,128)} %pad_maximum_fusion.3.refs_1_, bf16[4096,128]{1,0:T(8,128)(2,1)} %fusion.18.refs_2_), custom_call_target="tpu_custom_call" | custom-call | tf_op jit(solution)/shard_map/pallas_call | solution.py:281
  990.7 2.3 reduce_sum.392
  995.3 2.8 collective-permute-start
  998.9 2.3 collective-permute-start.1
  1001.2 2.3 reduce_sum.393
  1005.7 2.5 collective-permute-start.2
  1011.3 2.9 reduce_sum.394
  1016.5 3.7 collective-permute-start.4
  1024.0 2.2 convert_reduce_fusion.1
  1027.8 3.0 copy.58
  1030.8 3.0 copy.59
  1033.9 61.4 %collective-permute-done.4 = bf16[4,128,256]{2,1,0:T(8,128)(2,1)} collective-permute-done((bf16[4,128,256]{2,1,0:T(8,128)(2,1)S(1)}, bf16[4,128,256]{2,1,0:T(8,128)(2,1)}, u32[]{:S(2)}, u32[]{:S(2)}) %collective-permute-start.4) | collective-permute-done | bytes 262176 | tf_op jit(solution)/shard_map/ppermute | solution.py:118
  1095.3 5.2 collective-permute-start.3
  (212 shorter events, 76.5 us)
Async XLA Ops:
  7.2 1.7 copy-start
  7.2 441.6 %all-gather.2.cloned.1.call-start = ((), (), s32[]{:S(2)}) async-start(), calls=%async_computation.2 | async-start | bytes 4718592 | tf_op jit(solution)/shard_map/all_gather | solution.py:62
  38.4 4.4 copy-start.4
  44.8 0.9 copy-start.16
  44.8 1.0 copy-start.20
  216.0 2.0 copy-start.23
  260.0 3.0 copy-start.2
  264.0 40.3 %copy-start.25 = (s32[1,2]{1,0:T(1,128)S(1)}, s32[1,2]{1,0:T(1,128)}, u32[]{:S(2)}) copy-start(s32[1,2]{1,0:T(1,128)} %param.17) | copy-start | bytes 28
  304.2 240.8 %reduce-scatter.2.cloned.1.call-start = ((), (), s32[]{:S(2)}) async-start(), calls=%async_computation.1 | async-start | bytes 4718592 | tf_op jit(solution)/shard_map/reduce_scatter | solution.py:66
  390.2 1.0 copy-start.3
  448.8 9.5 copy-start.26
  448.8 9.5 copy-start.27
  448.8 9.5 copy-start.29
  534.2 4.6 copy-start.13
  534.2 4.5 copy-start.28
  549.8 54.1 %copy-start.31 = (bf16[1024,256]{1,0:T(8,128)(2,1)S(1)}, bf16[1024,256]{1,0:T(8,128)(2,1)}, u32[]{:S(2)}) copy-start(bf16[1024,256]{1,0:T(8,128)(2,1)} %get-tuple-element.56) | copy-start | bytes 1572868
  651.7 1.8 copy-start.14
  653.5 7.6 copy-start.8
  653.5 7.6 copy-start.9
  661.1 1.3 copy-start.19
  709.1 3.8 copy-start.30
  711.8 5.7 copy-start.6
  711.8 2.0 copy-start.11
  713.9 3.7 copy-start.21
  808.6 2.5 copy-start.1
  920.2 2.9 copy-start.7
  927.4 3.9 copy-start.5
  986.1 3.2 copy-start.17
  995.3 108.3 %collective-permute-start = (bf16[9,128,128]{2,1,0:T(8,128)(2,1)}, bf16[9,128,128]{2,1,0:T(8,128)(2,1)}, u32[]{:S(2)}, u32[]{:S(2)}) collective-permute-start(bf16[9,128,128]{2,1,0:T(8,128)(2,1)} %bitcast.220), channel_id=1, source_target_pairs={{0,0},{1,1},{2,8},{3,9},{4,16},{5,17},{6,24},{7,25},{8,2},{9,3},{1... | collective-permute-start | bytes 884744 | tf_op jit(solution)/shard_map/ppermute | solution.py:118
  998.9 105.8 %collective-permute-start.1 = (bf16[9,128,128]{2,1,0:T(8,128)(2,1)}, bf16[9,128,128]{2,1,0:T(8,128)(2,1)}, u32[]{:S(2)}, u32[]{:S(2)}) collective-permute-start(bf16[9,128,128]{2,1,0:T(8,128)(2,1)} %bitcast.219), channel_id=1, source_target_pairs={{0,1},{1,0},{2,9},{3,8},{4,17},{5,16},{6,25},{7,24},{8,3},{9,2},{1... | collective-permute-start | bytes 884744 | tf_op jit(solution)/shard_map/ppermute | solution.py:118
  1003.5 4.7 copy-start.22
  1003.5 4.7 copy-start.24
  1005.7 100.1 %collective-permute-start.2 = (bf16[9,128,128]{2,1,0:T(8,128)(2,1)}, bf16[9,128,128]{2,1,0:T(8,128)(2,1)}, u32[]{:S(2)}, u32[]{:S(2)}) collective-permute-start(bf16[9,128,128]{2,1,0:T(8,128)(2,1)} %bitcast.218), channel_id=1, source_target_pairs={{0,0},{1,1},{2,8},{3,9},{4,16},{5,17},{6,24},{7,25},{8,2},{9,3},{1... | collective-permute-start | bytes 884744 | tf_op jit(solution)/shard_map/ppermute | solution.py:118
  1015.4 5.8 copy-start.12
  1016.5 78.8 %collective-permute-start.4 = (bf16[4,128,256]{2,1,0:T(8,128)(2,1)S(1)}, bf16[4,128,256]{2,1,0:T(8,128)(2,1)}, u32[]{:S(2)}, u32[]{:S(2)}) collective-permute-start(bf16[4,128,256]{2,1,0:T(8,128)(2,1)S(1)} %bitcast.256), channel_id=1, source_target_pairs={{0,0},{1,1},{2,8},{3,9},{4,16},{5,17},{6,24},{7,25},{8,2},{9,3},{1... | collective-permute-start | bytes 786440 | tf_op jit(solution)/shard_map/ppermute | solution.py:118
  1020.2 81.2 %collective-permute-start.5 = (bf16[4,128,256]{2,1,0:T(8,128)(2,1)S(1)}, bf16[4,128,256]{2,1,0:T(8,128)(2,1)}, u32[]{:S(2)}, u32[]{:S(2)}) collective-permute-start(bf16[4,128,256]{2,1,0:T(8,128)(2,1)S(1)} %bitcast.255), channel_id=1, source_target_pairs={{0,1},{1,0},{2,9},{3,8},{4,17},{5,16},{6,25},{7,24},{8,3},{9,2},{1... | collective-permute-start | bytes 786440 | tf_op jit(solution)/shard_map/ppermute | solution.py:118
  1021.2 2.8 copy-start.10
  1024.0 2.3 copy-start.18
  1024.0 2.9 copy-start.15
  1095.3 12.7 %collective-permute-start.3 = (bf16[9,128,128]{2,1,0:T(8,128)(2,1)S(1)}, bf16[9,128,128]{2,1,0:T(8,128)(2,1)S(1)}, u32[]{:S(2)}, u32[]{:S(2)}) collective-permute-start(bf16[9,128,128]{2,1,0:T(8,128)(2,1)S(1)} %bitcast.254), channel_id=1, source_target_pairs={{0,1},{1,0},{2,9},{3,8},{4,17},{5,16},{6,25},{7,24},{8,3},{9,2},{1... | collective-permute-start | bytes 884744 | tf_op jit(solution)/shard_map/ppermute | solution.py:118
Sparse Core Ops, SparseCore 0:
  304.3 83.7 all-gather.1
  444.4 55.9 reduce-scatter.1

commit v4 on v3

--- a/solution.py
+++ b/solution.py
@@ -98,27 +98,17 @@
 
 def by_images(grad, m):
     taps, own, outs = grad.shape
-    return grad.astype(jnp.bfloat16).reshape(taps * own, m, outs // m).transpose(1, 0, 2)
-
-
-def turn_kernel(mine, taps, m, n):
-    own = mine.shape[0] // taps
-    outs = mine.shape[1] * m
-    ratio = n // m
-    pieces = mine.astype(jnp.bfloat16).reshape(taps, own, ratio, outs // n)
-    me = lax.axis_index("mp") % ratio
-    result = jnp.zeros((taps, ratio, own, outs // n), jnp.bfloat16)
-    for shift in range(ratio):
-        route = []
-        for i in range(m):
-            for j in range(n):
-                target = (j // ratio) * n + ratio * i + (j % ratio + shift) % ratio
-                route.append((i * n + j, target))
-        half = lax.dynamic_index_in_dim(pieces, (me + shift) % ratio, axis=2, keepdims=False)
-        moved = lax.ppermute(half, ("dp", "mp"), route)
-        place = (me - shift + ratio) % ratio
-        result = lax.dynamic_update_slice(result, moved[:, None], (0, place, 0, 0))
-    return result.reshape(taps, ratio * own, outs // n).astype(jnp.float32)
+    return grad.astype(jnp.bfloat16).reshape(taps * own, outs).T.reshape(m, outs // m, taps * own)
+
+
+def unturned(halves, taps):
+    count, outs, _ = halves.shape
+    return (
+        halves.astype(jnp.float32)
+        .reshape(count, outs, taps, -1)
+        .transpose(2, 0, 3, 1)
+        .reshape(taps, -1, outs)
+    )
 
 
 def added(received):
@@ -177,51 +167,87 @@
     def peer(self, axis, step):
         return lax.rem(self.index(axis) + step, self.count(axis))
 
+    def turned(self, half):
+        ratio = 2 * self.chips // self.images
+        return (self.mp // ratio, ratio * self.dp + half)
+
+    def stays(self, half):
+        ratio = 2 * self.chips // self.images
+        return jnp.logical_and(self.dp == self.mp // ratio, self.mp % ratio == half)
+
     def barrier(self, axes, neighbours):
         bar = pltpu.get_barrier_semaphore()
-        if "all" in axes:
-            axes = ("all",)
+        turn = "turn" in axes and "all" not in axes
+        axes = ("all",) if "all" in axes else tuple(axis for axis in axes if axis != "turn")
         steady = 0
         for axis in axes:
             for step in range(1, self.count(axis)):
                 target = self.place(axis, self.peer(axis, step))
                 pl.semaphore_signal(bar, inc=1, device_id=target, device_id_type=MESH)
             steady += self.count(axis) - 1
-        if "all" in axes or "mp" in axes or not neighbours:
-            pl.semaphore_wait(bar, steady)
-            return
-        pl.semaphore_signal(bar, inc=1, device_id=self.sibling, device_id_type=MESH)
-
-        @pl.when(self.has_up)
-        def _():
-            pl.semaphore_signal(bar, inc=1, device_id=self.up, device_id_type=MESH)
-
-        @pl.when(self.has_down)
-        def _():
-            pl.semaphore_signal(bar, inc=1, device_id=self.down, device_id_type=MESH)
-
-        middle = jnp.logical_and(self.has_up, self.has_down)
-
-        @pl.when(middle)
-        def _():
-            pl.semaphore_wait(bar, steady + 3)
-
-        @pl.when(jnp.logical_not(middle))
-        def _():
-            pl.semaphore_wait(bar, steady + 2)
+        cases = [(steady, None)]
+        if neighbours and not ("all" in axes or "mp" in axes):
+            pl.semaphore_signal(bar, inc=1, device_id=self.sibling, device_id_type=MESH)
+
+            @pl.when(self.has_up)
+            def _():
+                pl.semaphore_signal(bar, inc=1, device_id=self.up, device_id_type=MESH)
+
+            @pl.when(self.has_down)
+            def _():
+                pl.semaphore_signal(bar, inc=1, device_id=self.down, device_id_type=MESH)
+
+            middle = jnp.logical_and(self.has_up, self.has_down)
+            cases = [(steady + 3, middle), (steady + 2, jnp.logical_not(middle))]
+        if turn:
+            ratio = 2 * self.chips // self.images
+            for half in range(ratio):
+
+                @pl.when(jnp.logical_not(self.stays(half)))
+                def _():
+                    pl.semaphore_signal(
+                        bar, inc=1, device_id=self.turned(half), device_id_type=MESH
+                    )
+
+            same = self.dp == self.mp // ratio
+            cases = [
+                (count + ratio - less, here if when is None else jnp.logical_and(when, here))
+                for count, when in cases
+                for less, here in ((1, same), (0, jnp.logical_not(same)))
+            ]
+        for count, when in cases:
+            if when is None:
+                pl.semaphore_wait(bar, count)
+            else:
+
+                @pl.when(when)
+                def _():
+                    pl.semaphore_wait(bar, count)
 
 
 class Rider:
-    def __init__(self, axis, array, cut=None):
+    def __init__(self, axis, array, cut=None, beside=False):
+        self.axes = (axis,)
         self.axis = axis
         self.array = array
         self.cut = cut
-
-    def result(self, count):
+        self.beside = beside
+
+    def result(self, sizes):
+        count = sizes[self.axis]
         shape = list(self.array.shape)
         if self.cut is not None:
             shape[self.cut] //= count
-        return jax.ShapeDtypeStruct((count,) + tuple(shape), self.array.dtype)
+        self.columns = shape[-1]
+        if self.beside:
+            shape[-1] *= count
+        else:
+            shape = [count] + shape
+        return jax.ShapeDtypeStruct(tuple(shape), self.array.dtype)
+
+    def scratch(self, sizes):
+        count = sizes[self.axis]
+        return [pltpu.SemaphoreType.DMA((count,)), pltpu.SemaphoreType.DMA((count,))]
 
     def piece(self, ref, index, count):
         if self.cut is None:
@@ -233,13 +259,17 @@
 
     def copies(self, line, src, dst, send, recv):
         count, me = line.count(self.axis), line.index(self.axis)
-        made = [pltpu.make_async_copy(self.piece(src, me, count), dst.at[me], send.at[0])]
+        if self.beside:
+            land = dst.at[:, pl.ds(pl.multiple_of(me * self.columns, self.columns), self.columns)]
+        else:
+            land = dst.at[me]
+        made = [pltpu.make_async_copy(self.piece(src, me, count), land, send.at[0])]
         for step in range(1, count):
             peer = line.peer(self.axis, step)
             made.append(
                 remote(
                     self.piece(src, peer, count),
-                    dst.at[me],
+                    land,
                     send.at[step],
                     recv.at[step],
                     line.place(self.axis, peer),
@@ -247,12 +277,119 @@
             )
         return made
 
+    def start(self, line, src, dst, send, recv):
+        for copy in self.copies(line, src, dst, send, recv):
+            copy.start()
+
+    def middle(self, line, src, dst, send, recv):
+        pass
+
+    def finish(self, line, src, dst, send, recv):
+        for copy in self.copies(line, src, dst, send, recv):
+            copy.wait()
+
+
+class Turn:
+    def __init__(self, array):
+        self.axes = ("turn",)
+        self.array = array
+
+    def result(self, sizes):
+        self.ratio = sizes["mp"] // sizes["dp"]
+        rows, columns = self.array.shape[-2:]
+        return jax.ShapeDtypeStruct((self.ratio, rows // self.ratio, columns), self.array.dtype)
+
+    def scratch(self, sizes):
+        ratio = sizes["mp"] // sizes["dp"]
+        return [pltpu.SemaphoreType.DMA((ratio,)), pltpu.SemaphoreType.DMA((ratio,))]
+
+    def leave(self, line, src, dst, send, recv, half):
+        size = dst.shape[1]
+        piece = src.at[pl.ds(half * size, size)]
+        mine = line.mp % self.ratio
+        away = remote(piece, dst.at[mine], send.at[half], recv.at[mine], line.turned(half))
+        return away, pltpu.make_async_copy(piece, dst.at[half], send.at[half])
+
+    def start(self, line, src, dst, send, recv):
+        for half in range(self.ratio):
+            away, here = self.leave(line, src, dst, send, recv, half)
+
+            @pl.when(line.stays(half))
+            def _():
+                here.start()
+
+            @pl.when(jnp.logical_not(line.stays(half)))
+            def _():
+                away.start()
+
+    def middle(self, line, src, dst, send, recv):
+        pass
+
+    def finish(self, line, src, dst, send, recv):
+        for half in range(self.ratio):
+            away, here = self.leave(line, src, dst, send, recv, half)
+
+            @pl.when(line.stays(half))
+            def _():
+                here.wait()
+
+            @pl.when(jnp.logical_not(line.stays(half)))
+            def _():
+                away.wait_send()
+                remote(
+                    dst.at[half], dst.at[half], send.at[half], recv.at[half], line.turned(half)
+                ).wait_recv()
+
+
+class SumTurn:
+    def __init__(self, array):
+        self.axes = ("dp", "turn")
+        self.first = Rider("dp", array, 0)
+        self.second = Turn(array)
+        self.array = array
+
+    def result(self, sizes):
+        self.first.result(sizes)
+        return self.second.result(sizes)
+
+    def scratch(self, sizes):
+        shape = self.array.shape
+        return (
+            [
+                pltpu.VMEM((shape[0], 1) + shape[1:], self.array.dtype),
+                pltpu.VMEM(shape[1:], self.array.dtype),
+            ]
+            + self.first.scratch(sizes)
+            + self.second.scratch(sizes)
+        )
+
+    def start(self, line, src, dst, got, total, *sems):
+        self.first.start(line, src, got, *sems[:2])
+
+    def middle(self, line, src, dst, got, total, *sems):
+        self.first.finish(line, src, got, *sems[:2])
+        rows = total.shape[0]
+        tile = 32
+
+        @pl.loop(0, rows // tile)
+        def _(index):
+            where = pl.ds(pl.multiple_of(index * tile, tile), tile)
+            added_up = got[0, 0, where].astype(jnp.float32)
+            for image in range(1, got.shape[0]):
+                added_up += got[image, 0, where].astype(jnp.float32)
+            total[where] = added_up.astype(total.dtype)
+
+        self.second.start(line, total, dst, *sems[2:])
+
+    def finish(self, line, src, dst, got, total, *sems):
+        self.second.finish(line, total, dst, *sems[2:])
+
 
 def comm_call(kernel, inputs, out_shapes, scratch, riders, n, m, number, neighbours=True):
     chips = n // 2
     sizes = {"dp": m, "mp": n, "all": m * n}
-    counts = [sizes[rider.axis] for rider in riders]
-    ride_shapes = tuple(rider.result(count) for rider, count in zip(riders, counts))
+    ride_shapes = tuple(rider.result(sizes) for rider in riders)
+    ride_scratch = [rider.scratch(sizes) for rider in riders]
     any_spec = pl.BlockSpec(memory_space=pl.ANY)
     ni, nr, no = len(inputs), len(riders), len(out_shapes)
 
@@ -261,29 +398,27 @@
         rest = refs[ni + nr :]
         main_out, ride_out = rest[:no], rest[no : no + nr]
         rest = rest[no + nr :]
-        main_scratch, sems = rest[: len(scratch)], rest[len(scratch) :]
+        main_scratch, rest = rest[: len(scratch)], rest[len(scratch) :]
         line = Line(chips, m)
-        line.barrier(sorted(set(rider.axis for rider in riders)), neighbours)
-        copies = []
-        for index, rider in enumerate(riders):
-            copies += rider.copies(
-                line, ride_in[index], ride_out[index], sems[2 * index], sems[2 * index + 1]
-            )
-        for copy in copies:
-            copy.start()
+        line.barrier(sorted(set(axis for rider in riders for axis in rider.axes)), neighbours)
+        riding = []
+        for rider, src, dst, needs in zip(riders, ride_in, ride_out, ride_scratch):
+            riding.append((rider, (line, src, dst) + tuple(rest[: len(needs)])))
+            rest = rest[len(needs) :]
+        for rider, refs_in in riding:
+            rider.start(*refs_in)
         kernel(line, *main_in, *main_out, *main_scratch)
-        for copy in copies:
-            copy.wait()
-
-    ride_sems = []
-    for count in counts:
-        ride_sems += [pltpu.SemaphoreType.DMA((count,)), pltpu.SemaphoreType.DMA((count,))]
+        for rider, refs_in in riding:
+            rider.middle(*refs_in)
+        for rider, refs_in in riding:
+            rider.finish(*refs_in)
+
     return pl.pallas_call(
         body,
         out_shape=tuple(out_shapes) + ride_shapes,
         in_specs=whole(ni) + [any_spec] * nr,
         out_specs=tuple(whole(no) + [any_spec] * nr),
-        scratch_shapes=list(scratch) + ride_sems,
+        scratch_shapes=list(scratch) + [ref for needs in ride_scratch for ref in needs],
         compiler_params=comm_params(number),
     )(*inputs, *[rider.array for rider in riders])
 
@@ -612,7 +747,7 @@
     chips = line.chips
     pixels, own = g_ref.shape
     wide = w_ref.shape[1]
-    tile = 512
+    tile, long = 512, 1024
     zero = jnp.zeros((breadth, own), jnp.bfloat16)
     for block in range(2 * chips):
         held[block, pl.ds(0, breadth)] = zero
@@ -621,8 +756,9 @@
     def slot(block):
         return held.at[block, pl.ds(breadth, pixels)]
 
-    def pair(chip, rows):
-        return jnp.concatenate([held[2 * chip, rows], held[2 * chip + 1, rows]], axis=1)
+    def beside(base, count, chip):
+        rows = pl.ds(base, count)
+        return [held[2 * chip, rows], held[2 * chip + 1, rows]]
 
     def on_own():
         @pl.loop(0, pixels // tile)
@@ -637,30 +773,30 @@
         @pl.loop(0, pixels // tile)
         def _(index):
             base = pl.multiple_of(index * tile, tile)
-            total = acc_ref[pl.ds(base, tile)]
+            shifted = []
             for i in range(3):
-                total += lax.dot_general(
-                    pair(chip, pl.ds(base + (2 - i) * breadth, tile)),
-                    w_ref[i, :, columns],
-                    (((1,), (1,)), ((), ())),
-                    preferred_element_type=jnp.float32,
-                )
-            acc_ref[pl.ds(base, tile)] = total
-
-        for i in range(3):
-            sums[...] = jnp.zeros_like(sums)
-
-            @pl.loop(0, pixels // tile)
-            def _(index):
-                base = pl.multiple_of(index * tile, tile)
-                sums[...] += lax.dot_general(
-                    x_ref[pl.ds(base + i * breadth, tile)],
-                    pair(chip, pl.ds(base + breadth, tile)),
-                    (((0,), (0,)), ((), ())),
-                    preferred_element_type=jnp.float32,
-                )
-
-            wg_ref[chip, i] = sums[...].astype(jnp.bfloat16)
+                shifted += beside(base + (2 - i) * breadth, tile, chip)
+            acc_ref[pl.ds(base, tile)] += product(
+                jnp.concatenate(shifted, axis=1),
+                jnp.concatenate([w_ref[i, :, columns] for i in range(3)], axis=1),
+                True,
+            )
+
+        sums[...] = jnp.zeros_like(sums)
+
+        @pl.loop(0, pixels // long)
+        def _(index):
+            base = pl.multiple_of(index * long, long)
+            sums[...] += lax.dot_general(
+                jnp.concatenate(beside(base + breadth, long, chip), axis=1),
+                jnp.concatenate(
+                    [x_ref[pl.ds(base + i * breadth, long)] for i in range(3)], axis=1
+                ),
+                (((0,), (0,)), ((), ())),
+                preferred_element_type=jnp.float32,
+            )
+
+        wg_ref[chip] = sums[...].astype(jnp.bfloat16)
 
     line_gather(line, g_ref, slot, send, recv, on_own, on_pair)
 
@@ -674,11 +810,11 @@
         (grad_low, kernel.reshape(3, 3 * depth, kernel.shape[2]), spread),
         (
             jax.ShapeDtypeStruct((pixels, 3 * depth), jnp.float32),
-            jax.ShapeDtypeStruct((chips, 3, 3 * depth, 2 * own), jnp.bfloat16),
+            jax.ShapeDtypeStruct((chips, 2 * own, 9 * depth), jnp.bfloat16),
         ),
         [
             pltpu.VMEM((n, pixels + 2 * cols, own), jnp.bfloat16),
-            pltpu.VMEM((3 * depth, 2 * own), jnp.float32),
+            pltpu.VMEM((2 * own, 9 * depth), jnp.float32),
         ]
         + gather_sems(chips),
         riders,
@@ -1086,7 +1222,7 @@
         ),
     )
     grad_down = jnp.einsum(
-        "lk,le->ke", down_patch, all_stream, preferred_element_type=jnp.float32
+        "le,lk->ek", all_stream, down_patch, preferred_element_type=jnp.float32
     )
     ada_columns = added(ada_columns).reshape(-1)[: columns.shape[0]]
     grad_residual = (
@@ -1099,7 +1235,7 @@
             acc, parts, *ridden = conv_back_fused(
                 grad_low, spread, kernel, canvas_cols, n, m, number, riders
             )
-            return join_columns(acc, canvas_cols), parts.reshape(m, 9 * own, -1), ridden
+            return join_columns(acc, canvas_cols), parts, ridden
         grad_hidden, grad_kernel = conv_backward(grad_low, hidden, kernel, n)
         return grad_hidden, by_images(grad_kernel, m), exchange(riders, n, m, number)
 
@@ -1110,7 +1246,7 @@
         conv_second,
         10,
         (
-            Rider("dp", grad_down.astype(jnp.bfloat16), 1),
+            Rider("dp", grad_down.astype(jnp.bfloat16), 0),
             Rider("dp", jnp.concatenate([tiled_up(embedding[0]), tiled_up(ada_columns)])),
         ),
     )
@@ -1118,13 +1254,17 @@
         grad_hidden_second, normed_second, inverse_second, own_second, size
     )
     grad_shift = jnp.sum(grad_conv_output, axis=0)
-    grad_hidden_first, parts_first, (sums_second, every_shift) = back(
+    grad_hidden_first, parts_first, (sums_second, every_shift, turned_down) = back(
         grad_conv_output.astype(jnp.bfloat16),
         hidden_first,
         spread_first,
         conv_first,
         11,
-        (Rider("dp", parts_second, 0), Rider("dp", tiled_up(grad_shift))),
+        (
+            Rider("dp", parts_second, 0),
+            Rider("dp", tiled_up(grad_shift)),
+            Turn(added(sums_down).astype(jnp.bfloat16)),
+        ),
     )
     grad_base, grad_gain_first = group_backward(
         grad_hidden_first, normed_first, inverse_first, own_first, size
@@ -1136,14 +1276,18 @@
     small = jnp.concatenate(
         [tiled_up(embed_term[0]), tiled_up(jnp.concatenate([grad_gain_first, grad_gain_second]))]
     )
-    riders = (Rider("dp", parts_first, 0), Rider("all", small))
+    riders = (
+        SumTurn(parts_first),
+        Rider("all", small),
+        Turn(added(sums_second)[0].astype(jnp.bfloat16)),
+    )
     if fused:
-        sums_first, small, image_turned = exchange(
-            riders + (Rider("mp", image_turned, 0),), n, m, 13
+        turned_first, small, turned_second, image_turned = exchange(
+            riders + (Rider("mp", image_turned, 0, True),), n, m, 13
         )
-        image_grad = image_turned.transpose(1, 0, 2).reshape(image.shape)
+        image_grad = image_turned.reshape(image.shape)
     else:
-        sums_first, small = exchange(riders, n, m, 13)
+        turned_first, small, turned_second = exchange(riders, n, m, 13)
         image_grad = lax.all_to_all(
             image_turned.reshape(rows_all, canvas_cols, own), "mp", 0, 2, tiled=True
         )[None]
@@ -1170,17 +1314,19 @@
         every_small[:, gain_start : gain_start + columns.shape[0]],
         precision=PRECISE,
     )
-    qkv_grad = added(sums_qkv).reshape(-1, 3, local_width).transpose(1, 0, 2)
+    qkv_grad = jnp.stack(
+        [added(sums_qkv[:, :, j * local_width : (j + 1) * local_width]) for j in range(3)]
+    )
     return (
         output,
         image_grad,
         embedding_grad,
         gains[0],
-        turn_kernel(added(sums_first)[0], 9, m, n),
+        unturned(turned_first, 9),
         gains[1],
-        turn_kernel(added(sums_second)[0], 9, m, n),
+        unturned(turned_second, 9),
         grad_shift_weight,
-        turn_kernel(added(sums_down), 4, m, n),
+        unturned(turned_down, 4),
         grad_ada_weight,
         qkv_grad,
         added(sums_out),

time: 1130 us -> 1120 us (level)
  Pallas kernels: 835 us -> 917 us
  waiting for transfers between devices: 61.5 us -> 0.04 us
  starting transfers between devices: 17.5 us -> 0.08 us
    pallas_call x14, Pallas kernels: 835 us -> 917 us  [comm_call(): pl.pallas_call(body, out_shape=tuple(out_shapes) + ride_shapes, in_specs=...]
    ppermute x6 -> x0, waiting for transfers between devices: 61.5 us -> none  [turn_kernel(): moved = lax.ppermute(half, ('dp', 'mp'), route)]
    ppermute x6 -> x0, starting transfers between devices: 17.4 us -> none  [turn_kernel(): moved = lax.ppermute(half, ('dp', 'mp'), route)]
  transfers between devices with their start and end apart: 8 -> 2, of which waited for: 1 -> 0; matrix products, arithmetic and copies ran while one was open for 7% -> 4% of each run, Pallas kernels for 17% -> 17%
where the time goes in v4:
time: 1120 us; the launch traced here: 1110 us
  Pallas kernels  917 us (82%)
  other arithmetic  77.7 us (7%)
  matrix products  57 us (5%)
  local copies, waits for them, and re-layouts  44.9 us (4%)
  between operations  15 us (1%)
    pallas_call x14, Pallas kernels, comm_call(): pl.pallas_call(body, out_shape=tuple(out_shapes) + ride_shapes, in_specs=...  917 us
  transfers between devices with their start and end apart: 2, of which 0 were waited for; matrix products, arithmetic and copies ran while one was open for 4% of the time, Pallas kernels for 17%

profile of v4, /device:TPU:9, one launch (start us, length us, event | category | flops | bytes accessed | tf_op | source)
XLA Modules:
  0.0 1112.3 jit_solution(15659012620356525144)
XLA Ops:
  11.7 27.8 %shard_map.254 = (f32[8,8,128]{2,1,0:T(8,128)}, bf16[8,512,128]{2,1,0:T(8,128)(2,1)}) custom-call(f32[8,128]{1,0:T(8,128)} %bitcast.223, bf16[512,1024]{1,0:T(8,128)(2,1)} %bitcast.213), custom_call_target="tpu_custom_call" | custom-call | tf_op jit(solution)/shard_map/pallas_call | solution.py:416
  44.7 2.0 multiply_convert_fusion.1
  47.6 2.3 pad_maximum_fusion
  49.9 77.1 %shard_map.255 = f32[4096,128]{1,0:T(8,128)} custom-call(bf16[4352,384]{1,0:T(8,128)(2,1)} %bitcast.183, bf16[3,384,1024]{2,1,0:T(8,128)(2,1)} %bitcast.194), custom_call_target="tpu_custom_call" | custom-call | tf_op jit(solution)/shard_map/pallas_call | solution.py:416
  127.0 2.1 add_reduce_fusion
  129.5 2.2 multiply_reduce_fusion.2
  132.1 2.3 multiply_convert_fusion
  135.2 2.4 pad_maximum_fusion.1
  137.6 78.3 %shard_map.256 = f32[4096,128]{1,0:T(8,128)} custom-call(bf16[4352,384]{1,0:T(8,128)(2,1)} %bitcast.185, bf16[3,384,1024]{2,1,0:T(8,128)(2,1)} %bitcast.192), custom_call_target="tpu_custom_call" | custom-call | tf_op jit(solution)/shard_map/pallas_call | solution.py:416
  219.7 41.9 %shard_map.257 = f32[128,2048]{1,0:T(8,128)} custom-call(bf16[1024,512]{1,0:T(8,128)(2,1)} %reshape.568.refs_0_, bf16[1,512,2048]{2,1,0:T(8,128)(2,1)} %bitcast.196), custom_call_target="tpu_custom_call" | custom-call | tf_op jit(solution)/shard_map/pallas_call | solution.py:416
  265.6 40.1 %shard_map.258 = (bf16[1024,2048]{1,0:T(8,128)(2,1)}, bf16[1024,768]{1,0:T(8,128)(2,1)}) custom-call(bf16[128,2048]{1,0:T(8,128)(2,1)} %add_convert_fusion.3.refs_0_, bf16[3,2048,256]{2,1,0:T(8,128)(2,1)} %refs_1_.5), custom_call_target="tpu_custom_call" | custom-call | tf_op jit(solution)/shard_map/pallas_call | solution.py:416
  308.3 82.0 %shard_map.259 = (f32[128,2048]{1,0:T(8,128)}, bf16[1024,256]{1,0:T(8,128)(2,1)}) custom-call(bf16[1024,768]{1,0:T(8,128)(2,1)} %get-tuple-element.50.refs_0_.refs_2_, f32[8,1024]{1,0:T(8,128)} %broadcast_in_dim.28.refs_1_, bf16[256,2048]{1,0:T(8,128)(2,1)} %refs_1_.4), custom_call_target="tpu_custom_call" | custom-call | tf_op jit(solution)/shard_map/pallas_call | solution.py:416
  393.7 43.0 %shard_map.260 = (bf16[1024,2048]{1,0:T(8,128)(2,1)}, f32[1024,1024]{1,0:T(8,128)}, bf16[1024,1024]{1,0:T(8,128)(2,1)}) custom-call(bf16[128,2048]{1,0:T(8,128)(2,1)} %add_convert_fusion.2.refs_0_, bf16[1,2048,1024]{2,1,0:T(8,128)(2,1)} %bitcast.190), custom_call_target="tpu_custom_call" | custom-call | tf_op jit(solution)/shard_map/pallas_call | solution.py:416
  436.7 9.3 convolution_convert_fusion.2
  446.7 2.6 copy.42
  451.1 9.5 convolution_convert_fusion.1.refs_2_
  460.6 7.9 fusion.6.refs_0_
  468.6 65.2 %shard_map.261 = (f32[128,2048]{1,0:T(8,128)}, bf16[4,1024,512]{2,1,0:T(8,128)(2,1)}) custom-call(bf16[1024,1024]{1,0:T(8,128)(2,1)} %fusion.6.refs_0_, bf16[1,2048,1024]{2,1,0:T(8,128)(2,1)} %bitcast.191, bf16[1024,2048]{1,0:T(8,128)(2,1)} %convolution_convert_fusion.1.refs_2_), custom_call_target="tpu_custom_call" | custom-call | tf_op jit(solution)/shard_map/pallas_call | solution.py:416
  535.8 4.5 convert_reduce_fusion
  540.4 6.3 convolution_convert_fusion.refs_5_
  546.6 3.8 fusion.52
  551.4 54.2 %shard_map.262 = (bf16[1024,2048]{1,0:T(8,128)(2,1)}, bf16[1024,768]{1,0:T(8,128)(2,1)}, bf16[4,512,1024]{2,1,0:T(8,128)(2,1)}) custom-call(bf16[128,2048]{1,0:T(8,128)(2,1)} %get-tuple-element.99.refs_0_, bf16[256,2048]{1,0:T(8,128)(2,1)} %refs_1_.4, bf16[1024,768]{1,0:T(8,128)(2,1)} %get-tuple-element.50.refs_0_.refs_2_, ...), custom_call_target="tpu_custom_call" | custom-call | tf_op jit(solution)/shard_map/pallas_call | solution.py:416
  605.6 8.0 convolution_convert_fusion.3.refs_2_
  613.7 2.2 convolution_convert_fusion.5.refs_2_
  615.9 43.4 %shard_map.263 = (f32[128,2048]{1,0:T(8,128)}, bf16[4,256,512]{2,1,0:T(8,128)(2,1)}) custom-call(bf16[1024,768]{1,0:T(8,128)(2,1)} %get-tuple-element.57.refs_0_, bf16[3,2048,256]{2,1,0:T(8,128)(2,1)} %refs_1_.5, bf16[256,2048]{1,0:T(8,128)(2,1)} %convolution_convert_fusion.5.refs_2_), custom_call_target="tpu_custom_call" | custom-call | tf_op jit(solution)/shard_map/pallas_call | solution.py:416
  662.5 43.2 %shard_map.264 = (bf16[1024,2048]{1,0:T(8,128)(2,1)}, f32[1024,512]{1,0:T(8,128)}, bf16[4,512,768]{2,1,0:T(8,128)(2,1)}, f32[8,8,128]{2,1,0:T(8,128)}) custom-call(bf16[128,2048]{1,0:T(8,128)(2,1)} %add_convert_fusion.refs_0_, bf16[1,512,2048]{2,1,0:T(8,128)(2,1)} %bitcast.197, bf16[2048,768]{1,0:T(8,128)(2,1)} %convolution_convert_fusion.3.refs_2_, ...), custom_call_target="tpu_custom_call" | custom-call | tf_op jit(solution)/shard_map/pallas_call | solution.py:416
  705.7 3.5 reshape.570
  709.2 3.9 copy.43
  713.1 2.7 convert_element_type.134.refs_0_
  715.9 5.9 convolution_convert_fusion.4.refs_3_
  722.3 85.7 %shard_map.265 = (f32[4096,384]{1,0:T(8,128)}, bf16[4,256,1152]{2,1,0:T(8,128)(2,1)}, bf16[4,512,512]{2,1,0:T(8,128)(2,1)}, f32[4,16,128]{2,1,0:T(8,128)}) custom-call(bf16[4096,128]{1,0:T(8,128)(2,1)} %convert_element_type.134.refs_0_, bf16[3,384,1024]{2,1,0:T(8,128)(2,1)} %bitcast.193, bf16[4352,384]{1,0:T(8,128)(2,1)} %bitcast.186, ...), custom_call_target="tpu_custom_call" | custom-call | tf_op jit(solution)/shard_map/pallas_call | solution.py:416
  808.0 2.7 fusion.55
  810.8 2.4 fusion.11
  813.2 2.4 fusion.49
  817.2 4.0 fusion.22
  823.1 2.3 convert_reduce_fusion.1
  828.7 2.9 reduce_sum.392.refs_5_
  831.5 123.0 %shard_map.266 = (f32[4096,384]{1,0:T(8,128)}, bf16[4,256,1152]{2,1,0:T(8,128)(2,1)}, bf16[4,1,256,1152]{3,2,1,0:T(8,128)(2,1)}, f32[4,8,128]{2,1,0:T(8,128)}, bf16[2,256,512]{2,1,0:T(8,128)(2,1)}) custom-call(bf16[4096,128]{1,0:T(8,128)(2,1)} %get-tuple-element.110.refs_0_, bf16[3,384,1024]{2,1,0:T(8,128)(2,1)} %bitcast.195, bf16[4352,384]{1,0:T(8,128)(2,1)} %bitcast.184, ...), custom_call_target="tpu_custom_call" | custom-call | tf_op jit(solution)/shard_map/pallas_call | solution.py:416
  955.3 2.0 fusion.24
  958.4 3.0 reduce_sum.394.refs_2_
  964.1 2.9 fusion.54
  967.0 4.4 fusion.48
  973.5 4.6 fusion.18.refs_3_
  978.1 112.5 %shard_map.267 = (bf16[2,128,1152]{2,1,0:T(8,128)(2,1)}, f32[32,16,128]{2,1,0:T(8,128)}, bf16[2,128,1152]{2,1,0:T(8,128)(2,1)}, bf16[512,1024]{1,0:T(8,128)(2,1)}) custom-call(bf16[4,256,1152]{2,1,0:T(8,128)(2,1)} %get-tuple-element.68.refs_0_, f32[16,128]{1,0:T(8,128)} %pad_maximum_fusion.4.refs_1_, bf16[256,1152]{1,0:T(8,128)(2,1)} %reduce_sum.394.refs_2_, ...), custom_call_target="tpu_custom_call" | custom-call | tf_op jit(solution)/shard_map/pallas_call | solution.py:416
  1092.9 2.3 copy.44
  1095.2 2.4 copy.45
  1097.6 2.4 copy.46
  1100.0 2.4 copy.47
  (175 shorter events, 53.3 us)
Async XLA Ops:
  7.2 2.8 copy-start
  7.2 443.9 %all-gather.2.cloned.1.call-start = ((), (), s32[]{:S(2)}) async-start(), calls=%async_computation.2 | async-start | bytes 4718592 | tf_op jit(solution)/shard_map/all_gather | solution.py:62
  39.5 5.2 copy-start.4
  261.6 3.0 copy-start.2
  265.6 40.2 %copy-start.23 = (s32[1,2]{1,0:T(1,128)S(1)}, s32[1,2]{1,0:T(1,128)}, u32[]{:S(2)}) copy-start(s32[1,2]{1,0:T(1,128)} %param.17) | copy-start | bytes 28
  305.7 240.9 %reduce-scatter.2.cloned.1.call-start = ((), (), s32[]{:S(2)}) async-start(), calls=%async_computation.1 | async-start | bytes 4718592 | tf_op jit(solution)/shard_map/reduce_scatter | solution.py:66
  391.7 1.0 copy-start.3
  446.0 0.7 copy-start.20
  451.1 9.5 copy-start.24
  451.1 9.5 copy-start.25
  451.1 9.5 copy-start.27
  535.8 4.6 copy-start.12
  535.8 4.5 copy-start.26
  605.6 8.1 copy-start.28
  605.6 8.1 copy-start.29
  659.3 1.9 copy-start.7
  659.3 1.9 copy-start.8
  661.2 1.3 copy-start.19
  709.2 3.9 copy-start.21
  713.1 2.8 copy-start.10
  810.8 2.5 copy-start.1
  813.2 8.0 copy-start.18
  817.2 5.0 copy-start.16
  817.2 5.9 copy-start.9
  823.1 4.0 copy-start.11
  827.0 1.6 copy-start.22
  964.1 2.9 copy-start.6
  967.0 6.5 copy-start.5
  1097.6 4.9 copy-start.13
  1097.6 4.9 copy-start.14
  1100.0 2.5 copy-start.15
  1102.4 1.6 copy-start.17
Sparse Core Ops, SparseCore 0:
  305.9 83.7 all-gather.1
  446.1 55.6 reduce-scatter.1

commit v5 on v4

--- a/solution.py
+++ b/solution.py
@@ -96,18 +96,17 @@
     return (join_columns(acc, col_count), grad_kernel)
 
 
-def by_images(grad, m):
-    taps, own, outs = grad.shape
-    return grad.astype(jnp.bfloat16).reshape(taps * own, outs).T.reshape(m, outs // m, taps * own)
-
-
-def unturned(halves, taps):
-    count, outs, _ = halves.shape
+def unsettled(parts, m, n):
+    return parts.reshape(n, m, -1, parts.shape[-1])
+
+
+def settled(pieces, taps):
+    m, count, outs, _ = pieces.shape
     return (
-        halves.astype(jnp.float32)
-        .reshape(count, outs, taps, -1)
-        .transpose(2, 0, 3, 1)
-        .reshape(taps, -1, outs)
+        pieces.astype(jnp.float32)
+        .reshape(m, count, outs, taps, -1)
+        .transpose(3, 1, 4, 0, 2)
+        .reshape(taps, -1, m * outs)
     )
 
 
@@ -167,18 +166,9 @@
     def peer(self, axis, step):
         return lax.rem(self.index(axis) + step, self.count(axis))
 
-    def turned(self, half):
-        ratio = 2 * self.chips // self.images
-        return (self.mp // ratio, ratio * self.dp + half)
-
-    def stays(self, half):
-        ratio = 2 * self.chips // self.images
-        return jnp.logical_and(self.dp == self.mp // ratio, self.mp % ratio == half)
-
     def barrier(self, axes, neighbours):
         bar = pltpu.get_barrier_semaphore()
-        turn = "turn" in axes and "all" not in axes
-        axes = ("all",) if "all" in axes else tuple(axis for axis in axes if axis != "turn")
+        axes = ("all",) if "all" in axes else axes
         steady = 0
         for axis in axes:
             for step in range(1, self.count(axis)):
@@ -199,22 +189,6 @@
 
             middle = jnp.logical_and(self.has_up, self.has_down)
             cases = [(steady + 3, middle), (steady + 2, jnp.logical_not(middle))]
-        if turn:
-            ratio = 2 * self.chips // self.images
-            for half in range(ratio):
-
-                @pl.when(jnp.logical_not(self.stays(half)))
-                def _():
-                    pl.semaphore_signal(
-                        bar, inc=1, device_id=self.turned(half), device_id_type=MESH
-                    )
-
-            same = self.dp == self.mp // ratio
-            cases = [
-                (count + ratio - less, here if when is None else jnp.logical_and(when, here))
-                for count, when in cases
-                for less, here in ((1, same), (0, jnp.logical_not(same)))
-            ]
         for count, when in cases:
             if when is None:
                 pl.semaphore_wait(bar, count)
@@ -281,7 +255,7 @@
         for copy in self.copies(line, src, dst, send, recv):
             copy.start()
 
-    def middle(self, line, src, dst, send, recv):
+    def middle(self, phase, *refs):
         pass
 
     def finish(self, line, src, dst, send, recv):
@@ -289,100 +263,69 @@
             copy.wait()
 
 
-class Turn:
-    def __init__(self, array):
-        self.axes = ("turn",)
+class Settle:
+    def __init__(self, array, summed):
+        self.axes = ("dp", "mp")
         self.array = array
+        self.summed = summed
 
     def result(self, sizes):
-        self.ratio = sizes["mp"] // sizes["dp"]
-        rows, columns = self.array.shape[-2:]
-        return jax.ShapeDtypeStruct((self.ratio, rows // self.ratio, columns), self.array.dtype)
+        n, m = sizes["mp"], sizes["dp"]
+        self.ratio = n // m
+        self.tail = tuple(self.array.shape[-2:])
+        self.total = jax.ShapeDtypeStruct((n,) + self.tail, self.array.dtype)
+        self.out = jax.ShapeDtypeStruct((m, self.ratio) + self.tail, self.array.dtype)
+        self.add = Rider("dp", self.array, None if self.summed else 1)
+        self.outward = Rider("mp", self.total, 0)
+        self.inward = Rider("dp", self.total, 0)
+        return self.out
 
     def scratch(self, sizes):
-        ratio = sizes["mp"] // sizes["dp"]
-        return [pltpu.SemaphoreType.DMA((ratio,)), pltpu.SemaphoreType.DMA((ratio,))]
-
-    def leave(self, line, src, dst, send, recv, half):
-        size = dst.shape[1]
-        piece = src.at[pl.ds(half * size, size)]
-        mine = line.mp % self.ratio
-        away = remote(piece, dst.at[mine], send.at[half], recv.at[mine], line.turned(half))
-        return away, pltpu.make_async_copy(piece, dst.at[half], send.at[half])
-
-    def start(self, line, src, dst, send, recv):
-        for half in range(self.ratio):
-            away, here = self.leave(line, src, dst, send, recv, half)
-
-            @pl.when(line.stays(half))
-            def _():
-                here.start()
-
-            @pl.when(jnp.logical_not(line.stays(half)))
-            def _():
-                away.start()
-
-    def middle(self, line, src, dst, send, recv):
-        pass
-
-    def finish(self, line, src, dst, send, recv):
-        for half in range(self.ratio):
-            away, here = self.leave(line, src, dst, send, recv, half)
-
-            @pl.when(line.stays(half))
-            def _():
-                here.wait()
-
-            @pl.when(jnp.logical_not(line.stays(half)))
-            def _():
-                away.wait_send()
-                remote(
-                    dst.at[half], dst.at[half], send.at[half], recv.at[half], line.turned(half)
-                ).wait_recv()
-
-
-class SumTurn:
-    def __init__(self, array):
-        self.axes = ("dp", "turn")
-        self.first = Rider("dp", array, 0)
-        self.second = Turn(array)
-        self.array = array
-
-    def result(self, sizes):
-        self.first.result(sizes)
-        return self.second.result(sizes)
-
-    def scratch(self, sizes):
-        shape = self.array.shape
-        return (
-            [
-                pltpu.VMEM((shape[0], 1) + shape[1:], self.array.dtype),
-                pltpu.VMEM(shape[1:], self.array.dtype),
-            ]
-            + self.first.scratch(sizes)
-            + self.second.scratch(sizes)
-        )
-
-    def start(self, line, src, dst, got, total, *sems):
-        self.first.start(line, src, got, *sems[:2])
-
-    def middle(self, line, src, dst, got, total, *sems):
-        self.first.finish(line, src, got, *sems[:2])
-        rows = total.shape[0]
-        tile = 32
-
-        @pl.loop(0, rows // tile)
-        def _(index):
-            where = pl.ds(pl.multiple_of(index * tile, tile), tile)
-            added_up = got[0, 0, where].astype(jnp.float32)
-            for image in range(1, got.shape[0]):
-                added_up += got[image, 0, where].astype(jnp.float32)
-            total[where] = added_up.astype(total.dtype)
-
-        self.second.start(line, total, dst, *sems[2:])
-
-    def finish(self, line, src, dst, got, total, *sems):
-        self.second.finish(line, total, dst, *sems[2:])
+        n, m = sizes["mp"], sizes["dp"]
+        dtype = self.array.dtype
+        refs = [pltpu.VMEM((n, 1) + self.tail, dtype)]
+        if not self.summed:
+            refs += [pltpu.VMEM((m, n, 1) + self.tail, dtype), pltpu.VMEM((n,) + self.tail, dtype)]
+            refs += self.add.scratch(sizes)
+        return refs + self.outward.scratch(sizes) + self.inward.scratch(sizes)
+
+    def copies(self, step, line, src, dst, stage, *rest):
+        if not self.summed:
+            got, total = rest[:2]
+            if step == 0:
+                return self.add.copies(line, src, got, *rest[2:4])
+            src, rest = total, rest[4:]
+            step -= 1
+        if step == 0:
+            return self.outward.copies(line, src, stage, *rest[:2])
+        return self.inward.copies(line, stage.at[:, 0], dst, *rest[2:4])
+
+    def start(self, *refs):
+        for copy in self.copies(0, *refs):
+            copy.start()
+
+    def middle(self, phase, line, src, dst, stage, *rest):
+        if phase > (0 if self.summed else 1):
+            return
+        refs = (line, src, dst, stage) + rest
+        for copy in self.copies(phase, *refs):
+            copy.wait()
+        if not self.summed and phase == 0:
+            got, total = rest[:2]
+
+            @pl.loop(0, total.shape[0])
+            def _(index):
+                added_up = got[0, index, 0].astype(jnp.float32)
+                for image in range(1, got.shape[0]):
+                    added_up += got[image, index, 0].astype(jnp.float32)
+                total[index] = added_up.astype(total.dtype)
+
+        for copy in self.copies(phase + 1, *refs):
+            copy.start()
+
+    def finish(self, *refs):
+        for copy in self.copies(1 if self.summed else 2, *refs):
+            copy.wait()
 
 
 def comm_call(kernel, inputs, out_shapes, scratch, riders, n, m, number, neighbours=True):
@@ -408,8 +351,9 @@
         for rider, refs_in in riding:
             rider.start(*refs_in)
         kernel(line, *main_in, *main_out, *main_scratch)
-        for rider, refs_in in riding:
-            rider.middle(*refs_in)
+        for phase in range(2):
+            for rider, refs_in in riding:
+                rider.middle(phase, *refs_in)
         for rider, refs_in in riding:
             rider.finish(*refs_in)
 
@@ -878,10 +822,26 @@
     )
 
 
-def tokens_gather_kernel(turned, shape_out, outs, line, x_ref, w_ref, *refs):
+def add_outer(total, left, right, rows):
+    cut = min(left.shape[1], 512)
+    for start in range(0, left.shape[1], cut):
+        total[pl.ds(start, cut)] += lax.dot_general(
+            left[rows, pl.ds(start, cut)],
+            right[rows],
+            (((0,), (0,)), ((), ())),
+            preferred_element_type=jnp.float32,
+        )
+
+
+def tokens_gather_kernel(turned, shape_out, outs, side, line, x_ref, w_ref, *refs):
+    if side:
+        left, refs = refs[0], refs[1:]
     held = refs[0]
     results = refs[1 : 1 + outs]
-    send, recv = refs[1 + outs :]
+    refs = refs[1 + outs :]
+    if side:
+        grad, total, refs = refs[0], refs[1], refs[2:]
+    send, recv = refs
     tokens = x_ref.shape[0]
     across = w_ref.shape[1 if turned else 2]
     cut = min(across, 512)
@@ -897,19 +857,30 @@
                 values = shape_out(product(held[rows], w, turned))
                 for ref, value in zip(results, values):
                     ref[rows, pl.ds(j * across + start, cut)] = value.astype(ref.dtype)
-
-    line_gather(line, x_ref, slot, send, recv, lambda: None, on_pair)
-
-
-def tokens_gather(x, w, turned, kinds, shape_out, n, m, number, riders=()):
+        if side:
+            add_outer(total, held, left, rows)
+
+    def on_own():
+        if side:
+            total[...] = jnp.zeros_like(total)
+
+    line_gather(line, x_ref, slot, send, recv, on_own, on_pair)
+    if side:
+        grad[...] = total[...].astype(grad.dtype)
+
+
+def tokens_gather(x, w, turned, kinds, shape_out, n, m, number, riders=(), left=None):
     tokens, width = x.shape
     across = w.shape[0] * w.shape[1 if turned else 2]
+    side = left is not None
+    grads = ((width, left.shape[1]),) if side else ()
     return comm_call(
-        partial(tokens_gather_kernel, turned, shape_out, len(kinds)),
-        (x, w),
+        partial(tokens_gather_kernel, turned, shape_out, len(kinds), side),
+        (x, w) + ((left,) if side else ()),
         (jax.ShapeDtypeStruct((tokens * n, width), x.dtype),)
-        + tuple(jax.ShapeDtypeStruct((tokens * n, across), kind) for kind in kinds),
-        gather_sems(n // 2),
+        + tuple(jax.ShapeDtypeStruct((tokens * n, across), kind) for kind in kinds)
+        + tuple(jax.ShapeDtypeStruct(shape, jnp.bfloat16) for shape in grads),
+        [pltpu.VMEM(shape, jnp.float32) for shape in grads] + gather_sems(n // 2),
         riders,
         n,
         m,
@@ -978,7 +949,21 @@
 
 
 def attend_gather_kernel(
-    line, g_ref, w_ref, x_ref, kt_ref, valid_ref, held, grad_ref, keys_sum, values_sum, send, recv
+    line,
+    g_ref,
+    w_ref,
+    x_ref,
+    kt_ref,
+    valid_ref,
+    mixed_ref,
+    held,
+    grad_ref,
+    out_ref,
+    keys_sum,
+    values_sum,
+    out_sum,
+    send,
+    recv,
 ):
     tokens = g_ref.shape[0]
     wide = w_ref.shape[0]
@@ -991,6 +976,7 @@
     def on_own():
         keys_sum[...] = jnp.zeros_like(keys_sum)
         values_sum[...] = jnp.zeros_like(values_sum)
+        out_sum[...] = jnp.zeros_like(out_sum)
 
     def on_pair(chip):
         rows = pl.ds(pl.multiple_of(chip * 2 * tokens, 2 * tokens), 2 * tokens)
@@ -1011,13 +997,15 @@
             grad_ref[rows, where[0]] = product(kt_ref[place], grad_scores, False).T.astype(
                 jnp.bfloat16
             )
+        add_outer(out_sum, mixed_ref, held, rows)
 
     line_gather(line, g_ref, slot, send, recv, on_own, on_pair)
     grad_ref[:, pl.ds(wide, wide)] = keys_sum[...].astype(jnp.bfloat16)
     grad_ref[:, pl.ds(2 * wide, wide)] = values_sum[...].astype(jnp.bfloat16)
-
-
-def attend_gather(grad_mid, out_weight, qkv_rows, valid, n, m, number, riders):
+    out_ref[...] = out_sum[...].astype(jnp.bfloat16)
+
+
+def attend_gather(grad_mid, out_weight, qkv_rows, valid, mixed_low, n, m, number, riders):
     tokens, width = grad_mid.shape
     total = tokens * n
     wide = out_weight.shape[0]
@@ -1029,12 +1017,18 @@
             qkv_rows,
             qkv_rows[:, wide : 2 * wide].T,
             jnp.broadcast_to(valid[:, None], (total, 128)),
+            mixed_low,
         ),
         (
             jax.ShapeDtypeStruct((total, width), jnp.bfloat16),
             jax.ShapeDtypeStruct((total, 3 * wide), jnp.bfloat16),
+            jax.ShapeDtypeStruct((wide, width), jnp.bfloat16),
         ),
-        [pltpu.VMEM((total, wide), jnp.float32), pltpu.VMEM((total, wide), jnp.float32)]
+        [
+            pltpu.VMEM((total, wide), jnp.float32),
+            pltpu.VMEM((total, wide), jnp.float32),
+            pltpu.VMEM((wide, width), jnp.float32),
+        ]
         + gather_sems(n // 2),
         riders,
         n,
@@ -1178,19 +1172,19 @@
         grad_normed_mlp, normed_mlp, inverse_mlp, scale_mlp
     )
     grad_mid = grad_final + grad_mid_norm
-    all_mid, grad_qkv, sums_up = attend_gather(
+    all_mid, grad_qkv, grad_out, sums_up = attend_gather(
         grad_mid.astype(jnp.bfloat16),
         out_weight,
         qkv_rows,
         valid,
+        mixed_low,
         n,
         m,
         7,
         (Rider("dp", grad_up.astype(jnp.bfloat16), 0),),
     )
-    grad_out = jnp.einsum("lh,le->he", mixed_low, all_mid, preferred_element_type=jnp.float32)
     grad_normed_attend, sums_out = tokens_scatter(
-        grad_qkv, qkv_weight, True, n, m, 8, (Rider("dp", grad_out.astype(jnp.bfloat16), 1),)
+        grad_qkv, qkv_weight, True, n, m, 8, (Rider("dp", grad_out, 1),)
     )
     grad_qkv_weight = jnp.einsum(
         "le,lf->ef", all_attend, grad_qkv, preferred_element_type=jnp.float32
@@ -1207,7 +1201,7 @@
             ).reshape(n, -1)
         ]
     )
-    all_stream, grad_tap_patch, sums_qkv, ada_columns = tokens_gather(
+    all_stream, grad_tap_patch, grad_down, sums_qkv, ada_columns = tokens_gather(
         grad_stream.astype(jnp.bfloat16),
         down_matrix[None],
         True,
@@ -1220,9 +1214,7 @@
             Rider("dp", grad_qkv_weight.astype(jnp.bfloat16), 0),
             Rider("mp", grad_modulation, 0),
         ),
-    )
-    grad_down = jnp.einsum(
-        "le,lk->ek", all_stream, down_patch, preferred_element_type=jnp.float32
+        down_patch,
     )
     ada_columns = added(ada_columns).reshape(-1)[: columns.shape[0]]
     grad_residual = (
@@ -1237,7 +1229,8 @@
             )
             return join_columns(acc, canvas_cols), parts, ridden
         grad_hidden, grad_kernel = conv_backward(grad_low, hidden, kernel, n)
-        return grad_hidden, by_images(grad_kernel, m), exchange(riders, n, m, number)
+        parts = grad_kernel.astype(jnp.bfloat16).reshape(9 * own, -1).T
+        return grad_hidden, parts, exchange(riders, n, m, number)
 
     grad_hidden_second, parts_second, (sums_down, every_small) = back(
         grad_residual.astype(jnp.bfloat16),
@@ -1246,7 +1239,7 @@
         conv_second,
         10,
         (
-            Rider("dp", grad_down.astype(jnp.bfloat16), 0),
+            Rider("dp", unsettled(grad_down, m, n), 1),
             Rider("dp", jnp.concatenate([tiled_up(embedding[0]), tiled_up(ada_columns)])),
         ),
     )
@@ -1254,16 +1247,16 @@
         grad_hidden_second, normed_second, inverse_second, own_second, size
     )
     grad_shift = jnp.sum(grad_conv_output, axis=0)
-    grad_hidden_first, parts_first, (sums_second, every_shift, turned_down) = back(
+    grad_hidden_first, parts_first, (sums_second, every_shift, pieces_down) = back(
         grad_conv_output.astype(jnp.bfloat16),
         hidden_first,
         spread_first,
         conv_first,
         11,
         (
-            Rider("dp", parts_second, 0),
+            Rider("dp", unsettled(parts_second, m, n), 1),
             Rider("dp", tiled_up(grad_shift)),
-            Turn(added(sums_down).astype(jnp.bfloat16)),
+            Settle(added(sums_down)[:, 0].astype(jnp.bfloat16), True),
         ),
     )
     grad_base, grad_gain_first = group_backward(
@@ -1277,17 +1270,17 @@
         [tiled_up(embed_term[0]), tiled_up(jnp.concatenate([grad_gain_first, grad_gain_second]))]
     )
     riders = (
-        SumTurn(parts_first),
+        Settle(unsettled(parts_first, m, n), False),
         Rider("all", small),
-        Turn(added(sums_second)[0].astype(jnp.bfloat16)),
+        Settle(added(sums_second)[:, 0].astype(jnp.bfloat16), True),
     )
     if fused:
-        turned_first, small, turned_second, image_turned = exchange(
+        pieces_first, small, pieces_second, image_turned = exchange(
             riders + (Rider("mp", image_turned, 0, True),), n, m, 13
         )
         image_grad = image_turned.reshape(image.shape)
     else:
-        turned_first, small, turned_second = exchange(riders, n, m, 13)
+        pieces_first, small, pieces_second = exchange(riders, n, m, 13)
         image_grad = lax.all_to_all(
             image_turned.reshape(rows_all, canvas_cols, own), "mp", 0, 2, tiled=True
         )[None]
@@ -1322,11 +1315,11 @@
         image_grad,
         embedding_grad,
         gains[0],
-        unturned(turned_first, 9),
+        settled(pieces_first, 9),
         gains[1],
-        unturned(turned_second, 9),
+        settled(pieces_second, 9),
         grad_shift_weight,
-        unturned(turned_down, 4),
+        settled(pieces_down, 4),
         grad_ada_weight,
         qkv_grad,
         added(sums_out),

time: 1120 us -> 1080 us (0.964)
  Pallas kernels: 917 us -> 871 us
  local copies, waits for them, and re-layouts: 44.9 us -> 57.4 us
    pallas_call x14, Pallas kernels: 917 us -> 871 us  [comm_call(): pl.pallas_call(body, out_shape=tuple(out_shapes) + ride_shapes, in_specs=...]
  transfers between devices with their start and end apart: 2 -> 2, of which waited for: 0 -> 0; matrix products, arithmetic and copies ran while one was open for 4% -> 5% of each run, Pallas kernels for 17% -> 18%
where the time goes in v5:
time: 1080 us; the launch traced here: 1070 us
  Pallas kernels  871 us (81%)
  other arithmetic  78.8 us (7%)
  local copies, waits for them, and re-layouts  57.4 us (5%)
  matrix products  48.7 us (5%)
  between operations  15 us (1%)
    pallas_call x14, Pallas kernels, comm_call(): pl.pallas_call(body, out_shape=tuple(out_shapes) + ride_shapes, in_specs=...  871 us
  transfers between devices with their start and end apart: 2, of which 0 were waited for; matrix products, arithmetic and copies ran while one was open for 5% of the time, Pallas kernels for 18%

profile of v5, /device:TPU:9, one launch (start us, length us, event | category | flops | bytes accessed | tf_op | source)
XLA Modules:
  0.0 1070.9 jit_solution(7388895030280253037)
XLA Ops:
  11.7 27.8 %shard_map.254 = (f32[8,8,128]{2,1,0:T(8,128)}, bf16[8,512,128]{2,1,0:T(8,128)(2,1)}) custom-call(f32[8,128]{1,0:T(8,128)} %bitcast.229, bf16[512,1024]{1,0:T(8,128)(2,1)} %bitcast.220), custom_call_target="tpu_custom_call" | custom-call | tf_op jit(solution)/shard_map/pallas_call | solution.py:360
  47.6 2.3 pad_maximum_fusion
  49.9 77.4 %shard_map.255 = f32[4096,128]{1,0:T(8,128)} custom-call(bf16[4352,384]{1,0:T(8,128)(2,1)} %bitcast.189, bf16[3,384,1024]{2,1,0:T(8,128)(2,1)} %bitcast.200), custom_call_target="tpu_custom_call" | custom-call | tf_op jit(solution)/shard_map/pallas_call | solution.py:360
  127.2 2.1 add_reduce_fusion
  129.8 2.1 multiply_reduce_fusion.2
  132.3 2.3 multiply_convert_fusion
  135.5 2.4 pad_maximum_fusion.1
  137.8 78.3 %shard_map.256 = f32[4096,128]{1,0:T(8,128)} custom-call(bf16[4352,384]{1,0:T(8,128)(2,1)} %bitcast.191, bf16[3,384,1024]{2,1,0:T(8,128)(2,1)} %bitcast.198), custom_call_target="tpu_custom_call" | custom-call | tf_op jit(solution)/shard_map/pallas_call | solution.py:360
  219.9 41.9 %shard_map.257 = f32[128,2048]{1,0:T(8,128)} custom-call(bf16[1024,512]{1,0:T(8,128)(2,1)} %reshape.579.refs_0_.refs_2_, bf16[1,512,2048]{2,1,0:T(8,128)(2,1)} %bitcast.202), custom_call_target="tpu_custom_call" | custom-call | tf_op jit(solution)/shard_map/pallas_call | solution.py:360
  265.8 40.1 %shard_map.258 = (bf16[1024,2048]{1,0:T(8,128)(2,1)}, bf16[1024,768]{1,0:T(8,128)(2,1)}) custom-call(bf16[128,2048]{1,0:T(8,128)(2,1)} %add_convert_fusion.3.refs_0_, bf16[3,2048,256]{2,1,0:T(8,128)(2,1)} %refs_1_.5), custom_call_target="tpu_custom_call" | custom-call | tf_op jit(solution)/shard_map/pallas_call | solution.py:360
  308.5 81.9 %shard_map.259 = (f32[128,2048]{1,0:T(8,128)}, bf16[1024,256]{1,0:T(8,128)(2,1)}) custom-call(bf16[1024,768]{1,0:T(8,128)(2,1)} %get-tuple-element.50.refs_0_.refs_2_, f32[8,1024]{1,0:T(8,128)} %broadcast_in_dim.28.refs_1_, bf16[256,2048]{1,0:T(8,128)(2,1)} %refs_1_.4), custom_call_target="tpu_custom_call" | custom-call | tf_op jit(solution)/shard_map/pallas_call | solution.py:360
  393.9 42.6 %shard_map.260 = (bf16[1024,2048]{1,0:T(8,128)(2,1)}, f32[1024,1024]{1,0:T(8,128)}, bf16[1024,1024]{1,0:T(8,128)(2,1)}) custom-call(bf16[128,2048]{1,0:T(8,128)(2,1)} %add_convert_fusion.2.refs_0_, bf16[1,2048,1024]{2,1,0:T(8,128)(2,1)} %bitcast.196), custom_call_target="tpu_custom_call" | custom-call | tf_op jit(solution)/shard_map/pallas_call | solution.py:360
  436.5 9.3 convolution_convert_fusion.2
  446.5 2.6 copy.36
  450.9 9.5 convolution_convert_fusion.1.refs_2_
  460.4 7.9 fusion.6.refs_0_
  468.4 65.3 %shard_map.261 = (f32[128,2048]{1,0:T(8,128)}, bf16[4,1024,512]{2,1,0:T(8,128)(2,1)}) custom-call(bf16[1024,1024]{1,0:T(8,128)(2,1)} %fusion.6.refs_0_, bf16[1,2048,1024]{2,1,0:T(8,128)(2,1)} %bitcast.197, bf16[1024,2048]{1,0:T(8,128)(2,1)} %convolution_convert_fusion.1.refs_2_), custom_call_target="tpu_custom_call" | custom-call | tf_op jit(solution)/shard_map/pallas_call | solution.py:360
  535.6 4.5 convert_reduce_fusion
  540.2 6.3 convolution_convert_fusion.refs_6_
  546.4 3.8 fusion.52
  551.2 54.9 %shard_map.262 = (bf16[1024,2048]{1,0:T(8,128)(2,1)}, bf16[1024,768]{1,0:T(8,128)(2,1)}, bf16[256,2048]{1,0:T(8,128)(2,1)}, bf16[4,512,1024]{2,1,0:T(8,128)(2,1)}) custom-call(bf16[128,2048]{1,0:T(8,128)(2,1)} %get-tuple-element.113.refs_0_, bf16[256,2048]{1,0:T(8,128)(2,1)} %refs_1_.4, bf16[1024,768]{1,0:T(8,128)(2,1)} %get-tuple-element.50.refs_0_.refs_2_, ...), custom_call_target="tpu_custom_call" | custom-call | tf_op jit(solution)/shard_map/pallas_call | solution.py:360
  606.1 7.9 convolution_convert_fusion.3.refs_3_
  613.9 43.2 %shard_map.263 = (f32[128,2048]{1,0:T(8,128)}, bf16[4,256,512]{2,1,0:T(8,128)(2,1)}) custom-call(bf16[1024,768]{1,0:T(8,128)(2,1)} %get-tuple-element.58.refs_0_, bf16[3,2048,256]{2,1,0:T(8,128)(2,1)} %refs_1_.5, bf16[256,2048]{1,0:T(8,128)(2,1)} %get-tuple-element.59.refs_2_), custom_call_target="tpu_custom_call" | custom-call | tf_op jit(solution)/shard_map/pallas_call | solution.py:360
  660.4 44.1 %shard_map.264 = (bf16[1024,2048]{1,0:T(8,128)(2,1)}, f32[1024,512]{1,0:T(8,128)}, bf16[2048,512]{1,0:T(8,128)(2,1)}, bf16[4,512,768]{2,1,0:T(8,128)(2,1)}, f32[8,8,128]{2,1,0:T(8,128)}) custom-call(bf16[128,2048]{1,0:T(8,128)(2,1)} %add_convert_fusion.refs_0_, bf16[1,512,2048]{2,1,0:T(8,128)(2,1)} %bitcast.203, bf16[1024,512]{1,0:T(8,128)(2,1)} %reshape.579.refs_0_.refs_2_, ...), custom_call_target="tpu_custom_call" | custom-call | tf_op jit(solution)/shard_map/pallas_call | solution.py:360
  704.6 3.5 reshape.581
  708.1 3.9 copy.37
  712.0 2.7 convert_element_type.127.refs_0_
  715.2 85.5 %shard_map.265 = (f32[4096,384]{1,0:T(8,128)}, bf16[4,256,1152]{2,1,0:T(8,128)(2,1)}, bf16[4,8,1,64,512]{4,3,2,1,0:T(8,128)(2,1)}, f32[4,16,128]{2,1,0:T(8,128)}) custom-call(bf16[4096,128]{1,0:T(8,128)(2,1)} %convert_element_type.127.refs_0_, bf16[3,384,1024]{2,1,0:T(8,128)(2,1)} %bitcast.199, bf16[4352,384]{1,0:T(8,128)(2,1)} %bitcast.192, ...), custom_call_target="tpu_custom_call" | custom-call | tf_op jit(solution)/shard_map/pallas_call | solution.py:360
  800.8 2.7 fusion.55
  803.5 2.4 fusion.11
  806.0 2.4 fusion.49
  809.9 4.0 fusion.22
  815.8 2.3 convert_reduce_fusion.1
  821.4 2.9 reduce_sum.392.refs_5_
  824.3 105.4 %shard_map.266 = (f32[4096,384]{1,0:T(8,128)}, bf16[4,256,1152]{2,1,0:T(8,128)(2,1)}, bf16[4,8,1,32,1152]{4,3,2,1,0:T(8,128)(2,1)}, f32[4,8,128]{2,1,0:T(8,128)}, bf16[4,2,64,512]{3,2,1,0:T(8,128)(2,1)}) custom-call(bf16[4096,128]{1,0:T(8,128)(2,1)} %get-tuple-element.124.refs_0_, bf16[3,384,1024]{2,1,0:T(8,128)(2,1)} %bitcast.201, ...), custom_call_target="tpu_custom_call" | custom-call | tf_op jit(solution)/shard_map/pallas_call | solution.py:360
  930.4 2.0 fusion.24
  933.5 3.0 reduce_sum.394.refs_2_
  939.6 2.1 reshape.619
  943.0 2.9 fusion.54
  945.9 4.4 fusion.48
  952.4 4.6 fusion.18.refs_3_
  957.0 82.4 %shard_map.267 = (bf16[4,2,32,1152]{3,2,1,0:T(8,128)(2,1)}, f32[32,16,128]{2,1,0:T(8,128)}, bf16[4,2,32,1152]{3,2,1,0:T(8,128)(2,1)}, bf16[512,1024]{1,0:T(8,128)(2,1)}) custom-call(bf16[8,4,32,1152]{3,2,1,0:T(8,128)(2,1)} %bitcast.213, f32[16,128]{1,0:T(8,128)} %pad_maximum_fusion.4.refs_1_, bf16[8,32,1152]{2,1,0:T(8,128)(2,1)} %reduce_sum.394.refs_2_, ...), custom_call_target="tpu_custom_call" | custom-call | tf_op jit(solution)/shard_map/pallas_call | solution.py:360
  1041.7 2.5 reshape.624
  1044.2 2.5 copy.38
  1048.7 2.7 copy.41
  1053.0 2.5 copy.39
  1057.5 2.7 copy.42
  1060.2 2.4 pad_maximum_fusion.2
  (173 shorter events, 61.0 us)
Async XLA Ops:
  7.2 2.8 copy-start
  7.2 443.7 %all-gather.2.cloned.1.call-start = ((), (), s32[]{:S(2)}) async-start(), calls=%async_computation.2 | async-start | bytes 4718592 | tf_op jit(solution)/shard_map/all_gather | solution.py:62
  39.5 5.2 copy-start.4
  261.8 3.0 copy-start.2
  265.8 40.2 %copy-start.22 = (s32[1,2]{1,0:T(1,128)S(1)}, s32[1,2]{1,0:T(1,128)}, u32[]{:S(2)}) copy-start(s32[1,2]{1,0:T(1,128)} %param.17) | copy-start | bytes 28
  306.0 240.5 %reduce-scatter.2.cloned.1.call-start = ((), (), s32[]{:S(2)}) async-start(), calls=%async_computation.1 | async-start | bytes 4718592 | tf_op jit(solution)/shard_map/reduce_scatter | solution.py:66
  391.9 1.0 copy-start.3
  445.8 0.7 copy-start.19
  450.9 9.5 copy-start.23
  450.9 9.5 copy-start.24
  450.9 9.5 copy-start.26
  535.6 4.6 copy-start.11
  535.6 4.5 copy-start.25
  657.2 1.9 copy-start.7
  657.2 1.9 copy-start.8
  659.1 1.3 copy-start.18
  708.1 3.9 copy-start.20
  803.5 2.5 copy-start.1
  806.0 8.0 copy-start.16
  809.9 5.0 copy-start.14
  809.9 5.9 copy-start.9
  815.8 4.0 copy-start.10
  819.8 1.6 copy-start.21
  943.0 2.9 copy-start.6
  945.9 6.5 copy-start.5
  1048.7 2.7 copy-start.17
  1057.5 2.7 copy-start.12
  1057.5 2.8 copy-start.13
  1060.2 2.4 copy-start.15
Sparse Core Ops, SparseCore 0:
  306.1 83.4 all-gather.1
  445.9 55.5 reduce-scatter.1

commit v6 on v5

--- a/solution.py
+++ b/solution.py
@@ -101,6 +101,8 @@
 
 
 def settled(pieces, taps):
+    if pieces.ndim == 3:
+        return pieces
     m, count, outs, _ = pieces.shape
     return (
         pieces.astype(jnp.float32)
@@ -264,32 +266,37 @@
 
 
 class Settle:
-    def __init__(self, array, summed):
+    def __init__(self, array, summed, taps, placed):
         self.axes = ("dp", "mp")
         self.array = array
         self.summed = summed
+        self.taps = taps
+        self.placed = placed
 
     def result(self, sizes):
         n, m = sizes["mp"], sizes["dp"]
         self.ratio = n // m
         self.tail = tuple(self.array.shape[-2:])
         self.total = jax.ShapeDtypeStruct((n,) + self.tail, self.array.dtype)
-        self.out = jax.ShapeDtypeStruct((m, self.ratio) + self.tail, self.array.dtype)
+        self.land = (m, self.ratio) + self.tail
         self.add = Rider("dp", self.array, None if self.summed else 1)
         self.outward = Rider("mp", self.total, 0)
         self.inward = Rider("dp", self.total, 0)
-        return self.out
+        if not self.placed:
+            return jax.ShapeDtypeStruct(self.land, self.array.dtype)
+        shape = (self.taps, self.ratio * self.tail[1] // self.taps, m * self.tail[0])
+        return jax.ShapeDtypeStruct(shape, jnp.float32)
 
     def scratch(self, sizes):
         n, m = sizes["mp"], sizes["dp"]
         dtype = self.array.dtype
-        refs = [pltpu.VMEM((n, 1) + self.tail, dtype)]
+        refs = [pltpu.VMEM(self.land, dtype), pltpu.VMEM((n, 1) + self.tail, dtype)]
         if not self.summed:
             refs += [pltpu.VMEM((m, n, 1) + self.tail, dtype), pltpu.VMEM((n,) + self.tail, dtype)]
             refs += self.add.scratch(sizes)
         return refs + self.outward.scratch(sizes) + self.inward.scratch(sizes)
 
-    def copies(self, step, line, src, dst, stage, *rest):
+    def copies(self, step, line, src, dst, land, stage, *rest):
         if not self.summed:
             got, total = rest[:2]
             if step == 0:
@@ -298,20 +305,20 @@
             step -= 1
         if step == 0:
             return self.outward.copies(line, src, stage, *rest[:2])
-        return self.inward.copies(line, stage.at[:, 0], dst, *rest[2:4])
+        return self.inward.copies(line, stage.at[:, 0], land, *rest[2:4])
 
     def start(self, *refs):
         for copy in self.copies(0, *refs):
             copy.start()
 
-    def middle(self, phase, line, src, dst, stage, *rest):
-        if phase > (0 if self.summed else 1):
+    def middle(self, phase, *refs):
+        if self.summed and phase == 1:
+            self.end(*refs)
             return
-        refs = (line, src, dst, stage) + rest
         for copy in self.copies(phase, *refs):
             copy.wait()
         if not self.summed and phase == 0:
-            got, total = rest[:2]
+            got, total = refs[5:7]
 
             @pl.loop(0, total.shape[0])
             def _(index):
@@ -324,8 +331,27 @@
             copy.start()
 
     def finish(self, *refs):
+        if not self.summed:
+            self.end(*refs)
+
+    def end(self, *refs):
         for copy in self.copies(1 if self.summed else 2, *refs):
             copy.wait()
+        dst, land = refs[2:4]
+        if not self.placed:
+            dst[...] = land[...]
+            return
+        own = self.tail[1] // self.taps
+        for half in range(self.ratio):
+            for tap in range(self.taps):
+                block = jnp.concatenate(
+                    [
+                        land[image, half, :, pl.ds(tap * own, own)].astype(jnp.float32)
+                        for image in range(land.shape[0])
+                    ],
+                    axis=0,
+                )
+                dst[tap, pl.ds(half * own, own)] = block.T
 
 
 def comm_call(kernel, inputs, out_shapes, scratch, riders, n, m, number, neighbours=True):
@@ -361,7 +387,10 @@
         body,
         out_shape=tuple(out_shapes) + ride_shapes,
         in_specs=whole(ni) + [any_spec] * nr,
-        out_specs=tuple(whole(no) + [any_spec] * nr),
+        out_specs=tuple(
+            whole(no)
+            + [whole(1)[0] if isinstance(rider, Settle) else any_spec for rider in riders]
+        ),
         scratch_shapes=list(scratch) + [ref for needs in ride_scratch for ref in needs],
         compiler_params=comm_params(number),
     )(*inputs, *[rider.array for rider in riders])
@@ -488,7 +517,7 @@
     ]
 
 
-def line_scatter(line, scratch, parts, produce, finish, tile):
+def line_scatter(line, scratch, parts, produce, finish, tile, side=()):
     chips = line.chips
     z = line.z
     kept, out_ref, in_ref, moving, sems = scratch
@@ -606,10 +635,15 @@
         run(active, body)
 
     lag = 2
+    side = list(side)
     for index, item in enumerate(items):
         start(item)
         if index >= lag:
             close(items[index - lag])
+            if index % 2 == 0 and side:
+                side.pop(0)()
+    for step in side:
+        step()
     for item in items[-lag:]:
         close(item)
     for way, chip, part, active in items:
@@ -784,7 +818,25 @@
     )
 
 
-def tokens_scatter_kernel(turned, line, x_ref, w_ref, o_ref, *scratch):
+def outer_steps(grad, left, right, cut):
+    def step(start):
+        grad[pl.ds(start, cut)] = lax.dot_general(
+            left[:, pl.ds(start, cut)],
+            right[...],
+            (((0,), (0,)), ((), ())),
+            preferred_element_type=jnp.float32,
+        ).astype(grad.dtype)
+
+    return [partial(step, start) for start in range(0, left.shape[1], cut)]
+
+
+def tokens_scatter_kernel(turned, beside, line, x_ref, w_ref, *refs):
+    side = ()
+    if beside:
+        left, right, o_ref, grad, *scratch = refs
+        side = outer_steps(grad, left, right, 128)
+    else:
+        o_ref, *scratch = refs
     tokens, width = o_ref.shape
     cut = width // TOKEN_PARTS
     depth = x_ref.shape[1] // w_ref.shape[0]
@@ -804,16 +856,22 @@
     def finish(part, rows, total):
         o_ref[:, pl.ds(part * cut, cut)] = total
 
-    line_scatter(line, scratch, TOKEN_PARTS, produce, finish, tokens)
-
-
-def tokens_scatter(x, w, turned, n, m, number, riders=()):
+    line_scatter(line, scratch, TOKEN_PARTS, produce, finish, tokens, side)
+
+
+def outer_shapes(outer):
+    if not outer:
+        return ()
+    return (jax.ShapeDtypeStruct((outer[0].shape[1], outer[1].shape[1]), jnp.bfloat16),)
+
+
+def tokens_scatter(x, w, turned, n, m, number, riders=(), outer=()):
     tokens = x.shape[0] // n
     width = w.shape[1] if turned else w.shape[2]
     return comm_call(
-        partial(tokens_scatter_kernel, turned),
-        (x, w),
-        (jax.ShapeDtypeStruct((tokens, width), jnp.float32),),
+        partial(tokens_scatter_kernel, turned, len(outer) > 0),
+        (x, w) + tuple(outer),
+        (jax.ShapeDtypeStruct((tokens, width), jnp.float32),) + outer_shapes(outer),
         scatter_scratch(n // 2, TOKEN_PARTS * tokens, width // TOKEN_PARTS, TOKEN_PARTS),
         riders,
         n,
@@ -833,14 +891,15 @@
         )
 
 
-def tokens_gather_kernel(turned, shape_out, outs, side, line, x_ref, w_ref, *refs):
-    if side:
-        left, refs = refs[0], refs[1:]
-    held = refs[0]
-    results = refs[1 : 1 + outs]
-    refs = refs[1 + outs :]
-    if side:
-        grad, total, refs = refs[0], refs[1], refs[2:]
+def tokens_gather_kernel(turned, shape_out, outs, side, beside, cols, line, x_ref, w_ref, *refs):
+    refs = list(refs)
+    left = refs.pop(0) if side else None
+    outer = (refs.pop(0), refs.pop(0)) if beside else None
+    held = refs.pop(0)
+    results = [refs.pop(0) for _ in range(outs)]
+    grad = refs.pop(0) if side else None
+    outer_grad = refs.pop(0) if beside else None
+    total = refs.pop(0) if side else None
     send, recv = refs
     tokens = x_ref.shape[0]
     across = w_ref.shape[1 if turned else 2]
@@ -848,6 +907,16 @@
 
     def slot(block):
         return held.at[pl.ds(pl.multiple_of(block * tokens, tokens), tokens)]
+
+    def store_pixels(ref, chip, value):
+        depth = value.shape[1] // 4
+        base = chip * 8 * tokens
+        for row in range(4 * tokens // cols):
+            for tap in range(4):
+                start = base + (2 * row + tap // 2) * cols + tap % 2
+                ref[pl.Slice(start, cols // 2, 2)] = value[
+                    row * (cols // 2) : (row + 1) * (cols // 2), tap * depth : (tap + 1) * depth
+                ]
 
     def on_pair(chip):
         rows = pl.ds(pl.multiple_of(chip * 2 * tokens, 2 * tokens), 2 * tokens)
@@ -856,31 +925,43 @@
                 w = w_ref[j, pl.ds(start, cut)] if turned else w_ref[j, :, pl.ds(start, cut)]
                 values = shape_out(product(held[rows], w, turned))
                 for ref, value in zip(results, values):
-                    ref[rows, pl.ds(j * across + start, cut)] = value.astype(ref.dtype)
+                    if cols:
+                        store_pixels(ref, chip, value)
+                    else:
+                        ref[rows, pl.ds(j * across + start, cut)] = value.astype(ref.dtype)
         if side:
             add_outer(total, held, left, rows)
 
     def on_own():
         if side:
             total[...] = jnp.zeros_like(total)
+        if beside:
+            for step in outer_steps(outer_grad, *outer, 256):
+                step()
 
     line_gather(line, x_ref, slot, send, recv, on_own, on_pair)
     if side:
         grad[...] = total[...].astype(grad.dtype)
 
 
-def tokens_gather(x, w, turned, kinds, shape_out, n, m, number, riders=(), left=None):
+def tokens_gather(
+    x, w, turned, kinds, shape_out, n, m, number, riders=(), left=None, outer=(), cols=0
+):
     tokens, width = x.shape
     across = w.shape[0] * w.shape[1 if turned else 2]
     side = left is not None
     grads = ((width, left.shape[1]),) if side else ()
+    shape = (tokens * n * 4, across // 4) if cols else (tokens * n, across)
     return comm_call(
-        partial(tokens_gather_kernel, turned, shape_out, len(kinds), side),
-        (x, w) + ((left,) if side else ()),
+        partial(
+            tokens_gather_kernel, turned, shape_out, len(kinds), side, len(outer) > 0, cols
+        ),
+        (x, w) + ((left,) if side else ()) + tuple(outer),
         (jax.ShapeDtypeStruct((tokens * n, width), x.dtype),)
-        + tuple(jax.ShapeDtypeStruct((tokens * n, across), kind) for kind in kinds)
-        + tuple(jax.ShapeDtypeStruct(shape, jnp.bfloat16) for shape in grads),
-        [pltpu.VMEM(shape, jnp.float32) for shape in grads] + gather_sems(n // 2),
+        + tuple(jax.ShapeDtypeStruct(shape, kind) for kind in kinds)
+        + tuple(jax.ShapeDtypeStruct(grad, jnp.bfloat16) for grad in grads)
+        + outer_shapes(outer),
+        [pltpu.VMEM(grad, jnp.float32) for grad in grads] + gather_sems(n // 2),
         riders,
         n,
         m,
@@ -956,9 +1037,12 @@
     kt_ref,
     valid_ref,
     mixed_ref,
+    left,
+    right,
     held,
     grad_ref,
     out_ref,
+    outer_grad,
     keys_sum,
     values_sum,
     out_sum,
@@ -977,6 +1061,8 @@
         keys_sum[...] = jnp.zeros_like(keys_sum)
         values_sum[...] = jnp.zeros_like(values_sum)
         out_sum[...] = jnp.zeros_like(out_sum)
+        for step in outer_steps(outer_grad, left, right, 256):
+            step()
 
     def on_pair(chip):
         rows = pl.ds(pl.multiple_of(chip * 2 * tokens, 2 * tokens), 2 * tokens)
@@ -1005,7 +1091,7 @@
     out_ref[...] = out_sum[...].astype(jnp.bfloat16)
 
 
-def attend_gather(grad_mid, out_weight, qkv_rows, valid, mixed_low, n, m, number, riders):
+def attend_gather(grad_mid, out_weight, qkv_rows, valid, mixed_low, outer, n, m, number, riders):
     tokens, width = grad_mid.shape
     total = tokens * n
     wide = out_weight.shape[0]
@@ -1018,12 +1104,14 @@
             qkv_rows[:, wide : 2 * wide].T,
             jnp.broadcast_to(valid[:, None], (total, 128)),
             mixed_low,
-        ),
+        )
+        + tuple(outer),
         (
             jax.ShapeDtypeStruct((total, width), jnp.bfloat16),
             jax.ShapeDtypeStruct((total, 3 * wide), jnp.bfloat16),
             jax.ShapeDtypeStruct((wide, width), jnp.bfloat16),
-        ),
+        )
+        + outer_shapes(outer),
         [
             pltpu.VMEM((total, wide), jnp.float32),
             pltpu.VMEM((total, wide), jnp.float32),
@@ -1157,38 +1245,26 @@
     grad_act = jnp.einsum("le,fe->lf", all_final, proj_weight, preferred_element_type=jnp.float32)
     gelu_pull = jax.vjp(partial(jax.nn.gelu, approximate=True), upper_proj)[1]
     grad_upper = gelu_pull(grad_act)[0].astype(jnp.bfloat16)
-    grad_proj = jnp.einsum("lf,le->fe", activated, all_final, preferred_element_type=jnp.float32)
-    grad_normed_mlp, sums_proj = tokens_scatter(
-        grad_upper,
-        up_weight[None],
-        True,
-        n,
-        m,
-        6,
-        (Rider("dp", grad_proj.astype(jnp.bfloat16), 1),),
-    )
-    grad_up = jnp.einsum("le,lf->ef", all_mlp, grad_upper, preferred_element_type=jnp.float32)
+    grad_normed_mlp, grad_proj = tokens_scatter(
+        grad_upper, up_weight[None], True, n, m, 6, (), (activated, all_final)
+    )
     grad_mid_norm, grad_scale_mlp, grad_shift_mlp = layer_backward(
         grad_normed_mlp, normed_mlp, inverse_mlp, scale_mlp
     )
     grad_mid = grad_final + grad_mid_norm
-    all_mid, grad_qkv, grad_out, sums_up = attend_gather(
+    all_mid, grad_qkv, grad_out, grad_up, sums_proj = attend_gather(
         grad_mid.astype(jnp.bfloat16),
         out_weight,
         qkv_rows,
         valid,
         mixed_low,
+        (all_mlp, grad_upper),
         n,
         m,
         7,
-        (Rider("dp", grad_up.astype(jnp.bfloat16), 0),),
-    )
-    grad_normed_attend, sums_out = tokens_scatter(
-        grad_qkv, qkv_weight, True, n, m, 8, (Rider("dp", grad_out, 1),)
-    )
-    grad_qkv_weight = jnp.einsum(
-        "le,lf->ef", all_attend, grad_qkv, preferred_element_type=jnp.float32
-    )
+        (Rider("dp", grad_proj, 1),),
+    )
+    (grad_normed_attend,) = tokens_scatter(grad_qkv, qkv_weight, True, n, m, 8)
     grad_stream_norm, grad_scale_attend, grad_shift_attend = layer_backward(
         grad_normed_attend, normed_attend, inverse_attend, scale_attend
     )
@@ -1201,7 +1277,7 @@
             ).reshape(n, -1)
         ]
     )
-    all_stream, grad_tap_patch, grad_down, sums_qkv, ada_columns = tokens_gather(
+    all_stream, grad_residual, grad_down, grad_qkv_weight, sums_up, ada_columns = tokens_gather(
         grad_stream.astype(jnp.bfloat16),
         down_matrix[None],
         True,
@@ -1211,17 +1287,20 @@
         m,
         9,
         (
-            Rider("dp", grad_qkv_weight.astype(jnp.bfloat16), 0),
+            Rider("dp", grad_up, 0),
             Rider("mp", grad_modulation, 0),
         ),
         down_patch,
+        (all_attend, grad_qkv),
+        canvas_cols if fused else 0,
     )
     ada_columns = added(ada_columns).reshape(-1)[: columns.shape[0]]
-    grad_residual = (
-        grad_tap_patch.reshape(rows_all // 2, token_cols, 2, 2, own)
-        .transpose(0, 2, 1, 3, 4)
-        .reshape(pixel_total, own)
-    )
+    if not fused:
+        grad_residual = (
+            grad_residual.reshape(rows_all // 2, token_cols, 2, 2, own)
+            .transpose(0, 2, 1, 3, 4)
+            .reshape(pixel_total, own)
+        )
     def back(grad_low, hidden, spread, kernel, number, riders):
         if fused:
             acc, parts, *ridden = conv_back_fused(
@@ -1232,7 +1311,7 @@
         parts = grad_kernel.astype(jnp.bfloat16).reshape(9 * own, -1).T
         return grad_hidden, parts, exchange(riders, n, m, number)
 
-    grad_hidden_second, parts_second, (sums_down, every_small) = back(
+    grad_hidden_second, parts_second, (sums_down, sums_qkv, sums_out, every_small) = back(
         grad_residual.astype(jnp.bfloat16),
         hidden_second,
         spread_second,
@@ -1240,6 +1319,8 @@
         10,
         (
             Rider("dp", unsettled(grad_down, m, n), 1),
+            Rider("dp", grad_qkv_weight, 0),
+            Rider("dp", grad_out, 1),
             Rider("dp", jnp.concatenate([tiled_up(embedding[0]), tiled_up(ada_columns)])),
         ),
     )
@@ -1256,7 +1337,7 @@
         (
             Rider("dp", unsettled(parts_second, m, n), 1),
             Rider("dp", tiled_up(grad_shift)),
-            Settle(added(sums_down)[:, 0].astype(jnp.bfloat16), True),
+            Settle(added(sums_down)[:, 0].astype(jnp.bfloat16), True, 4, fused),
         ),
     )
     grad_base, grad_gain_first = group_backward(
@@ -1270,9 +1351,9 @@
         [tiled_up(embed_term[0]), tiled_up(jnp.concatenate([grad_gain_first, grad_gain_second]))]
     )
     riders = (
-        Settle(unsettled(parts_first, m, n), False),
+        Settle(unsettled(parts_first, m, n), False, 9, fused),
         Rider("all", small),
-        Settle(added(sums_second)[:, 0].astype(jnp.bfloat16), True),
+        Settle(added(sums_second)[:, 0].astype(jnp.bfloat16), True, 9, fused),
     )
     if fused:
         pieces_first, small, pieces_second, image_turned = exchange(

time: 1080 us -> 1050 us (0.972)
  local copies, waits for them, and re-layouts: 57.4 us -> 27.8 us
  matrix products: 48.7 us -> 28.8 us
  Pallas kernels: 871 us -> 890 us
    reshape x11 -> x0, local copies, waits for them, and re-layouts: 25.7 us -> none  [the longest x9 18.3 us: settled(): return pieces.astype(jnp.float32).reshape(m, count, outs, taps, -1).trans...]
    dot_general x3 -> x0, matrix products: 23.6 us -> none  [the longest x1 9.52 us: local(): jnp.einsum('lf,le->fe', activated, all_final, preferred_element_type=jnp....]
    pallas_call x14, Pallas kernels: 871 us -> 890 us  [comm_call(): pl.pallas_call(body, out_shape=tuple(out_shapes) + ride_shapes, in_specs=...]
  transfers between devices with their start and end apart: 2 -> 2, of which waited for: 0 -> 0; matrix products, arithmetic and copies ran while one was open for 5% -> 3% of each run, Pallas kernels for 18% -> 19%
where the time goes in v6:
time: 1050 us; the launch traced here: 1040 us
  Pallas kernels  890 us (85%)
  other arithmetic  75.1 us (7%)
  matrix products  28.8 us (3%)
  local copies, waits for them, and re-layouts  27.8 us (3%)
  between operations  15 us (1%)
    pallas_call x14, Pallas kernels, comm_call(): pl.pallas_call(body, out_shape=tuple(out_shapes) + ride_shapes, in_specs=...  890 us
  transfers between devices with their start and end apart: 2, of which 0 were waited for; matrix products, arithmetic and copies ran while one was open for 3% of the time, Pallas kernels for 19%

profile of v6, /device:TPU:9, one launch (start us, length us, event | category | flops | bytes accessed | tf_op | source)
XLA Modules:
  0.0 1036.5 jit_solution(11622609365101493889)
XLA Ops:
  8.9 1.7 fusion.7
  10.6 27.8 %shard_map.254 = (f32[8,8,128]{2,1,0:T(8,128)}, bf16[8,512,128]{2,1,0:T(8,128)(2,1)}) custom-call(f32[8,128]{1,0:T(8,128)} %bitcast.198, bf16[512,1024]{1,0:T(8,128)(2,1)} %bitcast.189), custom_call_target="tpu_custom_call" | custom-call | tf_op jit(solution)/shard_map/pallas_call | solution.py:386
  38.4 1.9 convert_reduce_fusion.6
  40.7 1.8 multiply_reduce_fusion.3
  42.8 2.0 multiply_convert_fusion.1
  45.9 2.4 pad_maximum_fusion
  48.3 77.4 %shard_map.255 = f32[4096,128]{1,0:T(8,128)} custom-call(bf16[4352,384]{1,0:T(8,128)(2,1)} %bitcast.163, bf16[3,384,1024]{2,1,0:T(8,128)(2,1)} %bitcast.172), custom_call_target="tpu_custom_call" | custom-call | tf_op jit(solution)/shard_map/pallas_call | solution.py:386
  125.7 2.1 add_reduce_fusion
  128.2 2.1 multiply_reduce_fusion.2
  130.7 2.3 multiply_convert_fusion
  133.9 2.2 pad_maximum_fusion.1
  136.1 78.3 %shard_map.256 = f32[4096,128]{1,0:T(8,128)} custom-call(bf16[4352,384]{1,0:T(8,128)(2,1)} %bitcast.165, bf16[3,384,1024]{2,1,0:T(8,128)(2,1)} %bitcast.170), custom_call_target="tpu_custom_call" | custom-call | tf_op jit(solution)/shard_map/pallas_call | solution.py:386
  214.4 1.8 fusion.20
  218.2 41.9 %shard_map.257 = f32[128,2048]{1,0:T(8,128)} custom-call(bf16[1024,512]{1,0:T(8,128)(2,1)} %reshape.543.refs_0_.refs_2_, bf16[1,512,2048]{2,1,0:T(8,128)(2,1)} %bitcast.174), custom_call_target="tpu_custom_call" | custom-call | tf_op jit(solution)/shard_map/pallas_call | solution.py:386
  260.1 1.4 reduce_sum.374
  261.6 1.5 multiply_reduce_fusion.9
  264.1 40.2 %shard_map.258 = (bf16[1024,2048]{1,0:T(8,128)(2,1)}, bf16[1024,768]{1,0:T(8,128)(2,1)}) custom-call(bf16[128,2048]{1,0:T(8,128)(2,1)} %add_convert_fusion.3.refs_0_, bf16[3,2048,256]{2,1,0:T(8,128)(2,1)} %refs_1_.5), custom_call_target="tpu_custom_call" | custom-call | tf_op jit(solution)/shard_map/pallas_call | solution.py:386
  306.9 82.0 %shard_map.259 = (f32[128,2048]{1,0:T(8,128)}, bf16[1024,256]{1,0:T(8,128)(2,1)}) custom-call(bf16[1024,768]{1,0:T(8,128)(2,1)} %get-tuple-element.52.refs_0_.refs_2_, f32[8,1024]{1,0:T(8,128)} %broadcast_in_dim.28.refs_1_, bf16[256,2048]{1,0:T(8,128)(2,1)} %refs_1_.4), custom_call_target="tpu_custom_call" | custom-call | tf_op jit(solution)/shard_map/pallas_call | solution.py:386
  392.3 42.4 %shard_map.260 = (bf16[1024,2048]{1,0:T(8,128)(2,1)}, f32[1024,1024]{1,0:T(8,128)}, bf16[1024,1024]{1,0:T(8,128)(2,1)}) custom-call(bf16[128,2048]{1,0:T(8,128)(2,1)} %add_convert_fusion.2.refs_0_, bf16[1,2048,1024]{2,1,0:T(8,128)(2,1)} %bitcast.168), custom_call_target="tpu_custom_call" | custom-call | tf_op jit(solution)/shard_map/pallas_call | solution.py:386
  434.7 9.3 convolution_convert_fusion
  444.0 2.6 copy.30
  446.6 1.9 slice_bitcast_fusion.refs_3_
  448.4 12.6 %fusion.6.refs_0_.refs_7_ = bf16[1024,1024]{1,0:T(8,128)(2,1)} fusion(f32[1024,1024]{1,0:T(8,128)} %get-tuple-element.56, bf16[1024,2048]{1,0:T(8,128)(2,1)} %all-gather.2.cloned.1.call-done.refs_3_, bf16[1024,2048]{1,0:T(8,128)(2,1)} %param.28), kind=kOutput, calls=%fused_computation.10 | convolution fusion | flops 4315938816 | bytes 14680064 | tf_op jit(solution)/shard_map/le,fe->lf/dot_general | solution.py:1245
  461.1 72.4 %shard_map.261 = (f32[128,2048]{1,0:T(8,128)}, bf16[1024,2048]{1,0:T(8,128)(2,1)}) custom-call(bf16[1024,1024]{1,0:T(8,128)(2,1)} %fusion.6.refs_0_.refs_7_, bf16[1,2048,1024]{2,1,0:T(8,128)(2,1)} %bitcast.169, bf16[1024,1024]{1,0:T(8,128)(2,1)} %get-tuple-element.54.refs_2_, bf16[1024,2048]{1,0:T(8,128)(2,1)} %all-gather.2.cloned.1.call-done.refs_3_), custom_call_target="tpu_custom_call" | custom-call | tf_op jit(solution)/shard_map/pallas_call | solution.py:386
  533.5 2.0 multiply_reduce_fusion.4
  535.5 3.8 fusion.52
  540.2 57.9 %shard_map.262 = (bf16[1024,2048]{1,0:T(8,128)(2,1)}, bf16[1024,768]{1,0:T(8,128)(2,1)}, bf16[256,2048]{1,0:T(8,128)(2,1)}, bf16[2048,1024]{1,0:T(8,128)(2,1)}, bf16[4,1024,512]{2,1,0:T(8,128)(2,1)}) custom-call(bf16[128,2048]{1,0:T(8,128)(2,1)} %get-tuple-element.103.refs_0_, bf16[256,2048]{1,0:T(8,128)(2,1)} %refs_1_.4, ...), custom_call_target="tpu_custom_call" | custom-call | tf_op jit(solution)/shard_map/pallas_call | solution.py:386
  598.1 43.4 %shard_map.263 = f32[128,2048]{1,0:T(8,128)} custom-call(bf16[1024,768]{1,0:T(8,128)(2,1)} %get-tuple-element.61.refs_0_.refs_4_, bf16[3,2048,256]{2,1,0:T(8,128)(2,1)} %refs_1_.5), custom_call_target="tpu_custom_call" | custom-call | tf_op jit(solution)/shard_map/pallas_call | solution.py:386
  641.5 1.8 multiply_reduce_fusion.5
  644.7 57.8 %shard_map.264 = (bf16[1024,2048]{1,0:T(8,128)(2,1)}, f32[4096,128]{1,0:T(8,128)}, bf16[2048,512]{1,0:T(8,128)(2,1)}, bf16[2048,768]{1,0:T(8,128)(2,1)}, bf16[4,...) custom-call(bf16[128,2048]{1,0:T(8,128)(2,1)} %add_convert_fusion.refs_0_, bf16[1,512,2048]{2,1,0:T(8,128)(2,1)} %bitcast.175, ...), custom_call_target="tpu_custom_call" | custom-call | tf_op jit(solution)/shard_map/pallas_call | solution.py:386
  702.5 2.7 convert_element_type.112.refs_0_
  705.8 78.5 %shard_map.265 = (f32[4096,384]{1,0:T(8,128)}, bf16[4,256,1152]{2,1,0:T(8,128)(2,1)}, bf16[4,8,1,64,512]{4,3,2,1,0:T(8,128)(2,1)}, bf16[4,512,768]{2,1,0:T(8,128...) custom-call(bf16[4096,128]{1,0:T(8,128)(2,1)} %convert_element_type.112.refs_0_, ...), custom_call_target="tpu_custom_call" | custom-call | tf_op jit(solution)/shard_map/pallas_call | solution.py:386
  784.4 2.7 fusion.55
  787.1 2.4 fusion.11
  789.6 2.4 fusion.49
  793.5 3.9 fusion.22
  798.3 2.9 reduce_sum.392.refs_5_
  801.2 104.8 %shard_map.266 = (f32[4096,384]{1,0:T(8,128)}, bf16[4,256,1152]{2,1,0:T(8,128)(2,1)}, bf16[4,8,1,32,1152]{4,3,2,1,0:T(8,128)(2,1)}, f32[4,8,128]{2,1,0:T(8,128)}, f32[4,256,256]{2,1,0:T(8,128)}) custom-call(bf16[4096,128]{1,0:T(8,128)(2,1)} %get-tuple-element.114.refs_0_, bf16[3,384,1024]{2,1,0:T(8,128)(2,1)} %bitcast.173, bf16[4352,384]{1,0:T(8,128)(2,1)} %bitcast.164, ...), custom_call_target="tpu_custom_call" | custom-call | tf_op jit(solution)/shard_map/pallas_call | solution.py:386
  906.0 2.9 fusion.54
  908.9 4.3 fusion.48
  913.2 1.7 fusion.59
  914.9 3.0 reduce_sum.394.refs_2_
  920.0 4.6 fusion.18.refs_3_
  924.6 85.1 %shard_map.267 = (f32[9,256,128]{2,1,0:T(8,128)}, f32[32,16,128]{2,1,0:T(8,128)}, f32[9,256,128]{2,1,0:T(8,128)}, bf16[512,1024]{1,0:T(8,128)(2,1)}) custom-call(bf16[8,4,32,1152]{3,2,1,0:T(8,128)(2,1)} %bitcast.182, f32[16,128]{1,0:T(8,128)} %pad_maximum_fusion.4.refs_1_, bf16[8,32,1152]{2,1,0:T(8,128)(2,1)} %reduce_sum.394.refs_2_, ...), custom_call_target="tpu_custom_call" | custom-call | tf_op jit(solution)/shard_map/pallas_call | solution.py:386
  1012.0 2.0 fusion.24
  1015.0 2.7 convert_reduce_fusion.5
  1018.7 2.3 convert_reduce_fusion.1
  1021.6 2.0 convert_reduce_fusion
  (153 shorter events, 32.3 us)
Async XLA Ops:
  7.2 1.7 copy-start
  7.2 441.3 %all-gather.2.cloned.1.call-start = ((), (), s32[]{:S(2)}) async-start(), calls=%async_computation.2 | async-start | bytes 4718592 | tf_op jit(solution)/shard_map/all_gather | solution.py:62
  38.4 4.4 copy-start.4
  44.8 0.9 copy-start.16
  44.8 1.0 copy-start.18
  216.2 2.0 copy-start.21
  260.1 3.0 copy-start.2
  264.1 40.3 %copy-start.23 = (s32[1,2]{1,0:T(1,128)S(1)}, s32[1,2]{1,0:T(1,128)}, u32[]{:S(2)}) copy-start(s32[1,2]{1,0:T(1,128)} %param.17) | copy-start | bytes 28
  304.3 231.1 %reduce-scatter.2.cloned.1.call-start = ((), (), s32[]{:S(2)}) async-start(), calls=%async_computation.1 | async-start | bytes 4718592 | tf_op jit(solution)/shard_map/reduce_scatter | solution.py:66
  390.3 1.0 copy-start.3
  641.5 1.9 copy-start.6
  641.5 1.9 copy-start.8
  643.4 1.3 copy-start.17
  702.5 2.7 copy-start.19
  787.1 2.5 copy-start.1
  906.0 2.9 copy-start.7
  913.1 6.9 copy-start.5
  924.6 87.3 %copy-start.20 = (f32[4,16,128]{2,1,0:T(8,128)S(1)}, f32[4,16,128]{2,1,0:T(8,128)}, u32[]{:S(2)}) copy-start(f32[4,16,128]{2,1,0:T(8,128)} %get-tuple-element.79) | copy-start | bytes 98308
  924.6 87.4 %copy-start.22 = (f32[4,8,128]{2,1,0:T(8,128)S(1)}, f32[4,8,128]{2,1,0:T(8,128)}, u32[]{:S(2)}) copy-start(f32[4,8,128]{2,1,0:T(8,128)} %get-tuple-element.80) | copy-start | bytes 49156
  1011.9 5.8 copy-start.13
  1015.0 3.6 copy-start.10
  1018.7 2.9 copy-start.9
  1023.6 1.7 copy-start.15
  1023.6 2.7 copy-start.12
  1025.3 2.0 copy-start.11
  1026.3 2.0 copy-start.14
Sparse Core Ops, SparseCore 0:
  304.4 83.4 all-gather.1
  444.1 61.3 reduce-scatter.1

commit v7 on v6

--- a/solution.py
+++ b/solution.py
@@ -721,7 +721,10 @@
     )
 
 
-def conv_back_kernel(breadth, line, g_ref, w_ref, x_ref, acc_ref, wg_ref, held, sums, send, recv):
+def conv_back_kernel(breadth, size, extra, line, g_ref, w_ref, x_ref, n_ref, v_ref, *refs):
+    refs = list(refs)
+    more_ref = refs.pop(0) if extra else None
+    low_ref, wg_ref, stat_ref, acc_ref, held, sums, send, recv = refs
     chips = line.chips
     pixels, own = g_ref.shape
     wide = w_ref.shape[1]
@@ -778,19 +781,61 @@
 
     line_gather(line, g_ref, slot, send, recv, on_own, on_pair)
 
-
-def conv_back_fused(grad_low, spread, kernel, cols, n, m, number, riders=()):
+    gain, inverse = v_ref[0:1], v_ref[1:2]
+    stat_ref[...] = jnp.zeros_like(stat_ref)
+    column = lax.broadcasted_iota(jnp.int32, (tile, own), 0) % breadth
+
+    @pl.loop(0, pixels // tile)
+    def _(index):
+        rows = pl.ds(pl.multiple_of(index * tile, tile), tile)
+        left = jnp.where(
+            column == breadth - 1, 0.0, pltpu.roll(acc_ref[rows, 0:own], tile - 1, 0)
+        )
+        right = jnp.where(column == 0, 0.0, pltpu.roll(acc_ref[rows, 2 * own : wide], 1, 0))
+        incoming = left + acc_ref[rows, own : 2 * own] + right
+        normed = n_ref[rows]
+        pre_act = normed * gain
+        sigmoid_part = 1.0 / (1.0 + jnp.exp(-pre_act))
+        through = incoming * sigmoid_part * (1.0 + pre_act * (1.0 - sigmoid_part))
+        acc_ref[rows, 0:own] = through
+        stat_ref[0:1] += jnp.sum(through * normed, axis=0, keepdims=True)
+        stat_ref[1:2] += jnp.sum(through, axis=0, keepdims=True)
+
+    groups = [lax.broadcasted_iota(jnp.int32, (own, own), axis) // size for axis in range(2)]
+    spread = jnp.where(groups[0] == groups[1], 1.0 / (pixels * size), 0.0)
+    means = jnp.dot(stat_ref[...] * gain, spread, precision=PRECISE)
+    second_mean, first_mean = means[0:1], means[1:2]
+
+    @pl.loop(0, pixels // tile)
+    def _(index):
+        rows = pl.ds(pl.multiple_of(index * tile, tile), tile)
+        outgoing = inverse * (
+            acc_ref[rows, 0:own] * gain - first_mean - n_ref[rows] * second_mean
+        )
+        stat_ref[2:3] += jnp.sum(outgoing, axis=0, keepdims=True)
+        if extra:
+            outgoing = outgoing + more_ref[rows]
+        low_ref[rows] = outgoing.astype(jnp.bfloat16)
+
+
+def conv_back_fused(
+    grad_low, spread, kernel, normed, inverse, gain, size, cols, n, m, number, riders, more=()
+):
     pixels, own = grad_low.shape
     depth = kernel.shape[1]
     chips = n // 2
+    vectors = jnp.concatenate([gain[None], inverse[None], jnp.zeros((6, own), jnp.float32)])
     return comm_call(
-        partial(conv_back_kernel, cols),
-        (grad_low, kernel.reshape(3, 3 * depth, kernel.shape[2]), spread),
+        partial(conv_back_kernel, cols, size, len(more) > 0),
+        (grad_low, kernel.reshape(3, 3 * depth, kernel.shape[2]), spread, normed, vectors)
+        + tuple(more),
         (
-            jax.ShapeDtypeStruct((pixels, 3 * depth), jnp.float32),
+            jax.ShapeDtypeStruct((pixels, depth), jnp.bfloat16),
             jax.ShapeDtypeStruct((chips, 2 * own, 9 * depth), jnp.bfloat16),
+            jax.ShapeDtypeStruct((8, own), jnp.float32),
         ),
         [
+            pltpu.VMEM((pixels, 3 * depth), jnp.float32),
             pltpu.VMEM((n, pixels + 2 * cols, own), jnp.bfloat16),
             pltpu.VMEM((2 * own, 9 * depth), jnp.float32),
         ]
@@ -891,14 +936,18 @@
         )
 
 
-def tokens_gather_kernel(turned, shape_out, outs, side, beside, cols, line, x_ref, w_ref, *refs):
+def tokens_gather_kernel(
+    turned, shape_out, outs, side, beside, cols, chained, line, x_ref, w_ref, *refs
+):
     refs = list(refs)
+    chain_w = refs.pop(0) if chained else None
     left = refs.pop(0) if side else None
     outer = (refs.pop(0), refs.pop(0)) if beside else None
     held = refs.pop(0)
     results = [refs.pop(0) for _ in range(outs)]
     grad = refs.pop(0) if side else None
     outer_grad = refs.pop(0) if beside else None
+    chain_out = refs.pop(0) if chained else None
     total = refs.pop(0) if side else None
     send, recv = refs
     tokens = x_ref.shape[0]
@@ -929,6 +978,12 @@
                         store_pixels(ref, chip, value)
                     else:
                         ref[rows, pl.ds(j * across + start, cut)] = value.astype(ref.dtype)
+        if chained:
+            for start in range(0, chain_w.shape[1], 512):
+                columns = pl.ds(start, 512)
+                chain_out[rows, columns] = product(
+                    results[-1][rows], chain_w[:, columns], False
+                ).astype(jnp.bfloat16)
         if side:
             add_outer(total, held, left, rows)
 
@@ -945,7 +1000,7 @@
 
 
 def tokens_gather(
-    x, w, turned, kinds, shape_out, n, m, number, riders=(), left=None, outer=(), cols=0
+    x, w, turned, kinds, shape_out, n, m, number, riders=(), left=None, outer=(), cols=0, chain=()
 ):
     tokens, width = x.shape
     across = w.shape[0] * w.shape[1 if turned else 2]
@@ -954,13 +1009,21 @@
     shape = (tokens * n * 4, across // 4) if cols else (tokens * n, across)
     return comm_call(
         partial(
-            tokens_gather_kernel, turned, shape_out, len(kinds), side, len(outer) > 0, cols
+            tokens_gather_kernel,
+            turned,
+            shape_out,
+            len(kinds),
+            side,
+            len(outer) > 0,
+            cols,
+            len(chain) > 0,
         ),
-        (x, w) + ((left,) if side else ()) + tuple(outer),
+        (x, w) + tuple(chain) + ((left,) if side else ()) + tuple(outer),
         (jax.ShapeDtypeStruct((tokens * n, width), x.dtype),)
         + tuple(jax.ShapeDtypeStruct(shape, kind) for kind in kinds)
         + tuple(jax.ShapeDtypeStruct(grad, jnp.bfloat16) for grad in grads)
-        + outer_shapes(outer),
+        + outer_shapes(outer)
+        + tuple(jax.ShapeDtypeStruct((tokens * n, w2.shape[1]), jnp.bfloat16) for w2 in chain),
         [pltpu.VMEM(grad, jnp.float32) for grad in grads] + gather_sems(n // 2),
         riders,
         n,
@@ -1224,7 +1287,7 @@
     stream_mid = stream + attended
     normed_mlp, inverse_mlp = layer_forward(stream_mid)
     input_mlp = (normed_mlp * (1.0 + scale_mlp) + shift_mlp).astype(jnp.bfloat16)
-    all_mlp, upper_proj, activated = tokens_gather(
+    all_mlp, upper_proj, activated, projected = tokens_gather(
         input_mlp,
         up_weight[None],
         False,
@@ -1233,10 +1296,9 @@
         n,
         m,
         5,
-    )
-    final_stream = stream_mid + scatter_rows(
-        jnp.dot(activated, proj_weight, preferred_element_type=jnp.float32)
-    )
+        chain=(proj_weight,),
+    )
+    final_stream = stream_mid + scatter_rows(projected)
     output = final_stream.astype(jnp.bfloat16).reshape(1, token_rows, token_cols, width_all)
 
     grad_final_low = cotangent[0].reshape(local_tokens, width_all)
@@ -1301,21 +1363,38 @@
             .transpose(0, 2, 1, 3, 4)
             .reshape(pixel_total, own)
         )
-    def back(grad_low, hidden, spread, kernel, number, riders):
+    def back(grad_low, hidden, spread, kernel, normed, inverse, gain, number, riders, more=()):
         if fused:
-            acc, parts, *ridden = conv_back_fused(
-                grad_low, spread, kernel, canvas_cols, n, m, number, riders
+            low, parts, sums, *ridden = conv_back_fused(
+                grad_low,
+                spread,
+                kernel,
+                normed,
+                inverse,
+                gain,
+                size,
+                canvas_cols,
+                n,
+                m,
+                number,
+                riders,
+                more,
             )
-            return join_columns(acc, canvas_cols), parts, ridden
+            return low, parts, sums[0], sums[2], ridden
         grad_hidden, grad_kernel = conv_backward(grad_low, hidden, kernel, n)
+        outgoing, gain_part = group_backward(grad_hidden, normed, inverse, gain, size)
         parts = grad_kernel.astype(jnp.bfloat16).reshape(9 * own, -1).T
-        return grad_hidden, parts, exchange(riders, n, m, number)
-
-    grad_hidden_second, parts_second, (sums_down, sums_qkv, sums_out, every_small) = back(
+        low = sum(more, outgoing).astype(jnp.bfloat16)
+        return low, parts, gain_part, jnp.sum(outgoing, axis=0), exchange(riders, n, m, number)
+
+    grad_conv_low, parts_second, grad_gain_second, grad_shift, rode_second = back(
         grad_residual.astype(jnp.bfloat16),
         hidden_second,
         spread_second,
         conv_second,
+        normed_second,
+        inverse_second,
+        own_second,
         10,
         (
             Rider("dp", unsettled(grad_down, m, n), 1),
@@ -1324,26 +1403,24 @@
             Rider("dp", jnp.concatenate([tiled_up(embedding[0]), tiled_up(ada_columns)])),
         ),
     )
-    grad_conv_output, grad_gain_second = group_backward(
-        grad_hidden_second, normed_second, inverse_second, own_second, size
-    )
-    grad_shift = jnp.sum(grad_conv_output, axis=0)
-    grad_hidden_first, parts_first, (sums_second, every_shift, pieces_down) = back(
-        grad_conv_output.astype(jnp.bfloat16),
+    sums_down, sums_qkv, sums_out, every_small = rode_second
+    image_turned, parts_first, grad_gain_first, _, rode_first = back(
+        grad_conv_low,
         hidden_first,
         spread_first,
         conv_first,
+        normed_first,
+        inverse_first,
+        own_first,
         11,
         (
             Rider("dp", unsettled(parts_second, m, n), 1),
             Rider("dp", tiled_up(grad_shift)),
             Settle(added(sums_down)[:, 0].astype(jnp.bfloat16), True, 4, fused),
         ),
-    )
-    grad_base, grad_gain_first = group_backward(
-        grad_hidden_first, normed_first, inverse_first, own_first, size
-    )
-    image_turned = (grad_residual + grad_base).astype(jnp.bfloat16)
+        (grad_residual,),
+    )
+    sums_second, every_shift, pieces_down = rode_first
     embed_term = jnp.dot(
         grad_shift[None], shift_weight.astype(jnp.float32).T, precision=PRECISE
     ) + jnp.dot(ada_columns[None], ada_weight.astype(jnp.float32).T, precision=PRECISE)

time: 1050 us -> 1020 us (0.971)
  other arithmetic: 75.1 us -> 57.7 us
    reduce_sum x3 -> x0, other arithmetic: 10.6 us -> none  [the longest x2 6.67 us: group_backward(): plain_part = jnp.sum(through, axis=0)]
  transfers between devices with their start and end apart: 2 -> 2, of which waited for: 0 -> 0; matrix products, arithmetic and copies ran while one was open for 3% -> 3% of each run, Pallas kernels for 19% -> 20%
where the time goes in v7:
time: 1020 us; the launch traced here: 1010 us
  Pallas kernels  894 us (88%)
  other arithmetic  57.7 us (6%)
  local copies, waits for them, and re-layouts  25.8 us (3%)
  matrix products  20.2 us (2%)
  between operations  14.7 us (1%)
    pallas_call x14, Pallas kernels, comm_call(): pl.pallas_call(body, out_shape=tuple(out_shapes) + ride_shapes, in_specs=...  894 us
  transfers between devices with their start and end apart: 2, of which 0 were waited for; matrix products, arithmetic and copies ran while one was open for 3% of the time, Pallas kernels for 20%

profile of v7, /device:TPU:9, one launch (start us, length us, event | category | flops | bytes accessed | tf_op | source)
XLA Modules:
  0.0 1012.7 jit_solution(8547458063691051627)
XLA Ops:
  7.2 1.5 copy-done
  8.8 1.7 fusion.7
  10.4 27.8 %shard_map.254 = (f32[8,8,128]{2,1,0:T(8,128)}, bf16[8,512,128]{2,1,0:T(8,128)(2,1)}) custom-call(f32[8,128]{1,0:T(8,128)} %bitcast.177, bf16[512,1024]{1,0:T(8,128)(2,1)} %bitcast.168), custom_call_target="tpu_custom_call" | custom-call | tf_op jit(solution)/shard_map/pallas_call | solution.py:386
  38.3 1.9 convert_reduce_fusion.6
  40.5 1.8 multiply_reduce_fusion.1
  46.0 2.3 pad_maximum_fusion
  48.3 77.2 %shard_map.255 = f32[4096,128]{1,0:T(8,128)} custom-call(bf16[4352,384]{1,0:T(8,128)(2,1)} %bitcast.146, bf16[3,384,1024]{2,1,0:T(8,128)(2,1)} %bitcast.153), custom_call_target="tpu_custom_call" | custom-call | tf_op jit(solution)/shard_map/pallas_call | solution.py:386
  125.6 2.1 add_reduce_fusion
  128.1 2.2 multiply_reduce_fusion
  130.6 3.6 multiply_convert_fusion
  135.1 2.4 pad_maximum_fusion.1
  137.4 78.3 %shard_map.256 = f32[4096,128]{1,0:T(8,128)} custom-call(bf16[4352,384]{1,0:T(8,128)(2,1)} %bitcast.148, bf16[3,384,1024]{2,1,0:T(8,128)(2,1)} %bitcast.155), custom_call_target="tpu_custom_call" | custom-call | tf_op jit(solution)/shard_map/pallas_call | solution.py:386
  215.7 3.3 fusion.11
  219.8 1.2 reshape.486.refs_0_.refs_2_
  221.0 41.9 %shard_map.257 = f32[128,2048]{1,0:T(8,128)} custom-call(bf16[1024,512]{1,0:T(8,128)(2,1)} %reshape.486.refs_0_.refs_2_, bf16[1,512,2048]{2,1,0:T(8,128)(2,1)} %bitcast.157), custom_call_target="tpu_custom_call" | custom-call | tf_op jit(solution)/shard_map/pallas_call | solution.py:386
  262.9 1.4 reduce_sum.293
  264.4 1.5 multiply_reduce_fusion.7
  265.9 1.0 add_convert_fusion.3.refs_0_
  266.9 40.1 %shard_map.258 = (bf16[1024,2048]{1,0:T(8,128)(2,1)}, bf16[1024,768]{1,0:T(8,128)(2,1)}) custom-call(bf16[128,2048]{1,0:T(8,128)(2,1)} %add_convert_fusion.3.refs_0_, bf16[3,2048,256]{2,1,0:T(8,128)(2,1)} %refs_1_.5), custom_call_target="tpu_custom_call" | custom-call | tf_op jit(solution)/shard_map/pallas_call | solution.py:386
  307.6 1.3 fusion.27
  309.6 82.0 %shard_map.259 = (f32[128,2048]{1,0:T(8,128)}, bf16[1024,256]{1,0:T(8,128)(2,1)}) custom-call(bf16[1024,768]{1,0:T(8,128)(2,1)} %get-tuple-element.55.refs_0_.refs_2_, f32[8,1024]{1,0:T(8,128)} %broadcast_in_dim.24.refs_1_, bf16[256,2048]{1,0:T(8,128)(2,1)} %refs_1_.4), custom_call_target="tpu_custom_call" | custom-call | tf_op jit(solution)/shard_map/pallas_call | solution.py:386
  391.6 1.4 fusion.38
  393.9 1.0 add_convert_fusion.2.refs_0_
  395.0 44.8 %shard_map.260 = (bf16[1024,2048]{1,0:T(8,128)(2,1)}, f32[1024,1024]{1,0:T(8,128)}, bf16[1024,1024]{1,0:T(8,128)(2,1)}, bf16[1024,2048]{1,0:T(8,128)(2,1)}) custom-call(bf16[128,2048]{1,0:T(8,128)(2,1)} %add_convert_fusion.2.refs_0_, bf16[1,2048,1024]{2,1,0:T(8,128)(2,1)} %bitcast.150, bf16[1024,2048]{1,0:T(8,128)(2,1)} %refs_2_.3), custom_call_target="tpu_custom_call" | custom-call | tf_op jit(solution)/shard_map/pallas_call | solution.py:386
  439.8 2.6 copy.30
  444.9 1.9 slice_bitcast_fusion.refs_3_
  446.7 12.6 %fusion.6.refs_0_.refs_7_ = bf16[1024,1024]{1,0:T(8,128)(2,1)} fusion(f32[1024,1024]{1,0:T(8,128)} %get-tuple-element.59, bf16[1024,2048]{1,0:T(8,128)(2,1)} %all-gather.2.cloned.1.call-done.refs_3_, bf16[1024,2048]{1,0:T(8,128)(2,1)} %refs_2_.3), kind=kOutput, calls=%fused_computation.10 | convolution fusion | flops 4315938816 | bytes 14680064 | tf_op jit(solution)/shard_map/le,fe->lf/dot_general | solution.py:1307
  459.4 71.2 %shard_map.261 = (f32[128,2048]{1,0:T(8,128)}, bf16[1024,2048]{1,0:T(8,128)(2,1)}) custom-call(bf16[1024,1024]{1,0:T(8,128)(2,1)} %fusion.6.refs_0_.refs_7_, bf16[1,2048,1024]{2,1,0:T(8,128)(2,1)} %bitcast.151, bf16[1024,1024]{1,0:T(8,128)(2,1)} %get-tuple-element.60.refs_2_, bf16[1024,2048]{1,0:T(8,128)(2,1)} %all-gather.2.cloned.1.call-done.refs_3_), custom_call_target="tpu_custom_call" | custom-call | tf_op jit(solution)/shard_map/pallas_call | solution.py:386
  530.6 2.0 multiply_reduce_fusion.2
  532.6 3.8 fusion.37
  537.4 57.8 %shard_map.262 = (bf16[1024,2048]{1,0:T(8,128)(2,1)}, bf16[1024,768]{1,0:T(8,128)(2,1)}, bf16[256,2048]{1,0:T(8,128)(2,1)}, bf16[2048,1024]{1,0:T(8,128)(2,1)}, bf16[4,1024,512]{2,1,0:T(8,128)(2,1)}) custom-call(bf16[128,2048]{1,0:T(8,128)(2,1)} %get-tuple-element.103.refs_0_, bf16[256,2048]{1,0:T(8,128)(2,1)} %refs_1_.4, ...), custom_call_target="tpu_custom_call" | custom-call | tf_op jit(solution)/shard_map/pallas_call | solution.py:386
  595.2 43.2 %shard_map.263 = f32[128,2048]{1,0:T(8,128)} custom-call(bf16[1024,768]{1,0:T(8,128)(2,1)} %get-tuple-element.65.refs_0_.refs_4_, bf16[3,2048,256]{2,1,0:T(8,128)(2,1)} %refs_1_.5), custom_call_target="tpu_custom_call" | custom-call | tf_op jit(solution)/shard_map/pallas_call | solution.py:386
  638.3 1.8 multiply_reduce_fusion.3
  640.3 1.3 add_convert_fusion.refs_0_
  641.6 57.6 %shard_map.264 = (bf16[1024,2048]{1,0:T(8,128)(2,1)}, f32[4096,128]{1,0:T(8,128)}, bf16[2048,512]{1,0:T(8,128)(2,1)}, bf16[2048,768]{1,0:T(8,128)(2,1)}, bf16[4,...) custom-call(bf16[128,2048]{1,0:T(8,128)(2,1)} %add_convert_fusion.refs_0_, bf16[1,512,2048]{2,1,0:T(8,128)(2,1)} %bitcast.158, ...), custom_call_target="tpu_custom_call" | custom-call | tf_op jit(solution)/shard_map/pallas_call | solution.py:386
  699.1 2.7 convert_element_type.102.refs_0_
  702.4 77.6 %shard_map.265 = (bf16[4096,128]{1,0:T(8,128)(2,1)}, bf16[4,256,1152]{2,1,0:T(8,128)(2,1)}, f32[8,128]{1,0:T(8,128)}, bf16[4,8,1,64,512]{4,3,2,1,0:T(8,128)(2,1)...) custom-call(bf16[4096,128]{1,0:T(8,128)(2,1)} %convert_element_type.102.refs_0_, ...), custom_call_target="tpu_custom_call" | custom-call | tf_op jit(solution)/shard_map/pallas_call | solution.py:386
  782.4 2.9 reduce_sum.306.refs_8_
  785.2 109.7 %shard_map.266 = (bf16[4096,128]{1,0:T(8,128)(2,1)}, bf16[4,256,1152]{2,1,0:T(8,128)(2,1)}, f32[8,128]{1,0:T(8,128)}, bf16[4,8,1,32,1152]{4,3,2,1,0:T(8,128)(2,1...) custom-call(bf16[4096,128]{1,0:T(8,128)(2,1)} %get-tuple-element.73.refs_0_, bf16[3,384,1024]{2,1,0:T(8,128)(2,1)} %bitcast.154, ...), custom_call_target="tpu_custom_call" | custom-call | tf_op jit(solution)/shard_map/pallas_call | solution.py:386
  895.6 1.7 fusion.40
  897.4 3.0 reduce_sum.307.refs_2_
  901.0 85.0 %shard_map.267 = (f32[9,256,128]{2,1,0:T(8,128)}, f32[32,16,128]{2,1,0:T(8,128)}, f32[9,256,128]{2,1,0:T(8,128)}, bf16[512,1024]{1,0:T(8,128)(2,1)}) custom-call(bf16[8,4,32,1152]{3,2,1,0:T(8,128)(2,1)} %bitcast.161, f32[16,128]{1,0:T(8,128)} %pad_maximum_fusion.4.refs_1_, bf16[8,32,1152]{2,1,0:T(8,128)(2,1)} %reduce_sum.307.refs_2_, ...), custom_call_target="tpu_custom_call" | custom-call | tf_op jit(solution)/shard_map/pallas_call | solution.py:386
  988.3 2.0 fusion.12
  990.3 1.1 fusion.29
  991.4 2.7 convert_reduce_fusion.5
  995.0 2.3 convert_reduce_fusion.1
  998.0 2.0 convert_reduce_fusion
  1000.0 1.2 pad_maximum_fusion.2
  (126 shorter events, 24.8 us)
Async XLA Ops:
  7.2 1.6 copy-start
  7.2 439.5 %all-gather.2.cloned.1.call-start = ((), (), s32[]{:S(2)}) async-start(), calls=%async_computation.2 | async-start | bytes 4718592 | tf_op jit(solution)/shard_map/all_gather | solution.py:62
  38.3 5.9 copy-start.3
  44.9 1.0 copy-start.13
  44.9 0.9 copy-start.15
  219.0 2.0 copy-start.17
  262.9 3.0 copy-start.1
  266.9 40.2 %copy-start.20 = (s32[1,2]{1,0:T(1,128)S(1)}, s32[1,2]{1,0:T(1,128)}, u32[]{:S(2)}) copy-start(s32[1,2]{1,0:T(1,128)} %param.17) | copy-start | bytes 28
  307.0 225.6 %reduce-scatter.2.cloned.1.call-start = ((), (), s32[]{:S(2)}) async-start(), calls=%async_computation.1 | async-start | bytes 4718592 | tf_op jit(solution)/shard_map/reduce_scatter | solution.py:66
  393.0 1.0 copy-start.2
  638.3 1.9 copy-start.4
  638.3 1.9 copy-start.5
  640.3 1.3 copy-start.14
  699.1 2.7 copy-start.16
  901.0 87.3 %copy-start.18 = (f32[4,16,128]{2,1,0:T(8,128)S(1)}, f32[4,16,128]{2,1,0:T(8,128)}, u32[]{:S(2)}) copy-start(f32[4,16,128]{2,1,0:T(8,128)} %get-tuple-element.85) | copy-start | bytes 98308
  901.0 87.3 %copy-start.19 = (f32[4,8,128]{2,1,0:T(8,128)S(1)}, f32[4,8,128]{2,1,0:T(8,128)}, u32[]{:S(2)}) copy-start(f32[4,8,128]{2,1,0:T(8,128)} %get-tuple-element.86) | copy-start | bytes 49156
  988.3 5.8 copy-start.10
  991.4 3.7 copy-start.7
  995.0 2.9 copy-start.6
  1000.0 1.7 copy-start.12
  1000.0 2.7 copy-start.9
  1001.7 2.0 copy-start.8
  1002.7 2.0 copy-start.11
Sparse Core Ops, SparseCore 0:
  307.1 83.3 all-gather.1
  440.0 60.1 reduce-scatter.1

commit v8 on v7

--- a/solution.py
+++ b/solution.py
@@ -151,6 +151,8 @@
         self.up = (self.dp, self.mp + 2)
         self.down = (self.dp, self.mp - 2)
         self.sibling = (self.dp, 2 * self.z + 1 - self.c)
+        self.ready = lambda: None
+        self.late = lambda: None
 
     def count(self, axis):
         return {"dp": self.images, "mp": 2 * self.chips, "all": 2 * self.chips * self.images}[axis]
@@ -361,14 +363,32 @@
     ride_scratch = [rider.scratch(sizes) for rider in riders]
     any_spec = pl.BlockSpec(memory_space=pl.ANY)
     ni, nr, no = len(inputs), len(riders), len(out_shapes)
+    large = [index for index in range(ni) if inputs[index].size * inputs[index].dtype.itemsize > 2**20]
 
     def body(*refs):
-        main_in, ride_in = refs[:ni], refs[ni : ni + nr]
+        main_in, ride_in = list(refs[:ni]), refs[ni : ni + nr]
         rest = refs[ni + nr :]
         main_out, ride_out = rest[:no], rest[no : no + nr]
         rest = rest[no + nr :]
         main_scratch, rest = rest[: len(scratch)], rest[len(scratch) :]
         line = Line(chips, m)
+        loads = []
+        if large:
+            load_sems, rest = rest[0], rest[1:]
+            for place, index in enumerate(large):
+                loads.append(
+                    pltpu.make_async_copy(main_in[index], rest[place], load_sems.at[place])
+                )
+                main_in[index] = rest[place]
+            rest = rest[len(large) :]
+        for load in loads:
+            load.start()
+
+        def ready():
+            for load in loads:
+                load.wait()
+
+        line.ready = ready
         line.barrier(sorted(set(axis for rider in riders for axis in rider.axes)), neighbours)
         riding = []
         for rider, src, dst, needs in zip(riders, ride_in, ride_out, ride_scratch):
@@ -376,8 +396,16 @@
             rest = rest[len(needs) :]
         for rider, refs_in in riding:
             rider.start(*refs_in)
+        phases = [0, 1]
+
+        def late():
+            phases.pop(0)
+            for rider, refs_in in riding:
+                rider.middle(0, *refs_in)
+
+        line.late = late
         kernel(line, *main_in, *main_out, *main_scratch)
-        for phase in range(2):
+        for phase in phases:
             for rider, refs_in in riding:
                 rider.middle(phase, *refs_in)
         for rider, refs_in in riding:
@@ -386,12 +414,16 @@
     return pl.pallas_call(
         body,
         out_shape=tuple(out_shapes) + ride_shapes,
-        in_specs=whole(ni) + [any_spec] * nr,
+        in_specs=[any_spec if index in large else whole(1)[0] for index in range(ni)]
+        + [any_spec] * nr,
         out_specs=tuple(
             whole(no)
             + [whole(1)[0] if isinstance(rider, Settle) else any_spec for rider in riders]
         ),
-        scratch_shapes=list(scratch) + [ref for needs in ride_scratch for ref in needs],
+        scratch_shapes=list(scratch)
+        + ([pltpu.SemaphoreType.DMA((len(large),))] if large else [])
+        + [pltpu.VMEM(inputs[index].shape, inputs[index].dtype) for index in large]
+        + [ref for needs in ride_scratch for ref in needs],
         compiler_params=comm_params(number),
     )(*inputs, *[rider.array for rider in riders])
 
@@ -431,11 +463,14 @@
 
     across(0, 0, x_ref, line.mp).start()
     slot(line.mp)[...] = x_ref[...]
+    line.ready()
     on_own()
     across(0, 0, x_ref, line.mp).wait_recv()
     on_pair(z)
     for step in range(1, chips):
         below, above = z - step, z + step
+        if step == chips - 1:
+            line.late()
 
         @pl.when(below >= 0)
         def _():
@@ -522,6 +557,7 @@
     z = line.z
     kept, out_ref, in_ref, moving, sems = scratch
     count = kept.shape[1] // parts
+    line.ready()
 
     def span(part):
         return pl.ds(part * count, count)
@@ -937,18 +973,20 @@
 
 
 def tokens_gather_kernel(
-    turned, shape_out, outs, side, beside, cols, chained, line, x_ref, w_ref, *refs
+    turned, shape_out, outs, keep, side, beside, cols, chained, line, x_ref, w_ref, *refs
 ):
     refs = list(refs)
     chain_w = refs.pop(0) if chained else None
     left = refs.pop(0) if side else None
     outer = (refs.pop(0), refs.pop(0)) if beside else None
-    held = refs.pop(0)
+    held = refs.pop(0) if keep else None
     results = [refs.pop(0) for _ in range(outs)]
     grad = refs.pop(0) if side else None
     outer_grad = refs.pop(0) if beside else None
     chain_out = refs.pop(0) if chained else None
     total = refs.pop(0) if side else None
+    if not keep:
+        held = refs.pop(0)
     send, recv = refs
     tokens = x_ref.shape[0]
     across = w_ref.shape[1 if turned else 2]
@@ -1000,7 +1038,20 @@
 
 
 def tokens_gather(
-    x, w, turned, kinds, shape_out, n, m, number, riders=(), left=None, outer=(), cols=0, chain=()
+    x,
+    w,
+    turned,
+    kinds,
+    shape_out,
+    n,
+    m,
+    number,
+    riders=(),
+    left=None,
+    outer=(),
+    cols=0,
+    chain=(),
+    keep=True,
 ):
     tokens, width = x.shape
     across = w.shape[0] * w.shape[1 if turned else 2]
@@ -1013,18 +1064,21 @@
             turned,
             shape_out,
             len(kinds),
+            keep,
             side,
             len(outer) > 0,
             cols,
             len(chain) > 0,
         ),
         (x, w) + tuple(chain) + ((left,) if side else ()) + tuple(outer),
-        (jax.ShapeDtypeStruct((tokens * n, width), x.dtype),)
+        tuple(jax.ShapeDtypeStruct((tokens * n, width), x.dtype) for _ in range(int(keep)))
         + tuple(jax.ShapeDtypeStruct(shape, kind) for kind in kinds)
         + tuple(jax.ShapeDtypeStruct(grad, jnp.bfloat16) for grad in grads)
         + outer_shapes(outer)
         + tuple(jax.ShapeDtypeStruct((tokens * n, w2.shape[1]), jnp.bfloat16) for w2 in chain),
-        [pltpu.VMEM(grad, jnp.float32) for grad in grads] + gather_sems(n // 2),
+        [pltpu.VMEM(grad, jnp.float32) for grad in grads]
+        + [pltpu.VMEM((tokens * n, width), x.dtype) for _ in range(int(not keep))]
+        + gather_sems(n // 2),
         riders,
         n,
         m,
@@ -1102,10 +1156,10 @@
     mixed_ref,
     left,
     right,
-    held,
     grad_ref,
     out_ref,
     outer_grad,
+    held,
     keys_sum,
     values_sum,
     out_sum,
@@ -1170,12 +1224,12 @@
         )
         + tuple(outer),
         (
-            jax.ShapeDtypeStruct((total, width), jnp.bfloat16),
             jax.ShapeDtypeStruct((total, 3 * wide), jnp.bfloat16),
             jax.ShapeDtypeStruct((wide, width), jnp.bfloat16),
         )
         + outer_shapes(outer),
         [
+            pltpu.VMEM((total, width), jnp.bfloat16),
             pltpu.VMEM((total, wide), jnp.float32),
             pltpu.VMEM((total, wide), jnp.float32),
             pltpu.VMEM((wide, width), jnp.float32),
@@ -1186,6 +1240,15 @@
         m,
         number,
     )
+
+
+def gelu_both(value):
+    factor = math.sqrt(2.0 / math.pi)
+    square = value * value
+    bent = jnp.tanh(factor * value * (1.0 + 0.044715 * square))
+    half = 0.5 * (1.0 + bent)
+    slope = half + 0.5 * value * (1.0 - bent * bent) * factor * (1.0 + 3 * 0.044715 * square)
+    return slope, value * half
 
 
 def local(
@@ -1287,12 +1350,12 @@
     stream_mid = stream + attended
     normed_mlp, inverse_mlp = layer_forward(stream_mid)
     input_mlp = (normed_mlp * (1.0 + scale_mlp) + shift_mlp).astype(jnp.bfloat16)
-    all_mlp, upper_proj, activated, projected = tokens_gather(
+    all_mlp, slope, activated, projected = tokens_gather(
         input_mlp,
         up_weight[None],
         False,
-        (jnp.float32, jnp.bfloat16),
-        lambda value: (value, jax.nn.gelu(value, approximate=True)),
+        (jnp.bfloat16, jnp.bfloat16),
+        gelu_both,
         n,
         m,
         5,
@@ -1305,8 +1368,7 @@
     grad_final = grad_final_low.astype(jnp.float32)
     all_final = gather_rows(lax.optimization_barrier((grad_final_low, qkv_rows))[0])
     grad_act = jnp.einsum("le,fe->lf", all_final, proj_weight, preferred_element_type=jnp.float32)
-    gelu_pull = jax.vjp(partial(jax.nn.gelu, approximate=True), upper_proj)[1]
-    grad_upper = gelu_pull(grad_act)[0].astype(jnp.bfloat16)
+    grad_upper = (grad_act * slope.astype(jnp.float32)).astype(jnp.bfloat16)
     grad_normed_mlp, grad_proj = tokens_scatter(
         grad_upper, up_weight[None], True, n, m, 6, (), (activated, all_final)
     )
@@ -1314,7 +1376,7 @@
         grad_normed_mlp, normed_mlp, inverse_mlp, scale_mlp
     )
     grad_mid = grad_final + grad_mid_norm
-    all_mid, grad_qkv, grad_out, grad_up, sums_proj = attend_gather(
+    grad_qkv, grad_out, grad_up, sums_proj = attend_gather(
         grad_mid.astype(jnp.bfloat16),
         out_weight,
         qkv_rows,
@@ -1339,7 +1401,7 @@
             ).reshape(n, -1)
         ]
     )
-    all_stream, grad_residual, grad_down, grad_qkv_weight, sums_up, ada_columns = tokens_gather(
+    grad_residual, grad_down, grad_qkv_weight, sums_up, ada_columns = tokens_gather(
         grad_stream.astype(jnp.bfloat16),
         down_matrix[None],
         True,
@@ -1355,6 +1417,7 @@
         down_patch,
         (all_attend, grad_qkv),
         canvas_cols if fused else 0,
+        keep=False,
     )
     ada_columns = added(ada_columns).reshape(-1)[: columns.shape[0]]
     if not fused:

time: 1020 us -> 996 us (0.976)
  Pallas kernels: 894 us -> 870 us
    pallas_call x14, Pallas kernels: 894 us -> 870 us  [comm_call(): pl.pallas_call(body, out_shape=tuple(out_shapes) + ride_shapes, in_specs=...]
  transfers between devices with their start and end apart: 2 -> 2, of which waited for: 0 -> 0; matrix products, arithmetic and copies ran while one was open for 3% -> 2% of each run, Pallas kernels for 20% -> 20%
where the time goes in v8:
time: 996 us; the launch traced here: 986 us
  Pallas kernels  870 us (87%)
  other arithmetic  57.6 us (6%)
  local copies, waits for them, and re-layouts  25.8 us (3%)
  matrix products  17.5 us (2%)
  between operations  15 us (2%)
    pallas_call x14, Pallas kernels, comm_call(): pl.pallas_call(body, out_shape=tuple(out_shapes) + ride_shapes, in_specs=...  870 us
  transfers between devices with their start and end apart: 2, of which 0 were waited for; matrix products, arithmetic and copies ran while one was open for 2% of the time, Pallas kernels for 20%

profile of v8, /device:TPU:9, one launch (start us, length us, event | category | flops | bytes accessed | tf_op | source)
XLA Modules:
  0.0 985.9 jit_solution(1500448917431511444)
XLA Ops:
  7.2 1.5 copy-done
  8.8 1.7 fusion
  10.4 27.8 %shard_map.254 = (f32[8,8,128]{2,1,0:T(8,128)}, bf16[8,512,128]{2,1,0:T(8,128)(2,1)}) custom-call(f32[8,128]{1,0:T(8,128)} %bitcast.177, bf16[512,1024]{1,0:T(8,128)(2,1)} %bitcast.168), custom_call_target="tpu_custom_call" | custom-call | tf_op jit(solution)/shard_map/pallas_call | solution.py:414
  38.3 1.9 convert_reduce_fusion.6
  40.5 1.8 multiply_reduce_fusion.1
  46.0 2.3 pad_maximum_fusion
  48.3 74.5 %shard_map.255 = f32[4096,128]{1,0:T(8,128)} custom-call(bf16[4352,384]{1,0:T(8,128)(2,1)} %bitcast.146, bf16[3,384,1024]{2,1,0:T(8,128)(2,1)} %bitcast.153), custom_call_target="tpu_custom_call" | custom-call | tf_op jit(solution)/shard_map/pallas_call | solution.py:414
  122.8 2.1 add_reduce_fusion
  125.3 2.2 multiply_reduce_fusion
  127.9 3.6 multiply_convert_fusion.1
  132.3 2.3 pad_maximum_fusion.1
  134.7 75.6 %shard_map.256 = f32[4096,128]{1,0:T(8,128)} custom-call(bf16[4352,384]{1,0:T(8,128)(2,1)} %bitcast.148, bf16[3,384,1024]{2,1,0:T(8,128)(2,1)} %bitcast.155), custom_call_target="tpu_custom_call" | custom-call | tf_op jit(solution)/shard_map/pallas_call | solution.py:414
  210.3 3.3 fusion.4
  214.3 1.2 reshape.486.refs_0_.refs_2_
  215.6 41.2 %shard_map.257 = f32[128,2048]{1,0:T(8,128)} custom-call(bf16[1024,512]{1,0:T(8,128)(2,1)} %reshape.486.refs_0_.refs_2_, bf16[1,512,2048]{2,1,0:T(8,128)(2,1)} %bitcast.157), custom_call_target="tpu_custom_call" | custom-call | tf_op jit(solution)/shard_map/pallas_call | solution.py:414
  256.8 1.4 reduce_sum.293
  258.2 1.5 multiply_reduce_fusion.7
  259.7 1.0 add_convert_fusion.3.refs_0_
  260.8 40.8 %shard_map.258 = (bf16[1024,2048]{1,0:T(8,128)(2,1)}, bf16[1024,768]{1,0:T(8,128)(2,1)}) custom-call(bf16[128,2048]{1,0:T(8,128)(2,1)} %add_convert_fusion.3.refs_0_, bf16[3,2048,256]{2,1,0:T(8,128)(2,1)} %refs_1_.5), custom_call_target="tpu_custom_call" | custom-call | tf_op jit(solution)/shard_map/pallas_call | solution.py:414
  302.2 1.3 fusion.20
  304.2 82.4 %shard_map.259 = (f32[128,2048]{1,0:T(8,128)}, bf16[1024,256]{1,0:T(8,128)(2,1)}) custom-call(bf16[1024,768]{1,0:T(8,128)(2,1)} %get-tuple-element.55.refs_0_.refs_2_, f32[8,1024]{1,0:T(8,128)} %broadcast_in_dim.24.refs_1_, bf16[256,2048]{1,0:T(8,128)(2,1)} %refs_1_.4), custom_call_target="tpu_custom_call" | custom-call | tf_op jit(solution)/shard_map/pallas_call | solution.py:414
  386.6 1.4 fusion.31
  388.9 1.0 add_convert_fusion.2.refs_0_
  390.0 40.8 %shard_map.260 = (bf16[1024,2048]{1,0:T(8,128)(2,1)}, bf16[1024,1024]{1,0:T(8,128)(2,1)}, bf16[1024,1024]{1,0:T(8,128)(2,1)}, bf16[1024,2048]{1,0:T(8,128)(2,1)}) custom-call(bf16[128,2048]{1,0:T(8,128)(2,1)} %add_convert_fusion.2.refs_0_, bf16[1,2048,1024]{2,1,0:T(8,128)(2,1)} %bitcast.150, bf16[1024,2048]{1,0:T(8,128)(2,1)} %refs_2_.3), custom_call_target="tpu_custom_call" | custom-call | tf_op jit(solution)/shard_map/pallas_call | solution.py:414
  430.8 2.6 copy.30
  435.9 1.9 slice_bitcast_fusion.refs_3_
  437.7 9.9 %multiply_convert_fusion.refs_0_.refs_7_ = bf16[1024,1024]{1,0:T(8,128)(2,1)} fusion(bf16[1024,1024]{1,0:T(8,128)(2,1)} %get-tuple-element.59, bf16[1024,2048]{1,0:T(8,128)(2,1)} %all-gather.2.cloned.1.call-done.refs_3_, bf16[1024,2048]{1,0:T(8,128)(2,1)} %refs_2_.3), kind=kOutput, calls=%fused_computation.2 | convolution fusion | flops 4298113024 | bytes 12582912 | tf_op jit(solution)/shard_map/le,fe->lf/dot_general | solution.py:1370
  447.7 74.0 %shard_map.261 = (f32[128,2048]{1,0:T(8,128)}, bf16[1024,2048]{1,0:T(8,128)(2,1)}) custom-call(bf16[1024,1024]{1,0:T(8,128)(2,1)} %multiply_convert_fusion.refs_0_.refs_7_, bf16[1,2048,1024]{2,1,0:T(8,128)(2,1)} %bitcast.151, bf16[1024,1024]{1,0:T(8,128)(2,1)} %get-tuple-element.60.refs_2_, bf16[1024,2048]{1,0:T(8,128)(2,1)} %all-gather.2.cloned.1.call-done.refs_3_), custom_call_target="tpu_custom_call" | custom-call | tf_op jit(solution)/shard_map/pallas_call | solution.py:414
  521.6 2.0 multiply_reduce_fusion.2
  523.7 3.8 fusion.30
  528.4 55.1 %shard_map.262 = (bf16[1024,768]{1,0:T(8,128)(2,1)}, bf16[256,2048]{1,0:T(8,128)(2,1)}, bf16[2048,1024]{1,0:T(8,128)(2,1)}, bf16[4,1024,512]{2,1,0:T(8,128)(2,1)}) custom-call(bf16[128,2048]{1,0:T(8,128)(2,1)} %get-tuple-element.103.refs_0_, bf16[256,2048]{1,0:T(8,128)(2,1)} %refs_1_.4, bf16[1024,768]{1,0:T(8,128)(2,1)} %get-tuple-element.55.refs_0_.refs_2_, ...), custom_call_target="tpu_custom_call" | custom-call | tf_op jit(solution)/shard_map/pallas_call | solution.py:414
  583.5 40.8 %shard_map.263 = f32[128,2048]{1,0:T(8,128)} custom-call(bf16[1024,768]{1,0:T(8,128)(2,1)} %get-tuple-element.65.refs_0_.refs_4_, bf16[3,2048,256]{2,1,0:T(8,128)(2,1)} %refs_1_.5), custom_call_target="tpu_custom_call" | custom-call | tf_op jit(solution)/shard_map/pallas_call | solution.py:414
  624.3 1.8 multiply_reduce_fusion.3
  626.3 1.3 add_convert_fusion.refs_0_
  627.6 55.2 %shard_map.264 = (f32[4096,128]{1,0:T(8,128)}, bf16[2048,512]{1,0:T(8,128)(2,1)}, bf16[2048,768]{1,0:T(8,128)(2,1)}, bf16[4,512,1024]{2,1,0:T(8,128)(2,1)}, f32[8,8,128]{2,1,0:T(8,128)}) custom-call(bf16[128,2048]{1,0:T(8,128)(2,1)} %add_convert_fusion.refs_0_, bf16[1,512,2048]{2,1,0:T(8,128)(2,1)} %bitcast.158, bf16[1024,512]{1,0:T(8,128)(2,1)} %reshape.486.refs_0_.refs_2_, ...), custom_call_target="tpu_custom_call" | custom-call | tf_op jit(solution)/shard_map/pallas_call | solution.py:414
  682.8 2.7 convert_element_type.106.refs_0_
  686.1 75.5 %shard_map.265 = (bf16[4096,128]{1,0:T(8,128)(2,1)}, bf16[4,256,1152]{2,1,0:T(8,128)(2,1)}, f32[8,128]{1,0:T(8,128)}, bf16[4,8,1,64,512]{4,3,2,1,0:T(8,128)(2,1)...) custom-call(bf16[4096,128]{1,0:T(8,128)(2,1)} %convert_element_type.106.refs_0_, ...), custom_call_target="tpu_custom_call" | custom-call | tf_op jit(solution)/shard_map/pallas_call | solution.py:414
  763.9 2.9 reduce_sum.306.refs_8_
  766.8 101.5 %shard_map.266 = (bf16[4096,128]{1,0:T(8,128)(2,1)}, bf16[4,256,1152]{2,1,0:T(8,128)(2,1)}, f32[8,128]{1,0:T(8,128)}, bf16[4,8,1,32,1152]{4,3,2,1,0:T(8,128)(2,1...) custom-call(bf16[4096,128]{1,0:T(8,128)(2,1)} %get-tuple-element.73.refs_0_, bf16[3,384,1024]{2,1,0:T(8,128)(2,1)} %bitcast.154, ...), custom_call_target="tpu_custom_call" | custom-call | tf_op jit(solution)/shard_map/pallas_call | solution.py:414
  869.0 1.7 fusion.33
  870.7 3.0 reduce_sum.307.refs_2_
  874.3 84.6 %shard_map.267 = (f32[9,256,128]{2,1,0:T(8,128)}, f32[32,16,128]{2,1,0:T(8,128)}, f32[9,256,128]{2,1,0:T(8,128)}, bf16[512,1024]{1,0:T(8,128)(2,1)}) custom-call(bf16[8,4,32,1152]{3,2,1,0:T(8,128)(2,1)} %bitcast.161, f32[16,128]{1,0:T(8,128)} %pad_maximum_fusion.4.refs_1_, bf16[8,32,1152]{2,1,0:T(8,128)(2,1)} %reduce_sum.307.refs_2_, ...), custom_call_target="tpu_custom_call" | custom-call | tf_op jit(solution)/shard_map/pallas_call | solution.py:414
  961.3 2.0 fusion.5
  963.3 1.1 fusion.22
  964.3 2.7 convert_reduce_fusion.5
  968.0 2.3 convert_reduce_fusion.1
  971.0 2.0 convert_reduce_fusion
  973.0 1.2 pad_maximum_fusion.2
  (126 shorter events, 24.8 us)
Async XLA Ops:
  7.2 1.6 copy-start
  7.2 430.5 %all-gather.2.cloned.1.call-start = ((), (), s32[]{:S(2)}) async-start(), calls=%async_computation.2 | async-start | bytes 4718592 | tf_op jit(solution)/shard_map/all_gather | solution.py:62
  38.3 5.9 copy-start.3
  44.9 1.0 copy-start.13
  44.9 0.9 copy-start.15
  213.6 2.0 copy-start.17
  256.8 3.0 copy-start.1
  260.8 40.9 %copy-start.20 = (s32[1,2]{1,0:T(1,128)S(1)}, s32[1,2]{1,0:T(1,128)}, u32[]{:S(2)}) copy-start(s32[1,2]{1,0:T(1,128)} %param.17) | copy-start | bytes 28
  301.6 222.1 %reduce-scatter.2.cloned.1.call-start = ((), (), s32[]{:S(2)}) async-start(), calls=%async_computation.1 | async-start | bytes 4718592 | tf_op jit(solution)/shard_map/reduce_scatter | solution.py:66
  388.0 1.0 copy-start.2
  624.3 1.9 copy-start.4
  624.3 1.9 copy-start.5
  626.2 1.3 copy-start.14
  682.8 2.7 copy-start.16
  874.3 86.9 %copy-start.18 = (f32[4,16,128]{2,1,0:T(8,128)S(1)}, f32[4,16,128]{2,1,0:T(8,128)}, u32[]{:S(2)}) copy-start(f32[4,16,128]{2,1,0:T(8,128)} %get-tuple-element.85) | copy-start | bytes 98308
  874.3 86.9 %copy-start.19 = (f32[4,8,128]{2,1,0:T(8,128)S(1)}, f32[4,8,128]{2,1,0:T(8,128)}, u32[]{:S(2)}) copy-start(f32[4,8,128]{2,1,0:T(8,128)} %get-tuple-element.86) | copy-start | bytes 49156
  961.3 5.8 copy-start.10
  964.3 3.7 copy-start.7
  968.0 2.9 copy-start.6
  972.9 1.7 copy-start.12
  972.9 2.7 copy-start.9
  974.6 2.0 copy-start.8
  975.6 2.0 copy-start.11
Sparse Core Ops, SparseCore 0:
  301.7 84.1 all-gather.1
  431.0 63.6 reduce-scatter.1

commit v9 on v8

--- a/solution.py
+++ b/solution.py
@@ -204,8 +204,10 @@
 
 
 class Rider:
-    def __init__(self, axis, array, cut=None, beside=False):
+    def __init__(self, axis, array, cut=None, beside=False, part=(0, 1), inside=False):
         self.axes = (axis,)
+        self.part = part
+        self.inside = inside
         self.axis = axis
         self.array = array
         self.cut = cut
@@ -216,6 +218,7 @@
         shape = list(self.array.shape)
         if self.cut is not None:
             shape[self.cut] //= count
+        shape[0] //= self.part[1]
         self.columns = shape[-1]
         if self.beside:
             shape[-1] *= count
@@ -233,6 +236,9 @@
         size = self.array.shape[self.cut] // count
         where = [slice(None)] * len(self.array.shape)
         where[self.cut] = pl.ds(pl.multiple_of(index * size, size), size)
+        if self.part[1] > 1:
+            rows = self.array.shape[0] // self.part[1]
+            where[0] = pl.ds(self.part[0] * rows, rows)
         return ref.at[tuple(where)]
 
     def copies(self, line, src, dst, send, recv):
@@ -270,6 +276,7 @@
 class Settle:
     def __init__(self, array, summed, taps, placed):
         self.axes = ("dp", "mp")
+        self.inside = True
         self.array = array
         self.summed = summed
         self.taps = taps
@@ -356,7 +363,9 @@
                 dst[tap, pl.ds(half * own, own)] = block.T
 
 
-def comm_call(kernel, inputs, out_shapes, scratch, riders, n, m, number, neighbours=True):
+def comm_call(
+    kernel, inputs, out_shapes, scratch, riders, n, m, number, neighbours=True, after=None
+):
     chips = n // 2
     sizes = {"dp": m, "mp": n, "all": m * n}
     ride_shapes = tuple(rider.result(sizes) for rider in riders)
@@ -410,6 +419,8 @@
                 rider.middle(phase, *refs_in)
         for rider, refs_in in riding:
             rider.finish(*refs_in)
+        if after is not None:
+            after(main_in, main_out, ride_out)
 
     return pl.pallas_call(
         body,
@@ -418,7 +429,7 @@
         + [any_spec] * nr,
         out_specs=tuple(
             whole(no)
-            + [whole(1)[0] if isinstance(rider, Settle) else any_spec for rider in riders]
+            + [whole(1)[0] if rider.inside else any_spec for rider in riders]
         ),
         scratch_shapes=list(scratch)
         + ([pltpu.SemaphoreType.DMA((len(large),))] if large else [])
@@ -706,7 +717,68 @@
     return jnp.where(c == 0, low, high), jnp.where(c == 0, high, low)
 
 
-def conv_scatter_kernel(breadth, line, x_ref, w_ref, o_ref, *scratch):
+def group_matrix(own, size, count):
+    groups = [lax.broadcasted_iota(jnp.int32, (own, own), axis) // size for axis in range(2)]
+    return jnp.where(groups[0] == groups[1], 1.0 / (count * size), 0.0)
+
+
+def norm_spread(values, gain, spread_ref, stat_ref, size, breadth):
+    pixels, own = values.shape
+    tile = 512
+    matrix = group_matrix(own, size, pixels)
+    stat_ref[...] = jnp.zeros_like(stat_ref)
+    column = lax.broadcasted_iota(jnp.int32, (tile, own), 0) % breadth
+
+    def tiles(body):
+        @pl.loop(0, pixels // tile)
+        def _(index):
+            base = pl.multiple_of(index * tile, tile)
+            body(base, pl.ds(base, tile))
+
+    def add(base, rows):
+        stat_ref[0:1] += jnp.sum(values[rows], axis=0, keepdims=True)
+
+    tiles(add)
+    average = jnp.dot(stat_ref[...], matrix, precision=PRECISE)[0:1]
+
+    def square(base, rows):
+        centre = values[rows] - average
+        stat_ref[1:2] += jnp.sum(centre * centre, axis=0, keepdims=True)
+
+    tiles(square)
+    inverse = lax.rsqrt(jnp.dot(stat_ref[...], matrix, precision=PRECISE)[1:2] + GROUP_EPSILON)
+    stat_ref[2:3] = inverse
+
+    def write(base, rows):
+        normed = (values[rows] - average) * inverse
+        values[rows] = normed
+        pre_act = normed * gain
+        hidden = pre_act / (1.0 + jnp.exp(-pre_act))
+        below = pl.ds(base + breadth, tile)
+        left = jnp.where(column == 0, 0.0, pltpu.roll(hidden, 1, 0))
+        right = jnp.where(column == breadth - 1, 0.0, pltpu.roll(hidden, tile - 1, 0))
+        for place, value in enumerate((left, hidden, right)):
+            spread_ref[below, place * own : (place + 1) * own] = value.astype(jnp.bfloat16)
+
+    tiles(write)
+    nothing = jnp.zeros((breadth, 3 * own), jnp.bfloat16)
+    spread_ref[pl.ds(0, breadth)] = nothing
+    spread_ref[pl.ds(breadth + pixels, breadth)] = nothing
+
+
+def norm_shapes(pixels, own, cols):
+    return (
+        jax.ShapeDtypeStruct((pixels, own), jnp.float32),
+        jax.ShapeDtypeStruct((pixels + 2 * cols, 3 * own), jnp.bfloat16),
+        jax.ShapeDtypeStruct((8, own), jnp.float32),
+    )
+
+
+def conv_scatter_kernel(breadth, size, line, x_ref, w_ref, *refs):
+    normed = size > 0
+    v_ref, refs = (refs[0], refs[1:]) if normed else (None, refs)
+    o_ref, refs = refs[0], refs[1:]
+    spread_ref, stat_ref, *scratch = refs if normed else (None, None) + tuple(refs)
     pixels, own = o_ref.shape
     tile = 512
 
@@ -728,9 +800,11 @@
             other[pl.ds(base, tile)] = second.astype(jnp.bfloat16)
 
     def finish(part, rows, total):
-        o_ref[rows] = total
+        o_ref[rows] = total + v_ref[0:1] if normed else total
 
     line_scatter(line, scratch, CONV_PARTS, produce, finish, tile)
+    if normed:
+        norm_spread(o_ref, v_ref[1:2], spread_ref, stat_ref, size, breadth)
 
 
 def side_by_side(hidden):
@@ -741,16 +815,22 @@
     )
 
 
-def conv_scatter_fused(spread, kernel, cols, n, m, number, riders=()):
+def rows_of(*vectors):
+    rows = jnp.stack(vectors)
+    return jnp.pad(rows, ((0, 8 - rows.shape[0]), (0, 0)))
+
+
+def conv_scatter_fused(spread, kernel, cols, n, m, number, shift=None, gain=None, size=0):
     own = kernel.shape[2] // n
     depth = kernel.shape[1]
     pixels = spread.shape[0] - 2 * cols
     return comm_call(
-        partial(conv_scatter_kernel, cols),
-        (spread, kernel.reshape(3, 3 * depth, kernel.shape[2])),
-        (jax.ShapeDtypeStruct((pixels, own), jnp.float32),),
+        partial(conv_scatter_kernel, cols, size),
+        (spread, kernel.reshape(3, 3 * depth, kernel.shape[2]))
+        + ((rows_of(shift, gain),) if size else ()),
+        norm_shapes(pixels, own, cols)[: 3 if size else 1],
         scatter_scratch(n // 2, pixels, own, CONV_PARTS),
-        riders,
+        (),
         n,
         m,
         number,
@@ -837,9 +917,7 @@
         stat_ref[0:1] += jnp.sum(through * normed, axis=0, keepdims=True)
         stat_ref[1:2] += jnp.sum(through, axis=0, keepdims=True)
 
-    groups = [lax.broadcasted_iota(jnp.int32, (own, own), axis) // size for axis in range(2)]
-    spread = jnp.where(groups[0] == groups[1], 1.0 / (pixels * size), 0.0)
-    means = jnp.dot(stat_ref[...] * gain, spread, precision=PRECISE)
+    means = jnp.dot(stat_ref[...] * gain, group_matrix(own, size, pixels), precision=PRECISE)
     second_mean, first_mean = means[0:1], means[1:2]
 
     @pl.loop(0, pixels // tile)
@@ -860,7 +938,7 @@
     pixels, own = grad_low.shape
     depth = kernel.shape[1]
     chips = n // 2
-    vectors = jnp.concatenate([gain[None], inverse[None], jnp.zeros((6, own), jnp.float32)])
+    vectors = rows_of(gain, inverse)
     return comm_call(
         partial(conv_back_kernel, cols, size, len(more) > 0),
         (grad_low, kernel.reshape(3, 3 * depth, kernel.shape[2]), spread, normed, vectors)
@@ -1090,6 +1168,35 @@
     return comm_call(lambda line: None, (), (), [], riders, n, m, number, neighbours=False)
 
 
+def exchange_norm(image_rows, gain, size, cols, riders, n, m, number):
+    own = image_rows.shape[1] // n
+    count = image_rows.shape[0]
+
+    def after(main_in, main_out, ride_out):
+        normed, spread_ref, stat_ref = main_out
+
+        @pl.loop(0, n)
+        def _(index):
+            normed[pl.ds(pl.multiple_of(index * count, count), count)] = ride_out[0][index].astype(
+                jnp.float32
+            )
+
+        norm_spread(normed, main_in[0][0:1], spread_ref, stat_ref, size, cols)
+
+    return comm_call(
+        lambda line, *refs: None,
+        (rows_of(gain),),
+        norm_shapes(count * n, own, cols),
+        [],
+        (Rider("mp", image_rows, 1, inside=True),) + tuple(riders),
+        n,
+        m,
+        number,
+        neighbours=False,
+        after=after,
+    )
+
+
 def tiled_up(vector):
     count = -(-vector.shape[0] // 1024) * 1024
     return jnp.pad(vector.astype(jnp.float32), (0, count - vector.shape[0])).reshape(-1, 128)
@@ -1151,7 +1258,6 @@
     g_ref,
     w_ref,
     x_ref,
-    kt_ref,
     valid_ref,
     mixed_ref,
     left,
@@ -1197,9 +1303,12 @@
             inner = jnp.sum(probs * grad_probs, axis=0, keepdims=True)
             grad_scores = (probs * (grad_probs - inner) * scale).astype(jnp.bfloat16)
             keys_sum[:, place] += product(grad_scores, query, False)
-            grad_ref[rows, where[0]] = product(kt_ref[place], grad_scores, False).T.astype(
-                jnp.bfloat16
-            )
+            grad_ref[rows, where[0]] = lax.dot_general(
+                grad_scores,
+                x_ref[:, where[1]],
+                (((0,), (0,)), ((), ())),
+                preferred_element_type=jnp.float32,
+            ).astype(jnp.bfloat16)
         add_outer(out_sum, mixed_ref, held, rows)
 
     line_gather(line, g_ref, slot, send, recv, on_own, on_pair)
@@ -1218,7 +1327,6 @@
             grad_mid,
             out_weight,
             qkv_rows,
-            qkv_rows[:, wide : 2 * wide].T,
             jnp.broadcast_to(valid[:, None], (total, 128)),
             mixed_low,
         )
@@ -1287,11 +1395,14 @@
     fused = own % 128 == 0 and n == 2 * m
     shift_vector = jnp.dot(embedding, shift_weight, preferred_element_type=jnp.float32)[0]
     columns = jnp.dot(embedding, ada_weight, preferred_element_type=jnp.float32)[0]
+    own_first = lax.dynamic_slice_in_dim(gain_first, me_mp * own, own)
+    own_second = lax.dynamic_slice_in_dim(gain_second, me_mp * own, own)
     riders = (Rider("mp", tiled_up(columns)),)
     if fused:
-        modulation, pixels_low = exchange(
-            riders + (Rider("mp", image[0].reshape(-1, channel_count), 1),), n, m, 12
+        normed_first, spread_first, stats, pixels_low, modulation = exchange_norm(
+            image[0].reshape(-1, channel_count), own_first, size, canvas_cols, riders, n, m, 12
         )
+        inverse_first = stats[2]
     else:
         (modulation,) = exchange(riders, n, m, 12)
         pixels_low = lax.all_to_all(image[0], "mp", 2, 0, tiled=True)
@@ -1300,32 +1411,30 @@
     shift_attend = modulation[width_all : 2 * width_all]
     scale_mlp = modulation[2 * width_all : 3 * width_all]
     shift_mlp = modulation[3 * width_all :]
-    own_first = lax.dynamic_slice_in_dim(gain_first, me_mp * own, own)
-    own_second = lax.dynamic_slice_in_dim(gain_second, me_mp * own, own)
 
     pixels = pixels_low.astype(jnp.float32).reshape(pixel_total, own)
-    normed_first, inverse_first = group_forward(pixels, size)
-    hidden_first = (
-        jax.nn.silu(normed_first * own_first)
-        .astype(jnp.bfloat16)
-        .reshape(rows_all, canvas_cols, own)
-    )
-    spread_first = side_by_side(hidden_first)
     if fused:
-        (conv_output,) = conv_scatter_fused(spread_first, conv_first, canvas_cols, n, m, 0)
-    else:
-        conv_output = conv_scatter(hidden_first, conv_first, n)
-    conv_output = conv_output + shift_vector
-    normed_second, inverse_second = group_forward(conv_output, size)
-    hidden_second = (
-        jax.nn.silu(normed_second * own_second)
-        .astype(jnp.bfloat16)
-        .reshape(rows_all, canvas_cols, own)
-    )
-    spread_second = side_by_side(hidden_second)
-    if fused:
+        hidden_first = hidden_second = None
+        normed_second, spread_second, stats = conv_scatter_fused(
+            spread_first, conv_first, canvas_cols, n, m, 0, shift_vector, own_second, size
+        )
+        inverse_second = stats[2]
         (conv_again,) = conv_scatter_fused(spread_second, conv_second, canvas_cols, n, m, 1)
     else:
+        spread_first = spread_second = None
+        normed_first, inverse_first = group_forward(pixels, size)
+        hidden_first = (
+            jax.nn.silu(normed_first * own_first)
+            .astype(jnp.bfloat16)
+            .reshape(rows_all, canvas_cols, own)
+        )
+        conv_output = conv_scatter(hidden_first, conv_first, n) + shift_vector
+        normed_second, inverse_second = group_forward(conv_output, size)
+        hidden_second = (
+            jax.nn.silu(normed_second * own_second)
+            .astype(jnp.bfloat16)
+            .reshape(rows_all, canvas_cols, own)
+        )
         conv_again = conv_scatter(hidden_second, conv_second, n)
     residual = pixels + conv_again
     down_patch = (
@@ -1376,7 +1485,7 @@
         grad_normed_mlp, normed_mlp, inverse_mlp, scale_mlp
     )
     grad_mid = grad_final + grad_mid_norm
-    grad_qkv, grad_out, grad_up, sums_proj = attend_gather(
+    grad_qkv, grad_out, grad_up = attend_gather(
         grad_mid.astype(jnp.bfloat16),
         out_weight,
         qkv_rows,
@@ -1386,9 +1495,17 @@
         n,
         m,
         7,
-        (Rider("dp", grad_proj, 1),),
-    )
-    (grad_normed_attend,) = tokens_scatter(grad_qkv, qkv_weight, True, n, m, 8)
+        (),
+    )
+    grad_normed_attend, sums_proj, sums_out = tokens_scatter(
+        grad_qkv,
+        qkv_weight,
+        True,
+        n,
+        m,
+        8,
+        (Rider("dp", grad_proj, 1, part=(0, 2)), Rider("dp", grad_out, 1)),
+    )
     grad_stream_norm, grad_scale_attend, grad_shift_attend = layer_backward(
         grad_normed_attend, normed_attend, inverse_attend, scale_attend
     )
@@ -1401,7 +1518,7 @@
             ).reshape(n, -1)
         ]
     )
-    grad_residual, grad_down, grad_qkv_weight, sums_up, ada_columns = tokens_gather(
+    grad_residual, grad_down, grad_qkv_weight, sums_more, ada_columns = tokens_gather(
         grad_stream.astype(jnp.bfloat16),
         down_matrix[None],
         True,
@@ -1411,7 +1528,7 @@
         m,
         9,
         (
-            Rider("dp", grad_up, 0),
+            Rider("dp", grad_proj, 1, part=(1, 2)),
             Rider("mp", grad_modulation, 0),
         ),
         down_patch,
@@ -1462,11 +1579,10 @@
         (
             Rider("dp", unsettled(grad_down, m, n), 1),
             Rider("dp", grad_qkv_weight, 0),
-            Rider("dp", grad_out, 1),
             Rider("dp", jnp.concatenate([tiled_up(embedding[0]), tiled_up(ada_columns)])),
         ),
     )
-    sums_down, sums_qkv, sums_out, every_small = rode_second
+    sums_down, sums_qkv, every_small = rode_second
     image_turned, parts_first, grad_gain_first, _, rode_first = back(
         grad_conv_low,
         hidden_first,
@@ -1480,10 +1596,11 @@
             Rider("dp", unsettled(parts_second, m, n), 1),
             Rider("dp", tiled_up(grad_shift)),
             Settle(added(sums_down)[:, 0].astype(jnp.bfloat16), True, 4, fused),
+            Rider("dp", grad_up, 0),
         ),
         (grad_residual,),
     )
-    sums_second, every_shift, pieces_down = rode_first
+    sums_second, every_shift, pieces_down, sums_up = rode_first
     embed_term = jnp.dot(
         grad_shift[None], shift_weight.astype(jnp.float32).T, precision=PRECISE
     ) + jnp.dot(ada_columns[None], ada_weight.astype(jnp.float32).T, precision=PRECISE)
@@ -1545,7 +1662,7 @@
         qkv_grad,
         added(sums_out),
         added(sums_up),
-        added(sums_proj),
+        jnp.concatenate([added(sums_proj), added(sums_more)]),
     )
 
 

time: 996 us -> 981 us (0.985)
  other arithmetic: 57.6 us -> 41.2 us
  transfers between devices with their start and end apart: 2 -> 2, of which waited for: 0 -> 0; matrix products, arithmetic and copies ran while one was open for 2% -> 2% of each run, Pallas kernels for 20% -> 21%
where the time goes in v9:
time: 981 us; the launch traced here: 971 us
  Pallas kernels  877 us (89%)
  other arithmetic  41.2 us (4%)
  local copies, waits for them, and re-layouts  19.3 us (2%)
  matrix products  18.6 us (2%)
  between operations  14.9 us (2%)
    pallas_call x14, Pallas kernels, comm_call(): pl.pallas_call(body, out_shape=tuple(out_shapes) + ride_shapes, in_specs=...  877 us
  transfers between devices with their start and end apart: 2, of which 0 were waited for; matrix products, arithmetic and copies ran while one was open for 2% of the time, Pallas kernels for 21%

profile of v9, /device:TPU:9, one launch (start us, length us, event | category | flops | bytes accessed | tf_op | source)
XLA Modules:
  0.0 971.4 jit_solution(1753245616916015400)
XLA Ops:
  7.2 1.3 fusion.16
  8.9 1.7 fusion
  11.9 34.4 %shard_map.254 = (f32[4096,128]{1,0:T(8,128)}, bf16[4352,384]{1,0:T(8,128)(2,1)}, f32[8,128]{1,0:T(8,128)}, bf16[8,512,128]{2,1,0:T(8,128)(2,1)}, f32[8,8,128]{2,1,0:T(8,128)}) custom-call(f32[8,128]{1,0:T(8,128)} %pad.22.refs_0_, bf16[512,1024]{1,0:T(8,128)(2,1)} %bitcast.152, f32[8,128]{1,0:T(8,128)} %bitcast.161), custom_call_target="tpu_custom_call" | custom-call | tf_op jit(solution)/shard_map/pallas_call | solution.py:425
  47.7 81.7 %shard_map.255 = (f32[4096,128]{1,0:T(8,128)}, bf16[4352,384]{1,0:T(8,128)(2,1)}, f32[8,128]{1,0:T(8,128)}) custom-call(bf16[4352,384]{1,0:T(8,128)(2,1)} %get-tuple-element.62.refs_0_.refs_2_, bf16[3,384,1024]{2,1,0:T(8,128)(2,1)} %bitcast.139, f32[8,128]{1,0:T(8,128)} %select_maximum_fusion.3.refs_2_), custom_call_target="tpu_custom_call" | custom-call | tf_op jit(solution)/shard_map/pallas_call | solution.py:425
  129.4 75.5 %shard_map.256 = f32[4096,128]{1,0:T(8,128)} custom-call(bf16[4352,384]{1,0:T(8,128)(2,1)} %get-tuple-element.63.refs_0_.refs_2_, bf16[3,384,1024]{2,1,0:T(8,128)(2,1)} %bitcast.137), custom_call_target="tpu_custom_call" | custom-call | tf_op jit(solution)/shard_map/pallas_call | solution.py:425
  204.9 1.8 fusion.3
  207.5 1.2 reshape.362.refs_0_.refs_2_
  208.7 41.2 %shard_map.257 = f32[128,2048]{1,0:T(8,128)} custom-call(bf16[1024,512]{1,0:T(8,128)(2,1)} %reshape.362.refs_0_.refs_2_, bf16[1,512,2048]{2,1,0:T(8,128)(2,1)} %bitcast.141), custom_call_target="tpu_custom_call" | custom-call | tf_op jit(solution)/shard_map/pallas_call | solution.py:425
  249.9 1.4 reduce_sum.222
  251.4 1.5 multiply_reduce_fusion.5
  252.8 1.0 add_convert_fusion.3.refs_0_
  253.9 39.1 %shard_map.258 = (bf16[1024,2048]{1,0:T(8,128)(2,1)}, bf16[1024,768]{1,0:T(8,128)(2,1)}) custom-call(bf16[128,2048]{1,0:T(8,128)(2,1)} %add_convert_fusion.3.refs_0_, bf16[3,2048,256]{2,1,0:T(8,128)(2,1)} %refs_1_.5), custom_call_target="tpu_custom_call" | custom-call | tf_op jit(solution)/shard_map/pallas_call | solution.py:425
  293.7 1.3 fusion.20
  295.6 81.7 %shard_map.259 = (f32[128,2048]{1,0:T(8,128)}, bf16[1024,256]{1,0:T(8,128)(2,1)}) custom-call(bf16[1024,768]{1,0:T(8,128)(2,1)} %get-tuple-element.65.refs_0_.refs_2_, f32[8,1024]{1,0:T(8,128)} %broadcast_in_dim.8.refs_1_, bf16[256,2048]{1,0:T(8,128)(2,1)} %refs_1_.4), custom_call_target="tpu_custom_call" | custom-call | tf_op jit(solution)/shard_map/pallas_call | solution.py:425
  377.3 1.4 fusion.31
  379.7 1.0 add_convert_fusion.2.refs_0_
  380.7 41.9 %shard_map.260 = (bf16[1024,2048]{1,0:T(8,128)(2,1)}, bf16[1024,1024]{1,0:T(8,128)(2,1)}, bf16[1024,1024]{1,0:T(8,128)(2,1)}, bf16[1024,2048]{1,0:T(8,128)(2,1)}) custom-call(bf16[128,2048]{1,0:T(8,128)(2,1)} %add_convert_fusion.2.refs_0_, bf16[1,2048,1024]{2,1,0:T(8,128)(2,1)} %bitcast.135, bf16[1024,2048]{1,0:T(8,128)(2,1)} %refs_2_.3), custom_call_target="tpu_custom_call" | custom-call | tf_op jit(solution)/shard_map/pallas_call | solution.py:425
  425.8 9.9 %multiply_convert_fusion.refs_0_.refs_6_ = bf16[1024,1024]{1,0:T(8,128)(2,1)} fusion(bf16[1024,1024]{1,0:T(8,128)(2,1)} %get-tuple-element.69, bf16[1024,2048]{1,0:T(8,128)(2,1)} %all-gather.2.cloned.1.call-done.refs_3_, bf16[1024,2048]{1,0:T(8,128)(2,1)} %refs_2_.3), kind=kOutput, calls=%fused_computation.3 | convolution fusion | flops 4298113024 | bytes 12582912 | tf_op jit(solution)/shard_map/le,fe->lf/dot_general | solution.py:1479
  435.7 77.2 %shard_map.261 = (f32[128,2048]{1,0:T(8,128)}, bf16[1024,2048]{1,0:T(8,128)(2,1)}) custom-call(bf16[1024,1024]{1,0:T(8,128)(2,1)} %multiply_convert_fusion.refs_0_.refs_6_, bf16[1,2048,1024]{2,1,0:T(8,128)(2,1)} %bitcast.136, bf16[1024,1024]{1,0:T(8,128)(2,1)} %get-tuple-element.70.refs_2_, bf16[1024,2048]{1,0:T(8,128)(2,1)} %all-gather.2.cloned.1.call-done.refs_3_), custom_call_target="tpu_custom_call" | custom-call | tf_op jit(solution)/shard_map/pallas_call | solution.py:425
  513.0 2.0 multiply_reduce_fusion
  515.0 3.8 fusion.30
  518.8 1.0 broadcast_in_dim.10.refs_3_
  519.8 41.2 %shard_map.262 = (bf16[1024,768]{1,0:T(8,128)(2,1)}, bf16[256,2048]{1,0:T(8,128)(2,1)}, bf16[2048,1024]{1,0:T(8,128)(2,1)}) custom-call(bf16[128,2048]{1,0:T(8,128)(2,1)} %get-tuple-element.119.refs_0_, bf16[256,2048]{1,0:T(8,128)(2,1)} %refs_1_.4, bf16[1024,768]{1,0:T(8,128)(2,1)} %get-tuple-element.65.refs_0_.refs_2_, ...), custom_call_target="tpu_custom_call" | custom-call | tf_op jit(solution)/shard_map/pallas_call | solution.py:425
  561.0 49.3 %shard_map.263 = (f32[128,2048]{1,0:T(8,128)}, bf16[4,512,512]{2,1,0:T(8,128)(2,1)}, bf16[4,256,512]{2,1,0:T(8,128)(2,1)}) custom-call(bf16[1024,768]{1,0:T(8,128)(2,1)} %get-tuple-element.74.refs_0_.refs_4_, bf16[3,2048,256]{2,1,0:T(8,128)(2,1)} %refs_1_.5, bf16[1024,2048]{1,0:T(8,128)(2,1)} %get-tuple-element.75.refs_2_.refs_5_, ...), custom_call_target="tpu_custom_call" | custom-call | tf_op jit(solution)/shard_map/pallas_call | solution.py:425
  610.3 1.8 multiply_reduce_fusion.1
  612.3 1.3 add_convert_fusion.refs_0_
  613.5 44.0 %shard_map.264 = (f32[4096,128]{1,0:T(8,128)}, bf16[2048,512]{1,0:T(8,128)(2,1)}, bf16[2048,768]{1,0:T(8,128)(2,1)}, bf16[4,512,512]{2,1,0:T(8,128)(2,1)}, f32[8,8,128]{2,1,0:T(8,128)}) custom-call(bf16[128,2048]{1,0:T(8,128)(2,1)} %add_convert_fusion.refs_0_, bf16[1,512,2048]{2,1,0:T(8,128)(2,1)} %bitcast.142, bf16[1024,512]{1,0:T(8,128)(2,1)} %reshape.362.refs_0_.refs_2_, ...), custom_call_target="tpu_custom_call" | custom-call | tf_op jit(solution)/shard_map/pallas_call | solution.py:425
  658.3 2.7 convert_element_type.100.refs_0_
  661.6 85.4 %shard_map.265 = (bf16[4096,128]{1,0:T(8,128)(2,1)}, bf16[4,256,1152]{2,1,0:T(8,128)(2,1)}, f32[8,128]{1,0:T(8,128)}, bf16[4,8,1,64,512]{4,3,2,1,0:T(8,128)(2,1)...) custom-call(bf16[4096,128]{1,0:T(8,128)(2,1)} %convert_element_type.100.refs_0_, bf16[3,384,1024]{2,1,0:T(8,128)(2,1)} %bitcast.138, ...), custom_call_target="tpu_custom_call" | custom-call | tf_op jit(solution)/shard_map/pallas_call | solution.py:425
  747.8 1.0 fusion.27
  748.8 1.0 convert_reduce_fusion.3
  749.8 1.7 fusion.33
  752.5 2.9 reduce_sum.235.refs_8_
  755.3 101.2 %shard_map.266 = (bf16[4096,128]{1,0:T(8,128)(2,1)}, bf16[4,256,1152]{2,1,0:T(8,128)(2,1)}, f32[8,128]{1,0:T(8,128)}, bf16[4,8,1,32,1152]{4,3,2,1,0:T(8,128)(2,1...) custom-call(bf16[4096,128]{1,0:T(8,128)(2,1)} %get-tuple-element.85.refs_0_, ...), custom_call_target="tpu_custom_call" | custom-call | tf_op jit(solution)/shard_map/pallas_call | solution.py:425
  857.9 2.0 fusion.4
  859.9 1.1 fusion.22
  861.0 3.0 reduce_sum.236.refs_2_
  864.6 83.5 %shard_map.267 = (f32[9,256,128]{2,1,0:T(8,128)}, f32[32,16,128]{2,1,0:T(8,128)}, f32[9,256,128]{2,1,0:T(8,128)}, bf16[512,1024]{1,0:T(8,128)(2,1)}) custom-call(bf16[8,4,32,1152]{3,2,1,0:T(8,128)(2,1)} %bitcast.145, f32[16,128]{1,0:T(8,128)} %pad_maximum_fusion.3.refs_1_, bf16[8,32,1152]{2,1,0:T(8,128)(2,1)} %reduce_sum.236.refs_2_, ...), custom_call_target="tpu_custom_call" | custom-call | tf_op jit(solution)/shard_map/pallas_call | solution.py:425
  948.1 1.0 reshape.372
  950.3 2.1 convert_reduce_fusion.2
  952.9 1.7 copy-done.5
  954.6 2.2 convert_reduce_fusion
  956.8 1.6 pad_maximum_fusion
  958.4 1.2 pad_maximum_fusion.1
  960.1 1.0 copy.59
  961.1 1.0 copy.60
  962.1 1.0 copy.61
  963.1 1.0 copy.62
  (91 shorter events, 16.8 us)
Async XLA Ops:
  7.2 1.7 copy-start
  7.2 418.6 %all-gather.2.cloned.1.call-start = ((), (), s32[]{:S(2)}) async-start(), calls=%async_computation.2 | async-start | bytes 4718592 | tf_op jit(solution)/shard_map/all_gather | solution.py:62
  129.3 75.5 %copy-start.14 = (bf16[8,512,128]{2,1,0:T(8,128)(2,1)S(1)}, bf16[8,512,128]{2,1,0:T(8,128)(2,1)}, u32[]{:S(2)}) copy-start(bf16[8,512,128]{2,1,0:T(8,128)(2,1)} %get-tuple-element.61) | copy-start | bytes 3145732
  249.9 3.0 copy-start.1
  253.9 39.2 %copy-start.18 = (s32[1,2]{1,0:T(1,128)S(1)}, s32[1,2]{1,0:T(1,128)}, u32[]{:S(2)}) copy-start(s32[1,2]{1,0:T(1,128)} %param.17) | copy-start | bytes 28
  293.0 222.0 %reduce-scatter.2.cloned.1.call-start = ((), (), s32[]{:S(2)}) async-start(), calls=%async_computation.1 | async-start | bytes 4718592 | tf_op jit(solution)/shard_map/reduce_scatter | solution.py:66
  378.7 1.0 copy-start.2
  422.6 0.7 copy-start.16
  610.3 1.9 copy-start.3
  610.3 1.9 copy-start.4
  612.2 1.3 copy-start.15
  661.6 86.3 %copy-start.13 = (bf16[1024,128]{1,0:T(8,128)(2,1)S(1)}, bf16[1024,128]{1,0:T(8,128)(2,1)}, u32[]{:S(2)}) copy-start(bf16[1024,128]{1,0:T(8,128)(2,1)} %param.22) | copy-start | bytes 786436
  661.6 87.2 %copy-start.10 = (bf16[4,256,512]{2,1,0:T(8,128)(2,1)S(1)}, bf16[4,256,512]{2,1,0:T(8,128)(2,1)}, u32[]{:S(2)}) copy-start(bf16[4,256,512]{2,1,0:T(8,128)(2,1)} %get-tuple-element.104) | copy-start | bytes 3145732
  747.0 4.5 copy-start.7
  751.5 0.9 copy-start.17
  949.1 3.3 copy-start.6
  952.4 2.2 copy-start.5
  958.4 1.7 copy-start.12
  958.4 2.7 copy-start.9
  960.1 2.0 copy-start.8
  961.1 2.0 copy-start.11
Sparse Core Ops, SparseCore 0:
  293.1 83.4 all-gather.1
  422.7 66.3 reduce-scatter.1

commit v10 on v9

--- a/solution.py
+++ b/solution.py
@@ -114,22 +114,6 @@
 
 def added(received):
     return jnp.sum(received.astype(jnp.float32), axis=0)
-
-
-def layer_forward(stream):
-    centre = stream - jnp.mean(stream, axis=1, keepdims=True)
-    inverse = lax.rsqrt(jnp.mean(centre * centre, axis=1, keepdims=True) + LAYER_EPSILON)
-    return (centre * inverse, inverse)
-
-
-def layer_backward(incoming, normed, inverse, scale_vec):
-    through = incoming * (1.0 + scale_vec)
-    outgoing = inverse * (
-        through
-        - jnp.mean(through, axis=1, keepdims=True)
-        - normed * jnp.mean(through * normed, axis=1, keepdims=True)
-    )
-    return (outgoing, jnp.sum(incoming * normed, axis=0), jnp.sum(incoming, axis=0))
 
 
 MESH = pl.DeviceIdType.MESH
@@ -989,6 +973,82 @@
     return [partial(step, start) for start in range(0, left.shape[1], cut)]
 
 
+class NormAfter:
+    def __init__(self, scale, shift, more=()):
+        self.inputs = (rows_of(scale, shift),) + tuple(more)
+
+    def shapes(self, tokens, width):
+        return (
+            jax.ShapeDtypeStruct((tokens, width), jnp.float32),
+            jax.ShapeDtypeStruct((tokens, 128), jnp.float32),
+            jax.ShapeDtypeStruct((tokens, width), jnp.bfloat16),
+        )
+
+    def run(self, in_refs, o_ref, out_refs):
+        v_ref, normed_ref, inverse_ref, low_ref = in_refs[0], *out_refs
+        tile = 16
+
+        @pl.loop(0, o_ref.shape[0] // tile)
+        def _(index):
+            rows = pl.ds(pl.multiple_of(index * tile, tile), tile)
+            stream = o_ref[rows]
+            for ref in in_refs[1:]:
+                stream = stream + ref[rows]
+            o_ref[rows] = stream
+            centre = stream - jnp.mean(stream, axis=1, keepdims=True)
+            inverse = lax.rsqrt(jnp.mean(centre * centre, axis=1, keepdims=True) + LAYER_EPSILON)
+            normed = centre * inverse
+            normed_ref[rows] = normed
+            inverse_ref[rows] = jnp.broadcast_to(inverse, (tile, 128))
+            low_ref[rows] = (normed * (1.0 + v_ref[0:1]) + v_ref[1:2]).astype(jnp.bfloat16)
+
+
+class NormBack:
+    def __init__(self, scale, normed, inverse, carry):
+        self.inputs = (rows_of(scale), normed, inverse, carry)
+
+    def shapes(self, tokens, width):
+        return (
+            jax.ShapeDtypeStruct((tokens, width), jnp.bfloat16),
+            jax.ShapeDtypeStruct((8, width), jnp.float32),
+        )
+
+    def run(self, in_refs, o_ref, out_refs):
+        v_ref, normed_ref, inverse_ref, carry_ref = in_refs
+        low_ref, sum_ref = out_refs
+        tile = 16
+        sum_ref[...] = jnp.zeros_like(sum_ref)
+
+        @pl.loop(0, o_ref.shape[0] // tile)
+        def _(index):
+            rows = pl.ds(pl.multiple_of(index * tile, tile), tile)
+            incoming, normed = o_ref[rows], normed_ref[rows]
+            sum_ref[0:1] += jnp.sum(incoming * normed, axis=0, keepdims=True)
+            sum_ref[1:2] += jnp.sum(incoming, axis=0, keepdims=True)
+            through = incoming * (1.0 + v_ref[0:1])
+            outgoing = inverse_ref[rows][:, 0:1] * (
+                through
+                - jnp.mean(through, axis=1, keepdims=True)
+                - normed * jnp.mean(through * normed, axis=1, keepdims=True)
+            )
+            grad = carry_ref[rows].astype(jnp.float32) + outgoing
+            o_ref[rows] = grad
+            low_ref[rows] = grad.astype(jnp.bfloat16)
+
+
+def followed(kernel, ni, no, post):
+    count = len(post.inputs)
+
+    def run(line, *refs):
+        inputs, more, rest = refs[:ni], refs[ni : ni + count], refs[ni + count :]
+        outputs, rest = rest[:no], rest[no:]
+        made = len(post.shapes(8, 128))
+        kernel(line, *inputs, *outputs, *rest[made:])
+        post.run(more, outputs[0], rest[:made])
+
+    return run
+
+
 def tokens_scatter_kernel(turned, beside, line, x_ref, w_ref, *refs):
     side = ()
     if beside:
@@ -1024,13 +1084,20 @@
     return (jax.ShapeDtypeStruct((outer[0].shape[1], outer[1].shape[1]), jnp.bfloat16),)
 
 
-def tokens_scatter(x, w, turned, n, m, number, riders=(), outer=()):
+def tokens_scatter(x, w, turned, n, m, number, post, riders=(), outer=()):
     tokens = x.shape[0] // n
     width = w.shape[1] if turned else w.shape[2]
     return comm_call(
-        partial(tokens_scatter_kernel, turned, len(outer) > 0),
-        (x, w) + tuple(outer),
-        (jax.ShapeDtypeStruct((tokens, width), jnp.float32),) + outer_shapes(outer),
+        followed(
+            partial(tokens_scatter_kernel, turned, len(outer) > 0),
+            2 + len(outer),
+            2 if outer else 1,
+            post,
+        ),
+        (x, w) + tuple(outer) + post.inputs,
+        (jax.ShapeDtypeStruct((tokens, width), jnp.float32),)
+        + outer_shapes(outer)
+        + post.shapes(tokens, width),
         scatter_scratch(n // 2, TOKEN_PARTS * tokens, width // TOKEN_PARTS, TOKEN_PARTS),
         riders,
         n,
@@ -1234,17 +1301,18 @@
     line_scatter(line, scratch, TOKEN_PARTS, produce, finish, tokens)
 
 
-def attend_scatter(qkv_rows, valid, out_weight, n, m, number):
+def attend_scatter(qkv_rows, valid, out_weight, n, m, number, post):
     total = qkv_rows.shape[0]
     tokens = total // n
     width = out_weight.shape[1]
     return comm_call(
-        attend_scatter_kernel,
-        (qkv_rows, jnp.broadcast_to(valid[None], (8, total)), out_weight),
+        followed(attend_scatter_kernel, 3, 2, post),
+        (qkv_rows, jnp.broadcast_to(valid[None], (8, total)), out_weight) + post.inputs,
         (
             jax.ShapeDtypeStruct((tokens, width), jnp.float32),
             jax.ShapeDtypeStruct((total, out_weight.shape[0]), jnp.bfloat16),
-        ),
+        )
+        + post.shapes(tokens, width),
         scatter_scratch(n // 2, TOKEN_PARTS * tokens, width // TOKEN_PARTS, TOKEN_PARTS),
         (),
         n,
@@ -1444,9 +1512,9 @@
         .reshape(token_total, 4 * own)
     )
     down_matrix = down_weight.reshape(4 * own, width_all)
-    (stream,) = tokens_scatter(down_patch, down_matrix[None], False, n, m, 2)
-    normed_attend, inverse_attend = layer_forward(stream)
-    input_attend = (normed_attend * (1.0 + scale_attend) + shift_attend).astype(jnp.bfloat16)
+    stream, normed_attend, inverse_attend, input_attend = tokens_scatter(
+        down_patch, down_matrix[None], False, n, m, 2, NormAfter(scale_attend, shift_attend)
+    )
     all_attend, qkv_rows = tokens_gather(
         input_attend, qkv_weight, False, (jnp.bfloat16,), lambda value: (value,), n, m, 3
     )
@@ -1455,10 +1523,9 @@
         token_index % token_cols < extents[0, 1]
     )
     valid = key_valid.astype(jnp.float32)
-    attended, mixed_low = attend_scatter(qkv_rows, valid, out_weight, n, m, 4)
-    stream_mid = stream + attended
-    normed_mlp, inverse_mlp = layer_forward(stream_mid)
-    input_mlp = (normed_mlp * (1.0 + scale_mlp) + shift_mlp).astype(jnp.bfloat16)
+    stream_mid, mixed_low, normed_mlp, inverse_mlp, input_mlp = attend_scatter(
+        qkv_rows, valid, out_weight, n, m, 4, NormAfter(scale_mlp, shift_mlp, (stream,))
+    )
     all_mlp, slope, activated, projected = tokens_gather(
         input_mlp,
         up_weight[None],
@@ -1474,19 +1541,22 @@
     output = final_stream.astype(jnp.bfloat16).reshape(1, token_rows, token_cols, width_all)
 
     grad_final_low = cotangent[0].reshape(local_tokens, width_all)
-    grad_final = grad_final_low.astype(jnp.float32)
     all_final = gather_rows(lax.optimization_barrier((grad_final_low, qkv_rows))[0])
     grad_act = jnp.einsum("le,fe->lf", all_final, proj_weight, preferred_element_type=jnp.float32)
     grad_upper = (grad_act * slope.astype(jnp.float32)).astype(jnp.bfloat16)
-    grad_normed_mlp, grad_proj = tokens_scatter(
-        grad_upper, up_weight[None], True, n, m, 6, (), (activated, all_final)
-    )
-    grad_mid_norm, grad_scale_mlp, grad_shift_mlp = layer_backward(
-        grad_normed_mlp, normed_mlp, inverse_mlp, scale_mlp
-    )
-    grad_mid = grad_final + grad_mid_norm
+    grad_mid, grad_proj, grad_mid_low, mlp_sums = tokens_scatter(
+        grad_upper,
+        up_weight[None],
+        True,
+        n,
+        m,
+        6,
+        NormBack(scale_mlp, normed_mlp, inverse_mlp, grad_final_low),
+        (),
+        (activated, all_final),
+    )
     grad_qkv, grad_out, grad_up = attend_gather(
-        grad_mid.astype(jnp.bfloat16),
+        grad_mid_low,
         out_weight,
         qkv_rows,
         valid,
@@ -1497,29 +1567,24 @@
         7,
         (),
     )
-    grad_normed_attend, sums_proj, sums_out = tokens_scatter(
+    _, grad_stream_low, attend_sums, sums_proj, sums_out = tokens_scatter(
         grad_qkv,
         qkv_weight,
         True,
         n,
         m,
         8,
+        NormBack(scale_attend, normed_attend, inverse_attend, grad_mid),
         (Rider("dp", grad_proj, 1, part=(0, 2)), Rider("dp", grad_out, 1)),
     )
-    grad_stream_norm, grad_scale_attend, grad_shift_attend = layer_backward(
-        grad_normed_attend, normed_attend, inverse_attend, scale_attend
-    )
-    grad_stream = grad_mid + grad_stream_norm
     grad_modulation = jnp.concatenate(
         [
             tiled_up(piece)
-            for piece in jnp.concatenate(
-                [grad_scale_attend, grad_shift_attend, grad_scale_mlp, grad_shift_mlp]
-            ).reshape(n, -1)
+            for piece in jnp.concatenate([attend_sums[:2], mlp_sums[:2]]).reshape(n, -1)
         ]
     )
     grad_residual, grad_down, grad_qkv_weight, sums_more, ada_columns = tokens_gather(
-        grad_stream.astype(jnp.bfloat16),
+        grad_stream_low,
         down_matrix[None],
         True,
         (jnp.float32,),

time: 981 us -> 973 us (level)
  other arithmetic: 41.2 us -> 27.8 us
  transfers between devices with their start and end apart: 2 -> 2, of which waited for: 0 -> 0; matrix products, arithmetic and copies ran while one was open for 2% -> 5% of each run, Pallas kernels for 21% -> 63%
where the time goes in v10:
time: 973 us; the launch traced here: 964 us
  Pallas kernels  885 us (91%)
  other arithmetic  27.8 us (3%)
  local copies, waits for them, and re-layouts  18.8 us (2%)
  matrix products  16.8 us (2%)
  between operations  14.7 us (2%)
    pallas_call x14, Pallas kernels, comm_call(): pl.pallas_call(body, out_shape=tuple(out_shapes) + ride_shapes, in_specs=...  885 us
  transfers between devices with their start and end apart: 2, of which 0 were waited for; matrix products, arithmetic and copies ran while one was open for 5% of the time, Pallas kernels for 63%

profile of v10, /device:TPU:9, one launch (start us, length us, event | category | flops | bytes accessed | tf_op | source)
XLA Modules:
  0.0 963.6 jit_solution(5749320064253349155)
XLA Ops:
  7.3 1.5 copy-done
  8.8 1.7 fusion
  10.6 0.8 dynamic-slice_bitcast_fusion.1
  12.6 34.5 %shard_map.254 = (f32[4096,128]{1,0:T(8,128)}, bf16[4352,384]{1,0:T(8,128)(2,1)}, f32[8,128]{1,0:T(8,128)}, bf16[8,512,128]{2,1,0:T(8,128)(2,1)}, f32[8,8,128]{2,1,0:T(8,128)}) custom-call(f32[8,128]{1,0:T(8,128)} %pad.36.refs_0_, bf16[512,1024]{1,0:T(8,128)(2,1)} %bitcast.123, f32[8,128]{1,0:T(8,128)} %bitcast.136), custom_call_target="tpu_custom_call" | custom-call | tf_op jit(solution)/shard_map/pallas_call | solution.py:409
  47.0 81.7 %shard_map.255 = (f32[4096,128]{1,0:T(8,128)}, bf16[4352,384]{1,0:T(8,128)(2,1)}, f32[8,128]{1,0:T(8,128)}) custom-call(bf16[4352,384]{1,0:T(8,128)(2,1)} %get-tuple-element.72.refs_0_.refs_2_, bf16[3,384,1024]{2,1,0:T(8,128)(2,1)} %bitcast.109, f32[8,128]{1,0:T(8,128)} %select_maximum_fusion.5.refs_2_), custom_call_target="tpu_custom_call" | custom-call | tf_op jit(solution)/shard_map/pallas_call | solution.py:409
  128.8 75.5 %shard_map.256 = f32[4096,128]{1,0:T(8,128)} custom-call(bf16[4352,384]{1,0:T(8,128)(2,1)} %get-tuple-element.73.refs_0_.refs_2_, bf16[3,384,1024]{2,1,0:T(8,128)(2,1)} %bitcast.107), custom_call_target="tpu_custom_call" | custom-call | tf_op jit(solution)/shard_map/pallas_call | solution.py:409
  204.3 1.8 fusion.3
  206.1 0.8 copy.44
  206.9 1.2 reshape.214.refs_0_.refs_2_
  208.1 0.7 fusion.32
  208.8 43.2 %shard_map.257 = (f32[128,2048]{1,0:T(8,128)}, f32[128,2048]{1,0:T(8,128)}, f32[128,128]{1,0:T(8,128)}, bf16[128,2048]{1,0:T(8,128)(2,1)}) custom-call(bf16[1024,512]{1,0:T(8,128)(2,1)} %reshape.214.refs_0_.refs_2_, bf16[1,512,2048]{2,1,0:T(8,128)(2,1)} %bitcast.111, f32[8,2048]{1,0:T(8,128)} %get-tuple-element.144.refs_2_), custom_call_target="tpu_custom_call" | custom-call | tf_op jit(solution)/shard_map/pallas_call | solution.py:409
  252.1 39.2 %shard_map.258 = (bf16[1024,2048]{1,0:T(8,128)(2,1)}, bf16[1024,768]{1,0:T(8,128)(2,1)}) custom-call(bf16[128,2048]{1,0:T(8,128)(2,1)} %get-tuple-element.75.refs_0_, bf16[3,2048,256]{2,1,0:T(8,128)(2,1)} %refs_1_.5), custom_call_target="tpu_custom_call" | custom-call | tf_op jit(solution)/shard_map/pallas_call | solution.py:409
  291.9 1.3 fusion.20
  293.2 0.7 fusion.33
  294.5 83.0 %shard_map.259 = (f32[128,2048]{1,0:T(8,128)}, bf16[1024,256]{1,0:T(8,128)(2,1)}, f32[128,2048]{1,0:T(8,128)}, f32[128,128]{1,0:T(8,128)}, bf16[128,2048]{1,0:T(8,128)(2,1)}) custom-call(bf16[1024,768]{1,0:T(8,128)(2,1)} %get-tuple-element.76.refs_0_.refs_2_, f32[8,1024]{1,0:T(8,128)} %broadcast_in_dim.8.refs_1_, bf16[256,2048]{1,0:T(8,128)(2,1)} %refs_1_.4, ...), custom_call_target="tpu_custom_call" | custom-call | tf_op jit(solution)/shard_map/pallas_call | solution.py:409
  377.5 42.4 %shard_map.260 = (bf16[1024,2048]{1,0:T(8,128)(2,1)}, bf16[1024,1024]{1,0:T(8,128)(2,1)}, bf16[1024,1024]{1,0:T(8,128)(2,1)}, bf16[1024,2048]{1,0:T(8,128)(2,1)}) custom-call(bf16[128,2048]{1,0:T(8,128)(2,1)} %get-tuple-element.79.refs_0_, bf16[1,2048,1024]{2,1,0:T(8,128)(2,1)} %bitcast.105, bf16[1024,2048]{1,0:T(8,128)(2,1)} %refs_2_.3), custom_call_target="tpu_custom_call" | custom-call | tf_op jit(solution)/shard_map/pallas_call | solution.py:409
  420.0 0.7 slice.81
  420.7 0.7 slice.82
  422.6 9.9 %multiply_convert_fusion.refs_0_.refs_6_ = bf16[1024,1024]{1,0:T(8,128)(2,1)} fusion(bf16[1024,1024]{1,0:T(8,128)(2,1)} %get-tuple-element.82, bf16[1024,2048]{1,0:T(8,128)(2,1)} %all-gather.2.cloned.1.call-done.refs_3_, bf16[1024,2048]{1,0:T(8,128)(2,1)} %refs_2_.3), kind=kOutput, calls=%fused_computation.3 | convolution fusion | flops 4298113024 | bytes 12582912 | tf_op jit(solution)/shard_map/le,fe->lf/dot_general | solution.py:1545
  432.5 77.9 %shard_map.261 = (f32[128,2048]{1,0:T(8,128)}, bf16[1024,2048]{1,0:T(8,128)(2,1)}, bf16[128,2048]{1,0:T(8,128)(2,1)}, f32[8,2048]{1,0:T(8,128)}) custom-call(bf16[1024,1024]{1,0:T(8,128)(2,1)} %multiply_convert_fusion.refs_0_.refs_6_, bf16[1,2048,1024]{2,1,0:T(8,128)(2,1)} %bitcast.106, bf16[1024,1024]{1,0:T(8,128)(2,1)} %get-tuple-element.83.refs_2_, ...), custom_call_target="tpu_custom_call" | custom-call | tf_op jit(solution)/shard_map/pallas_call | solution.py:409
  510.4 0.8 slice.80
  511.3 1.0 broadcast_in_dim.10.refs_3_
  512.3 41.2 %shard_map.262 = (bf16[1024,768]{1,0:T(8,128)(2,1)}, bf16[256,2048]{1,0:T(8,128)(2,1)}, bf16[2048,1024]{1,0:T(8,128)(2,1)}) custom-call(bf16[128,2048]{1,0:T(8,128)(2,1)} %get-tuple-element.86.refs_0_, bf16[256,2048]{1,0:T(8,128)(2,1)} %refs_1_.4, bf16[1024,768]{1,0:T(8,128)(2,1)} %get-tuple-element.76.refs_0_.refs_2_, ...), custom_call_target="tpu_custom_call" | custom-call | tf_op jit(solution)/shard_map/pallas_call | solution.py:409
  553.5 52.5 %shard_map.263 = (f32[128,2048]{1,0:T(8,128)}, bf16[128,2048]{1,0:T(8,128)(2,1)}, f32[8,2048]{1,0:T(8,128)}, bf16[4,512,512]{2,1,0:T(8,128)(2,1)}, bf16[4,256,512]{2,1,0:T(8,128)(2,1)}) custom-call(bf16[1024,768]{1,0:T(8,128)(2,1)} %get-tuple-element.89.refs_0_.refs_4_, bf16[3,2048,256]{2,1,0:T(8,128)(2,1)} %refs_1_.5, ...), custom_call_target="tpu_custom_call" | custom-call | tf_op jit(solution)/shard_map/pallas_call | solution.py:409
  606.0 0.8 slice.79
  607.6 43.8 %shard_map.264 = (f32[4096,128]{1,0:T(8,128)}, bf16[2048,512]{1,0:T(8,128)(2,1)}, bf16[2048,768]{1,0:T(8,128)(2,1)}, bf16[4,512,512]{2,1,0:T(8,128)(2,1)}, f32[8,8,128]{2,1,0:T(8,128)}) custom-call(bf16[128,2048]{1,0:T(8,128)(2,1)} %get-tuple-element.95.refs_0_, bf16[1,512,2048]{2,1,0:T(8,128)(2,1)} %bitcast.112, ...), custom_call_target="tpu_custom_call" | custom-call | tf_op jit(solution)/shard_map/pallas_call | solution.py:409
  651.5 2.7 convert_element_type.86.refs_0_
  654.7 85.3 %shard_map.265 = (bf16[4096,128]{1,0:T(8,128)(2,1)}, bf16[4,256,1152]{2,1,0:T(8,128)(2,1)}, f32[8,128]{1,0:T(8,128)}, bf16[4,8,1,64,512]{4,3,2,1,0:T(8,128)(2,1)...) custom-call(bf16[4096,128]{1,0:T(8,128)(2,1)} %convert_element_type.86.refs_0_, bf16[3,384,1024]{2,1,0:T(8,128)(2,1)} %bitcast.108, ...), custom_call_target="tpu_custom_call" | custom-call | tf_op jit(solution)/shard_map/pallas_call | solution.py:409
  740.1 2.9 reduce_sum.115.refs_8_
  743.6 101.3 %shard_map.266 = (bf16[4096,128]{1,0:T(8,128)(2,1)}, bf16[4,256,1152]{2,1,0:T(8,128)(2,1)}, f32[8,128]{1,0:T(8,128)}, bf16[4,8,1,32,1152]{4,3,2,1,0:T(8,128)(2,1...) custom-call(bf16[4096,128]{1,0:T(8,128)(2,1)} %get-tuple-element.105.refs_0_, ...), custom_call_target="tpu_custom_call" | custom-call | tf_op jit(solution)/shard_map/pallas_call | solution.py:409
  844.8 3.0 reduce_sum.116.refs_2_
  847.8 0.7 slice_bitcast_fusion.3
  848.8 1.7 fusion.35
  851.2 83.6 %shard_map.267 = (f32[9,256,128]{2,1,0:T(8,128)}, f32[32,16,128]{2,1,0:T(8,128)}, f32[9,256,128]{2,1,0:T(8,128)}, bf16[512,1024]{1,0:T(8,128)(2,1)}) custom-call(bf16[8,4,32,1152]{3,2,1,0:T(8,128)(2,1)} %bitcast.115, f32[16,128]{1,0:T(8,128)} %pad_maximum_fusion.4.refs_1_, bf16[8,32,1152]{2,1,0:T(8,128)(2,1)} %reduce_sum.116.refs_2_, ...), custom_call_target="tpu_custom_call" | custom-call | tf_op jit(solution)/shard_map/pallas_call | solution.py:409
  934.8 1.0 reshape.233
  936.6 2.6 convert_reduce_fusion.6
  939.1 1.2 pad_maximum_fusion.1
  940.8 0.9 convert_reduce_fusion.3
  942.1 0.7 copy-done.2
  943.1 1.5 pad_maximum_fusion
  945.1 1.1 fusion.22
  946.1 2.0 fusion.4
  948.1 2.3 convert_reduce_fusion
  950.4 2.1 add_convert_fusion
  952.5 1.0 copy.59
  953.5 1.0 copy.60
  954.5 1.0 copy.61
  955.5 1.0 copy.62
  (83 shorter events, 9.1 us)
Async XLA Ops:
  7.2 1.6 copy-start
  7.2 3.2 copy-start.13
  7.2 3.2 copy-start.10
  7.2 415.4 %all-gather.2.cloned.1.call-start = ((), (), s32[]{:S(2)}) async-start(), calls=%async_computation.2 | async-start | bytes 4718592 | tf_op jit(solution)/shard_map/all_gather | solution.py:62
  128.8 75.5 %copy-start.11 = (bf16[8,512,128]{2,1,0:T(8,128)(2,1)S(1)}, bf16[8,512,128]{2,1,0:T(8,128)(2,1)}, u32[]{:S(2)}) copy-start(bf16[8,512,128]{2,1,0:T(8,128)(2,1)} %get-tuple-element.71) | copy-start | bytes 3145732
  206.1 2.0 copy-start.16
  252.0 39.3 %copy-start.19 = (s32[1,2]{1,0:T(1,128)S(1)}, s32[1,2]{1,0:T(1,128)}, u32[]{:S(2)}) copy-start(s32[1,2]{1,0:T(1,128)} %param.17) | copy-start | bytes 28
  291.3 659.1 %reduce-scatter.2.cloned.1.call-start = ((), (), s32[]{:S(2)}) async-start(), calls=%async_computation.1 | async-start | bytes 4718592 | tf_op jit(solution)/shard_map/reduce_scatter | solution.py:66
  607.0 0.6 copy-start.12
  651.4 2.7 copy-start.14
  740.1 2.9 copy-start.18
  851.2 84.6 %copy-start.15 = (f32[4,16,128]{2,1,0:T(8,128)S(1)}, f32[4,16,128]{2,1,0:T(8,128)}, u32[]{:S(2)}) copy-start(f32[4,16,128]{2,1,0:T(8,128)} %get-tuple-element.120) | copy-start | bytes 98308
  851.2 84.7 %copy-start.17 = (f32[4,8,128]{2,1,0:T(8,128)S(1)}, f32[4,8,128]{2,1,0:T(8,128)}, u32[]{:S(2)}) copy-start(f32[4,8,128]{2,1,0:T(8,128)} %get-tuple-element.121) | copy-start | bytes 49156
  939.1 1.7 copy-start.6
  939.1 2.6 copy-start.3
  940.8 1.9 copy-start.2
  943.0 5.1 copy-start.1
  948.1 2.3 copy-start.7
  950.4 2.1 copy-start.9
  950.4 3.1 copy-start.5
  952.5 2.0 copy-start.4
  953.5 2.0 copy-start.8
Sparse Core Ops, SparseCore 0:
  291.4 83.3 all-gather.1
  420.1 64.9 reduce-scatter.1

commit v11 on v10

--- a/solution.py
+++ b/solution.py
@@ -136,6 +136,7 @@
         self.down = (self.dp, self.mp - 2)
         self.sibling = (self.dp, 2 * self.z + 1 - self.c)
         self.ready = lambda: None
+        self.early = lambda: None
         self.late = lambda: None
 
     def count(self, axis):
@@ -249,6 +250,9 @@
         for copy in self.copies(line, src, dst, send, recv):
             copy.start()
 
+    def early(self, *refs):
+        pass
+
     def middle(self, phase, *refs):
         pass
 
@@ -272,7 +276,7 @@
         self.tail = tuple(self.array.shape[-2:])
         self.total = jax.ShapeDtypeStruct((n,) + self.tail, self.array.dtype)
         self.land = (m, self.ratio) + self.tail
-        self.add = Rider("dp", self.array, None if self.summed else 1)
+        self.add = None if self.summed else Rider("dp", self.array, 1)
         self.outward = Rider("mp", self.total, 0)
         self.inward = Rider("dp", self.total, 0)
         if not self.placed:
@@ -284,51 +288,59 @@
         n, m = sizes["mp"], sizes["dp"]
         dtype = self.array.dtype
         refs = [pltpu.VMEM(self.land, dtype), pltpu.VMEM((n, 1) + self.tail, dtype)]
-        if not self.summed:
-            refs += [pltpu.VMEM((m, n, 1) + self.tail, dtype), pltpu.VMEM((n,) + self.tail, dtype)]
-            refs += self.add.scratch(sizes)
+        refs += [pltpu.VMEM((m, n, 1) + self.tail, dtype), pltpu.VMEM((n,) + self.tail, dtype)]
+        refs += [pltpu.SemaphoreType.DMA((1,))] if self.summed else self.add.scratch(sizes)
         return refs + self.outward.scratch(sizes) + self.inward.scratch(sizes)
 
-    def copies(self, step, line, src, dst, land, stage, *rest):
-        if not self.summed:
-            got, total = rest[:2]
-            if step == 0:
-                return self.add.copies(line, src, got, *rest[2:4])
-            src, rest = total, rest[4:]
-            step -= 1
+    def copies(self, step, line, src, dst, land, stage, got, total, *sems):
+        if step == 0 and self.summed:
+            return [pltpu.make_async_copy(src, got, sems[0].at[0])]
         if step == 0:
-            return self.outward.copies(line, src, stage, *rest[:2])
-        return self.inward.copies(line, stage.at[:, 0], land, *rest[2:4])
+            return self.add.copies(line, src, got, *sems[:2])
+        if step == 1:
+            return self.outward.copies(line, total, stage, *sems[-4:-2])
+        return self.inward.copies(line, stage.at[:, 0], land, *sems[-2:])
 
     def start(self, *refs):
         for copy in self.copies(0, *refs):
             copy.start()
 
+    def add_up(self, *refs):
+        for copy in self.copies(0, *refs):
+            copy.wait()
+        got, total = refs[5:7]
+
+        @pl.loop(0, total.shape[0])
+        def _(index):
+            added_up = got[0, index, 0].astype(jnp.float32)
+            for image in range(1, got.shape[0]):
+                added_up += got[image, index, 0].astype(jnp.float32)
+            total[index] = added_up.astype(total.dtype)
+
+        for copy in self.copies(1, *refs):
+            copy.start()
+
+    def early(self, *refs):
+        if self.summed:
+            self.add_up(*refs)
+
     def middle(self, phase, *refs):
-        if self.summed and phase == 1:
+        if phase == 0 and not self.summed:
+            self.add_up(*refs)
+        elif phase == 1 and self.summed:
             self.end(*refs)
-            return
-        for copy in self.copies(phase, *refs):
-            copy.wait()
-        if not self.summed and phase == 0:
-            got, total = refs[5:7]
-
-            @pl.loop(0, total.shape[0])
-            def _(index):
-                added_up = got[0, index, 0].astype(jnp.float32)
-                for image in range(1, got.shape[0]):
-                    added_up += got[image, index, 0].astype(jnp.float32)
-                total[index] = added_up.astype(total.dtype)
-
-        for copy in self.copies(phase + 1, *refs):
-            copy.start()
+        else:
+            for copy in self.copies(1, *refs):
+                copy.wait()
+            for copy in self.copies(2, *refs):
+                copy.start()
 
     def finish(self, *refs):
         if not self.summed:
             self.end(*refs)
 
     def end(self, *refs):
-        for copy in self.copies(1 if self.summed else 2, *refs):
+        for copy in self.copies(2, *refs):
             copy.wait()
         dst, land = refs[2:4]
         if not self.placed:
@@ -389,15 +401,23 @@
             rest = rest[len(needs) :]
         for rider, refs_in in riding:
             rider.start(*refs_in)
-        phases = [0, 1]
+        phases = [-1, 0, 1]
+
+        def early():
+            phases.pop(0)
+            for rider, refs_in in riding:
+                rider.early(*refs_in)
 
         def late():
             phases.pop(0)
             for rider, refs_in in riding:
                 rider.middle(0, *refs_in)
 
+        line.early = early
         line.late = late
         kernel(line, *main_in, *main_out, *main_scratch)
+        if -1 in phases:
+            early()
         for phase in phases:
             for rider, refs_in in riding:
                 rider.middle(phase, *refs_in)
@@ -458,6 +478,7 @@
 
     across(0, 0, x_ref, line.mp).start()
     slot(line.mp)[...] = x_ref[...]
+    line.early()
     line.ready()
     on_own()
     across(0, 0, x_ref, line.mp).wait_recv()
@@ -1660,7 +1681,7 @@
         (
             Rider("dp", unsettled(parts_second, m, n), 1),
             Rider("dp", tiled_up(grad_shift)),
-            Settle(added(sums_down)[:, 0].astype(jnp.bfloat16), True, 4, fused),
+            Settle(sums_down, True, 4, fused),
             Rider("dp", grad_up, 0),
         ),
         (grad_residual,),
@@ -1675,7 +1696,7 @@
     riders = (
         Settle(unsettled(parts_first, m, n), False, 9, fused),
         Rider("all", small),
-        Settle(added(sums_second)[:, 0].astype(jnp.bfloat16), True, 9, fused),
+        Settle(sums_second, True, 9, fused),
     )
     if fused:
         pieces_first, small, pieces_second, image_turned = exchange(

time: 973 us -> 967 us (level)
  transfers between devices with their start and end apart: 2 -> 2, of which waited for: 0 -> 0; matrix products, arithmetic and copies ran while one was open for 5% -> 4% of each run, Pallas kernels for 63% -> 64%
where the time goes in v11:
time: 967 us; the launch traced here: 957 us
  Pallas kernels  884 us (91%)
  other arithmetic  22 us (2%)
  local copies, waits for them, and re-layouts  19.6 us (2%)
  matrix products  16.8 us (2%)
  between operations  14.7 us (2%)
    pallas_call x14, Pallas kernels, comm_call(): pl.pallas_call(body, out_shape=tuple(out_shapes) + ride_shapes, in_specs=...  884 us
  transfers between devices with their start and end apart: 2, of which 0 were waited for; matrix products, arithmetic and copies ran while one was open for 4% of the time, Pallas kernels for 64%

profile of v11, /device:TPU:9, one launch (start us, length us, event | category | flops | bytes accessed | tf_op | source)
XLA Modules:
  0.0 957.1 jit_solution(6212409231173321530)
XLA Ops:
  7.3 1.5 copy-done
  8.8 1.7 fusion
  10.6 0.8 dynamic-slice_bitcast_fusion.1
  12.6 34.4 %shard_map.254 = (f32[4096,128]{1,0:T(8,128)}, bf16[4352,384]{1,0:T(8,128)(2,1)}, f32[8,128]{1,0:T(8,128)}, bf16[8,512,128]{2,1,0:T(8,128)(2,1)}, f32[8,8,128]{2,1,0:T(8,128)}) custom-call(f32[8,128]{1,0:T(8,128)} %pad.36.refs_0_, bf16[512,1024]{1,0:T(8,128)(2,1)} %bitcast.123, f32[8,128]{1,0:T(8,128)} %bitcast.136), custom_call_target="tpu_custom_call" | custom-call | tf_op jit(solution)/shard_map/pallas_call | solution.py:429
  47.0 81.7 %shard_map.255 = (f32[4096,128]{1,0:T(8,128)}, bf16[4352,384]{1,0:T(8,128)(2,1)}, f32[8,128]{1,0:T(8,128)}) custom-call(bf16[4352,384]{1,0:T(8,128)(2,1)} %get-tuple-element.72.refs_0_.refs_2_, bf16[3,384,1024]{2,1,0:T(8,128)(2,1)} %bitcast.107, f32[8,128]{1,0:T(8,128)} %select_maximum_fusion.5.refs_2_), custom_call_target="tpu_custom_call" | custom-call | tf_op jit(solution)/shard_map/pallas_call | solution.py:429
  128.7 75.6 %shard_map.256 = f32[4096,128]{1,0:T(8,128)} custom-call(bf16[4352,384]{1,0:T(8,128)(2,1)} %get-tuple-element.73.refs_0_.refs_2_, bf16[3,384,1024]{2,1,0:T(8,128)(2,1)} %bitcast.109), custom_call_target="tpu_custom_call" | custom-call | tf_op jit(solution)/shard_map/pallas_call | solution.py:429
  204.3 1.8 fusion.3
  206.1 0.8 copy.44
  206.9 1.2 reshape.210.refs_0_.refs_2_
  208.1 0.7 fusion.32
  208.8 43.3 %shard_map.257 = (f32[128,2048]{1,0:T(8,128)}, f32[128,2048]{1,0:T(8,128)}, f32[128,128]{1,0:T(8,128)}, bf16[128,2048]{1,0:T(8,128)(2,1)}) custom-call(bf16[1024,512]{1,0:T(8,128)(2,1)} %reshape.210.refs_0_.refs_2_, bf16[1,512,2048]{2,1,0:T(8,128)(2,1)} %bitcast.111, f32[8,2048]{1,0:T(8,128)} %get-tuple-element.144.refs_2_), custom_call_target="tpu_custom_call" | custom-call | tf_op jit(solution)/shard_map/pallas_call | solution.py:429
  252.1 39.2 %shard_map.258 = (bf16[1024,2048]{1,0:T(8,128)(2,1)}, bf16[1024,768]{1,0:T(8,128)(2,1)}) custom-call(bf16[128,2048]{1,0:T(8,128)(2,1)} %get-tuple-element.75.refs_0_, bf16[3,2048,256]{2,1,0:T(8,128)(2,1)} %refs_1_.5), custom_call_target="tpu_custom_call" | custom-call | tf_op jit(solution)/shard_map/pallas_call | solution.py:429
  291.9 1.3 fusion.20
  293.2 0.7 fusion.33
  294.5 83.0 %shard_map.259 = (f32[128,2048]{1,0:T(8,128)}, bf16[1024,256]{1,0:T(8,128)(2,1)}, f32[128,2048]{1,0:T(8,128)}, f32[128,128]{1,0:T(8,128)}, bf16[128,2048]{1,0:T(8,128)(2,1)}) custom-call(bf16[1024,768]{1,0:T(8,128)(2,1)} %get-tuple-element.76.refs_0_.refs_2_, f32[8,1024]{1,0:T(8,128)} %broadcast_in_dim.8.refs_1_, bf16[256,2048]{1,0:T(8,128)(2,1)} %refs_1_.4, ...), custom_call_target="tpu_custom_call" | custom-call | tf_op jit(solution)/shard_map/pallas_call | solution.py:429
  377.5 42.5 %shard_map.260 = (bf16[1024,2048]{1,0:T(8,128)(2,1)}, bf16[1024,1024]{1,0:T(8,128)(2,1)}, bf16[1024,1024]{1,0:T(8,128)(2,1)}, bf16[1024,2048]{1,0:T(8,128)(2,1)}) custom-call(bf16[128,2048]{1,0:T(8,128)(2,1)} %get-tuple-element.79.refs_0_, bf16[1,2048,1024]{2,1,0:T(8,128)(2,1)} %bitcast.105, bf16[1024,2048]{1,0:T(8,128)(2,1)} %refs_2_.3), custom_call_target="tpu_custom_call" | custom-call | tf_op jit(solution)/shard_map/pallas_call | solution.py:429
  420.0 0.7 slice.81
  420.7 0.7 slice.82
  422.6 9.9 %multiply_convert_fusion.refs_0_.refs_6_ = bf16[1024,1024]{1,0:T(8,128)(2,1)} fusion(bf16[1024,1024]{1,0:T(8,128)(2,1)} %get-tuple-element.82, bf16[1024,2048]{1,0:T(8,128)(2,1)} %all-gather.2.cloned.1.call-done.refs_3_, bf16[1024,2048]{1,0:T(8,128)(2,1)} %refs_2_.3), kind=kOutput, calls=%fused_computation.3 | convolution fusion | flops 4298113024 | bytes 12582912 | tf_op jit(solution)/shard_map/le,fe->lf/dot_general | solution.py:1566
  432.5 77.9 %shard_map.261 = (f32[128,2048]{1,0:T(8,128)}, bf16[1024,2048]{1,0:T(8,128)(2,1)}, bf16[128,2048]{1,0:T(8,128)(2,1)}, f32[8,2048]{1,0:T(8,128)}) custom-call(bf16[1024,1024]{1,0:T(8,128)(2,1)} %multiply_convert_fusion.refs_0_.refs_6_, bf16[1,2048,1024]{2,1,0:T(8,128)(2,1)} %bitcast.106, bf16[1024,1024]{1,0:T(8,128)(2,1)} %get-tuple-element.83.refs_2_, ...), custom_call_target="tpu_custom_call" | custom-call | tf_op jit(solution)/shard_map/pallas_call | solution.py:429
  510.4 0.8 slice.80
  511.3 1.0 broadcast_in_dim.10.refs_3_
  512.3 41.3 %shard_map.262 = (bf16[1024,768]{1,0:T(8,128)(2,1)}, bf16[256,2048]{1,0:T(8,128)(2,1)}, bf16[2048,1024]{1,0:T(8,128)(2,1)}) custom-call(bf16[128,2048]{1,0:T(8,128)(2,1)} %get-tuple-element.86.refs_0_, bf16[256,2048]{1,0:T(8,128)(2,1)} %refs_1_.4, bf16[1024,768]{1,0:T(8,128)(2,1)} %get-tuple-element.76.refs_0_.refs_2_, ...), custom_call_target="tpu_custom_call" | custom-call | tf_op jit(solution)/shard_map/pallas_call | solution.py:429
  553.6 52.4 %shard_map.263 = (f32[128,2048]{1,0:T(8,128)}, bf16[128,2048]{1,0:T(8,128)(2,1)}, f32[8,2048]{1,0:T(8,128)}, bf16[4,512,512]{2,1,0:T(8,128)(2,1)}, bf16[4,256,512]{2,1,0:T(8,128)(2,1)}) custom-call(bf16[1024,768]{1,0:T(8,128)(2,1)} %get-tuple-element.89.refs_0_.refs_4_, bf16[3,2048,256]{2,1,0:T(8,128)(2,1)} %refs_1_.5, ...), custom_call_target="tpu_custom_call" | custom-call | tf_op jit(solution)/shard_map/pallas_call | solution.py:429
  606.1 0.8 slice.79
  607.7 43.9 %shard_map.264 = (f32[4096,128]{1,0:T(8,128)}, bf16[2048,512]{1,0:T(8,128)(2,1)}, bf16[2048,768]{1,0:T(8,128)(2,1)}, bf16[4,512,512]{2,1,0:T(8,128)(2,1)}, f32[8,8,128]{2,1,0:T(8,128)}) custom-call(bf16[128,2048]{1,0:T(8,128)(2,1)} %get-tuple-element.95.refs_0_, bf16[1,512,2048]{2,1,0:T(8,128)(2,1)} %bitcast.112, ...), custom_call_target="tpu_custom_call" | custom-call | tf_op jit(solution)/shard_map/pallas_call | solution.py:429
  651.6 2.7 convert_element_type.82.refs_0_
  654.8 85.3 %shard_map.265 = (bf16[4096,128]{1,0:T(8,128)(2,1)}, bf16[4,256,1152]{2,1,0:T(8,128)(2,1)}, f32[8,128]{1,0:T(8,128)}, bf16[4,8,1,64,512]{4,3,2,1,0:T(8,128)(2,1)...) custom-call(bf16[4096,128]{1,0:T(8,128)(2,1)} %convert_element_type.82.refs_0_, bf16[3,384,1024]{2,1,0:T(8,128)(2,1)} %bitcast.110, ...), custom_call_target="tpu_custom_call" | custom-call | tf_op jit(solution)/shard_map/pallas_call | solution.py:429
  740.1 0.8 slice_bitcast_fusion.2
  741.5 101.1 %shard_map.266 = (bf16[4096,128]{1,0:T(8,128)(2,1)}, bf16[4,256,1152]{2,1,0:T(8,128)(2,1)}, f32[8,128]{1,0:T(8,128)}, bf16[4,8,1,32,1152]{4,3,2,1,0:T(8,128)(2,1...) custom-call(bf16[4096,128]{1,0:T(8,128)(2,1)} %get-tuple-element.105.refs_0_, ...), custom_call_target="tpu_custom_call" | custom-call | tf_op jit(solution)/shard_map/pallas_call | solution.py:429
  842.5 0.7 slice_bitcast_fusion.3
  843.5 1.7 fusion.35
  845.3 0.6 pad_maximum_fusion.4.refs_1_
  845.9 82.4 %shard_map.267 = (f32[9,256,128]{2,1,0:T(8,128)}, f32[32,16,128]{2,1,0:T(8,128)}, f32[9,256,128]{2,1,0:T(8,128)}, bf16[512,1024]{1,0:T(8,128)(2,1)}) custom-call(bf16[8,4,32,1152]{3,2,1,0:T(8,128)(2,1)} %bitcast.116, f32[16,128]{1,0:T(8,128)} %pad_maximum_fusion.4.refs_1_, bf16[4,8,1,32,1152]{4,3,2,1,0:T(8,128)(2,1)} %get-tuple-element.114.refs_2_, ...), custom_call_target="tpu_custom_call" | custom-call | tf_op jit(solution)/shard_map/pallas_call | solution.py:429
  928.3 1.0 reshape.229
  930.1 2.6 convert_reduce_fusion.6
  932.7 1.2 pad_maximum_fusion.1
  934.4 0.9 convert_reduce_fusion.3
  935.6 0.7 copy-done.2
  936.6 1.5 pad_maximum_fusion
  938.6 1.1 fusion.22
  939.7 2.0 fusion.4
  941.7 2.3 convert_reduce_fusion
  944.0 2.1 add_convert_fusion
  946.1 1.0 copy.59
  947.1 1.0 copy.60
  948.1 1.0 copy.61
  949.1 1.0 copy.62
  (81 shorter events, 8.4 us)
Async XLA Ops:
  7.2 1.6 copy-start
  7.2 3.2 copy-start.13
  7.2 3.2 copy-start.10
  7.2 415.4 %all-gather.2.cloned.1.call-start = ((), (), s32[]{:S(2)}) async-start(), calls=%async_computation.2 | async-start | bytes 4718592 | tf_op jit(solution)/shard_map/all_gather | solution.py:62
  128.7 75.6 %copy-start.11 = (bf16[8,512,128]{2,1,0:T(8,128)(2,1)S(1)}, bf16[8,512,128]{2,1,0:T(8,128)(2,1)}, u32[]{:S(2)}) copy-start(bf16[8,512,128]{2,1,0:T(8,128)(2,1)} %get-tuple-element.71) | copy-start | bytes 3145732
  206.1 2.0 copy-start.16
  252.1 39.3 %copy-start.19 = (s32[1,2]{1,0:T(1,128)S(1)}, s32[1,2]{1,0:T(1,128)}, u32[]{:S(2)}) copy-start(s32[1,2]{1,0:T(1,128)} %param.17) | copy-start | bytes 28
  291.3 652.7 %reduce-scatter.2.cloned.1.call-start = ((), (), s32[]{:S(2)}) async-start(), calls=%async_computation.1 | async-start | bytes 4718592 | tf_op jit(solution)/shard_map/reduce_scatter | solution.py:66
  607.1 0.6 copy-start.12
  651.5 2.7 copy-start.14
  741.5 101.8 %copy-start.18 = (f32[8,128]{1,0:T(8,128)S(1)}, f32[8,128]{1,0:T(8,128)}, u32[]{:S(2)}) copy-start(f32[8,128]{1,0:T(8,128)} %get-tuple-element.109) | copy-start | bytes 12292
  845.9 83.5 %copy-start.15 = (f32[4,16,128]{2,1,0:T(8,128)S(1)}, f32[4,16,128]{2,1,0:T(8,128)}, u32[]{:S(2)}) copy-start(f32[4,16,128]{2,1,0:T(8,128)} %get-tuple-element.120) | copy-start | bytes 98308
  845.9 83.5 %copy-start.17 = (f32[4,8,128]{2,1,0:T(8,128)S(1)}, f32[4,8,128]{2,1,0:T(8,128)}, u32[]{:S(2)}) copy-start(f32[4,8,128]{2,1,0:T(8,128)} %get-tuple-element.121) | copy-start | bytes 49156
  932.7 1.7 copy-start.6
  932.7 2.6 copy-start.3
  934.4 1.9 copy-start.2
  936.6 5.1 copy-start.1
  941.7 2.3 copy-start.7
  944.0 2.1 copy-start.9
  944.0 3.1 copy-start.5
  946.1 2.0 copy-start.4
  947.1 2.0 copy-start.8
Sparse Core Ops, SparseCore 0:
  291.4 83.2 all-gather.1
  420.1 64.9 reduce-scatter.1
